TPU v7x, 128 devices: a whole 4x4x4 slice. The times are simulated.
128 devices in a mesh: pat: 8 (over y, core), tile: 16 (over z, x).
Axes of the slice: x: 4, y: 4, z: 4, core: 2. Of those that a mesh axis runs over, the one named last changes fastest.
Arguments:
- intensity: float32 [128, 256, 256], P(('pat', 'tile')), may hold values from 0.25 to 36, as said below
- positions: int32 [128, 2], P(('pat', 'tile')), may hold values from 0 to 3840, as said below
- object_init: float32 [2, 4096, 1024], P(None, 'tile'), may hold values from -4 to 4
- probe_init: float32 [4, 2, 256, 256], replicated, may hold values from -3 to 3
Outputs:
- object_out: float32 [2, 4096, 1024], P(None, 'tile')
- probe_out: float32 [4, 2, 256, 256], replicated
Inputs may be any that keep to these rules, and one draw needn't show every extreme that they name: positions[i, 0] is pattern i's first object row and positions[i, 1] its first object column; every patch of 256 x 256 pixels lies inside the object, and pattern i's first row lies within 128 rows of ((i) % 16) * 256. `intensity`: positive measured intensities.
All inputs are finite; a program needn't handle non-finite values.
Results may differ from a plain program's by a relative error of at most 0.0001.
Values sent between devices are 32-bit elements; how exact they have to be, the bound alone decides.
No kernel may reach another device: no remote copies, remote signals or barrier semaphores. Data moves between devices by JAX's collectives and lax.ppermute only.
A program may use at most 128 MiB of HBM per device.

v0:
```python
import math

import jax
import jax.numpy as jnp
from jax import lax
from jax.sharding import PartitionSpec as P

ITERS = 2


FLOOR = 0.5
RIDGE = 1.0
PRECISE = lax.Precision.HIGHEST


def with_halo(block, sides, width):
    for axis, dim in sides:
        count = lax.axis_size(axis)
        forward = [(i, i + 1) for i in range(count - 1)]
        backward = [(target, source) for source, target in forward]
        low = lax.ppermute(
            lax.slice_in_dim(block, block.shape[dim] - width, None, axis=dim), axis, forward
        )
        high = lax.ppermute(lax.slice_in_dim(block, 0, width, axis=dim), axis, backward)
        block = jnp.concatenate([low, block, high], axis=dim)
    return block


def shifted(value, axis, steps):
    count = lax.axis_size(axis)
    first, last = (max(0, -steps), min(count, count - steps))
    return lax.ppermute(value, axis, [(source, source + steps) for source in range(first, last)])


def fourier_tables(size):
    indices = jnp.arange(size, dtype=jnp.int32)
    product = indices[:, None] * indices[None, :] % size
    angles = product.astype(jnp.float32) * (-2.0 * math.pi / size)
    factor = 1.0 / math.sqrt(size)
    return (jnp.cos(angles) * factor, jnp.sin(angles) * factor)


def transform(real_part, imag_part, cos_table, sin_table, orient):
    stacked = jnp.stack([real_part, imag_part])
    with_cos = jnp.einsum("zmab,bc->zmac", stacked, cos_table, precision=PRECISE)
    with_sin = jnp.einsum("zmab,bc->zmac", stacked, sin_table, precision=PRECISE)
    stacked = jnp.stack([with_cos[0] - orient * with_sin[1], with_cos[1] + orient * with_sin[0]])
    with_cos = jnp.einsum("ab,zmbc->zmac", cos_table, stacked, precision=PRECISE)
    with_sin = jnp.einsum("ab,zmbc->zmac", sin_table, stacked, precision=PRECISE)
    return (with_cos[0] - orient * with_sin[1], with_cos[1] + orient * with_sin[0])


def cut_patches(field, row_offsets, column_offsets, patch_size):
    pieces = [
        lax.dynamic_slice(
            field, (0, row_offsets[0], column_offsets[0]), (field.shape[0], patch_size, patch_size)
        )
    ]
    return jnp.stack(pieces, axis=1)


def accumulate_patch(field, addend, row, column):
    return lax.dynamic_update_slice(field, addend, (0, row, column))


def extend_object(field, margin):
    extended = with_halo(field, (("tile", 1),), margin)
    return extended


def fold_rims(extended_sum, margin):
    inner = extended_sum[:, margin:-margin]
    from_next = shifted(extended_sum[:, :margin], "tile", -1)
    from_prev = shifted(extended_sum[:, -margin:], "tile", 1)
    inner = inner.at[:, -margin:].add(from_next)
    return inner.at[:, :margin].add(from_prev)


def body(intensity, positions, object_init, probe_init):
    patch_size = intensity.shape[1]
    margin = patch_size // 2
    pattern_count = intensity.shape[0]
    tile_rows = object_init.shape[1]
    top_row = lax.axis_index("tile") * tile_rows - margin
    row_offsets = positions[:, 0] - top_row
    column_offsets = positions[:, 1]
    cos_table, sin_table = fourier_tables(patch_size)
    object_now = object_init
    probe_now = probe_init
    for iteration in range(ITERS):
        extended = extend_object(object_now, margin)
        patches = cut_patches(extended, row_offsets, column_offsets, patch_size)
        probe_real = probe_now[:, 0][None]
        probe_imag = probe_now[:, 1][None]
        patch_real = patches[0][:, None]
        patch_imag = patches[1][:, None]
        wave_real = (probe_real * patch_real - probe_imag * patch_imag).reshape(
            -1, patch_size, patch_size
        )
        wave_imag = (probe_real * patch_imag + probe_imag * patch_real).reshape(
            -1, patch_size, patch_size
        )
        far_real, far_imag = transform(wave_real, wave_imag, cos_table, sin_table, 1.0)
        far_real = far_real.reshape(pattern_count, -1, patch_size, patch_size)
        far_imag = far_imag.reshape(pattern_count, -1, patch_size, patch_size)
        modelled = jnp.sum(far_real * far_real + far_imag * far_imag, axis=1)
        rescale = (jnp.sqrt(intensity / jnp.maximum(modelled, FLOOR)) - 1.0)[:, None]
        diff_real, diff_imag = transform(
            (rescale * far_real).reshape(-1, patch_size, patch_size),
            (rescale * far_imag).reshape(-1, patch_size, patch_size),
            cos_table,
            sin_table,
            -1.0,
        )
        diff_real = diff_real.reshape(far_real.shape)
        diff_imag = diff_imag.reshape(far_imag.shape)
        object_real = jnp.sum(probe_real * diff_real + probe_imag * diff_imag, axis=1)
        object_imag = jnp.sum(probe_real * diff_imag - probe_imag * diff_real, axis=1)
        power = jnp.sum(probe_real * probe_real + probe_imag * probe_imag, axis=1)[0]
        summand_terms = jnp.stack([object_real[0], object_imag[0], power])
        collected_values = jnp.zeros((3,) + extended.shape[1:], jnp.float32)
        collected_values = accumulate_patch(
            collected_values, summand_terms, row_offsets[0], column_offsets[0]
        )
        folded = fold_rims(collected_values, margin)
        grad_real = jnp.sum(patch_real * diff_real + patch_imag * diff_imag, axis=0)
        grad_imag = jnp.sum(patch_real * diff_imag - patch_imag * diff_real, axis=0)
        grad_probe = jnp.stack([grad_real, grad_imag], axis=1)
        illum_probe = jnp.sum(patches[0] * patches[0] + patches[1] * patches[1], axis=0)
        probe_total, illum_total = lax.psum((grad_probe, illum_probe), ("pat", "tile"))
        dir_probe = probe_total / (illum_total + RIDGE)
        totals = lax.psum(folded, "pat")
        direction = totals[:2] / (totals[2:3] + RIDGE)
        ext_dir = with_halo(direction, (("tile", 1),), margin)
        dir_patches = cut_patches(ext_dir, row_offsets, column_offsets, patch_size)
        dir_real = dir_patches[0][:, None]
        dir_imag = dir_patches[1][:, None]
        along_obj_real = probe_real * dir_real - probe_imag * dir_imag
        along_obj_imag = probe_real * dir_imag + probe_imag * dir_real
        step_real = dir_probe[:, 0][None]
        step_imag = dir_probe[:, 1][None]
        along_pr_real = patch_real * step_real - patch_imag * step_imag
        along_pr_imag = patch_real * step_imag + patch_imag * step_real
        partial_sums = jnp.stack(
            [
                jnp.sum(along_obj_real * along_obj_real + along_obj_imag * along_obj_imag),
                jnp.sum(along_obj_real * along_pr_real + along_obj_imag * along_pr_imag),
                jnp.sum(along_pr_real * along_pr_real + along_pr_imag * along_pr_imag),
                jnp.sum(along_obj_real * diff_real + along_obj_imag * diff_imag),
                jnp.sum(along_pr_real * diff_real + along_pr_imag * diff_imag),
            ]
        )
        sums = lax.psum(partial_sums, ("pat", "tile"))
        object_power, cross_term, probe_power, object_pull, probe_pull = (
            sums[0],
            sums[1],
            sums[2],
            sums[3],
            sums[4],
        )
        ridge_term = 0.1 * (object_power + probe_power) + 1e-06
        determinant = (object_power + ridge_term) * (
            probe_power + ridge_term
        ) - cross_term * cross_term
        object_step = (
            (probe_power + ridge_term) * object_pull - cross_term * probe_pull
        ) / determinant
        probe_step = (
            (object_power + ridge_term) * probe_pull - cross_term * object_pull
        ) / determinant
        object_now = object_now + object_step * direction
        probe_now = probe_now + probe_step * dir_probe
    return (object_now, probe_now)


def solution(mesh):
    placed = (P(("pat", "tile"), None, None), P(("pat", "tile"), None), P(None, "tile", None), P())
    return jax.shard_map(
        body, mesh=mesh, in_specs=placed, out_specs=(P(None, "tile", None), P()), check_vma=False
    )
```

profile of v0, /device:TPU:1, one launch (start us, length us, event | category | flops | bytes accessed | tf_op | source)
XLA Modules:
  0.0 928.7 jit_solution(8936331376989705411)
XLA Ops:
  7.2 3.1 fusion.179
  10.4 4.0 collective-permute-start
  18.8 17.6 %collective-permute-done = f32[2,128,1024]{2,1,0:T(8,128)S(1)} collective-permute-done((f32[2,128,1024]{2,1,0:T(8,128)}, f32[2,128,1024]{2,1,0:T(8,128)S(1)}, u32[]{:S(2)}, u32[]{:S(2)}) %collective-permute-start) | collective-permute-done | bytes 1048608 | tf_op jit(solution)/shard_map/ppermute | solution.py:21
  37.4 2.9 collective-permute-done.1
  42.9 2.9 fusion.15
  45.8 2.9 fusion.14
  49.0 4.4 fusion.16
  53.4 4.7 fusion.17
  58.8 4.4 fusion.11
  63.2 16.0 %fusion.10 = f32[2,4,256,256]{3,2,1,0:T(8,128)S(1)} fusion(f32[1,4,256,256]{2,3,1,0:T(8,128)S(1)} %get-tuple-element.87, f32[1,4,256,256]{2,3,1,0:T(8,128)S(1)} %get-tuple-element.86), kind=kOutput, calls=%fused_computation.38 | convolution fusion | flops 1612120064 | bytes 4194304 | tf_op jit(solution)/shard_map/zmab,bc->zmac/dot_general | solution.py:46
  79.5 3.0 fusion.18
  82.5 3.0 fusion.19
  89.4 3.5 broadcast.492.clone
  92.8 9.2 dynamic_update_slice.6
  102.1 2.3 fusion.175
  105.8 4.1 collective-permute-start.3
  109.9 1.9 slice.450
  111.8 29.2 %collective-permute-done.2 = f32[3,128,1024]{2,1,0:T(8,128)S(1)} collective-permute-done((f32[3,128,1024]{2,1,0:T(8,128)S(1)}, f32[3,128,1024]{2,1,0:T(8,128)S(1)}, u32[]{:S(2)}, u32[]{:S(2)}) %collective-permute-start.2) | collective-permute-done | bytes 1572896 | tf_op jit(solution)/shard_map/ppermute | solution.py:32
  142.4 2.8 fusion.26
  145.3 3.0 pad_maximum_fusion.4
  148.3 72.6 %all-reduce.7.cloned.1.call-done = f32[3,256,1024]{2,1,0:T(8,128)} async-done(((f32[3,256,1024]{2,1,0:T(8,128)}), f32[3,256,1024]{2,1,0:T(8,128)}) %all-reduce.7.cloned.1.call-update) | async-done | bytes 3145744 | tf_op jit(solution)/shard_map/psum | solution.py:132
  222.3 2.3 slice_divide_fusion.1
  224.6 1.6 fusion.178
  226.6 4.1 collective-permute-start.4
  232.0 152.6 %all-reduce.13.cloned.1.call-done = (f32[4,2,256,256]{3,2,0,1:T(8,128)}, f32[256,256]{1,0:T(8,128)}) async-done(((f32[4,2,256,256]{3,2,0,1:T(8,128)}, f32[256,256]{1,0:T(8,128)}), (f32[4,2,256,256]{3,2,0,1:T(8,128)}, f32[256,256]{1,0:T(8,128)})) %all-reduce.13.cloned.1.call-update) | async-done | bytes 2359312 | tf_op jit(solution)/shard_map/psum | solution.py:130
  385.5 1.9 broadcast_divide_fusion.1
  390.3 1.7 add_reduce_fusion.8
  391.9 3.2 stack.109
  395.1 64.0 %psum.59 = f32[5]{0:T(128)S(1)} all-reduce(f32[5]{0:T(128)S(1)} %stack.109), channel_id=1, replica_groups=mesh['pat'=8,'tile'=16] {'pat','tile'}, use_global_device_ids=true, to_apply=%region_12.13 | all-reduce | flops 5 | bytes 40 | tf_op jit(solution)/shard_map/psum | solution.py:153
  465.3 2.5 multiply_add_fusion.3
  467.8 1.6 fusion.177
  469.8 2.8 collective-permute-start.6
  472.6 1.7 collective-permute-start.7
  476.2 2.7 multiply_add_fusion.2
  478.9 15.8 %collective-permute-done.6 = f32[2,128,1024]{2,1,0:T(8,128)S(1)} collective-permute-done((f32[2,128,1024]{2,1,0:T(8,128)}, f32[2,128,1024]{2,1,0:T(8,128)S(1)}, u32[]{:S(2)}, u32[]{:S(2)}) %collective-permute-start.6) | collective-permute-done | bytes 1048608 | tf_op jit(solution)/shard_map/ppermute | solution.py:21
  495.7 2.9 collective-permute-done.7
  500.8 2.9 fusion.7
  503.7 2.9 fusion.6
  506.9 4.4 fusion.20
  511.4 4.6 fusion.21
  517.3 4.4 fusion.3
  521.7 4.6 fusion.2
  526.7 3.0 fusion.22
  529.7 3.0 fusion.23
  534.0 1.6 add_reduce_fusion.6
  536.6 3.5 broadcast.492
  540.1 9.2 dynamic_update_slice.7
  549.3 2.3 fusion.174
  553.0 4.1 collective-permute-start.9
  557.1 1.9 slice.485
  559.0 29.5 %collective-permute-done.8 = f32[3,128,1024]{2,1,0:T(8,128)S(1)} collective-permute-done((f32[3,128,1024]{2,1,0:T(8,128)S(1)}, f32[3,128,1024]{2,1,0:T(8,128)S(1)}, u32[]{:S(2)}, u32[]{:S(2)}) %collective-permute-start.8) | collective-permute-done | bytes 1572896 | tf_op jit(solution)/shard_map/ppermute | solution.py:32
  589.9 2.8 fusion.24
  592.9 3.0 pad_maximum_fusion.9
  595.9 69.3 %all-reduce.9.cloned.1.call-done = f32[3,256,1024]{2,1,0:T(8,128)} async-done(((f32[3,256,1024]{2,1,0:T(8,128)}), f32[3,256,1024]{2,1,0:T(8,128)}) %all-reduce.9.cloned.1.call-update) | async-done | bytes 3145744 | tf_op jit(solution)/shard_map/psum | solution.py:132
  666.4 2.3 slice_divide_fusion
  668.7 1.7 fusion.176
  670.7 4.3 collective-permute-start.10
  676.3 152.8 %all-reduce.11.cloned.1.call-done = (f32[4,2,256,256]{3,2,0,1:T(8,128)}, f32[256,256]{1,0:T(8,128)}) async-done(((f32[4,2,256,256]{3,2,0,1:T(8,128)}, f32[256,256]{1,0:T(8,128)}), (f32[4,2,256,256]{3,2,0,1:T(8,128)}, f32[256,256]{1,0:T(8,128)})) %all-reduce.11.cloned.1.call-update) | async-done | bytes 2359312 | tf_op jit(solution)/shard_map/psum | solution.py:130
  830.8 1.9 broadcast_divide_fusion
  836.7 1.7 add_reduce_fusion
  838.4 3.2 stack.123
  841.6 64.0 %psum.63 = f32[5]{0:T(128)S(1)} all-reduce(f32[5]{0:T(128)S(1)} %stack.123), channel_id=1, replica_groups=mesh['pat'=8,'tile'=16] {'pat','tile'}, use_global_device_ids=true, to_apply=%region_25.26 | all-reduce | flops 5 | bytes 40 | tf_op jit(solution)/shard_map/psum | solution.py:153
  913.7 1.9 multiply_add_fusion
  918.2 3.5 multiply_add_fusion.1
  (122 shorter events, 43.7 us)
Async XLA Ops:
  7.2 8.5 copy-start.31
  7.2 10.9 %copy-start.30 = (f32[1,256,256]{2,1,0:T(8,128)S(1)}, f32[1,256,256]{2,1,0:T(8,128)}, u32[]{:S(2)}) copy-start(f32[1,256,256]{2,1,0:T(8,128)} %param.12) | copy-start | bytes 786436
  7.2 213.8 %all-reduce.7.cloned.1.call-start = ((), (), s32[]{:S(2)}) async-start(), calls=%async_computation | async-start | bytes 6291456 | tf_op jit(solution)/shard_map/psum | solution.py:132
  10.4 26.1 %collective-permute-start = (f32[2,128,1024]{2,1,0:T(8,128)}, f32[2,128,1024]{2,1,0:T(8,128)S(1)}, u32[]{:S(2)}, u32[]{:S(2)}) collective-permute-start(f32[2,128,1024]{2,1,0:T(8,128)} %get-tuple-element.117), channel_id=1, source_target_pairs={{0,1},{1,2},{2,3},{3,4},{4,5},{5,6},{6,7},{7,8},{8,9},{9,10},{10,1... | collective-permute-start | bytes 3145736 | tf_op jit(solution)/shard_map/ppermute | solution.py:21
  14.4 25.9 %collective-permute-start.1 = (f32[2,128,1024]{2,1,0:T(8,128)}, f32[2,128,1024]{2,1,0:T(8,128)}, u32[]{:S(2)}, u32[]{:S(2)}) collective-permute-start(f32[2,128,1024]{2,1,0:T(8,128)} %get-tuple-element.116), channel_id=1, source_target_pairs={{1,0},{2,1},{3,2},{4,3},{5,4},{6,5},{7,6},{8,7},{9,8},{10,9},{11,1... | collective-permute-start | bytes 3145736 | tf_op jit(solution)/shard_map/ppermute | solution.py:24
  18.2 40.2 %copy-start.22 = (f32[1,256,256]{1,2,0:T(8,128)}, f32[1,256,256]{1,2,0:T(8,128)S(1)}, u32[]{:S(2)}) copy-start(f32[1,256,256]{1,2,0:T(8,128)S(1)} %copy.32) | copy-start | bytes 786436
  18.8 23.8 %copy-start = (f32[4,2,256,256]{3,2,1,0:T(8,128)S(1)}, f32[4,2,256,256]{3,2,1,0:T(8,128)}, u32[]{:S(2)}) copy-start(f32[4,2,256,256]{3,2,1,0:T(8,128)} %param.15) | copy-start | bytes 6291460
  36.4 1.0 copy-start.28
  42.6 44.2 %copy-start.18 = (f32[256,256]{1,0:T(8,128)}, f32[256,256]{1,0:T(8,128)S(1)}, u32[]{:S(2)}) copy-start(f32[256,256]{1,0:T(8,128)S(1)} %get-tuple-element.127) | copy-start | bytes 786436
  86.9 1.6 copy-start.13
  102.1 7.8 copy-start.5
  104.3 36.6 %collective-permute-start.2 = (f32[3,128,1024]{2,1,0:T(8,128)S(1)}, f32[3,128,1024]{2,1,0:T(8,128)S(1)}, u32[]{:S(2)}, u32[]{:S(2)}) collective-permute-start(f32[3,128,1024]{2,1,0:T(8,128)S(1)} %get-tuple-element.83), channel_id=1, source_target_pairs={{1,0},{2,1},{3,2},{4,3},{5,4},{6,5},{7,6},{8,7},{9,8},{10,9},{11,1... | collective-permute-start | bytes 4718600 | tf_op jit(solution)/shard_map/ppermute | solution.py:32
  105.8 36.6 %collective-permute-start.3 = (f32[3,128,1024]{2,1,0:T(8,128)S(1)}, f32[3,128,1024]{2,1,0:T(8,128)S(1)}, u32[]{:S(2)}, u32[]{:S(2)}) collective-permute-start(f32[3,128,1024]{2,1,0:T(8,128)S(1)} %get-tuple-element.82), channel_id=1, source_target_pairs={{0,1},{1,2},{2,3},{3,4},{4,5},{5,6},{6,7},{7,8},{8,9},{9,10},{10,1... | collective-permute-start | bytes 4718600 | tf_op jit(solution)/shard_map/ppermute | solution.py:32
  145.2 239.3 %all-reduce.13.cloned.1.call-start = ((), (), s32[]{:S(2)}) async-start(), calls=%async_computation.3 | async-start | bytes 4718592 | tf_op jit(solution)/shard_map/psum | solution.py:130
  148.3 516.8 %all-reduce.9.cloned.1.call-start = ((), (), s32[]{:S(2)}) async-start(), calls=%async_computation.1 | async-start | bytes 6291456 | tf_op jit(solution)/shard_map/psum | solution.py:132
  222.3 2.3 copy-start.17
  224.6 2.0 copy-start.8
  226.6 160.9 %collective-permute-start.4 = (f32[2,128,1024]{2,1,0:T(8,128)}, f32[2,128,1024]{2,1,0:T(8,128)}, u32[]{:S(2)}, u32[]{:S(2)}) collective-permute-start(f32[2,128,1024]{2,1,0:T(8,128)} %get-tuple-element.114), channel_id=1, source_target_pairs={{0,1},{1,2},{2,3},{3,4},{4,5},{5,6},{6,7},{7,8},{8,9},{9,10},{10,1... | collective-permute-start | bytes 3145736 | tf_op jit(solution)/shard_map/ppermute | solution.py:21
  230.7 156.8 %collective-permute-start.5 = (f32[2,128,1024]{2,1,0:T(8,128)}, f32[2,128,1024]{2,1,0:T(8,128)}, u32[]{:S(2)}, u32[]{:S(2)}) collective-permute-start(f32[2,128,1024]{2,1,0:T(8,128)} %get-tuple-element.113), channel_id=1, source_target_pairs={{1,0},{2,1},{3,2},{4,3},{5,4},{6,5},{7,6},{8,7},{9,8},{10,9},{11,1... | collective-permute-start | bytes 3145736 | tf_op jit(solution)/shard_map/ppermute | solution.py:24
  385.5 2.0 copy-start.24
  385.5 2.3 copy-start.9
  387.5 1.6 copy-start.19
  389.1 1.2 copy-start.14
  390.3 75.0 %copy-start.10 = (f32[2,256,1024]{2,1,0:T(8,128)S(1)}, f32[2,256,1024]{2,1,0:T(8,128)}, u32[]{:S(2)}) copy-start(f32[2,256,1024]{2,1,0:T(8,128)} %param.14) | copy-start | bytes 6291460
  467.8 2.0 copy-start.1
  467.8 8.4 copy-start.25
  469.8 24.9 %collective-permute-start.6 = (f32[2,128,1024]{2,1,0:T(8,128)}, f32[2,128,1024]{2,1,0:T(8,128)S(1)}, u32[]{:S(2)}, u32[]{:S(2)}) collective-permute-start(f32[2,128,1024]{2,1,0:T(8,128)} %get-tuple-element.112), channel_id=1, source_target_pairs={{0,1},{1,2},{2,3},{3,4},{4,5},{5,6},{6,7},{7,8},{8,9},{9,10},{10,1... | collective-permute-start | bytes 3145736 | tf_op jit(solution)/shard_map/ppermute | solution.py:21
  472.6 26.0 %collective-permute-start.7 = (f32[2,128,1024]{2,1,0:T(8,128)}, f32[2,128,1024]{2,1,0:T(8,128)}, u32[]{:S(2)}, u32[]{:S(2)}) collective-permute-start(f32[2,128,1024]{2,1,0:T(8,128)} %get-tuple-element.111), channel_id=1, source_target_pairs={{1,0},{2,1},{3,2},{4,3},{5,4},{6,5},{7,6},{8,7},{9,8},{10,9},{11,1... | collective-permute-start | bytes 3145736 | tf_op jit(solution)/shard_map/ppermute | solution.py:24
  476.2 22.4 %copy-start.2 = (f32[2,256,1024]{2,1,0:T(8,128)S(1)}, f32[2,256,1024]{2,1,0:T(8,128)}, u32[]{:S(2)}) copy-start(f32[2,256,1024]{2,1,0:T(8,128)} %copy-done.1) | copy-start | bytes 6291460
  494.7 1.0 copy-start.29
  500.6 33.5 %copy-start.20 = (f32[256,256]{1,0:T(8,128)}, f32[256,256]{1,0:T(8,128)S(1)}, u32[]{:S(2)}) copy-start(f32[256,256]{1,0:T(8,128)S(1)} %get-tuple-element.122) | copy-start | bytes 786436
  516.0 1.0 copy-start.23
  534.0 1.6 copy-start.11
  549.3 7.8 copy-start.4
  551.6 36.9 %collective-permute-start.8 = (f32[3,128,1024]{2,1,0:T(8,128)S(1)}, f32[3,128,1024]{2,1,0:T(8,128)S(1)}, u32[]{:S(2)}, u32[]{:S(2)}) collective-permute-start(f32[3,128,1024]{2,1,0:T(8,128)S(1)} %get-tuple-element.81), channel_id=1, source_target_pairs={{1,0},{2,1},{3,2},{4,3},{5,4},{6,5},{7,6},{8,7},{9,8},{10,9},{11,1... | collective-permute-start | bytes 4718600 | tf_op jit(solution)/shard_map/ppermute | solution.py:32
  553.0 36.9 %collective-permute-start.9 = (f32[3,128,1024]{2,1,0:T(8,128)S(1)}, f32[3,128,1024]{2,1,0:T(8,128)S(1)}, u32[]{:S(2)}, u32[]{:S(2)}) collective-permute-start(f32[3,128,1024]{2,1,0:T(8,128)S(1)} %get-tuple-element.80), channel_id=1, source_target_pairs={{0,1},{1,2},{2,3},{3,4},{4,5},{5,6},{6,7},{7,8},{8,9},{9,10},{10,1... | collective-permute-start | bytes 4718600 | tf_op jit(solution)/shard_map/ppermute | solution.py:32
  592.8 236.3 %all-reduce.11.cloned.1.call-start = ((), (), s32[]{:S(2)}) async-start(), calls=%async_computation.2 | async-start | bytes 4718592 | tf_op jit(solution)/shard_map/psum | solution.py:130
  666.4 2.3 copy-start.15
  668.7 2.0 copy-start.6
  670.7 162.3 %collective-permute-start.10 = (f32[2,128,1024]{2,1,0:T(8,128)}, f32[2,128,1024]{2,1,0:T(8,128)}, u32[]{:S(2)}, u32[]{:S(2)}) collective-permute-start(f32[2,128,1024]{2,1,0:T(8,128)} %get-tuple-element.109), channel_id=1, source_target_pairs={{0,1},{1,2},{2,3},{3,4},{4,5},{5,6},{6,7},{7,8},{8,9},{9,10},{10,1... | collective-permute-start | bytes 3145736 | tf_op jit(solution)/shard_map/ppermute | solution.py:21
  675.0 158.0 %collective-permute-start.11 = (f32[2,128,1024]{2,1,0:T(8,128)}, f32[2,128,1024]{2,1,0:T(8,128)}, u32[]{:S(2)}, u32[]{:S(2)}) collective-permute-start(f32[2,128,1024]{2,1,0:T(8,128)} %get-tuple-element.108), channel_id=1, source_target_pairs={{1,0},{2,1},{3,2},{4,3},{5,4},{6,5},{7,6},{8,7},{9,8},{10,9},{11,1... | collective-permute-start | bytes 3145736 | tf_op jit(solution)/shard_map/ppermute | solution.py:24
  830.1 0.7 copy-start.26
  830.8 1.9 copy-start.21
  832.7 1.6 copy-start.7
  835.5 1.2 copy-start.12
  836.7 77.0 %copy-start.27 = (f32[256,256]{1,0:T(8,128)S(1)}, f32[256,256]{1,0:T(8,128)}, u32[]{:S(2)}) copy-start(f32[256,256]{1,0:T(8,128)} %copy-done.26) | copy-start | bytes 786436
  915.6 2.4 copy-start.3
  915.6 2.6 copy-start.16
Sparse Core Ops, SparseCore 0:
  145.3 75.5 all-reduce.6
  226.4 158.0 all-reduce.12
  592.9 72.1 all-reduce.8
  671.2 157.8 all-reduce.10
where the time goes:
time: 940 us; the launch traced here: 929 us
  waiting for transfers between devices  545 us (58%)
  blocking collectives  128 us (14%)
  matrix products  70.9 us (8%)
  local copies, waits for them, and re-layouts  60.4 us (6%)
  other arithmetic  60 us (6%)
  between operations  32.2 us (3%)
  starting transfers between devices  32 us (3%)
    psum x2, waiting for transfers between devices, body(): lax.psum((grad_probe, illum_probe), ('pat', 'tile'))  305 us
    psum x2, waiting for transfers between devices, body(): totals = lax.psum(folded, 'pat')  142 us
    psum x2, blocking collectives, body(): sums = lax.psum(partial_sums, ('pat', 'tile'))  128 us
    ppermute x4, waiting for transfers between devices, shifted(): lax.ppermute(value, axis, [(source, source + steps) for source in range(f...  58.7 us
    ppermute x4, waiting for transfers between devices, with_halo(): lax.ppermute(lax.slice_in_dim(block, block.shape[dim] - width, None, axis...  33.4 us
    dot_general x4, matrix products, transform(): jnp.einsum('zmab,bc->zmac', stacked, sin_table, precision=PRECISE)  26.3 us
  transfers between devices with their start and end apart: 16, of which 10 were waited for; matrix products, arithmetic and copies ran while one was open for 4% of the time, Pallas kernels for 0%

commit v1 on v0

v1 whole, which is shorter than its diff:
```python
import math

import jax
import jax.numpy as jnp
import ml_dtypes
import numpy as np
from jax import lax
from jax.experimental import pallas as pl
from jax.experimental.pallas import tpu as pltpu
from jax.sharding import PartitionSpec as P

ITERS = 2
FLOOR = 0.5
RIDGE = 1.0
N = 256
H = 128
F32 = jnp.float32
BF16 = jnp.bfloat16
BOTH = ("pat", "tile")
VMEM = pl.BlockSpec(memory_space=pltpu.VMEM)
SMEM = pl.BlockSpec(memory_space=pltpu.SMEM)


def real_tables():
    near = np.arange(H)[:, None]
    far = np.arange(H)[None, :]
    found = []
    for parity in range(2):
        angle = -2.0 * math.pi * ((near * (2 * far + parity)) % N) / N
        real, imag = np.cos(angle) / 16.0, np.sin(angle) / 16.0
        found.append(np.block([[real, imag], [-imag, real]]))
    even, odd = found
    out = []
    for table in (even, odd, even.T, odd.T):
        high = table.astype(np.float32).astype(ml_dtypes.bfloat16)
        low = (table - high.astype(np.float64)).astype(np.float32).astype(ml_dtypes.bfloat16)
        out.append(np.stack([high, low]))
    return np.stack(out)


def halves(value):
    high = value.astype(BF16)
    return high, (value - high.astype(F32)).astype(BF16)


def dot(left, right):
    return jnp.dot(left, right, preferred_element_type=F32)


def times_table(value, table):
    high, low = halves(value)
    return dot(high, table[0]) + (dot(low, table[0]) + dot(high, table[1]))


def table_times(table, value):
    high, low = halves(value)
    return dot(table[0], high) + (dot(table[0], low) + dot(table[1], high))


def patterns_kernel(first, *refs):
    if first:
        geo, patch, probe, measured, tab = refs[:5]
        keep, send, mine, other, psi, model, obj = refs[5:]
        patch_now, probe_now = patch, probe
    else:
        geo, steps, patch, probe, measured, tab, dirp, dprobe = refs[:8]
        patch_now, probe_now, keep, send, mine, other, psi, model, obj = refs[8:]
        for part in range(2):
            patch_now[part] = patch[part] + steps[0] * dirp[part]
    e0, y, c = geo[0], geo[1], geo[2]
    first_core = c == 0

    model[...] = jnp.zeros_like(model)
    obj[...] = jnp.zeros_like(obj)

    def gather(plane, value):
        obj[plane, 0] += value[:, :H]
        obj[plane, 1] += value[:, H:]

    def forward(k, carry):
        if not first:
            for part in range(2):
                probe_now[k, part] = probe[k, part] + steps[1] * dprobe[k, part]
        pr, pi = probe_now[k, 0], probe_now[k, 1]
        orr, oi = patch_now[0], patch_now[1]
        gather(2, pr * pr + pi * pi)
        xr = pr * orr - pi * oi
        xi = pr * oi + pi * orr
        even = times_table(
            jnp.concatenate([xr[:, :H] + xr[:, H:], xi[:, :H] + xi[:, H:]], axis=1), tab.at[0]
        )
        odd = times_table(
            jnp.concatenate([xr[:, :H] - xr[:, H:], xi[:, :H] - xi[:, H:]], axis=1), tab.at[1]
        )
        re = jnp.concatenate([even[:, :H], odd[:, :H]], axis=1)
        im = jnp.concatenate([even[:, H:], odd[:, H:]], axis=1)
        for row, sign in ((0, 1.0), (1, -1.0)):
            folded = jnp.concatenate(
                [re[:H] + sign * re[H:], im[:H] + sign * im[H:]], axis=0
            )
            far = table_times(tab.at[2 + row], folded)
            psi[k, row] = far
            model[row] += far[:H] * far[:H] + far[H:] * far[H:]
        return carry

    lax.fori_loop(0, 4, forward, 0)
    for row in range(2):
        model[row] = jnp.sqrt(measured[row] / jnp.maximum(model[row], FLOOR)) - 1.0

    def put(plane, value):
        low = value[:H].reshape(16, 8, N)
        high = value[H:].reshape(16, 8, N)
        keep[:, plane] = jnp.where(first_core, low, high)
        send[:, plane] = jnp.where(first_core, high, low)

    def backward(k, carry):
        parts = []
        for row in range(2):
            scale = model[row]
            weighted = psi[k, row] * jnp.concatenate([scale, scale], axis=0)
            parts.append(table_times(tab.at[row], weighted))
        ee, oo = parts
        re = jnp.concatenate([ee[:H] + oo[:H], ee[:H] - oo[:H]], axis=0)
        im = jnp.concatenate([ee[H:] + oo[H:], ee[H:] - oo[H:]], axis=0)
        even = times_table(jnp.concatenate([re[:, :H], im[:, :H]], axis=1), tab.at[2])
        odd = times_table(jnp.concatenate([re[:, H:], im[:, H:]], axis=1), tab.at[3])
        dr = jnp.concatenate([even[:, :H] + odd[:, :H], even[:, :H] - odd[:, :H]], axis=1)
        di = jnp.concatenate([even[:, H:] + odd[:, H:], even[:, H:] - odd[:, H:]], axis=1)
        pr, pi = probe_now[k, 0], probe_now[k, 1]
        orr, oi = patch_now[0], patch_now[1]
        gather(0, pr * dr + pi * di)
        gather(1, pr * di - pi * dr)
        put(2 * k, orr * dr + oi * di)
        put(2 * k + 1, orr * di - oi * dr)
        return carry

    lax.fori_loop(0, 4, backward, 0)
    orr, oi = patch_now[0], patch_now[1]
    put(8, orr * orr + oi * oi)
    for s in range(4):
        for which, dest in ((c, mine), (1 - c, other)):
            owner = 2 * lax.rem(y + s, 4) + which
            start = lax.rem(owner - e0 + 1024, 8)
            for plane in range(3):
                for half in range(2):
                    rows = obj[plane, half, pl.ds(start, 32, stride=8), :]
                    dest[s, plane, :, half * H : half * H + H] = rows


def place_of(geo, owner, pattern):
    e0 = geo[pattern]
    col = geo[8 + pattern]
    start = lax.rem(owner - e0 + 1024, 8)
    row = lax.shift_right_logical(e0 + start - owner, 3)
    block = lax.shift_right_logical(col, 7)
    base = pl.multiple_of(lax.shift_right_logical(row, 3) * 8, 8)
    return base, lax.rem(row, 8), pl.multiple_of(block * 128, 128), lax.rem(col, 128)


def place_kernel(geo, mine, part, b1, b2, b3, low, high, acc):
    y, c = geo[16], geo[17]
    owner = 2 * y + c
    acc[...] = jnp.zeros_like(acc)
    blank = jnp.zeros((32, 128), F32)
    under = jnp.zeros((8, 384), F32)
    for s in range(4):
        for which in range(2):
            pattern = 2 * lax.rem(y - s + 4, 4) + (c if which == 0 else 1 - c)
            row, turn, block, shift = place_of(geo, owner, pattern)
            for plane in range(3):
                if s == 0:
                    piece = (mine, part)[which][0, plane]
                else:
                    piece = (b1, b2, b3)[s - 1][which, plane]
                wide = pltpu.roll(jnp.concatenate([piece, blank], axis=1), shift, axis=1)
                wide = pltpu.roll(jnp.concatenate([wide, under], axis=0), turn, axis=0)
                acc[plane, pl.ds(row, 40), pl.ds(block, 384)] += wide
    low[...] = acc[:, :32, :1024]
    high[...] = acc[:, 32:64, :1024]


def direction_kernel(geo, low, high, above, below, band, sums, r0, r1, r2, r3, wide):
    y, c = geo[16], geo[17]
    owner = 2 * y + c
    wide[...] = jnp.zeros_like(wide)
    total_a = jnp.zeros((16, 1024), F32)
    total_n = jnp.zeros((16, 1024), F32)
    for at, (own, came) in enumerate(((low, above), (high, below))):
        illum = own[2] + came[2]
        scale = 1.0 / (illum + RIDGE)
        real = (own[0] + came[0]) * scale
        imag = (own[1] + came[1]) * scale
        rows = slice(32 * at, 32 * at + 32)
        wide[0, rows, :1024] = real
        wide[1, rows, :1024] = imag
        inner = slice(16, 32) if at == 0 else slice(0, 16)
        real, imag, illum = real[inner], imag[inner], illum[inner]
        band[0, 16 * at : 16 * at + 16] = real
        band[1, 16 * at : 16 * at + 16] = imag
        size = real * real + imag * imag
        total_n += size
        total_a += illum * size
    sums[0, 0] = jnp.sum(total_a)
    sums[0, 1] = jnp.sum(total_n)
    for s, dest in enumerate((r0, r1, r2, r3)):
        for which in range(2):
            pattern = 2 * lax.rem(y + s, 4) + (c if which == 0 else 1 - c)
            row, turn, block, shift = place_of(geo, owner, pattern)
            for part in range(2):
                piece = wide[part, pl.ds(row, 40), pl.ds(block, 384)]
                piece = pltpu.roll(piece, lax.rem(40 - turn, 40), axis=0)[:32]
                dest[which, part] = pltpu.roll(piece, lax.rem(384 - shift, 384), axis=1)[:, :N]


def cross_kernel(geo, r0, r1, r2, r3, oth, dmine, doth, patch, probe, dirp, dprobe, sums, rows):
    y, c = geo[16], geo[17]
    e0 = geo[2 * y + c]
    for s in range(4):
        for which in range(2):
            owner = 2 * lax.rem(y - s + 4, 4) + (c if which == 0 else 1 - c)
            start = lax.rem(owner - e0 + 1024, 8)
            for part in range(2):
                if which == 0:
                    piece = (r0, r1, r2, r3)[s][0, part]
                else:
                    piece = oth[s, part]
                for half in range(2):
                    at = pl.ds(start, 32, stride=8)
                    rows[part, half, at, :] = piece[:, half * H : half * H + H]
    for part in range(2):
        for half in range(2):
            dirp[part, :, half * H : half * H + H] = rows[part, half]
    first_core = c == 0
    s_real = jnp.zeros((N, N), F32)
    s_imag = jnp.zeros((N, N), F32)
    for k in range(4):
        pair = []
        for part in range(2):
            own = dmine[:, 2 * k + part].reshape(H, N)
            far = doth[:, 2 * k + part].reshape(H, N)
            value = jnp.concatenate(
                [jnp.where(first_core, own, far), jnp.where(first_core, far, own)], axis=0
            )
            dprobe[k, part] = value
            pair.append(value)
        pr, pi = probe[k, 0], probe[k, 1]
        s_real += pr * pair[0] + pi * pair[1]
        s_imag += pr * pair[1] - pi * pair[0]
    t_real = dirp[0] * patch[0] + dirp[1] * patch[1]
    t_imag = dirp[0] * patch[1] - dirp[1] * patch[0]
    sums[0, 0] = jnp.sum(t_real * s_real - t_imag * s_imag)


def finish_kernel(geo, steps1, steps2, field, probe, dprobe, *refs):
    bands, (field_out, probe_out, lanes) = refs[:10], refs[10:]
    y, c = geo[16], geo[17]
    for s in range(4):
        for which in range(2):
            owner = 2 * lax.rem(y - s + 4, 4) + (c if which == 0 else 1 - c)
            rows = pl.ds(owner, 32, stride=8)
            for part in range(2):
                pair = [
                    bands[at + s][part] if which == 0 else bands[at + 4][s, part]
                    for at in (0, 5)
                ]
                moved = steps1[0] * pair[0] + steps2[0] * pair[1]
                for at in range(8):
                    lanes[part, at, rows, :] = moved[:, at * H : at * H + H]
    for part in range(2):
        for at in range(8):
            here = slice(at * H, at * H + H)
            field_out[part, :, here] = field[part, :, here] + lanes[part, at]
    for k in range(4):
        for part in range(2):
            probe_out[k, part] = probe[k, part] + steps2[1] * dprobe[k, part]


def call(kernel, outs, args, smem_in, scratch=(), smem_out=(), flops=0):
    shapes = [jax.ShapeDtypeStruct(shape, F32) for shape in outs]
    moved = 4 * (sum(math.prod(s) for s in outs) + sum(a.size for a in args))
    return pl.pallas_call(
        kernel,
        out_shape=shapes,
        in_specs=[SMEM if i in smem_in else VMEM for i in range(len(args))],
        out_specs=[SMEM if i in smem_out else VMEM for i in range(len(outs))],
        scratch_shapes=[pltpu.VMEM(shape, F32) for shape in scratch],
        compiler_params=pltpu.CompilerParams(vmem_limit_bytes=48 * 2**20),
        cost_estimate=pl.CostEstimate(flops=flops, bytes_accessed=moved, transcendentals=0),
    )(*args)


def along_y(value, s):
    return lax.ppermute(value, "pat", [(i, (i + 2 * s) % 8) for i in range(8)])


def partner(value):
    return lax.ppermute(value, "pat", [(i, i ^ 1) for i in range(8)])


def up(value):
    return lax.ppermute(value, "tile", [(i, i + 1) for i in range(15)])


def down(value):
    return lax.ppermute(value, "tile", [(i + 1, i) for i in range(15)])


def spread(value, axes, count):
    return lax.all_to_all(jnp.broadcast_to(value[None], (count,) + value.shape), axes, 0, 0)


def first_patch(field, e0, col, c):
    edge = (2, H, 512)
    from_above = up(lax.dynamic_slice(field, (0, H, 512 * c), edge))
    from_below = down(lax.dynamic_slice(field, (0, 0, 512 * c), edge))
    both = jnp.stack([from_above, from_below])
    far = partner(both)
    left = jnp.where(c == 0, both, far)
    right = jnp.where(c == 0, far, both)
    rims = jnp.concatenate([left, right], axis=-1)
    extended = jnp.concatenate([rims[0], field, rims[1]], axis=1)
    return lax.dynamic_slice(extended, (0, e0, col), (2, N, N))


def body(intensity, positions, object_init, probe_init):
    tile = lax.axis_index("tile")
    pat = lax.axis_index("pat")
    y, c = pat // 2, pat % 2
    top = tile * N - H
    e0 = positions[0, 0] - top
    col = positions[0, 1]
    own = jnp.stack([e0, y, c]).astype(jnp.int32)
    table = jnp.asarray(real_tables())
    measured = intensity[0].reshape(H, 2, H, 2).transpose(1, 0, 3, 2).reshape(2, H, N)
    patch = first_patch(object_init, e0, col, c)
    places = spread(jnp.broadcast_to(positions, (8, 2)), "pat", 8)[:, 0]
    geo = jnp.concatenate(
        [places[:, 0] - top, places[:, 1], jnp.stack([y, c, tile, pat])]
    ).astype(jnp.int32)
    probe = probe_init
    steps = dirp = dprobe = None
    bands = []
    sent = (16, 9, 8, N)
    pieces = (4, 3, 32, N)
    scratch = ((4, 2, N, N), (2, H, N), (3, 2, N, H))
    for iteration in range(ITERS):
        if iteration == 0:
            keep, send, mine, other = call(
                lambda *refs: patterns_kernel(True, *refs),
                (sent, sent, pieces, pieces),
                (own, patch, probe, measured, table),
                (0,),
                scratch,
                flops=6 * 10**9,
            )
        else:
            patch, probe, keep, send, mine, other = call(
                lambda *refs: patterns_kernel(False, *refs),
                ((2, N, N), (4, 2, N, N), sent, sent, pieces, pieces),
                (own, steps, patch, probe, measured, table, dirp, dprobe),
                (0, 1),
                scratch,
                flops=6 * 10**9,
            )
        part = partner(other)
        chip = keep + partner(send)
        came = [
            along_y(jnp.stack([mine[s], part[s]]), s) for s in range(1, 4)
        ]
        shares = lax.all_to_all(chip, "tile", 0, 0)
        share = jnp.sum(shares, axis=0)
        low, high = call(
            place_kernel,
            ((3, 32, 1024), (3, 32, 1024)),
            (geo, mine, part, *came),
            (0,),
            ((3, 72, 1152),),
        )
        above = up(high)
        below = down(low)
        total = share + along_y(share, 1) + along_y(share, 2) + along_y(share, 3)
        illum = total[8:]
        d_share = total[:8] / (illum + RIDGE)
        d_size = d_share * d_share
        d_sum = 0.25 * jnp.sum(illum * d_size)
        f_sum = d_sum + 0.25 * jnp.sum(d_size)
        band, ae, r0, r1, r2, r3 = call(
            direction_kernel,
            ((2, 32, 1024), (1, 2)) + ((2, 2, 32, N),) * 4,
            (geo, low, high, above, below),
            (0,),
            ((2, 72, 1152),),
            smem_out=(1,),
        )
        back = [r0] + [along_y(r, s) for s, r in ((1, r1), (2, r2), (3, r3))]
        dmine = spread(d_share, "tile", 16)
        oth = partner(jnp.stack([r[1] for r in back]))
        doth = partner(dmine)
        dirp, dprobe, cross = call(
            cross_kernel,
            ((2, N, N), (4, 2, N, N), (1, 1)),
            (geo, *back, oth, dmine, doth, patch, probe),
            (0,),
            ((2, 2, N, H),),
            smem_out=(2,),
        )
        mixed = jnp.stack([ae[0, 0], cross[0, 0], d_sum, ae[0, 0] + ae[0, 1], f_sum])
        everyone = spread(jnp.broadcast_to(mixed[:, None], (5, 128)), BOTH, 128)
        sums = jnp.sum(everyone[:, :, 0], axis=0)
        object_power, cross_term, probe_power, object_pull, probe_pull = (
            sums[0],
            sums[1],
            sums[2],
            sums[3],
            sums[4],
        )
        ridge_term = 0.1 * (object_power + probe_power) + 1e-06
        determinant = (object_power + ridge_term) * (
            probe_power + ridge_term
        ) - cross_term * cross_term
        object_step = (
            (probe_power + ridge_term) * object_pull - cross_term * probe_pull
        ) / determinant
        probe_step = (
            (object_power + ridge_term) * probe_pull - cross_term * object_pull
        ) / determinant
        old_steps, steps = steps, jnp.stack([object_step, probe_step])
        bands.append(band)
        bands.extend(along_y(band, s) for s in range(1, 4))
        bands.append(partner(jnp.stack(bands[-4:])))
    return call(
        finish_kernel,
        (object_init.shape, probe_init.shape),
        (geo, old_steps, steps, object_init, probe, dprobe, *bands),
        (0, 1, 2),
        ((2, 8, N, H),),
    )


def solution(mesh):
    placed = (P(("pat", "tile"), None, None), P(("pat", "tile"), None), P(None, "tile", None), P())
    return jax.shard_map(
        body, mesh=mesh, in_specs=placed, out_specs=(P(None, "tile", None), P()), check_vma=False
    )
```

time: 940 us -> 368 us (0.39); the launches traced: 929 us -> 366 us
  waiting for transfers between devices: 545 us -> 74.2 us
  matrix products: 70.9 us -> 0 us
  other arithmetic: 60 us -> 11.8 us
  Pallas kernels: 0 us -> 40.5 us
  starting transfers between devices: 32 us -> 71 us
  blocking collectives: 128 us -> 93.2 us
    psum x4 -> x0, waiting for transfers between devices: 447 us -> none  [the longest x2 305 us: body(): lax.psum((grad_probe, illum_probe), ('pat', 'tile'))]
    psum x2 -> x0, blocking collectives: 128 us -> none  [body(): sums = lax.psum(partial_sums, ('pat', 'tile'))]
    all_to_all x0 -> x4, blocking collectives: none -> 93.2 us  [the longest x2 48.2 us: body(): shares = lax.all_to_all(chip, 'tile', 0, 0)]
    dot_general x16 -> x0, matrix products: 70.9 us -> none  [the longest x4 26.3 us: transform(): jnp.einsum('zmab,bc->zmac', stacked, sin_table, precision=PRECISE)]
    pallas_call x0 -> x9, Pallas kernels: none -> 40.5 us  [call(): pl.pallas_call(kernel, out_shape=shapes, in_specs=[SMEM if i in smem_in e...]
    ppermute x12 -> x41, waiting for transfers between devices: 97.9 us -> 61.3 us  [the longest x24 33.5 us: along_y(): return lax.ppermute(value, 'pat', [(i, (i + 2 * s) % 8) for i in range(8)])]
    ppermute x12 -> x41, starting transfers between devices: 31.8 us -> 58 us  [the longest x24 24.5 us: along_y(): return lax.ppermute(value, 'pat', [(i, (i + 2 * s) % 8) for i in range(8)])]
    dynamic_update_slice x2 -> x0, local copies, waits for them, and re-layouts: 18.5 us -> none  [accumulate_patch(): return lax.dynamic_update_slice(field, addend, (0, row, column))]
  transfers between devices with their start and end apart: 16 -> 44, of which waited for: 10 -> 21; matrix products, arithmetic and copies ran while one was open for 4% -> 11% of each run, Pallas kernels for 0% -> 3%
where the time goes in v1:
time: 368 us; the launch traced here: 366 us
  blocking collectives  93.2 us (25%)
  waiting for transfers between devices  74.2 us (20%)
  starting transfers between devices  71 us (19%)
  local copies, waits for them, and re-layouts  51.5 us (14%)
  Pallas kernels  40.5 us (11%)
  between operations  24.4 us (7%)
  other arithmetic  11.8 us (3%)
    all_to_all x2, blocking collectives, body(): shares = lax.all_to_all(chip, 'tile', 0, 0)  48.2 us
    all_to_all x2, blocking collectives, spread(): lax.all_to_all(jnp.broadcast_to(value[None], (count,) + value.shape), axe...  44.9 us
    pallas_call x9, Pallas kernels, call(): pl.pallas_call(kernel, out_shape=shapes, in_specs=[SMEM if i in smem_in e...  40.5 us
    ppermute x24, waiting for transfers between devices, along_y(): return lax.ppermute(value, 'pat', [(i, (i + 2 * s) % 8) for i in range(8)])  33.5 us
    ppermute x24, starting transfers between devices, along_y(): return lax.ppermute(value, 'pat', [(i, (i + 2 * s) % 8) for i in range(8)])  24.5 us
    another operation x1, local copies, waits for them, and re-layouts, body(): intensity[0].reshape(H, 2, H, 2).transpose(1, 0, 3, 2).reshape(2, H, N)  18.1 us
    ppermute x11, starting transfers between devices, partner(): return lax.ppermute(value, 'pat', [(i, i ^ 1) for i in range(8)])  16.9 us
    unnamed x58, local copies, waits for them, and re-layouts  13.1 us
  transfers between devices with their start and end apart: 44, of which 21 were waited for; matrix products, arithmetic and copies ran while one was open for 11% of the time, Pallas kernels for 3%

profile of v1, /device:TPU:1, one launch (start us, length us, event | category | flops | bytes accessed | tf_op | source)
XLA Modules:
  0.0 366.5 jit_solution(9074920426698375825)
XLA Ops:
  0.7 1.3 constant_dynamic-slice_fusion.1
  2.0 4.0 %collective-permute-start = (f32[2,128,512]{2,1,0:T(8,128)S(1)}, f32[2,128,512]{2,1,0:T(8,128)S(1)}, u32[]{:S(2)}, u32[]{:S(2)}) collective-permute-start(f32[2,128,512]{2,1,0:T(8,128)S(1)} %get-tuple-element.74), channel_id=1, source_target_pairs={{0,1},{1,2},{2,3},{3,4},{4,5},{5,6},{6,7},{7,8},{8,9},{9,10},{10,1... | collective-permute-start | bytes 1572872 | tf_op jit(solution)/shard_map/ppermute | solution.py:301
  6.0 1.3 collective-permute-start.1
  7.3 9.2 %collective-permute-done = f32[2,128,512]{2,1,0:T(8,128)S(1)} collective-permute-done((f32[2,128,512]{2,1,0:T(8,128)S(1)}, f32[2,128,512]{2,1,0:T(8,128)S(1)}, u32[]{:S(2)}, u32[]{:S(2)}) %collective-permute-start) | collective-permute-done | bytes 524320 | tf_op jit(solution)/shard_map/ppermute | solution.py:301
  16.5 3.8 %collective-permute-done.1 = f32[2,128,512]{2,1,0:T(8,128)S(1)} collective-permute-done((f32[2,128,512]{2,1,0:T(8,128)S(1)}, f32[2,128,512]{2,1,0:T(8,128)S(1)}, u32[]{:S(2)}, u32[]{:S(2)}) %collective-permute-start.1) | collective-permute-done | bytes 524320 | tf_op jit(solution)/shard_map/ppermute | solution.py:305
  20.4 1.9 collective-permute-start.2
  24.9 18.1 %reshape_squeeze.3 = f32[128,2,128,2]{3,2,1,0:T(8,128)} reshape(f32[1,256,256]{2,1,0:T(8,128)S(1)} %copy-done.27) | data formatting | bytes 524288 | tf_op jit(solution)/shard_map/reshape;squeeze | solution.py:334
  43.0 9.5 %copy.16 = f32[2,128,2,128]{3,2,1,0:T(2,128)S(1)} copy(f32[2,128,2,128]{2,3,0,1:T(8,128)} %bitcast.69) | data formatting | bytes 524288 | tf_op jit(solution)/shard_map/transpose | solution.py:334
  53.5 1.6 broadcast_select_fusion
  55.3 1.4 copy-done.26
  57.9 8.5 %shard_map.71 = (f32[16,9,8,256]{3,2,1,0:T(8,128)S(1)}, f32[16,9,8,256]{3,2,1,0:T(8,128)S(1)}, f32[4,3,32,256]{3,2,1,0:T(8,128)S(1)}, f32[4,3,32,256]{3,2,1,0:T(8,128)S(1)}) custom-call(s32[3]{0:T(128)S(1)} %pad_add_fusion.refs_0_, f32[2,256,256]{2,1,0:T(8,128)S(1)} %fusion.4.refs_1_.patch.refs_2_, f32[4,2,256,256]{3,2,1,0:T(8,128)} %refs_3_.1, ...), custom_call_target="tpu_custom_call" | custom-call | flops 6000000000 | bytes 8126476 | tf_op jit(solution)/shard_map/pallas_call | solution.py:281
  66.6 2.8 collective-permute-done.13
  69.5 27.5 %all_to_all.35 = f32[16,9,8,256]{3,2,1,0:T(8,128)} all-to-all(f32[16,9,8,256]{3,2,1,0:T(8,128)S(1)} %add.92), channel_id=1, replica_groups=mesh['pat'=8,'tile'=16] {'tile'}, dimensions={0} | all-to-all | bytes 2359296 | tf_op jit(solution)/shard_map/all_to_all | solution.py:370
  97.0 1.3 reduce_sum.72
  98.4 2.8 collective-permute-start.16
  102.9 5.6 %all-to-all-start = ((s32[8,8,2]{1,2,0:T(2,128)}), s32[8,8,2]{1,2,0:T(2,128)S(1)}, u32[]{:S(2)}, u32[]{:S(2)}) async-start(s32[8,8,2]{1,2,0:T(2,128)} %broadcast_in_dim_broadcast_in_dim_broadcast_in_dim.6), calls=%async_computation | async-start | bytes 16384 | tf_op jit(solution)/shard_map/all_to_all | solution.py:309
  109.3 3.9 %all-to-all-done = s32[8,8,2]{1,2,0:T(2,128)S(1)} async-done(((s32[8,8,2]{1,2,0:T(2,128)}), s32[8,8,2]{1,2,0:T(2,128)S(1)}, u32[]{:S(2)}, u32[]{:S(2)}) %all-to-all-start) | async-done | bytes 544 | tf_op jit(solution)/shard_map/all_to_all | solution.py:309
  114.2 3.7 all-to-all-start.2
  118.8 1.2 collective-permute-done.3.part
  121.7 1.8 collective-permute-start.5
  125.1 9.0 %all-to-all-done.2.dmine = f32[16,8,8,256]{3,2,1,0:T(8,128)S(1)} async-done(((f32[16,8,8,256]{3,2,1,0:T(8,128)}), f32[16,8,8,256]{3,2,1,0:T(8,128)S(1)}, u32[]{:S(2)}, u32[]{:S(2)}) %all-to-all-start.2) | async-done | bytes 1048608 | tf_op jit(solution)/shard_map/all_to_all | solution.py:309
  134.1 2.2 collective-permute-start.17
  136.5 1.7 shard_map.72
  138.2 1.3 collective-permute-start.8
  139.5 4.0 %collective-permute-start.7 = (f32[3,32,1024]{2,1,0:T(8,128)S(1)}, f32[3,32,1024]{2,1,0:T(8,128)S(1)}, u32[]{:S(2)}, u32[]{:S(2)}) collective-permute-start(f32[3,32,1024]{2,1,0:T(8,128)S(1)} %get-tuple-element.36.high), channel_id=1, source_target_pairs={{0,1},{1,2},{2,3},{3,4},{4,5},{5,6},{6,7},{7,8},{8,9},{9,10},{10,1... | collective-permute-start | bytes 1179656 | tf_op jit(solution)/shard_map/ppermute | solution.py:301
  143.5 7.3 %collective-permute-done.8.below = f32[3,32,1024]{2,1,0:T(8,128)S(1)} collective-permute-done((f32[3,32,1024]{2,1,0:T(8,128)S(1)}, f32[3,32,1024]{2,1,0:T(8,128)S(1)}, u32[]{:S(2)}, u32[]{:S(2)}) %collective-permute-start.8) | collective-permute-done | bytes 393248 | tf_op jit(solution)/shard_map/ppermute | solution.py:305
  151.7 1.5 shard_map.73
  153.5 1.6 collective-permute-start.10
  156.2 4.2 %collective-permute-done.9.r1 = f32[2,2,32,256]{3,2,1,0:T(8,128)S(1)} collective-permute-done((f32[2,2,32,256]{3,2,1,0:T(8,128)S(1)}, f32[2,2,32,256]{3,2,1,0:T(8,128)S(1)}, u32[]{:S(2)}, u32[]{:S(2)}) %collective-permute-start.9) | collective-permute-done | bytes 131104 | tf_op jit(solution)/shard_map/ppermute | solution.py:293
  162.2 2.3 collective-permute-start.12
  167.7 3.6 shard_map.74
  171.4 1.3 copy-done.19
  173.5 1.4 stack.141
  175.0 23.0 %all_to_all.36 = f32[128,5,128]{2,1,0:T(8,128)S(1)} all-to-all(f32[128,5,128]{2,1,0:T(8,128)S(1)} %broadcast_in_dim_broadcast_in_dim_broadcast_in_dim.7), channel_id=1, replica_groups=mesh['pat'=8,'tile'=16] {'pat','tile'}, dimensions={0} | all-to-all | bytes 655360 | tf_op jit(solution)/shard_map/all_to_all | solution.py:309
  206.8 1.2 copy-done.25
  208.1 10.8 %shard_map.75 = (f32[2,256,256]{2,1,0:T(8,128)S(1)}, f32[4,2,256,256]{3,2,1,0:T(8,128)}, f32[16,9,8,256]{3,2,1,0:T(8,128)S(1)}, f32[16,9,8,256]{3,2,1,0:T(8,128)...) custom-call(s32[3]{0:T(128)S(1)} %pad_add_fusion.refs_0_, f32[2]{0:T(128)S(1)} %pad_maximum_fusion.12.refs_1_.steps1, ...), custom_call_target="tpu_custom_call" | custom-call | flops 6000000000 | bytes 13369364 | tf_op jit(solution)/shard_map/pallas_call | solution.py:281
  219.4 2.5 collective-permute-done.28
  222.0 20.7 %all_to_all.37 = f32[16,9,8,256]{3,2,1,0:T(8,128)S(1)} all-to-all(f32[16,9,8,256]{3,2,1,0:T(8,128)S(1)} %add.103), channel_id=1, replica_groups=mesh['pat'=8,'tile'=16] {'tile'}, dimensions={0} | all-to-all | bytes 2359296 | tf_op jit(solution)/shard_map/all_to_all | solution.py:370
  243.9 1.3 collective-permute-start.30
  245.3 1.9 collective-permute-start.18
  247.2 1.4 collective-permute-done.30
  251.5 3.7 all-to-all-start.5
  255.3 1.8 collective-permute-start.20
  257.1 1.4 collective-permute-start.21
  258.6 5.1 %collective-permute-done.19.b1 = f32[2,3,32,256]{3,2,1,0:T(8,128)S(1)} collective-permute-done((f32[2,3,32,256]{3,2,1,0:T(8,128)S(1)}, f32[2,3,32,256]{3,2,1,0:T(8,128)S(1)}, u32[]{:S(2)}, u32[]{:S(2)}) %collective-permute-start.19) | collective-permute-done | bytes 196640 | tf_op jit(solution)/shard_map/ppermute | solution.py:293
  264.6 1.9 shard_map.76
  266.5 1.3 collective-permute-start.23
  268.5 4.7 %collective-permute-start.22 = (f32[3,32,1024]{2,1,0:T(8,128)}, f32[3,32,1024]{2,1,0:T(8,128)}, u32[]{:S(2)}, u32[]{:S(2)}) collective-permute-start(f32[3,32,1024]{2,1,0:T(8,128)} %get-tuple-element.50.high), channel_id=1, source_target_pairs={{0,1},{1,2},{2,3},{3,4},{4,5},{5,6},{6,7},{7,8},{8,9},{9,10},{10,1... | collective-permute-start | bytes 1179656 | tf_op jit(solution)/shard_map/ppermute | solution.py:301
  273.3 4.3 %collective-permute-start.35 = (f32[2,32,1024]{2,1,0:T(8,128)S(1)}, f32[2,32,1024]{2,1,0:T(8,128)S(1)}, u32[]{:S(2)}, u32[]{:S(2)}) collective-permute-start(f32[2,32,1024]{2,1,0:T(8,128)S(1)} %get-tuple-element.62.refs_0_), channel_id=1, source_target_pairs={{0,96},{16,112},{32,0},{48,16},{64,32},{80,48},{96,64},{112,80},{1... | collective-permute-start | bytes 786440 | tf_op jit(solution)/shard_map/ppermute | solution.py:293
  277.5 3.0 collective-permute-start.32
  281.9 2.2 shard_map.77
  284.0 2.4 collective-permute-start.24
  287.7 2.4 collective-permute-done.34.refs_2_
  290.1 5.1 %collective-permute-done.33.refs_1_ = f32[2,32,1024]{2,1,0:T(8,128)S(1)} collective-permute-done((f32[2,32,1024]{2,1,0:T(8,128)S(1)}, f32[2,32,1024]{2,1,0:T(8,128)S(1)}, u32[]{:S(2)}, u32[]{:S(2)}) %collective-permute-start.33) | collective-permute-done | bytes 262176 | tf_op jit(solution)/shard_map/ppermute | solution.py:293
  295.9 2.2 collective-permute-done.24.r1
  298.1 3.2 collective-permute-done.25.r2
  302.3 4.5 %collective-permute-done.26.r3 = f32[2,2,32,256]{3,2,1,0:T(8,128)S(1)} collective-permute-done((f32[2,2,32,256]{3,2,1,0:T(8,128)S(1)}, f32[2,2,32,256]{3,2,1,0:T(8,128)S(1)}, u32[]{:S(2)}, u32[]{:S(2)}) %collective-permute-start.26) | collective-permute-done | bytes 131104 | tf_op jit(solution)/shard_map/ppermute | solution.py:293
  306.8 3.6 collective-permute-start.36
  310.5 2.3 collective-permute-done.37.refs_6_
  322.8 3.8 %shard_map.78 = (f32[2,256,256]{2,1,0:T(8,128)}, f32[4,2,256,256]{3,2,1,0:T(8,128)S(1)}, f32[1,1]{1,0:T(1,128)}) custom-call(s32[20]{0:T(128)S(1)} %concatenate.9.geo, f32[2,2,32,256]{3,2,1,0:T(8,128)S(1)} %get-tuple-element.52.r0, f32[2,2,32,256]{3,2,1,0:T(8,128)S(1)} %copy-done.12, f32[2,2,32,256]{3,2,1,0:T(8,128)S(1)} %copy-done.14, ...), custom_call_target="tpu_custom_call" | custom-call | bytes 8126548 | tf_op jit(solution)/shard_map/pallas_call | solution.py:281
  326.6 1.4 copy-done
  328.0 1.4 stack.152
  329.5 22.0 %all_to_all.38 = f32[128,5,128]{2,1,0:T(8,128)S(1)} all-to-all(f32[128,5,128]{2,1,0:T(8,128)S(1)} %broadcast_in_dim_broadcast_in_dim_broadcast_in_dim.8), channel_id=1, replica_groups=mesh['pat'=8,'tile'=16] {'pat','tile'}, dimensions={0} | all-to-all | bytes 655360 | tf_op jit(solution)/shard_map/all_to_all | solution.py:309
  360.0 6.5 %shard_map.79 = (f32[2,256,1024]{2,1,0:T(8,128)}, f32[4,2,256,256]{3,2,1,0:T(8,128)}) custom-call(s32[20]{0:T(128)S(1)} %concatenate.9.geo, f32[2]{0:T(128)S(1)} %pad_maximum_fusion.12.refs_1_.steps1, f32[2]{0:T(128)S(1)} %pad_maximum_fusion.13.steps2, f32[2,256,1024]{2,1,0:T(8,128)} %field.1, f32[4,2,256,256]{3,2,1,0:T(8,128)} %get-tuple-element.59.probe, ...), custom_call_target="tpu_custom_call" | custom-call | bytes 14680160 | tf_op jit(solution)/shard_map/pallas_call | solution.py:281
  (155 shorter events, 36.4 us)
Async XLA Ops:
  0.6 21.7 %copy-start.28 = (s32[1,2]{1,0:T(1,128)S(1)}, s32[1,2]{1,0:T(1,128)}, u32[]{:S(2)}) copy-start(s32[1,2]{1,0:T(1,128)} %param.6) | copy-start | bytes 28
  0.7 24.3 %copy-start.27 = (f32[1,256,256]{2,1,0:T(8,128)S(1)}, f32[1,256,256]{2,1,0:T(8,128)}, u32[]{:S(2)}) copy-start(f32[1,256,256]{2,1,0:T(8,128)} %param.5) | copy-start | bytes 786436
  2.0 14.5 %collective-permute-start = (f32[2,128,512]{2,1,0:T(8,128)S(1)}, f32[2,128,512]{2,1,0:T(8,128)S(1)}, u32[]{:S(2)}, u32[]{:S(2)}) collective-permute-start(f32[2,128,512]{2,1,0:T(8,128)S(1)} %get-tuple-element.74), channel_id=1, source_target_pairs={{0,1},{1,2},{2,3},{3,4},{4,5},{5,6},{6,7},{7,8},{8,9},{9,10},{10,1... | collective-permute-start | bytes 1572872 | tf_op jit(solution)/shard_map/ppermute | solution.py:301
  6.0 14.4 %collective-permute-start.1 = (f32[2,128,512]{2,1,0:T(8,128)S(1)}, f32[2,128,512]{2,1,0:T(8,128)S(1)}, u32[]{:S(2)}, u32[]{:S(2)}) collective-permute-start(f32[2,128,512]{2,1,0:T(8,128)S(1)} %get-tuple-element.75), channel_id=1, source_target_pairs={{1,0},{2,1},{3,2},{4,3},{5,4},{6,5},{7,6},{8,7},{9,8},{10,9},{11,1... | collective-permute-start | bytes 1572872 | tf_op jit(solution)/shard_map/ppermute | solution.py:305
  20.4 33.1 %collective-permute-start.2 = (f32[2,2,128,512]{3,2,1,0:T(8,128)S(1)}, f32[2,2,128,512]{3,2,1,0:T(8,128)}, u32[]{:S(2)}, u32[]{:S(2)}) collective-permute-start(f32[2,2,128,512]{3,2,1,0:T(8,128)S(1)} %pad_maximum_fusion.1), channel_id=1, source_target_pairs={{0,16},{16,0},{32,48},{48,32},{64,80},{80,64},{96,112},{112,96},{1... | collective-permute-start | bytes 3145736 | tf_op jit(solution)/shard_map/ppermute | solution.py:297
  52.7 4.4 %copy-start.17 = (f32[2,128,256]{2,1,0:T(8,128)}, f32[2,128,256]{2,1,0:T(8,128)S(1)}, u32[]{:S(2)}) copy-start(f32[2,128,256]{2,1,0:T(8,128)S(1)} %reshape.16.refs_3_.refs_4_) | copy-start | bytes 786436
  55.1 1.6 copy-start.26
  66.4 30.6 %copy-start.22 = (f32[4,3,32,256]{3,2,1,0:T(8,128)}, f32[4,3,32,256]{3,2,1,0:T(8,128)S(1)}, u32[]{:S(2)}) copy-start(f32[4,3,32,256]{3,2,1,0:T(8,128)S(1)} %get-tuple-element.34) | copy-start | bytes 1179652
  66.5 2.9 collective-permute-start.13
  98.4 19.5 %copy-start.23 = (f32[4,3,32,256]{3,2,1,0:T(8,128)S(1)}, f32[4,3,32,256]{3,2,1,0:T(8,128)}, u32[]{:S(2)}) copy-start(f32[4,3,32,256]{3,2,1,0:T(8,128)} %copy-done.22) | copy-start | bytes 1179652
  98.4 10.2 %collective-permute-start.16 = (f32[9,8,256]{2,1,0:T(8,128)S(1)}, f32[9,8,256]{2,1,0:T(8,128)S(1)}, u32[]{:S(2)}, u32[]{:S(2)}) collective-permute-start(f32[9,8,256]{2,1,0:T(8,128)S(1)} %reduce_sum.72), channel_id=1, source_target_pairs={{0,96},{16,112},{32,0},{48,16},{64,32},{80,48},{96,64},{112,80},{1... | collective-permute-start | bytes 221192 | tf_op jit(solution)/shard_map/ppermute | solution.py:293
  101.2 7.4 %collective-permute-start.15 = (f32[9,8,256]{2,1,0:T(8,128)S(1)}, f32[9,8,256]{2,1,0:T(8,128)S(1)}, u32[]{:S(2)}, u32[]{:S(2)}) collective-permute-start(f32[9,8,256]{2,1,0:T(8,128)S(1)} %reduce_sum.72), channel_id=1, source_target_pairs={{0,64},{16,80},{32,96},{48,112},{64,0},{80,16},{96,32},{112,48},{1... | collective-permute-start | bytes 221192 | tf_op jit(solution)/shard_map/ppermute | solution.py:293
  101.5 7.0 %collective-permute-start.14 = (f32[9,8,256]{2,1,0:T(8,128)S(1)}, f32[9,8,256]{2,1,0:T(8,128)S(1)}, u32[]{:S(2)}, u32[]{:S(2)}) collective-permute-start(f32[9,8,256]{2,1,0:T(8,128)S(1)} %reduce_sum.72), channel_id=1, source_target_pairs={{0,32},{16,48},{32,64},{48,80},{64,96},{80,112},{96,0},{112,16},{1... | collective-permute-start | bytes 221192 | tf_op jit(solution)/shard_map/ppermute | solution.py:293
  102.9 10.3 %all-to-all-start = ((s32[8,8,2]{1,2,0:T(2,128)}), s32[8,8,2]{1,2,0:T(2,128)S(1)}, u32[]{:S(2)}, u32[]{:S(2)}) async-start(s32[8,8,2]{1,2,0:T(2,128)} %broadcast_in_dim_broadcast_in_dim_broadcast_in_dim.6), calls=%async_computation | async-start | bytes 16384 | tf_op jit(solution)/shard_map/all_to_all | solution.py:309
  114.2 19.9 %all-to-all-start.2 = ((f32[16,8,8,256]{3,2,1,0:T(8,128)}), f32[16,8,8,256]{3,2,1,0:T(8,128)S(1)}, u32[]{:S(2)}, u32[]{:S(2)}) async-start(f32[16,8,8,256]{3,2,1,0:T(8,128)} %broadcast_in_dim.4), calls=%async_computation.2 | async-start | bytes 2097152 | tf_op jit(solution)/shard_map/all_to_all | solution.py:309
  117.9 2.1 collective-permute-start.3
  120.8 15.7 %collective-permute-start.4 = (f32[2,3,32,256]{3,2,1,0:T(8,128)}, f32[2,3,32,256]{3,2,1,0:T(8,128)}, u32[]{:S(2)}, u32[]{:S(2)}) collective-permute-start(f32[2,3,32,256]{3,2,1,0:T(8,128)} %pad_maximum_fusion.6), channel_id=1, source_target_pairs={{0,32},{16,48},{32,64},{48,80},{64,96},{80,112},{96,0},{112,16},{1... | collective-permute-start | bytes 589832 | tf_op jit(solution)/shard_map/ppermute | solution.py:293
  121.7 14.7 %collective-permute-start.5 = (f32[2,3,32,256]{3,2,1,0:T(8,128)}, f32[2,3,32,256]{3,2,1,0:T(8,128)}, u32[]{:S(2)}, u32[]{:S(2)}) collective-permute-start(f32[2,3,32,256]{3,2,1,0:T(8,128)} %pad_maximum_fusion.7), channel_id=1, source_target_pairs={{0,64},{16,80},{32,96},{48,112},{64,0},{80,16},{96,32},{112,48},{1... | collective-permute-start | bytes 589832 | tf_op jit(solution)/shard_map/ppermute | solution.py:293
  124.2 12.2 %collective-permute-start.6 = (f32[2,3,32,256]{3,2,1,0:T(8,128)}, f32[2,3,32,256]{3,2,1,0:T(8,128)}, u32[]{:S(2)}, u32[]{:S(2)}) collective-permute-start(f32[2,3,32,256]{3,2,1,0:T(8,128)} %pad_maximum_fusion.8), channel_id=1, source_target_pairs={{0,96},{16,112},{32,0},{48,16},{64,32},{80,48},{96,64},{112,80},{1... | collective-permute-start | bytes 589832 | tf_op jit(solution)/shard_map/ppermute | solution.py:293
  134.1 33.6 %collective-permute-start.17 = (f32[16,8,8,256]{3,2,1,0:T(8,128)S(1)}, f32[16,8,8,256]{3,2,1,0:T(8,128)S(1)}, u32[]{:S(2)}, u32[]{:S(2)}) collective-permute-start(f32[16,8,8,256]{3,2,1,0:T(8,128)S(1)} %all-to-all-done.2.dmine), channel_id=1, source_target_pairs={{0,16},{16,0},{32,48},{48,32},{64,80},{80,64},{96,112},{112,96},{1... | collective-permute-start | bytes 3145736 | tf_op jit(solution)/shard_map/ppermute | solution.py:297
  138.2 12.6 %collective-permute-start.8 = (f32[3,32,1024]{2,1,0:T(8,128)S(1)}, f32[3,32,1024]{2,1,0:T(8,128)S(1)}, u32[]{:S(2)}, u32[]{:S(2)}) collective-permute-start(f32[3,32,1024]{2,1,0:T(8,128)S(1)} %get-tuple-element.35.low), channel_id=1, source_target_pairs={{1,0},{2,1},{3,2},{4,3},{5,4},{6,5},{7,6},{8,7},{9,8},{10,9},{11,1... | collective-permute-start | bytes 1179656 | tf_op jit(solution)/shard_map/ppermute | solution.py:305
  139.5 12.2 %collective-permute-start.7 = (f32[3,32,1024]{2,1,0:T(8,128)S(1)}, f32[3,32,1024]{2,1,0:T(8,128)S(1)}, u32[]{:S(2)}, u32[]{:S(2)}) collective-permute-start(f32[3,32,1024]{2,1,0:T(8,128)S(1)} %get-tuple-element.36.high), channel_id=1, source_target_pairs={{0,1},{1,2},{2,3},{3,4},{4,5},{5,6},{6,7},{7,8},{8,9},{9,10},{10,1... | collective-permute-start | bytes 1179656 | tf_op jit(solution)/shard_map/ppermute | solution.py:301
  153.2 7.2 %collective-permute-start.9 = (f32[2,2,32,256]{3,2,1,0:T(8,128)S(1)}, f32[2,2,32,256]{3,2,1,0:T(8,128)S(1)}, u32[]{:S(2)}, u32[]{:S(2)}) collective-permute-start(f32[2,2,32,256]{3,2,1,0:T(8,128)S(1)} %get-tuple-element.39), channel_id=1, source_target_pairs={{0,32},{16,48},{32,64},{48,80},{64,96},{80,112},{96,0},{112,16},{1... | collective-permute-start | bytes 393224 | tf_op jit(solution)/shard_map/ppermute | solution.py:293
  153.5 6.9 %collective-permute-start.10 = (f32[2,2,32,256]{3,2,1,0:T(8,128)S(1)}, f32[2,2,32,256]{3,2,1,0:T(8,128)S(1)}, u32[]{:S(2)}, u32[]{:S(2)}) collective-permute-start(f32[2,2,32,256]{3,2,1,0:T(8,128)S(1)} %get-tuple-element.40), channel_id=1, source_target_pairs={{0,64},{16,80},{32,96},{48,112},{64,0},{80,16},{96,32},{112,48},{1... | collective-permute-start | bytes 393224 | tf_op jit(solution)/shard_map/ppermute | solution.py:293
  155.1 6.4 %collective-permute-start.11 = (f32[2,2,32,256]{3,2,1,0:T(8,128)S(1)}, f32[2,2,32,256]{3,2,1,0:T(8,128)S(1)}, u32[]{:S(2)}, u32[]{:S(2)}) collective-permute-start(f32[2,2,32,256]{3,2,1,0:T(8,128)S(1)} %get-tuple-element.41), channel_id=1, source_target_pairs={{0,96},{16,112},{32,0},{48,16},{64,32},{80,48},{96,64},{112,80},{1... | collective-permute-start | bytes 393224 | tf_op jit(solution)/shard_map/ppermute | solution.py:293
  162.2 5.5 %collective-permute-start.12 = (f32[4,2,32,256]{3,2,1,0:T(8,128)}, f32[4,2,32,256]{3,2,1,0:T(8,128)}, u32[]{:S(2)}, u32[]{:S(2)}) collective-permute-start(f32[4,2,32,256]{3,2,1,0:T(8,128)} %pad_maximum_fusion.4), channel_id=1, source_target_pairs={{0,16},{16,0},{32,48},{48,32},{64,80},{80,64},{96,112},{112,96},{1... | collective-permute-start | bytes 786440 | tf_op jit(solution)/shard_map/ppermute | solution.py:297
  171.4 1.3 copy-start.19
  173.5 33.3 %copy-start.18 = (f32[2,128,256]{2,1,0:T(8,128)S(1)}, f32[2,128,256]{2,1,0:T(8,128)}, u32[]{:S(2)}) copy-start(f32[2,128,256]{2,1,0:T(8,128)} %copy-done.17) | copy-start | bytes 786436
  173.5 33.3 %copy-start.21 = (f32[2,256,256]{2,1,0:T(8,128)S(1)}, f32[2,256,256]{2,1,0:T(8,128)}, u32[]{:S(2)}) copy-start(f32[2,256,256]{2,1,0:T(8,128)} %copy-done.20) | copy-start | bytes 1572868
  206.8 1.2 copy-start.25
  218.8 3.2 copy-start.7
  218.8 3.0 collective-permute-start.28
  242.9 4.4 %collective-permute-start.31 = (f32[9,8,256]{2,1,0:T(8,128)S(1)}, f32[9,8,256]{2,1,0:T(8,128)S(1)}, u32[]{:S(2)}, u32[]{:S(2)}) collective-permute-start(f32[9,8,256]{2,1,0:T(8,128)S(1)} %reduce_sum.76), channel_id=1, source_target_pairs={{0,96},{16,112},{32,0},{48,16},{64,32},{80,48},{96,64},{112,80},{1... | collective-permute-start | bytes 221192 | tf_op jit(solution)/shard_map/ppermute | solution.py:293
  243.9 4.7 %collective-permute-start.30 = (f32[9,8,256]{2,1,0:T(8,128)S(1)}, f32[9,8,256]{2,1,0:T(8,128)S(1)}, u32[]{:S(2)}, u32[]{:S(2)}) collective-permute-start(f32[9,8,256]{2,1,0:T(8,128)S(1)} %reduce_sum.76), channel_id=1, source_target_pairs={{0,64},{16,80},{32,96},{48,112},{64,0},{80,16},{96,32},{112,48},{1... | collective-permute-start | bytes 221192 | tf_op jit(solution)/shard_map/ppermute | solution.py:293
  245.3 4.4 %collective-permute-start.29 = (f32[9,8,256]{2,1,0:T(8,128)S(1)}, f32[9,8,256]{2,1,0:T(8,128)S(1)}, u32[]{:S(2)}, u32[]{:S(2)}) collective-permute-start(f32[9,8,256]{2,1,0:T(8,128)S(1)} %reduce_sum.76), channel_id=1, source_target_pairs={{0,32},{16,48},{32,64},{48,80},{64,96},{80,112},{96,0},{112,16},{1... | collective-permute-start | bytes 221192 | tf_op jit(solution)/shard_map/ppermute | solution.py:293
  245.3 9.8 %collective-permute-start.18 = (f32[4,3,32,256]{3,2,1,0:T(8,128)S(1)}, f32[4,3,32,256]{3,2,1,0:T(8,128)S(1)}, u32[]{:S(2)}, u32[]{:S(2)}) collective-permute-start(f32[4,3,32,256]{3,2,1,0:T(8,128)S(1)} %get-tuple-element.48), channel_id=1, source_target_pairs={{0,16},{16,0},{32,48},{48,32},{64,80},{80,64},{96,112},{112,96},{1... | collective-permute-start | bytes 1179656 | tf_op jit(solution)/shard_map/ppermute | solution.py:297
  251.5 26.1 %all-to-all-start.5 = ((f32[16,8,8,256]{3,2,1,0:T(8,128)}), f32[16,8,8,256]{3,2,1,0:T(8,128)S(1)}, u32[]{:S(2)}, u32[]{:S(2)}) async-start(f32[16,8,8,256]{3,2,1,0:T(8,128)} %broadcast_in_dim.5), calls=%async_computation.5 | async-start | bytes 2097152 | tf_op jit(solution)/shard_map/all_to_all | solution.py:309
  255.2 8.5 %collective-permute-start.19 = (f32[2,3,32,256]{3,2,1,0:T(8,128)S(1)}, f32[2,3,32,256]{3,2,1,0:T(8,128)S(1)}, u32[]{:S(2)}, u32[]{:S(2)}) collective-permute-start(f32[2,3,32,256]{3,2,1,0:T(8,128)S(1)} %pad_maximum_fusion.9), channel_id=1, source_target_pairs={{0,32},{16,48},{32,64},{48,80},{64,96},{80,112},{96,0},{112,16},{1... | collective-permute-start | bytes 589832 | tf_op jit(solution)/shard_map/ppermute | solution.py:293
  255.3 8.4 %collective-permute-start.20 = (f32[2,3,32,256]{3,2,1,0:T(8,128)S(1)}, f32[2,3,32,256]{3,2,1,0:T(8,128)S(1)}, u32[]{:S(2)}, u32[]{:S(2)}) collective-permute-start(f32[2,3,32,256]{3,2,1,0:T(8,128)S(1)} %pad_maximum_fusion.10), channel_id=1, source_target_pairs={{0,64},{16,80},{32,96},{48,112},{64,0},{80,16},{96,32},{112,48},{1... | collective-permute-start | bytes 589832 | tf_op jit(solution)/shard_map/ppermute | solution.py:293
  257.1 7.5 %collective-permute-start.21 = (f32[2,3,32,256]{3,2,1,0:T(8,128)S(1)}, f32[2,3,32,256]{3,2,1,0:T(8,128)S(1)}, u32[]{:S(2)}, u32[]{:S(2)}) collective-permute-start(f32[2,3,32,256]{3,2,1,0:T(8,128)S(1)} %pad_maximum_fusion.11), channel_id=1, source_target_pairs={{0,96},{16,112},{32,0},{48,16},{64,32},{80,48},{96,64},{112,80},{1... | collective-permute-start | bytes 589832 | tf_op jit(solution)/shard_map/ppermute | solution.py:293
  266.5 14.1 %collective-permute-start.23 = (f32[3,32,1024]{2,1,0:T(8,128)S(1)}, f32[3,32,1024]{2,1,0:T(8,128)}, u32[]{:S(2)}, u32[]{:S(2)}) collective-permute-start(f32[3,32,1024]{2,1,0:T(8,128)S(1)} %get-tuple-element.49.low), channel_id=1, source_target_pairs={{1,0},{2,1},{3,2},{4,3},{5,4},{6,5},{7,6},{8,7},{9,8},{10,9},{11,1... | collective-permute-start | bytes 1179656 | tf_op jit(solution)/shard_map/ppermute | solution.py:305
  268.5 12.3 %collective-permute-start.22 = (f32[3,32,1024]{2,1,0:T(8,128)}, f32[3,32,1024]{2,1,0:T(8,128)}, u32[]{:S(2)}, u32[]{:S(2)}) collective-permute-start(f32[3,32,1024]{2,1,0:T(8,128)} %get-tuple-element.50.high), channel_id=1, source_target_pairs={{0,1},{1,2},{2,3},{3,4},{4,5},{5,6},{6,7},{7,8},{8,9},{9,10},{10,1... | collective-permute-start | bytes 1179656 | tf_op jit(solution)/shard_map/ppermute | solution.py:301
  273.3 13.2 %collective-permute-start.35 = (f32[2,32,1024]{2,1,0:T(8,128)S(1)}, f32[2,32,1024]{2,1,0:T(8,128)S(1)}, u32[]{:S(2)}, u32[]{:S(2)}) collective-permute-start(f32[2,32,1024]{2,1,0:T(8,128)S(1)} %get-tuple-element.62.refs_0_), channel_id=1, source_target_pairs={{0,96},{16,112},{32,0},{48,16},{64,32},{80,48},{96,64},{112,80},{1... | collective-permute-start | bytes 786440 | tf_op jit(solution)/shard_map/ppermute | solution.py:293
  277.5 41.5 %collective-permute-start.32 = (f32[16,8,8,256]{3,2,1,0:T(8,128)S(1)}, f32[16,8,8,256]{3,2,1,0:T(8,128)S(1)}, u32[]{:S(2)}, u32[]{:S(2)}) collective-permute-start(f32[16,8,8,256]{3,2,1,0:T(8,128)S(1)} %all-to-all-done.5.dmine), channel_id=1, source_target_pairs={{0,16},{16,0},{32,48},{48,32},{64,80},{80,64},{96,112},{112,96},{1... | collective-permute-start | bytes 3145736 | tf_op jit(solution)/shard_map/ppermute | solution.py:297
  280.5 9.5 %collective-permute-start.34 = (f32[2,32,1024]{2,1,0:T(8,128)S(1)}, f32[2,32,1024]{2,1,0:T(8,128)S(1)}, u32[]{:S(2)}, u32[]{:S(2)}) collective-permute-start(f32[2,32,1024]{2,1,0:T(8,128)S(1)} %get-tuple-element.62.refs_0_), channel_id=1, source_target_pairs={{0,64},{16,80},{32,96},{48,112},{64,0},{80,16},{96,32},{112,48},{1... | collective-permute-start | bytes 786440 | tf_op jit(solution)/shard_map/ppermute | solution.py:293
  280.5 14.7 %collective-permute-start.33 = (f32[2,32,1024]{2,1,0:T(8,128)S(1)}, f32[2,32,1024]{2,1,0:T(8,128)S(1)}, u32[]{:S(2)}, u32[]{:S(2)}) collective-permute-start(f32[2,32,1024]{2,1,0:T(8,128)S(1)} %get-tuple-element.62.refs_0_), channel_id=1, source_target_pairs={{0,32},{16,48},{32,64},{48,80},{64,96},{80,112},{96,0},{112,16},{1... | collective-permute-start | bytes 786440 | tf_op jit(solution)/shard_map/ppermute | solution.py:293
  284.0 14.1 %collective-permute-start.24 = (f32[2,2,32,256]{3,2,1,0:T(8,128)S(1)}, f32[2,2,32,256]{3,2,1,0:T(8,128)S(1)}, u32[]{:S(2)}, u32[]{:S(2)}) collective-permute-start(f32[2,2,32,256]{3,2,1,0:T(8,128)S(1)} %get-tuple-element.53), channel_id=1, source_target_pairs={{0,32},{16,48},{32,64},{48,80},{64,96},{80,112},{96,0},{112,16},{1... | collective-permute-start | bytes 393224 | tf_op jit(solution)/shard_map/ppermute | solution.py:293
  286.4 14.8 %collective-permute-start.25 = (f32[2,2,32,256]{3,2,1,0:T(8,128)S(1)}, f32[2,2,32,256]{3,2,1,0:T(8,128)S(1)}, u32[]{:S(2)}, u32[]{:S(2)}) collective-permute-start(f32[2,2,32,256]{3,2,1,0:T(8,128)S(1)} %get-tuple-element.54), channel_id=1, source_target_pairs={{0,64},{16,80},{32,96},{48,112},{64,0},{80,16},{96,32},{112,48},{1... | collective-permute-start | bytes 393224 | tf_op jit(solution)/shard_map/ppermute | solution.py:293
  290.0 20.4 %collective-permute-start.39 = (f32[2,32,1024]{2,1,0:T(8,128)S(1)}, f32[2,32,1024]{2,1,0:T(8,128)S(1)}, u32[]{:S(2)}, u32[]{:S(2)}) collective-permute-start(f32[2,32,1024]{2,1,0:T(8,128)S(1)} %get-tuple-element.63.refs_5_), channel_id=1, source_target_pairs={{0,96},{16,112},{32,0},{48,16},{64,32},{80,48},{96,64},{112,80},{1... | collective-permute-start | bytes 786440 | tf_op jit(solution)/shard_map/ppermute | solution.py:293
  295.3 15.2 %collective-permute-start.38 = (f32[2,32,1024]{2,1,0:T(8,128)S(1)}, f32[2,32,1024]{2,1,0:T(8,128)S(1)}, u32[]{:S(2)}, u32[]{:S(2)}) collective-permute-start(f32[2,32,1024]{2,1,0:T(8,128)S(1)} %get-tuple-element.63.refs_5_), channel_id=1, source_target_pairs={{0,64},{16,80},{32,96},{48,112},{64,0},{80,16},{96,32},{112,48},{1... | collective-permute-start | bytes 786440 | tf_op jit(solution)/shard_map/ppermute | solution.py:293
  298.1 15.8 %copy-start.11 = (f32[2,2,32,256]{3,2,1,0:T(8,128)}, f32[2,2,32,256]{3,2,1,0:T(8,128)S(1)}, u32[]{:S(2)}) copy-start(f32[2,2,32,256]{3,2,1,0:T(8,128)S(1)} %collective-permute-done.24.r1) | copy-start | bytes 393220
  298.1 14.7 %collective-permute-start.37 = (f32[2,32,1024]{2,1,0:T(8,128)S(1)}, f32[2,32,1024]{2,1,0:T(8,128)S(1)}, u32[]{:S(2)}, u32[]{:S(2)}) collective-permute-start(f32[2,32,1024]{2,1,0:T(8,128)S(1)} %get-tuple-element.63.refs_5_), channel_id=1, source_target_pairs={{0,32},{16,48},{32,64},{48,80},{64,96},{80,112},{96,0},{112,16},{1... | collective-permute-start | bytes 786440 | tf_op jit(solution)/shard_map/ppermute | solution.py:293
  301.3 12.6 %copy-start.13 = (f32[2,2,32,256]{3,2,1,0:T(8,128)}, f32[2,2,32,256]{3,2,1,0:T(8,128)S(1)}, u32[]{:S(2)}) copy-start(f32[2,2,32,256]{3,2,1,0:T(8,128)S(1)} %collective-permute-done.25.r2) | copy-start | bytes 393220
  301.3 5.6 %collective-permute-start.26 = (f32[2,2,32,256]{3,2,1,0:T(8,128)S(1)}, f32[2,2,32,256]{3,2,1,0:T(8,128)S(1)}, u32[]{:S(2)}, u32[]{:S(2)}) collective-permute-start(f32[2,2,32,256]{3,2,1,0:T(8,128)S(1)} %get-tuple-element.55), channel_id=1, source_target_pairs={{0,96},{16,112},{32,0},{48,16},{64,32},{80,48},{96,64},{112,80},{1... | collective-permute-start | bytes 393224 | tf_op jit(solution)/shard_map/ppermute | solution.py:293
  306.8 8.9 %copy-start.15 = (f32[2,2,32,256]{3,2,1,0:T(8,128)}, f32[2,2,32,256]{3,2,1,0:T(8,128)S(1)}, u32[]{:S(2)}) copy-start(f32[2,2,32,256]{3,2,1,0:T(8,128)S(1)} %collective-permute-done.26.r3) | copy-start | bytes 393220
  306.8 53.1 %collective-permute-start.36 = (f32[4,2,32,1024]{3,2,1,0:T(8,128)}, f32[4,2,32,1024]{3,2,1,0:T(8,128)}, u32[]{:S(2)}, u32[]{:S(2)}) collective-permute-start(f32[4,2,32,1024]{3,2,1,0:T(8,128)} %pad_maximum_fusion.2), channel_id=1, source_target_pairs={{0,16},{16,0},{32,48},{48,32},{64,80},{80,64},{96,112},{112,96},{1... | collective-permute-start | bytes 3145736 | tf_op jit(solution)/shard_map/ppermute | solution.py:297
  310.5 3.4 copy-start.3
  312.8 2.3 copy-start.5
  314.6 45.4 %collective-permute-start.40 = (f32[4,2,32,1024]{3,2,1,0:T(8,128)}, f32[4,2,32,1024]{3,2,1,0:T(8,128)}, u32[]{:S(2)}, u32[]{:S(2)}) collective-permute-start(f32[4,2,32,1024]{3,2,1,0:T(8,128)} %pad_maximum_fusion.3), channel_id=1, source_target_pairs={{0,16},{16,0},{32,48},{48,32},{64,80},{80,64},{96,112},{112,96},{1... | collective-permute-start | bytes 3145736 | tf_op jit(solution)/shard_map/ppermute | solution.py:297
  315.8 3.2 collective-permute-start.27
  326.6 1.4 copy-start
  328.0 32.0 %copy-start.2 = (f32[2,32,1024]{2,1,0:T(8,128)S(1)}, f32[2,32,1024]{2,1,0:T(8,128)}, u32[]{:S(2)}) copy-start(f32[2,32,1024]{2,1,0:T(8,128)} %copy-done.1) | copy-start | bytes 786436
  328.0 32.0 %copy-start.4 = (f32[2,32,1024]{2,1,0:T(8,128)S(1)}, f32[2,32,1024]{2,1,0:T(8,128)}, u32[]{:S(2)}) copy-start(f32[2,32,1024]{2,1,0:T(8,128)} %copy-done.3) | copy-start | bytes 786436
  328.0 32.0 %copy-start.6 = (f32[2,32,1024]{2,1,0:T(8,128)S(1)}, f32[2,32,1024]{2,1,0:T(8,128)}, u32[]{:S(2)}) copy-start(f32[2,32,1024]{2,1,0:T(8,128)} %copy-done.5) | copy-start | bytes 786436
  (9 other events, 8.2 us)

commit v2 on v1

v2 whole, which is shorter than its diff:
```python
import math

import jax
import jax.numpy as jnp
import ml_dtypes
import numpy as np
from jax import lax
from jax.experimental import pallas as pl
from jax.experimental.pallas import tpu as pltpu
from jax.sharding import PartitionSpec as P

ITERS = 2
FLOOR = 0.5
RIDGE = 1.0
N = 256
H = 128
F32 = jnp.float32
BF16 = jnp.bfloat16
BOTH = ("pat", "tile")
VMEM = pl.BlockSpec(memory_space=pltpu.VMEM)
SMEM = pl.BlockSpec(memory_space=pltpu.SMEM)
ANY = pl.BlockSpec(memory_space=pl.ANY)


def real_tables():
    near = np.arange(H)[:, None]
    far = np.arange(H)[None, :]
    found = []
    for parity in range(2):
        angle = -2.0 * math.pi * ((near * (2 * far + parity)) % N) / N
        real, imag = np.cos(angle) / 16.0, np.sin(angle) / 16.0
        found.append(np.block([[real, imag], [-imag, real]]))
    even, odd = found
    out = []
    for table in (even, odd, even.T, odd.T):
        high = table.astype(np.float32).astype(ml_dtypes.bfloat16)
        low = (table - high.astype(np.float64)).astype(np.float32).astype(ml_dtypes.bfloat16)
        out.append(np.stack([high, low]))
    return np.stack(out)


def halves(value):
    high = value.astype(BF16)
    return high, (value - high.astype(F32)).astype(BF16)


def dot(left, right):
    return jnp.dot(left, right, preferred_element_type=F32)


def times_table(value, table):
    high, low = halves(value)
    return dot(high, table[0]) + (dot(low, table[0]) + dot(high, table[1]))


def table_times(table, value):
    high, low = halves(value)
    return dot(table[0], high) + (dot(table[0], low) + dot(table[1], high))


def thirds(value):
    high, mid = halves(value)
    return high, mid, (value - high.astype(F32) - mid.astype(F32)).astype(BF16)


def step_sizes(everyone):
    total = jnp.sum(everyone[...], axis=0, keepdims=True)
    lane = lax.broadcasted_iota(jnp.int32, (1, 128), 1)
    object_power, cross_term, probe_power, object_pull, probe_pull = (
        jnp.broadcast_to(
            jnp.sum(jnp.where(lane == at, total, 0.0), axis=1, keepdims=True), (1, 128)
        )
        for at in range(5)
    )
    ridge = 0.1 * (object_power + probe_power) + 1e-06
    determinant = (object_power + ridge) * (probe_power + ridge) - cross_term * cross_term
    object_step = ((probe_power + ridge) * object_pull - cross_term * probe_pull) / determinant
    probe_step = ((object_power + ridge) * probe_pull - cross_term * object_pull) / determinant
    return object_step, probe_step


def twice(value):
    return jnp.concatenate([value, value], axis=1)


def joined(first_core, mine, other, plane):
    own, far = mine[plane], other[plane]
    return jnp.concatenate(
        [jnp.where(first_core, own, far), jnp.where(first_core, far, own)], axis=0
    )


def window_of(here):
    col = here[0, 1]
    block = pl.multiple_of(lax.min(lax.shift_right_logical(col, 7), 5) * H, H)
    return block, col - block


def cut(rows, e0, shift):
    rows = pltpu.roll(rows, lax.rem(2 * N - e0, N), axis=0)
    return pltpu.roll(rows, lax.rem(384 - shift, 384), axis=1)[:, :N]


def prepare_kernel(where, here, near, measured, swap, field, out, base, token):
    high, mid, low = thirds(measured[...])
    across, down_rows = swap[0], swap[1]
    high, mid, low = thirds(dot(high, across) + dot(mid, across) + dot(low, across))
    value = dot(down_rows, high) + dot(down_rows, mid) + dot(down_rows, low)
    out[0] = value[:H]
    out[1] = value[H:]
    e0 = here[0, 0] - where[3]
    block, shift = window_of(here)
    row = lax.broadcasted_iota(jnp.int32, (N, N), 0) + e0
    inside = (row >= H) & (row < H + N)
    for part in range(2):
        rows = field[part, :, pl.ds(block, 384)]
        rows = jnp.concatenate([rows[H:], rows[:H]], axis=0)
        base[part] = jnp.where(inside, cut(rows, e0, shift), 0.0)
    token[0, 0] = 0.0


def edge_kernel(where, field, top_rows, low_rows, sems):
    c = where[1]
    copies = [
        pltpu.make_async_copy(field.at[c, pl.ds(0, H), :], top_rows, sems.at[0]),
        pltpu.make_async_copy(field.at[c, pl.ds(H, H), :], low_rows, sems.at[1]),
    ]
    for copy in copies:
        copy.start()
    for copy in copies:
        copy.wait()


def edges(where, field):
    rows = pltpu.HBM((H, field.shape[2]), F32)
    hbm = pl.BlockSpec(memory_space=pltpu.HBM)
    return pl.pallas_call(
        edge_kernel,
        out_shape=[rows, rows],
        in_specs=[SMEM, ANY],
        out_specs=[hbm, hbm],
        scratch_shapes=[pltpu.SemaphoreType.DMA((2,))],
        compiler_params=pltpu.CompilerParams(vmem_limit_bytes=2**20),
    )(where, field)


def announce_kernel(here, above, below, out):
    lane = lax.broadcasted_iota(jnp.int32, (8, 128), 1)
    value = jnp.zeros((8, 128), jnp.int32)
    for at, place in enumerate((here, above, below)):
        value = jnp.where(lane == 2 * at, place[0, 0], value)
        value = jnp.where(lane == 2 * at + 1, place[0, 1], value)
    out[...] = value


def side_kernel(where, near, token, above, below, own, far):
    y, c, top = where[0], where[1], where[3]
    own_row = near[2 * y + c, 0] - top
    far_row = near[2 * y + 1 - c, 0] - top
    own[...] = jnp.where(own_row < H, above[...], below[...])
    far[...] = jnp.where(far_row < H, above[...], below[...])


def add_side(where, here, base, own_side, far_side, patch):
    e0, first_core = here[0, 0] - where[3], where[1] == 0
    block, shift = window_of(here)
    row = lax.broadcasted_iota(jnp.int32, (N, N), 0) + e0
    outside = (row < H) | (row >= H + N)
    own, far = own_side[:, pl.ds(block, 384)], far_side[:, pl.ds(block, 384)]
    for part in range(2):
        rows = jnp.where(first_core == (part == 0), own, far)
        rows = cut(jnp.concatenate([rows, rows], axis=0), e0, shift)
        patch[part] = jnp.where(outside, rows, base[part])


def patterns_kernel(first, ready, *refs):
    if first:
        where, here, base, own_side, far_side, probe_now, measured, tab = refs[:8]
        patch_now, keep, send, mine, other, power, token, psi, model, obj = refs[8:]
        token[0, 0] = 0.0
        add_side(where, here, base, own_side, far_side, patch_now)
    else:
        where, here, everyone, patch, probe, measured, tab, dirp, dmine, doth = refs[:10]
        patch_now, probe_now = refs[10:12]
        keep, send, mine, other, power, psi, model, obj = refs[12:]
        object_step, probe_step = map(twice, step_sizes(everyone))
        ready(3)
        ready(7)
        for part in range(2):
            patch_now[part] = patch[part] + object_step * dirp[part]
    y, c = where[0], where[1]
    e0 = here[0, 0] - where[3]
    first_core = c == 0
    model[...] = jnp.zeros_like(model)
    obj[...] = jnp.zeros_like(obj)
    power[...] = jnp.zeros_like(power)

    def gather(plane, value):
        obj[plane, 0] += value[:, :H]
        obj[plane, 1] += value[:, H:]

    def forward(k):
        if first:
            ready(5, k)
        else:
            ready(4, k)
            for part in range(2):
                ready(8, 2 * k + part)
                ready(9, 2 * k + part)
                moved = probe_step * joined(first_core, dmine, doth, 2 * k + part)
                probe_now[k, part] = probe[k, part] + moved
        pr, pi = probe_now[k, 0], probe_now[k, 1]
        orr, oi = patch_now[0], patch_now[1]
        power[...] += pr * pr + pi * pi
        xr = pr * orr - pi * oi
        xi = pr * oi + pi * orr
        even = times_table(
            jnp.concatenate([xr[:, :H] + xr[:, H:], xi[:, :H] + xi[:, H:]], axis=1), tab.at[0]
        )
        odd = times_table(
            jnp.concatenate([xr[:, :H] - xr[:, H:], xi[:, :H] - xi[:, H:]], axis=1), tab.at[1]
        )
        re = jnp.concatenate([even[:, :H], odd[:, :H]], axis=1)
        im = jnp.concatenate([even[:, H:], odd[:, H:]], axis=1)
        for row, sign in ((0, 1.0), (1, -1.0)):
            folded = jnp.concatenate(
                [re[:H] + sign * re[H:], im[:H] + sign * im[H:]], axis=0
            )
            far = table_times(tab.at[2 + row], folded)
            psi[k, row] = far
            model[row] += far[:H] * far[:H] + far[H:] * far[H:]

    ready(7 if first else 6)
    for k in range(4):
        forward(k)
    ready(6 if first else 5)
    for row in range(2):
        model[row] = jnp.sqrt(measured[row] / jnp.maximum(model[row], FLOOR)) - 1.0

    def put(plane, value):
        low = value[:H].reshape(16, 8, N)
        high = value[H:].reshape(16, 8, N)
        keep[:, plane] = jnp.where(first_core, low, high)
        send[:, plane] = jnp.where(first_core, high, low)

    def backward(k):
        parts = []
        for row in range(2):
            scale = model[row]
            weighted = psi[k, row] * jnp.concatenate([scale, scale], axis=0)
            parts.append(table_times(tab.at[row], weighted))
        ee, oo = parts
        re = jnp.concatenate([ee[:H] + oo[:H], ee[:H] - oo[:H]], axis=0)
        im = jnp.concatenate([ee[H:] + oo[H:], ee[H:] - oo[H:]], axis=0)
        even = times_table(jnp.concatenate([re[:, :H], im[:, :H]], axis=1), tab.at[2])
        odd = times_table(jnp.concatenate([re[:, H:], im[:, H:]], axis=1), tab.at[3])
        dr = jnp.concatenate([even[:, :H] + odd[:, :H], even[:, :H] - odd[:, :H]], axis=1)
        di = jnp.concatenate([even[:, H:] + odd[:, H:], even[:, H:] - odd[:, H:]], axis=1)
        pr, pi = probe_now[k, 0], probe_now[k, 1]
        orr, oi = patch_now[0], patch_now[1]
        gather(0, pr * dr + pi * di)
        gather(1, pr * di - pi * dr)
        put(2 * k, orr * dr + oi * di)
        put(2 * k + 1, orr * di - oi * dr)

    for k in range(4):
        backward(k)
    orr, oi = patch_now[0], patch_now[1]
    put(8, orr * orr + oi * oi)
    for s in range(4):
        for which, dest in ((c, mine), (1 - c, other)):
            owner = 2 * lax.rem(y + s, 4) + which
            start = lax.rem(owner - e0 + 1024, 8)
            for plane in range(2):
                for half in range(2):
                    rows = obj[plane, half, pl.ds(start, 32, stride=8), :]
                    dest[s, plane, :, half * H : half * H + H] = rows


def place_of(where, places, owner, pattern, band=0):
    e0 = places[pattern, 2 * band] - where[3]
    col = places[pattern, 2 * band + 1]
    start = lax.rem(owner - e0 + 1024, 8)
    row = lax.shift_right_logical(e0 + 256 + start - owner, 3)
    base = pl.multiple_of(lax.shift_right_logical(row, 3) * 8, 8)
    block = pl.multiple_of(lax.shift_right_logical(col, 7) * 128, 128)
    return start, base, lax.rem(row, 8), block, lax.rem(col, 128)


def place(acc, piece, base, turn, block, shift):
    wide = pltpu.roll(jnp.concatenate([piece, jnp.zeros((32, 128), F32)], axis=1), shift, axis=1)
    wide = pltpu.roll(jnp.concatenate([wide, jnp.zeros((8, 384), F32)], axis=0), turn, axis=0)
    acc[pl.ds(base, 40), pl.ds(block, 384)] += wide


def illum_kernel(where, near, token, total, out, power, acc):
    owner = 2 * where[0] + where[1]
    acc[...] = jnp.zeros_like(acc)
    power[0] = total[:, :H]
    power[1] = total[:, H:]

    def from_band(band):
        def one(pattern, carry):
            start, base, turn, block, shift = place_of(where, near, owner, pattern, band)
            rows = pl.ds(start, 32, stride=8)
            piece = jnp.concatenate([power[0, rows, :], power[1, rows, :]], axis=1)
            place(acc, piece, base, turn, block, shift)
            return carry

        return one

    tile = where[2]
    lax.fori_loop(0, 8, from_band(0), 0)
    lax.fori_loop(0, jnp.where(tile == 0, 0, 8), from_band(1), 0)
    lax.fori_loop(0, jnp.where(tile == 15, 0, 8), from_band(2), 0)
    out[...] = acc[32:96, :1024]


def place_kernel(where, near, b0, b1, b2, b3, low, high, token, acc):
    token[0, 0] = 0.0
    y, c = where[0], where[1]
    owner = 2 * y + c
    acc[...] = jnp.zeros_like(acc)
    for s in range(4):
        for which in range(2):
            pattern = 2 * lax.rem(y - s + 4, 4) + (c if which == 0 else 1 - c)
            start, base, turn, block, shift = place_of(where, near, owner, pattern)
            for plane in range(2):
                piece = (b0, b1, b2, b3)[s][which, plane]
                place(acc.at[plane], piece, base - 32, turn, block, shift)
    low[...] = acc[:, :32, :1024]
    high[...] = acc[:, 32:64, :1024]


def direction_kernel(
    where, near, token, illum, low, high, above, below, band, sums, r0, r1, r2, r3, wide
):
    y, c = where[0], where[1]
    owner = 2 * y + c
    wide[...] = jnp.zeros_like(wide)
    total_a = jnp.zeros((16, 1024), F32)
    total_n = jnp.zeros((16, 1024), F32)
    for at, (own, came) in enumerate(((low, above), (high, below))):
        rows = slice(32 * at, 32 * at + 32)
        light = illum[rows]
        scale = 1.0 / (light + RIDGE)
        real = (own[0] + came[0]) * scale
        imag = (own[1] + came[1]) * scale
        wide[0, rows, :1024] = real
        wide[1, rows, :1024] = imag
        inner = slice(16, 32) if at == 0 else slice(0, 16)
        real, imag, light = real[inner], imag[inner], light[inner]
        band[0, 16 * at : 16 * at + 16] = real
        band[1, 16 * at : 16 * at + 16] = imag
        size = real * real + imag * imag
        total_n += size
        total_a += light * size
    sums[0, 0] = jnp.sum(total_a)
    sums[0, 1] = jnp.sum(total_n)
    for s, dest in enumerate((r0, r1, r2, r3)):
        for which in range(2):
            pattern = 2 * lax.rem(y + s, 4) + (c if which == 0 else 1 - c)
            start, base, turn, block, shift = place_of(where, near, owner, pattern)
            for part in range(2):
                piece = wide[part, pl.ds(base - 32, 40), pl.ds(block, 384)]
                piece = pltpu.roll(piece, lax.rem(40 - turn, 40), axis=0)[:32]
                dest[which, part] = pltpu.roll(piece, lax.rem(384 - shift, 384), axis=1)[:, :N]


def stack_kernel(r0, r1, r2, r3, out):
    for s, came in enumerate((r0, r1, r2, r3)):
        out[s] = came[1]


def patch_kernel(where, near, r0, r1, r2, r3, oth, patch, dirp, kept, sent, lanes):
    y, c = where[0], where[1]
    e0 = near[2 * y + c, 0] - where[3]
    for s, came in enumerate((r0, r1, r2, r3)):
        for which in range(2):
            owner = 2 * lax.rem(y - s + 4, 4) + (c if which == 0 else 1 - c)
            rows = pl.ds(lax.rem(owner - e0 + 1024, 8), 32, stride=8)
            for part in range(2):
                piece = came[0, part] if which == 0 else oth[s, part]
                for half in range(2):
                    lanes[part, half, rows, :] = piece[:, half * H : half * H + H]
    for part in range(2):
        for half in range(2):
            dirp[part, :, half * H : half * H + H] = lanes[part, half]
    for which, dest in ((c, kept), (1 - c, sent)):
        rows = pl.ds(pl.multiple_of(which * H, H), H)
        dr, di = dirp[0, rows, :], dirp[1, rows, :]
        orr, oi = patch[0, rows, :], patch[1, rows, :]
        dest[0] = dr * orr + di * oi
        dest[1] = dr * oi - di * orr


def pack_kernel(keep, came, mine, part, chip, b0, b1, b2, b3):
    chip[...] = keep[...] + came[...]
    for s, dest in enumerate((b0, b1, b2, b3)):
        dest[0] = mine[s]
        dest[1] = part[s]


def sum_kernel(before, shares, out, token):
    out[...] = jnp.sum(shares[...], axis=0)
    token[0, 0] = 0.0


def share_kernel(own, a, b, d, above, below, light, spread_out, sums):
    total = own[...] + a[...] + b[...] + d[...]
    illum = total[8]
    value = total[:8] * (1.0 / (illum + RIDGE))
    spread_out[...] = jnp.broadcast_to(value[None], (16, 8, 8, N))
    size = jnp.sum(value * value, axis=0)
    sums[0, 0] = jnp.sum(size * illum)
    sums[0, 1] = jnp.sum(size)


def relay_kernel(token, gathered, out):
    for plane in range(8):
        out[plane] = gathered[:, plane].reshape(H, N)


def message_kernel(where, gathered, probe, kept, came, ae, df, out, token, half, sem):
    token[0, 0] = 0.0
    rows = pl.ds(pl.multiple_of(where[1] * H, H), H)
    copy = pltpu.make_async_copy(probe.at[:, :, rows, :], half, sem)
    copy.start()
    total = jnp.zeros((H, N), F32)
    mixed_real = kept[0] + came[0]
    mixed_imag = kept[1] + came[1]
    copy.wait()
    for k in range(4):
        dr = gathered[:, 2 * k].reshape(H, N)
        di = gathered[:, 2 * k + 1].reshape(H, N)
        pr, pi = half[k, 0], half[k, 1]
        total += mixed_real * (pr * dr + pi * di) - mixed_imag * (pr * di - pi * dr)
    cross = jnp.sum(total)
    d_sum = 0.25 * df[0, 0]
    values = (ae[0, 0], cross, d_sum, ae[0, 0] + ae[0, 1], d_sum + 0.25 * df[0, 1])
    lane = lax.broadcasted_iota(jnp.int32, (128, 128), 1)
    message = jnp.zeros((128, 128), F32)
    for at, value in enumerate(values):
        message = jnp.where(lane == at, value, message)
    out[...] = message


def finish_kernel(
    where, one, two, field, band1, band2, probe, dmine, doth, field_out, probe_out, steps, lanes
):
    at = pl.program_id(0)

    @pl.when(at == 0)
    def _():
        steps[0:1] = step_sizes(one)[0]
        object_step, probe_step = step_sizes(two)
        steps[1:2] = object_step
        steps[2:3] = probe_step

    first = jnp.concatenate([steps[0:1]] * 8, axis=1)
    second = jnp.concatenate([steps[1:2]] * 8, axis=1)
    probe_step = twice(steps[2:3])
    for part in range(2):
        for owner in range(8):
            rows = pl.ds(owner, 8, stride=8)
            moved = first * band1[owner, part] + second * band2[owner, part]
            for column in range(8):
                lanes[part, column, rows, :] = moved[:, column * H : column * H + H]
        for column in range(8):
            here = slice(column * H, column * H + H)
            field_out[part, :, here] = field[part, :, here] + lanes[part, column]
    local = lax.shift_right_logical(at, 1) == where[1]
    for k in range(4):
        for part in range(2):
            plane = 2 * k + part
            value = jnp.where(local, dmine[plane], doth[plane])
            probe_out[k, part] = probe[k, part] + probe_step * value


def finish(where, one, two, field, band1, band2, probe, dmine, doth):
    rows = pl.BlockSpec((2, 64, 1024), lambda i: (0, i, 0))
    classes = pl.BlockSpec((8, 2, 8, 1024), lambda i: (0, 0, i, 0))
    modes = pl.BlockSpec((4, 2, 64, N), lambda i: (0, 0, i, 0))
    gathered = pl.BlockSpec((8, 64, N), lambda i: (0, lax.rem(i, 2), 0))
    whole = pl.BlockSpec((128, 128), lambda i: (0, 0))
    return pl.pallas_call(
        finish_kernel,
        grid=(4,),
        out_shape=[
            jax.ShapeDtypeStruct(field.shape, F32),
            jax.ShapeDtypeStruct(probe.shape, F32),
        ],
        in_specs=[SMEM, whole, whole, rows, classes, classes, modes, gathered, gathered],
        out_specs=[rows, modes],
        scratch_shapes=[pltpu.VMEM((8, 128), F32), pltpu.VMEM((2, 8, 64, H), F32)],
        compiler_params=pltpu.CompilerParams(vmem_limit_bytes=14 * 2**20),
    )(
        where,
        one,
        two,
        *[
            pltpu.with_memory_space_constraint(a, pltpu.HBM)
            for a in (field, band1, band2, probe, dmine, doth)
        ],
    )


def call(
    kernel,
    outs,
    args,
    smem_in,
    scratch=(),
    smem_out=(),
    hbm_out=(),
    vmem_out=(),
    hbm_in=(),
    any_in=(),
    lazy=False,
    flops=0,
    room=12,
    name=None,
):
    outs = [out if isinstance(out[0], tuple) else (out, F32) for out in outs]
    shapes = [
        pltpu.HBM(*out)
        if i in hbm_out
        else pltpu.VMEM(*out)
        if i in vmem_out
        else jax.ShapeDtypeStruct(*out)
        for i, out in enumerate(outs)
    ]
    hbm_in = hbm_in if isinstance(hbm_in, dict) else {index: 1 for index in hbm_in}
    moved = 4 * (sum(math.prod(out[0]) for out in outs) + sum(a.size for a in args))
    stage_in = [pltpu.VMEM(args[i].shape, args[i].dtype) for i in hbm_in]
    stage_out = [pltpu.VMEM(*outs[i]) for i in hbm_out]
    args = [
        pltpu.with_memory_space_constraint(a, pltpu.HBM) if i in hbm_in else a
        for i, a in enumerate(args)
    ]
    first, last = len(args), len(args) + len(outs)
    pieces = sum(hbm_in.values())

    def run(*refs):
        given, results = list(refs[:first]), list(refs[first:last])
        rest = refs[last:]
        staged = rest[len(scratch) : len(scratch) + len(stage_in) + len(stage_out)]
        sems = rest[-1] if staged else None
        arrivals, at = {}, 0
        for slot, (index, count) in enumerate(hbm_in.items()):
            stage, source = staged[slot], given[index]
            for piece in range(count):
                pair = (source, stage) if count == 1 else (source.at[piece], stage.at[piece])
                copy = pltpu.make_async_copy(*pair, sems.at[at])
                copy.start()
                arrivals[index, piece] = copy
                at += 1
            given[index] = stage
        departures = []
        for slot, index in enumerate(hbm_out):
            stage = staged[len(stage_in) + slot]
            departures.append(pltpu.make_async_copy(stage, results[index], sems.at[at + slot]))
            results[index] = stage

        def ready(index, piece=0):
            arrivals[index, piece].wait()

        if lazy:
            kernel(ready, *given, *results, *rest[: len(scratch)])
        else:
            for copy in arrivals.values():
                copy.wait()
            kernel(*given, *results, *rest[: len(scratch)])
        for copy in departures:
            copy.start()
        for copy in departures:
            copy.wait()

    def space(index, smem, hbm):
        return SMEM if index in smem else ANY if index in hbm or index in any_in else VMEM

    extra = stage_in + stage_out
    if extra:
        extra.append(pltpu.SemaphoreType.DMA((pieces + len(stage_out),)))
    hbm = pl.BlockSpec(memory_space=pltpu.HBM)
    return pl.pallas_call(
        run,
        out_shape=shapes,
        in_specs=[space(i, smem_in, hbm_in) for i in range(len(args))],
        out_specs=[
            hbm if i in hbm_out else SMEM if i in smem_out else VMEM for i in range(len(outs))
        ],
        scratch_shapes=[
            pltpu.VMEM(shape, F32) if shape else pltpu.SemaphoreType.DMA for shape in scratch
        ]
        + extra,
        name=name or kernel.__name__,
        compiler_params=pltpu.CompilerParams(vmem_limit_bytes=room * 2**20),
        cost_estimate=pl.CostEstimate(flops=flops, bytes_accessed=moved, transcendentals=0),
    )(*args)


def along_y(value, s):
    return lax.ppermute(value, "pat", [(i, (i + 2 * s) % 8) for i in range(8)])


def partner(value):
    return lax.ppermute(value, "pat", [(i, i ^ 1) for i in range(8)])


def up(value):
    return lax.ppermute(value, "tile", [(i, i + 1) for i in range(15)])


def down(value):
    return lax.ppermute(value, "tile", [(i + 1, i) for i in range(15)])


def spread(value, axes, count):
    return lax.all_to_all(jnp.broadcast_to(value[None], (count,) + value.shape), axes, 0, 0)


def one_hot():
    order = np.concatenate([np.arange(0, N, 2), np.arange(1, N, 2)])
    across = np.zeros((N, N), np.float32)
    across[order, np.arange(N)] = 1.0
    return np.stack([across, across.T]).astype(ml_dtypes.bfloat16)


def body(intensity, positions, object_init, probe_init):
    tile = lax.axis_index("tile")
    pat = lax.axis_index("pat")
    y, c = pat // 2, pat % 2
    top = tile * N - H
    where = jnp.stack([y, c, tile, top]).astype(jnp.int32)
    neighbours = up(positions), down(positions)
    top_rows, low_rows = edges(where, object_init)
    from_above, from_below = up(low_rows), down(top_rows)
    (news,) = call(
        announce_kernel, (((8, 128), jnp.int32),), (positions, *neighbours), (0, 1, 2), room=1
    )
    near = lax.all_to_all(news, "pat", 0, 0)
    table = jnp.asarray(real_tables())
    measured, base, token = call(
        prepare_kernel,
        ((2, H, N), (2, N, N), (1, 1)),
        (
            where,
            positions,
            near,
            intensity[0],
            jnp.asarray(one_hot()),
            object_init,
        ),
        (0, 1, 2),
        hbm_in=(3, 4, 5),
        smem_out=(2,),
        hbm_out=(0,),
        room=16,
    )
    own_side, far_side = call(
        side_kernel,
        ((H, 1024), (H, 1024)),
        (where, near, token, from_above, from_below),
        (0, 1, 2),
        room=4,
    )
    far_side = partner(far_side)

    probe = probe_init
    sent = (16, 9, 8, N)
    pieces = (4, 2, 32, N)
    scratch = ((4, 2, N, N), (2, H, N), (2, 2, N, H))
    outs = (sent, sent, pieces, pieces, (N, N))
    messages, bands = [], []

    for iteration in range(ITERS):
        if iteration == 0:
            patch, keep, send, mine, other, power, token = call(
                lambda *refs: patterns_kernel(True, *refs),
                ((2, N, N),) + outs + ((1, 1),),
                (where, positions, base, own_side, far_side, probe, measured, table),
                (0, 1),
                scratch,
                hbm_in={5: 4, 6: 1, 7: 1},
                lazy=True,
                smem_out=(6,),
                flops=6 * 10**9,
                room=28,
                name="patterns",
            )
        else:
            patch, probe, keep, send, mine, other, power = call(
                lambda *refs: patterns_kernel(False, *refs),
                ((2, N, N), (4, 2, N, N)) + outs,
                (where, positions, messages[-1], patch, probe, measured, table, dirp, dmine, doth),
                (0, 1),
                scratch,
                hbm_in={3: 1, 4: 4, 5: 1, 6: 1, 7: 1, 8: 8, 9: 8},
                lazy=True,
                hbm_out=(0, 1),
                flops=6 * 10**9,
                room=30,
                name="patterns",
            )
        chip, b0, b1, b2, b3 = call(
            pack_kernel,
            (sent,) + ((2, 2, 32, N),) * 4,
            (keep, partner(send), mine, partner(other)),
            (),
            hbm_out=(0, 2, 3, 4),
        )
        came = [b0, along_y(b1, 1), along_y(b2, 2), along_y(b3, 3)]
        low, high, token = call(
            place_kernel,
            ((2, 32, 1024), (2, 32, 1024), (1, 1)),
            (where, near, *came),
            (0, 1),
            ((2, 72, 1152),),
            smem_out=(2,),
            hbm_out=(0, 1),
        )
        above, below = up(high), down(low)
        shares = lax.all_to_all(chip, "tile", 0, 0)
        share, token = call(
            sum_kernel, ((9, 8, N), (1, 1)), (token, shares), (0,), smem_out=(1,)
        )
        (illum,) = call(
            illum_kernel,
            ((64, 1024),),
            (where, near, token, power),
            (0, 1, 2),
            ((2, N, H), (136, 1152)),
        )
        probe_dir, df = call(
            share_kernel,
            ((16, 8, 8, N), (1, 2)),
            (share, *[along_y(share, s) for s in range(1, 4)], above, below, illum),
            (),
            smem_out=(1,),
            hbm_out=(0,),
            any_in=(4, 5, 6),
        )
        gathered = lax.all_to_all(probe_dir, "tile", 0, 0)
        band, ae, r0, r1, r2, r3 = call(
            direction_kernel,
            ((2, 32, 1024), (1, 2)) + ((2, 2, 32, N),) * 4,
            (where, near, df, illum, low, high, above, below),
            (0, 1, 2),
            ((2, 72, 1152),),
            smem_out=(1,),
            hbm_out=(0, 3, 4, 5),
            hbm_in=(4, 5, 6, 7),
        )
        bands.append(lax.all_gather(band, "pat"))
        back = [r0] + [along_y(r, s) for s, r in ((1, r1), (2, r2), (3, r3))]
        (oth,) = call(stack_kernel, ((4, 2, 32, N),), back, (), room=4)
        dirp, kept, sent_mixed = call(
            patch_kernel,
            ((2, N, N), (2, H, N), (2, H, N)),
            (where, near, *back, partner(oth), patch),
            (0, 1),
            ((2, 2, N, H),),
        )
        message, token = call(
            message_kernel,
            ((128, 128), (1, 1)),
            (
                where,
                gathered,
                pltpu.with_memory_space_constraint(probe, pltpu.HBM),
                kept,
                partner(sent_mixed),
                ae,
                df,
            ),
            (0, 5, 6),
            ((4, 2, H, N), None),
            any_in=(2,),
            smem_out=(1,),
            hbm_out=(0,),
        )
        (dmine,) = call(relay_kernel, ((8, H, N),), (token, gathered), (0,))
        doth = partner(dmine)
        messages.append(lax.all_to_all(message, BOTH, 0, 0))
    return finish(where, *messages, object_init, *bands, probe, dmine, doth)


def solution(mesh):
    placed = (P(("pat", "tile"), None, None), P(("pat", "tile"), None), P(None, "tile", None), P())
    return jax.shard_map(
        body, mesh=mesh, in_specs=placed, out_specs=(P(None, "tile", None), P()), check_vma=False
    )
```

time: 368 us -> 268 us (0.73)
  blocking collectives: 93.2 us -> 29.3 us
  local copies, waits for them, and re-layouts: 51.5 us -> 4.49 us
  Pallas kernels: 40.5 us -> 72.3 us
  starting transfers between devices: 71 us -> 89 us
  waiting for transfers between devices: 74.2 us -> 56.9 us
  other arithmetic: 11.8 us -> 0.08 us
  between operations: 24.4 us -> 14.7 us
    all_to_all x4 -> x2, blocking collectives: 93.2 us -> 29.3 us  [the longest x1 18.6 us: body(): messages.append(lax.all_to_all(message, BOTH, 0, 0))]
    pallas_call x9 -> x27, Pallas kernels: 40.5 us -> 72.3 us  [the longest x25 63.6 us: call(): pl.pallas_call(run, out_shape=shapes, in_specs=[space(i, smem_in, hbm_in)...]
    all_to_all x3 -> x5, starting transfers between devices: 13 us -> 36.2 us  [the longest x2 13.3 us: body(): shares = lax.all_to_all(chip, 'tile', 0, 0)]
    another operation x6 -> x0, local copies, waits for them, and re-layouts: 21.8 us -> none  [the longest x1 18.1 us: body(): intensity[0].reshape(H, 2, H, 2).transpose(1, 0, 3, 2).reshape(2, H, N)]
    ppermute x24 -> x18, waiting for transfers between devices: 33.5 us -> 22.1 us  [along_y(): return lax.ppermute(value, 'pat', [(i, (i + 2 * s) % 8) for i in range(8)])]
    ppermute x3 -> x4, waiting for transfers between devices: 10.1 us -> 0.01 us  [up(): return lax.ppermute(value, 'tile', [(i, i + 1) for i in range(15)])]
    transpose x1 -> x0, local copies, waits for them, and re-layouts: 9.49 us -> none  [body(): intensity[0].reshape(H, 2, H, 2).transpose(1, 0, 3, 2).reshape(2, H, N)]
    unnamed x58 -> x46, local copies, waits for them, and re-layouts: 13.1 us -> 4.49 us
  transfers between devices with their start and end apart: 44 -> 44, of which waited for: 21 -> 27; matrix products, arithmetic and copies ran while one was open for 11% -> 0% of each run, Pallas kernels for 3% -> 17%
where the time goes in v2:
time: 268 us; the launch traced here: 267 us
  starting transfers between devices  89 us (33%)
  Pallas kernels  72.3 us (27%)
  waiting for transfers between devices  56.9 us (21%)
  blocking collectives  29.3 us (11%)
  between operations  14.7 us (5%)
  local copies, waits for them, and re-layouts  4.49 us (2%)
    pallas_call x25, Pallas kernels, call(): pl.pallas_call(run, out_shape=shapes, in_specs=[space(i, smem_in, hbm_in)...  63.6 us
    ppermute x18, waiting for transfers between devices, along_y(): return lax.ppermute(value, 'pat', [(i, (i + 2 * s) % 8) for i in range(8)])  22.1 us
    ppermute x18, starting transfers between devices, along_y(): return lax.ppermute(value, 'pat', [(i, (i + 2 * s) % 8) for i in range(8)])  18.6 us
    all_to_all x1, blocking collectives, body(): messages.append(lax.all_to_all(message, BOTH, 0, 0))  18.6 us
    ppermute x11, starting transfers between devices, partner(): return lax.ppermute(value, 'pat', [(i, i ^ 1) for i in range(8)])  14.6 us
    ppermute x4, starting transfers between devices, up(): return lax.ppermute(value, 'tile', [(i, i + 1) for i in range(15)])  14.4 us
    all_to_all x2, starting transfers between devices, body(): shares = lax.all_to_all(chip, 'tile', 0, 0)  13.3 us
    all_to_all x2, starting transfers between devices, body(): gathered = lax.all_to_all(probe_dir, 'tile', 0, 0)  13.2 us
  transfers between devices with their start and end apart: 44, of which 27 were waited for; matrix products, arithmetic and copies ran while one was open for 0% of the time, Pallas kernels for 17%

profile of v2, /device:TPU:1, one launch (start us, length us, event | category | flops | bytes accessed | tf_op | source)
XLA Modules:
  0.0 266.8 jit_solution(8439478562080113304)
XLA Ops:
  7.3 1.6 copy-done
  8.9 1.5 shard_map.77
  10.4 4.0 %collective-permute-start.2 = (f32[128,1024]{1,0:T(8,128)}, f32[128,1024]{1,0:T(8,128)S(1)}, u32[]{:S(2)}, u32[]{:S(2)}) collective-permute-start(f32[128,1024]{1,0:T(8,128)} %get-tuple-element.69), channel_id=1, source_target_pairs={{0,1},{1,2},{2,3},{3,4},{4,5},{5,6},{6,7},{7,8},{8,9},{9,10},{10,1... | collective-permute-start | bytes 1572872 | tf_op jit(solution)/shard_map/ppermute | solution.py:612
  14.4 1.3 collective-permute-start.3
  15.7 1.3 collective-permute-start.1
  17.0 4.6 %collective-permute-start = (s32[1,2]{1,0:T(1,128)S(1)}, s32[1,2]{1,0:T(1,128)S(1)}, u32[]{:S(2)}, u32[]{:S(2)}) collective-permute-start(s32[1,2]{1,0:T(1,128)S(1)} %copy-done.9), channel_id=1, source_target_pairs={{0,1},{1,2},{2,3},{3,4},{4,5},{5,6},{6,7},{7,8},{8,9},{9,10},{10,1... | collective-permute-start | bytes 32 | tf_op jit(solution)/shard_map/ppermute | solution.py:612
  21.6 7.3 %collective-permute-done.1.refs_2_ = s32[1,2]{1,0:T(1,128)S(1)} collective-permute-done((s32[1,2]{1,0:T(1,128)S(1)}, s32[1,2]{1,0:T(1,128)S(1)}, u32[]{:S(2)}, u32[]{:S(2)}) %collective-permute-start.1) | collective-permute-done | bytes 40 | tf_op jit(solution)/shard_map/ppermute | solution.py:616
  29.5 10.8 %all_to_all.53 = s32[8,1,128]{2,1,0:T(1,128)S(1)} all-to-all(s32[8,1,128]{2,1,0:T(1,128)S(1)} %bitcast.32), channel_id=1, replica_groups=mesh['pat'=8,'tile'=16] {'pat'}, dimensions={0} | all-to-all | bytes 8192 | tf_op jit(solution)/shard_map/all_to_all | solution.py:642
  40.3 4.4 %prepare_kernel.1 = (f32[2,128,256]{2,1,0:T(8,128)}, f32[2,256,256]{2,1,0:T(8,128)S(1)}, f32[1,1]{1,0:T(1,128)}) custom-call(s32[4]{0:T(128)S(1)} %pad_add_fusion.refs_0_.where, s32[1,2]{1,0:T(1,128)S(1)} %copy-done.9, s32[8,128]{1,0:T(8,128)S(1)} %bitcast.19, f32[256,256]{1,0:T(8,128)} %bitcast.35, bf16[2,256,256]{2,1,0:T(8,128)(2,1)} %constant.43.clone.refs_4_, ...), custom_call_target="tpu_custom_call" | custom-call | bytes 3674140 | tf_op jit(solution)/shard_map/prepare_kernel/pallas_call | solution.py:586
  44.7 1.3 side_kernel.1
  46.8 1.5 collective-permute-done.4.refs_4_
  48.3 9.2 %patterns.2 = (f32[2,256,256]{2,1,0:T(8,128)S(1)}, f32[16,9,8,256]{3,2,1,0:T(8,128)S(1)}, f32[16,9,8,256]{3,2,1,0:T(8,128)S(1)}, f32[4,2,32,256]{3,2,1,0:T(8,128...) custom-call(s32[4]{0:T(128)S(1)} %pad_add_fusion.refs_0_.where, ...), custom_call_target="tpu_custom_call" | custom-call | flops 6000000000 | bytes 9699356 | tf_op jit(solution)/shard_map/patterns/pallas_call | solution.py:586
  58.2 2.7 %collective-permute-done.6.refs_3_ = f32[4,2,32,256]{3,2,1,0:T(8,128)S(1)} collective-permute-done((f32[4,2,32,256]{3,2,1,0:T(8,128)S(1)}, f32[4,2,32,256]{3,2,1,0:T(8,128)S(1)}, u32[]{:S(2)}, u32[]{:S(2)}) %collective-permute-start.6) | collective-permute-done | bytes 262176 | tf_op jit(solution)/shard_map/ppermute | solution.py:608
  60.9 1.3 pack_kernel.2
  62.2 9.4 %all-to-all-start.1 = ((f32[16,9,8,256]{3,2,1,0:T(8,128)}), f32[16,9,8,256]{3,2,1,0:T(8,128)S(1)}, u32[]{:S(2)}, u32[]{:S(2)}) async-start(f32[16,9,8,256]{3,2,1,0:T(8,128)} %get-tuple-element.83), calls=%async_computation.1 | async-start | bytes 2359296 | tf_op jit(solution)/shard_map/all_to_all | solution.py:724
  72.0 1.8 collective-permute-start.8
  74.7 3.3 %collective-permute-done.7.refs_3_ = f32[2,2,32,256]{3,2,1,0:T(8,128)S(1)} collective-permute-done((f32[2,2,32,256]{3,2,1,0:T(8,128)S(1)}, f32[2,2,32,256]{3,2,1,0:T(8,128)S(1)}, u32[]{:S(2)}, u32[]{:S(2)}) %collective-permute-start.7) | collective-permute-done | bytes 131104 | tf_op jit(solution)/shard_map/ppermute | solution.py:604
  78.0 1.6 collective-permute-done.8.refs_4_
  80.5 2.3 place_kernel.2
  82.9 3.0 %collective-permute-start.13 = (f32[2,32,1024]{2,1,0:T(8,128)}, f32[2,32,1024]{2,1,0:T(8,128)S(1)}, u32[]{:S(2)}, u32[]{:S(2)}) collective-permute-start(f32[2,32,1024]{2,1,0:T(8,128)} %get-tuple-element.85.refs_5_), channel_id=1, source_target_pairs={{0,1},{1,2},{2,3},{3,4},{4,5},{5,6},{6,7},{7,8},{8,9},{9,10},{10,1... | collective-permute-start | bytes 786440 | tf_op jit(solution)/shard_map/ppermute | solution.py:612
  85.9 1.3 collective-permute-start.14
  87.2 2.4 all-to-all-done.1.refs_1_
  89.6 1.2 sum_kernel.2
  93.0 3.0 %illum_kernel.2.refs_6_.refs_3_ = f32[64,1024]{1,0:T(8,128)S(1)} custom-call(s32[4]{0:T(128)S(1)} %pad_add_fusion.refs_0_.where, s32[8,128]{1,0:T(8,128)S(1)} %bitcast.22, f32[1,1]{1,0:T(1,128)} %get-tuple-element.87.refs_2_, f32[256,256]{1,0:T(8,128)S(1)} %get-tuple-element.88.refs_3_), custom_call_target="tpu_custom_call" | custom-call | bytes 528404 | tf_op jit(solution)/shard_map/illum_kernel/pallas_call | solution.py:586
  97.4 1.7 share_kernel.2
  99.1 7.1 %all-to-all-start.2 = ((f32[16,8,8,256]{3,2,1,0:T(8,128)}), f32[16,8,8,256]{3,2,1,0:T(8,128)S(1)}, u32[]{:S(2)}, u32[]{:S(2)}) async-start(f32[16,8,8,256]{3,2,1,0:T(8,128)} %get-tuple-element.89), calls=%async_computation.2 | async-start | bytes 2097152 | tf_op jit(solution)/shard_map/all_to_all | solution.py:744
  106.2 3.6 %direction_kernel.2 = (f32[2,32,1024]{2,1,0:T(8,128)}, f32[1,2]{1,0:T(1,128)S(1)}, f32[2,2,32,256]{3,2,1,0:T(8,128)S(1)}, f32[2,2,32,256]{3,2,1,0:T(8,128)}, f32...) custom-call(s32[4]{0:T(128)S(1)} %pad_add_fusion.refs_0_.where, s32[8,128]{1,0:T(8,128)S(1)} %bitcast.23, ...), custom_call_target="tpu_custom_call" | custom-call | bytes 2101280 | tf_op jit(solution)/shard_map/direction_kernel/pallas_call | solution.py:586
  109.8 1.4 collective-permute-start.15
  111.3 1.4 collective-permute-start.16
  112.7 1.3 collective-permute-start.17
  114.0 1.5 collective-permute-done.15.refs_1_.refs_3_
  115.4 1.8 collective-permute-done.16.refs_2_.refs_4_
  117.5 4.4 %collective-permute-start.18 = (f32[4,2,32,256]{3,2,1,0:T(8,128)S(1)}, f32[4,2,32,256]{3,2,1,0:T(8,128)S(1)}, u32[]{:S(2)}, u32[]{:S(2)}) collective-permute-start(f32[4,2,32,256]{3,2,1,0:T(8,128)S(1)} %stack_kernel.2), channel_id=1, source_target_pairs={{0,16},{16,0},{32,48},{48,32},{64,80},{80,64},{96,112},{112,96},{1... | collective-permute-start | bytes 786440 | tf_op jit(solution)/shard_map/ppermute | solution.py:608
  121.9 1.2 collective-permute-done.18.refs_6_
  125.1 1.2 collective-permute-done.19.refs_4_
  126.3 3.4 %message_kernel.2 = (f32[128,128]{1,0:T(8,128)}, f32[1,1]{1,0:T(1,128)}) custom-call(s32[4]{0:T(128)S(1)} %pad_add_fusion.refs_0_.where, f32[16,8,8,256]{3,2,1,0:T(8,128)S(1)} %all-to-all-done.2.refs_1_, f32[4,2,256,256]{3,2,1,0:T(8,128)} %refs_4_.2, f32[2,128,256]{2,1,0:T(8,128)S(1)} %get-tuple-element.96.refs_3_, ...), custom_call_target="tpu_custom_call" | custom-call | bytes 3735588 | tf_op jit(solution)/shard_map/message_kernel/pallas_call | solution.py:586
  131.0 18.6 %all_to_all.54 = f32[128,1,128]{2,1,0:T(1,128)S(1)} all-to-all(f32[128,1,128]{2,1,0:T(1,128)S(1)} %bitcast.36), channel_id=1, replica_groups=mesh['pat'=8,'tile'=16] {'pat','tile'}, dimensions={0} | all-to-all | bytes 131072 | tf_op jit(solution)/shard_map/all_to_all | solution.py:785
  150.5 11.0 %patterns.3 = (f32[2,256,256]{2,1,0:T(8,128)}, f32[4,2,256,256]{3,2,1,0:T(8,128)}, f32[16,9,8,256]{3,2,1,0:T(8,128)S(1)}, f32[16,9,8,256]{3,2,1,0:T(8,128)S(1)},...) custom-call(s32[4]{0:T(128)S(1)} %pad_add_fusion.refs_0_.where, ...), custom_call_target="tpu_custom_call" | custom-call | flops 6000000000 | bytes 13434904 | tf_op jit(solution)/shard_map/patterns/pallas_call | solution.py:586
  162.5 2.8 %collective-permute-done.22.refs_3_ = f32[4,2,32,256]{3,2,1,0:T(8,128)S(1)} collective-permute-done((f32[4,2,32,256]{3,2,1,0:T(8,128)S(1)}, f32[4,2,32,256]{3,2,1,0:T(8,128)S(1)}, u32[]{:S(2)}, u32[]{:S(2)}) %collective-permute-start.22) | collective-permute-done | bytes 262176 | tf_op jit(solution)/shard_map/ppermute | solution.py:608
  165.2 1.3 pack_kernel.3
  166.6 3.8 %all-to-all-start.4 = ((f32[16,9,8,256]{3,2,1,0:T(8,128)}), f32[16,9,8,256]{3,2,1,0:T(8,128)S(1)}, u32[]{:S(2)}, u32[]{:S(2)}) async-start(f32[16,9,8,256]{3,2,1,0:T(8,128)} %get-tuple-element.111), calls=%async_computation.4 | async-start | bytes 2359296 | tf_op jit(solution)/shard_map/all_to_all | solution.py:724
  170.9 1.7 collective-permute-start.24
  173.4 3.7 %collective-permute-done.23.refs_3_ = f32[2,2,32,256]{3,2,1,0:T(8,128)S(1)} collective-permute-done((f32[2,2,32,256]{3,2,1,0:T(8,128)S(1)}, f32[2,2,32,256]{3,2,1,0:T(8,128)S(1)}, u32[]{:S(2)}, u32[]{:S(2)}) %collective-permute-start.23) | collective-permute-done | bytes 131104 | tf_op jit(solution)/shard_map/ppermute | solution.py:604
  177.1 1.6 collective-permute-done.24.refs_4_
  179.6 2.3 place_kernel.3
  182.0 2.8 %collective-permute-start.29 = (f32[2,32,1024]{2,1,0:T(8,128)}, f32[2,32,1024]{2,1,0:T(8,128)S(1)}, u32[]{:S(2)}, u32[]{:S(2)}) collective-permute-start(f32[2,32,1024]{2,1,0:T(8,128)} %get-tuple-element.113.refs_5_), channel_id=1, source_target_pairs={{0,1},{1,2},{2,3},{3,4},{4,5},{5,6},{6,7},{7,8},{8,9},{9,10},{10,1... | collective-permute-start | bytes 786440 | tf_op jit(solution)/shard_map/ppermute | solution.py:612
  184.8 1.3 collective-permute-start.30
  186.1 3.5 %all-to-all-done.4.refs_1_ = f32[16,9,8,256]{3,2,1,0:T(8,128)S(1)} async-done(((f32[16,9,8,256]{3,2,1,0:T(8,128)}), f32[16,9,8,256]{3,2,1,0:T(8,128)S(1)}, u32[]{:S(2)}, u32[]{:S(2)}) %all-to-all-start.4) | async-done | bytes 1179680 | tf_op jit(solution)/shard_map/all_to_all | solution.py:724
  191.7 1.3 collective-permute-start.27
  193.0 3.2 %illum_kernel.3.refs_6_.refs_3_ = f32[64,1024]{1,0:T(8,128)S(1)} custom-call(s32[4]{0:T(128)S(1)} %pad_add_fusion.refs_0_.where, s32[8,128]{1,0:T(8,128)S(1)} %bitcast.26, f32[1,1]{1,0:T(1,128)} %get-tuple-element.115.refs_2_, f32[256,256]{1,0:T(8,128)S(1)} %get-tuple-element.116.refs_3_), custom_call_target="tpu_custom_call" | custom-call | bytes 528404 | tf_op jit(solution)/shard_map/illum_kernel/pallas_call | solution.py:586
  197.4 1.7 share_kernel.3
  199.1 3.6 %direction_kernel.3 = (f32[2,32,1024]{2,1,0:T(8,128)}, f32[1,2]{1,0:T(1,128)S(1)}, f32[2,2,32,256]{3,2,1,0:T(8,128)S(1)}, f32[2,2,32,256]{3,2,1,0:T(8,128)}, f32...) custom-call(s32[4]{0:T(128)S(1)} %pad_add_fusion.refs_0_.where, s32[8,128]{1,0:T(8,128)S(1)} %bitcast.27, ...), custom_call_target="tpu_custom_call" | custom-call | bytes 2101280 | tf_op jit(solution)/shard_map/direction_kernel/pallas_call | solution.py:586
  202.8 6.1 %all-to-all-start.5 = ((f32[16,8,8,256]{3,2,1,0:T(8,128)}), f32[16,8,8,256]{3,2,1,0:T(8,128)S(1)}, u32[]{:S(2)}, u32[]{:S(2)}) async-start(f32[16,8,8,256]{3,2,1,0:T(8,128)} %get-tuple-element.117), calls=%async_computation.5 | async-start | bytes 2097152 | tf_op jit(solution)/shard_map/all_to_all | solution.py:744
  208.9 1.7 collective-permute-start.31
  210.5 1.6 collective-permute-start.32
  214.0 2.1 collective-permute-done.32.refs_2_.refs_4_
  217.1 6.2 %collective-permute-start.34 = (f32[4,2,32,256]{3,2,1,0:T(8,128)S(1)}, f32[4,2,32,256]{3,2,1,0:T(8,128)S(1)}, u32[]{:S(2)}, u32[]{:S(2)}) collective-permute-start(f32[4,2,32,256]{3,2,1,0:T(8,128)S(1)} %stack_kernel.3), channel_id=1, source_target_pairs={{0,16},{16,0},{32,48},{48,32},{64,80},{80,64},{96,112},{112,96},{1... | collective-permute-start | bytes 786440 | tf_op jit(solution)/shard_map/ppermute | solution.py:608
  223.3 1.2 collective-permute-done.34.refs_6_
  224.5 1.7 patch_kernel.3
  226.5 1.2 collective-permute-done.35.refs_4_
  227.7 3.4 %message_kernel.3 = (f32[128,128]{1,0:T(8,128)}, f32[1,1]{1,0:T(1,128)}) custom-call(s32[4]{0:T(128)S(1)} %pad_add_fusion.refs_0_.where, f32[16,8,8,256]{3,2,1,0:T(8,128)S(1)} %all-to-all-done.5.refs_1_, f32[4,2,256,256]{3,2,1,0:T(8,128)} %get-tuple-element.118.refs_2_.probe, f32[2,128,256]{2,1,0:T(8,128)S(1)} %get-tuple-element.125.refs_3_, ...), custom_call_target="tpu_custom_call" | custom-call | bytes 3735588 | tf_op jit(solution)/shard_map/message_kernel/pallas_call | solution.py:586
  232.3 9.7 %all-to-all-start.6 = ((f32[128,1,128]{2,1,0:T(1,128)}), f32[128,1,128]{2,1,0:T(1,128)S(1)}, u32[]{:S(2)}, u32[]{:S(2)}) async-start(f32[128,1,128]{2,1,0:T(1,128)} %bitcast.12), calls=%async_computation.6 | async-start | bytes 131072 | tf_op jit(solution)/shard_map/all_to_all | solution.py:785
  242.1 9.7 %all-to-all-done.6 = f32[128,1,128]{2,1,0:T(1,128)S(1)} async-done(((f32[128,1,128]{2,1,0:T(1,128)}), f32[128,1,128]{2,1,0:T(1,128)S(1)}, u32[]{:S(2)}, u32[]{:S(2)}) %all-to-all-start.6) | async-done | bytes 65568 | tf_op jit(solution)/shard_map/all_to_all | solution.py:785
  252.8 7.2 %shard_map.78 = (f32[2,256,1024]{2,1,0:T(8,128)}, f32[4,2,256,256]{3,2,1,0:T(8,128)}) custom-call(s32[4]{0:T(128)S(1)} %pad_add_fusion.refs_0_.where, f32[128,128]{1,0:T(8,128)S(1)} %bitcast.30, f32[128,128]{1,0:T(8,128)S(1)} %bitcast.31, f32[2,256,1024]{2,1,0:T(8,128)} %field.3, f32[8,2,32,1024]{3,2,1,0:T(8,128)} %bitcast.33, f32[8,2,32,1024]{3,2,1,0:T(8,128)} %bitcast.34, ...), custom_call_target="tpu_custom_call" | custom-call | tf_op jit(solution)/shard_map/pallas_call | solution.py:486
  (102 shorter events, 24.3 us)
Async XLA Ops:
  7.2 8.5 %copy-start.9 = (s32[1,2]{1,0:T(1,128)S(1)}, s32[1,2]{1,0:T(1,128)}, u32[]{:S(2)}) copy-start(s32[1,2]{1,0:T(1,128)} %refs_1_.5) | copy-start | bytes 28
  7.3 1.6 copy-start
  10.4 34.3 %collective-permute-start.2 = (f32[128,1024]{1,0:T(8,128)}, f32[128,1024]{1,0:T(8,128)S(1)}, u32[]{:S(2)}, u32[]{:S(2)}) collective-permute-start(f32[128,1024]{1,0:T(8,128)} %get-tuple-element.69), channel_id=1, source_target_pairs={{0,1},{1,2},{2,3},{3,4},{4,5},{5,6},{6,7},{7,8},{8,9},{9,10},{10,1... | collective-permute-start | bytes 1572872 | tf_op jit(solution)/shard_map/ppermute | solution.py:612
  14.4 30.3 %collective-permute-start.3 = (f32[128,1024]{1,0:T(8,128)}, f32[128,1024]{1,0:T(8,128)S(1)}, u32[]{:S(2)}, u32[]{:S(2)}) collective-permute-start(f32[128,1024]{1,0:T(8,128)} %get-tuple-element.70), channel_id=1, source_target_pairs={{1,0},{2,1},{3,2},{4,3},{5,4},{6,5},{7,6},{8,7},{9,8},{10,9},{11,1... | collective-permute-start | bytes 1572872 | tf_op jit(solution)/shard_map/ppermute | solution.py:616
  15.7 13.3 %collective-permute-start.1 = (s32[1,2]{1,0:T(1,128)S(1)}, s32[1,2]{1,0:T(1,128)S(1)}, u32[]{:S(2)}, u32[]{:S(2)}) collective-permute-start(s32[1,2]{1,0:T(1,128)S(1)} %copy-done.9), channel_id=1, source_target_pairs={{1,0},{2,1},{3,2},{4,3},{5,4},{6,5},{7,6},{8,7},{9,8},{10,9},{11,1... | collective-permute-start | bytes 32 | tf_op jit(solution)/shard_map/ppermute | solution.py:616
  17.0 12.0 %collective-permute-start = (s32[1,2]{1,0:T(1,128)S(1)}, s32[1,2]{1,0:T(1,128)S(1)}, u32[]{:S(2)}, u32[]{:S(2)}) collective-permute-start(s32[1,2]{1,0:T(1,128)S(1)} %copy-done.9), channel_id=1, source_target_pairs={{0,1},{1,2},{2,3},{3,4},{4,5},{5,6},{6,7},{7,8},{8,9},{9,10},{10,1... | collective-permute-start | bytes 32 | tf_op jit(solution)/shard_map/ppermute | solution.py:612
  46.0 2.3 collective-permute-start.4
  57.6 65.5 %copy-start.7 = (f32[2,256,256]{2,1,0:T(8,128)}, f32[2,256,256]{2,1,0:T(8,128)S(1)}, u32[]{:S(2)}) copy-start(f32[2,256,256]{2,1,0:T(8,128)S(1)} %get-tuple-element.95.refs_7_.refs_3_) | copy-start | bytes 1572868
  57.6 3.3 %collective-permute-start.5 = (f32[16,9,8,256]{3,2,1,0:T(8,128)S(1)}, f32[16,9,8,256]{3,2,1,0:T(8,128)S(1)}, u32[]{:S(2)}, u32[]{:S(2)}) collective-permute-start(f32[16,9,8,256]{3,2,1,0:T(8,128)S(1)} %get-tuple-element.75), channel_id=1, source_target_pairs={{0,16},{16,0},{32,48},{48,32},{64,80},{80,64},{96,112},{112,96},{1... | collective-permute-start | bytes 3538952 | tf_op jit(solution)/shard_map/ppermute | solution.py:608
  58.0 2.9 %collective-permute-start.6 = (f32[4,2,32,256]{3,2,1,0:T(8,128)S(1)}, f32[4,2,32,256]{3,2,1,0:T(8,128)S(1)}, u32[]{:S(2)}, u32[]{:S(2)}) collective-permute-start(f32[4,2,32,256]{3,2,1,0:T(8,128)S(1)} %get-tuple-element.77), channel_id=1, source_target_pairs={{0,16},{16,0},{32,48},{48,32},{64,80},{80,64},{96,112},{112,96},{1... | collective-permute-start | bytes 786440 | tf_op jit(solution)/shard_map/ppermute | solution.py:608
  62.2 9.5 %copy-start.22 = (f32[2,2,32,256]{3,2,1,0:T(8,128)S(1)}, f32[2,2,32,256]{3,2,1,0:T(8,128)}, u32[]{:S(2)}) copy-start(f32[2,2,32,256]{3,2,1,0:T(8,128)} %get-tuple-element.79) | copy-start | bytes 393220
  62.2 9.8 %copy-start.20 = (f32[2,2,32,256]{3,2,1,0:T(8,128)S(1)}, f32[2,2,32,256]{3,2,1,0:T(8,128)}, u32[]{:S(2)}) copy-start(f32[2,2,32,256]{3,2,1,0:T(8,128)} %get-tuple-element.80) | copy-start | bytes 393220
  62.2 11.6 %copy-start.18 = (f32[2,2,32,256]{3,2,1,0:T(8,128)S(1)}, f32[2,2,32,256]{3,2,1,0:T(8,128)}, u32[]{:S(2)}) copy-start(f32[2,2,32,256]{3,2,1,0:T(8,128)} %get-tuple-element.81) | copy-start | bytes 393220
  62.2 27.4 %all-to-all-start.1 = ((f32[16,9,8,256]{3,2,1,0:T(8,128)}), f32[16,9,8,256]{3,2,1,0:T(8,128)S(1)}, u32[]{:S(2)}, u32[]{:S(2)}) async-start(f32[16,9,8,256]{3,2,1,0:T(8,128)} %get-tuple-element.83), calls=%async_computation.1 | async-start | bytes 2359296 | tf_op jit(solution)/shard_map/all_to_all | solution.py:724
  71.7 6.3 %collective-permute-start.7 = (f32[2,2,32,256]{3,2,1,0:T(8,128)S(1)}, f32[2,2,32,256]{3,2,1,0:T(8,128)S(1)}, u32[]{:S(2)}, u32[]{:S(2)}) collective-permute-start(f32[2,2,32,256]{3,2,1,0:T(8,128)S(1)} %copy-done.22), channel_id=1, source_target_pairs={{0,32},{16,48},{32,64},{48,80},{64,96},{80,112},{96,0},{112,16},{1... | collective-permute-start | bytes 393224 | tf_op jit(solution)/shard_map/ppermute | solution.py:604
  72.0 7.5 %collective-permute-start.8 = (f32[2,2,32,256]{3,2,1,0:T(8,128)S(1)}, f32[2,2,32,256]{3,2,1,0:T(8,128)S(1)}, u32[]{:S(2)}, u32[]{:S(2)}) collective-permute-start(f32[2,2,32,256]{3,2,1,0:T(8,128)S(1)} %copy-done.20), channel_id=1, source_target_pairs={{0,64},{16,80},{32,96},{48,112},{64,0},{80,16},{96,32},{112,48},{1... | collective-permute-start | bytes 393224 | tf_op jit(solution)/shard_map/ppermute | solution.py:604
  73.8 6.7 %collective-permute-start.9 = (f32[2,2,32,256]{3,2,1,0:T(8,128)S(1)}, f32[2,2,32,256]{3,2,1,0:T(8,128)S(1)}, u32[]{:S(2)}, u32[]{:S(2)}) collective-permute-start(f32[2,2,32,256]{3,2,1,0:T(8,128)S(1)} %copy-done.18), channel_id=1, source_target_pairs={{0,96},{16,112},{32,0},{48,16},{64,32},{80,48},{96,64},{112,80},{1... | collective-permute-start | bytes 393224 | tf_op jit(solution)/shard_map/ppermute | solution.py:604
  82.9 13.1 %collective-permute-start.13 = (f32[2,32,1024]{2,1,0:T(8,128)}, f32[2,32,1024]{2,1,0:T(8,128)S(1)}, u32[]{:S(2)}, u32[]{:S(2)}) collective-permute-start(f32[2,32,1024]{2,1,0:T(8,128)} %get-tuple-element.85.refs_5_), channel_id=1, source_target_pairs={{0,1},{1,2},{2,3},{3,4},{4,5},{5,6},{6,7},{7,8},{8,9},{9,10},{10,1... | collective-permute-start | bytes 786440 | tf_op jit(solution)/shard_map/ppermute | solution.py:612
  85.9 10.1 %collective-permute-start.14 = (f32[2,32,1024]{2,1,0:T(8,128)}, f32[2,32,1024]{2,1,0:T(8,128)S(1)}, u32[]{:S(2)}, u32[]{:S(2)}) collective-permute-start(f32[2,32,1024]{2,1,0:T(8,128)} %get-tuple-element.86.refs_4_), channel_id=1, source_target_pairs={{1,0},{2,1},{3,2},{4,3},{5,4},{6,5},{7,6},{8,7},{9,8},{10,9},{11,1... | collective-permute-start | bytes 786440 | tf_op jit(solution)/shard_map/ppermute | solution.py:616
  90.8 5.2 %collective-permute-start.12 = (f32[9,8,256]{2,1,0:T(8,128)S(1)}, f32[9,8,256]{2,1,0:T(8,128)S(1)}, u32[]{:S(2)}, u32[]{:S(2)}) collective-permute-start(f32[9,8,256]{2,1,0:T(8,128)S(1)} %get-tuple-element.84.refs_0_), channel_id=1, source_target_pairs={{0,96},{16,112},{32,0},{48,16},{64,32},{80,48},{96,64},{112,80},{1... | collective-permute-start | bytes 221192 | tf_op jit(solution)/shard_map/ppermute | solution.py:604
  91.9 4.7 %collective-permute-start.11 = (f32[9,8,256]{2,1,0:T(8,128)S(1)}, f32[9,8,256]{2,1,0:T(8,128)S(1)}, u32[]{:S(2)}, u32[]{:S(2)}) collective-permute-start(f32[9,8,256]{2,1,0:T(8,128)S(1)} %get-tuple-element.84.refs_0_), channel_id=1, source_target_pairs={{0,64},{16,80},{32,96},{48,112},{64,0},{80,16},{96,32},{112,48},{1... | collective-permute-start | bytes 221192 | tf_op jit(solution)/shard_map/ppermute | solution.py:604
  92.9 4.5 %collective-permute-start.10 = (f32[9,8,256]{2,1,0:T(8,128)S(1)}, f32[9,8,256]{2,1,0:T(8,128)S(1)}, u32[]{:S(2)}, u32[]{:S(2)}) collective-permute-start(f32[9,8,256]{2,1,0:T(8,128)S(1)} %get-tuple-element.84.refs_0_), channel_id=1, source_target_pairs={{0,32},{16,48},{32,64},{48,80},{64,96},{80,112},{96,0},{112,16},{1... | collective-permute-start | bytes 221192 | tf_op jit(solution)/shard_map/ppermute | solution.py:604
  96.0 3.1 %copy-start.3 = (f32[2,32,1024]{2,1,0:T(8,128)}, f32[2,32,1024]{2,1,0:T(8,128)S(1)}, u32[]{:S(2)}) copy-start(f32[2,32,1024]{2,1,0:T(8,128)S(1)} %collective-permute-done.13.refs_4_.refs_6_) | copy-start | bytes 786436
  96.0 3.1 %copy-start.4 = (f32[2,32,1024]{2,1,0:T(8,128)}, f32[2,32,1024]{2,1,0:T(8,128)S(1)}, u32[]{:S(2)}) copy-start(f32[2,32,1024]{2,1,0:T(8,128)S(1)} %collective-permute-done.14.refs_5_.refs_7_) | copy-start | bytes 786436
  99.1 27.2 %all-to-all-start.2 = ((f32[16,8,8,256]{3,2,1,0:T(8,128)}), f32[16,8,8,256]{3,2,1,0:T(8,128)S(1)}, u32[]{:S(2)}, u32[]{:S(2)}) async-start(f32[16,8,8,256]{3,2,1,0:T(8,128)} %get-tuple-element.89), calls=%async_computation.2 | async-start | bytes 2097152 | tf_op jit(solution)/shard_map/all_to_all | solution.py:744
  106.2 135.9 %all-gather.5.cloned.1.call-start = ((), (), s32[]{:S(2)}) async-start(), calls=%async_computation.7 | async-start | bytes 2359296 | tf_op jit(solution)/shard_map/all_gather | solution.py:755
  109.8 5.6 %collective-permute-start.15 = (f32[2,2,32,256]{3,2,1,0:T(8,128)}, f32[2,2,32,256]{3,2,1,0:T(8,128)S(1)}, u32[]{:S(2)}, u32[]{:S(2)}) collective-permute-start(f32[2,2,32,256]{3,2,1,0:T(8,128)} %get-tuple-element.92), channel_id=1, source_target_pairs={{0,32},{16,48},{32,64},{48,80},{64,96},{80,112},{96,0},{112,16},{1... | collective-permute-start | bytes 393224 | tf_op jit(solution)/shard_map/ppermute | solution.py:604
  111.3 5.9 %collective-permute-start.16 = (f32[2,2,32,256]{3,2,1,0:T(8,128)}, f32[2,2,32,256]{3,2,1,0:T(8,128)S(1)}, u32[]{:S(2)}, u32[]{:S(2)}) collective-permute-start(f32[2,2,32,256]{3,2,1,0:T(8,128)} %get-tuple-element.93), channel_id=1, source_target_pairs={{0,64},{16,80},{32,96},{48,112},{64,0},{80,16},{96,32},{112,48},{1... | collective-permute-start | bytes 393224 | tf_op jit(solution)/shard_map/ppermute | solution.py:604
  112.7 4.8 %collective-permute-start.17 = (f32[2,2,32,256]{3,2,1,0:T(8,128)}, f32[2,2,32,256]{3,2,1,0:T(8,128)S(1)}, u32[]{:S(2)}, u32[]{:S(2)}) collective-permute-start(f32[2,2,32,256]{3,2,1,0:T(8,128)} %get-tuple-element.94), channel_id=1, source_target_pairs={{0,96},{16,112},{32,0},{48,16},{64,32},{80,48},{96,64},{112,80},{1... | collective-permute-start | bytes 393224 | tf_op jit(solution)/shard_map/ppermute | solution.py:604
  117.5 5.6 %collective-permute-start.18 = (f32[4,2,32,256]{3,2,1,0:T(8,128)S(1)}, f32[4,2,32,256]{3,2,1,0:T(8,128)S(1)}, u32[]{:S(2)}, u32[]{:S(2)}) collective-permute-start(f32[4,2,32,256]{3,2,1,0:T(8,128)S(1)} %stack_kernel.2), channel_id=1, source_target_pairs={{0,16},{16,0},{32,48},{48,32},{64,80},{80,64},{96,112},{112,96},{1... | collective-permute-start | bytes 786440 | tf_op jit(solution)/shard_map/ppermute | solution.py:608
  124.8 1.5 collective-permute-start.19
  129.7 1.3 copy-start.12
  130.5 19.1 %copy-start.2 = (f32[8,128,256]{2,1,0:T(8,128)}, f32[8,128,256]{2,1,0:T(8,128)S(1)}, u32[]{:S(2)}) copy-start(f32[8,128,256]{2,1,0:T(8,128)S(1)} %relay_kernel.2.refs_8_) | copy-start | bytes 3145732
  130.5 19.0 %collective-permute-start.20 = (f32[8,128,256]{2,1,0:T(8,128)S(1)}, f32[8,128,256]{2,1,0:T(8,128)S(1)}, u32[]{:S(2)}, u32[]{:S(2)}) collective-permute-start(f32[8,128,256]{2,1,0:T(8,128)S(1)} %relay_kernel.2.refs_8_), channel_id=1, source_target_pairs={{0,16},{16,0},{32,48},{48,32},{64,80},{80,64},{96,112},{112,96},{1... | collective-permute-start | bytes 3145736 | tf_op jit(solution)/shard_map/ppermute | solution.py:608
  161.5 3.7 %collective-permute-start.21 = (f32[16,9,8,256]{3,2,1,0:T(8,128)S(1)}, f32[16,9,8,256]{3,2,1,0:T(8,128)S(1)}, u32[]{:S(2)}, u32[]{:S(2)}) collective-permute-start(f32[16,9,8,256]{3,2,1,0:T(8,128)S(1)} %get-tuple-element.103), channel_id=1, source_target_pairs={{0,16},{16,0},{32,48},{48,32},{64,80},{80,64},{96,112},{112,96},{1... | collective-permute-start | bytes 3538952 | tf_op jit(solution)/shard_map/ppermute | solution.py:608
  162.4 2.8 %collective-permute-start.22 = (f32[4,2,32,256]{3,2,1,0:T(8,128)S(1)}, f32[4,2,32,256]{3,2,1,0:T(8,128)S(1)}, u32[]{:S(2)}, u32[]{:S(2)}) collective-permute-start(f32[4,2,32,256]{3,2,1,0:T(8,128)S(1)} %get-tuple-element.105), channel_id=1, source_target_pairs={{0,16},{16,0},{32,48},{48,32},{64,80},{80,64},{96,112},{112,96},{1... | collective-permute-start | bytes 786440 | tf_op jit(solution)/shard_map/ppermute | solution.py:608
  166.5 3.9 %copy-start.21 = (f32[2,2,32,256]{3,2,1,0:T(8,128)S(1)}, f32[2,2,32,256]{3,2,1,0:T(8,128)}, u32[]{:S(2)}) copy-start(f32[2,2,32,256]{3,2,1,0:T(8,128)} %get-tuple-element.107) | copy-start | bytes 393220
  166.5 4.4 %copy-start.19 = (f32[2,2,32,256]{3,2,1,0:T(8,128)S(1)}, f32[2,2,32,256]{3,2,1,0:T(8,128)}, u32[]{:S(2)}) copy-start(f32[2,2,32,256]{3,2,1,0:T(8,128)} %get-tuple-element.108) | copy-start | bytes 393220
  166.5 6.0 %copy-start.17 = (f32[2,2,32,256]{3,2,1,0:T(8,128)S(1)}, f32[2,2,32,256]{3,2,1,0:T(8,128)}, u32[]{:S(2)}) copy-start(f32[2,2,32,256]{3,2,1,0:T(8,128)} %get-tuple-element.109) | copy-start | bytes 393220
  166.6 23.1 %all-to-all-start.4 = ((f32[16,9,8,256]{3,2,1,0:T(8,128)}), f32[16,9,8,256]{3,2,1,0:T(8,128)S(1)}, u32[]{:S(2)}, u32[]{:S(2)}) async-start(f32[16,9,8,256]{3,2,1,0:T(8,128)} %get-tuple-element.111), calls=%async_computation.4 | async-start | bytes 2359296 | tf_op jit(solution)/shard_map/all_to_all | solution.py:724
  170.4 81.3 %all-gather.7.cloned.1.call-start = ((), (), s32[]{:S(2)}) async-start(), calls=%async_computation.8 | async-start | bytes 2359296 | tf_op jit(solution)/shard_map/all_gather | solution.py:755
  170.5 6.6 %collective-permute-start.23 = (f32[2,2,32,256]{3,2,1,0:T(8,128)S(1)}, f32[2,2,32,256]{3,2,1,0:T(8,128)S(1)}, u32[]{:S(2)}, u32[]{:S(2)}) collective-permute-start(f32[2,2,32,256]{3,2,1,0:T(8,128)S(1)} %copy-done.21), channel_id=1, source_target_pairs={{0,32},{16,48},{32,64},{48,80},{64,96},{80,112},{96,0},{112,16},{1... | collective-permute-start | bytes 393224 | tf_op jit(solution)/shard_map/ppermute | solution.py:604
  170.9 7.8 %collective-permute-start.24 = (f32[2,2,32,256]{3,2,1,0:T(8,128)S(1)}, f32[2,2,32,256]{3,2,1,0:T(8,128)S(1)}, u32[]{:S(2)}, u32[]{:S(2)}) collective-permute-start(f32[2,2,32,256]{3,2,1,0:T(8,128)S(1)} %copy-done.19), channel_id=1, source_target_pairs={{0,64},{16,80},{32,96},{48,112},{64,0},{80,16},{96,32},{112,48},{1... | collective-permute-start | bytes 393224 | tf_op jit(solution)/shard_map/ppermute | solution.py:604
  172.6 7.1 %collective-permute-start.25 = (f32[2,2,32,256]{3,2,1,0:T(8,128)S(1)}, f32[2,2,32,256]{3,2,1,0:T(8,128)S(1)}, u32[]{:S(2)}, u32[]{:S(2)}) collective-permute-start(f32[2,2,32,256]{3,2,1,0:T(8,128)S(1)} %copy-done.17), channel_id=1, source_target_pairs={{0,96},{16,112},{32,0},{48,16},{64,32},{80,48},{96,64},{112,80},{1... | collective-permute-start | bytes 393224 | tf_op jit(solution)/shard_map/ppermute | solution.py:604
  182.0 14.3 %collective-permute-start.29 = (f32[2,32,1024]{2,1,0:T(8,128)}, f32[2,32,1024]{2,1,0:T(8,128)S(1)}, u32[]{:S(2)}, u32[]{:S(2)}) collective-permute-start(f32[2,32,1024]{2,1,0:T(8,128)} %get-tuple-element.113.refs_5_), channel_id=1, source_target_pairs={{0,1},{1,2},{2,3},{3,4},{4,5},{5,6},{6,7},{7,8},{8,9},{9,10},{10,1... | collective-permute-start | bytes 786440 | tf_op jit(solution)/shard_map/ppermute | solution.py:612
  184.8 11.4 %collective-permute-start.30 = (f32[2,32,1024]{2,1,0:T(8,128)}, f32[2,32,1024]{2,1,0:T(8,128)S(1)}, u32[]{:S(2)}, u32[]{:S(2)}) collective-permute-start(f32[2,32,1024]{2,1,0:T(8,128)} %get-tuple-element.114.refs_4_), channel_id=1, source_target_pairs={{1,0},{2,1},{3,2},{4,3},{5,4},{6,5},{7,6},{8,7},{9,8},{10,9},{11,1... | collective-permute-start | bytes 786440 | tf_op jit(solution)/shard_map/ppermute | solution.py:616
  190.8 5.5 %collective-permute-start.28 = (f32[9,8,256]{2,1,0:T(8,128)S(1)}, f32[9,8,256]{2,1,0:T(8,128)S(1)}, u32[]{:S(2)}, u32[]{:S(2)}) collective-permute-start(f32[9,8,256]{2,1,0:T(8,128)S(1)} %get-tuple-element.112.refs_0_), channel_id=1, source_target_pairs={{0,96},{16,112},{32,0},{48,16},{64,32},{80,48},{96,64},{112,80},{1... | collective-permute-start | bytes 221192 | tf_op jit(solution)/shard_map/ppermute | solution.py:604
  191.7 4.7 %collective-permute-start.27 = (f32[9,8,256]{2,1,0:T(8,128)S(1)}, f32[9,8,256]{2,1,0:T(8,128)S(1)}, u32[]{:S(2)}, u32[]{:S(2)}) collective-permute-start(f32[9,8,256]{2,1,0:T(8,128)S(1)} %get-tuple-element.112.refs_0_), channel_id=1, source_target_pairs={{0,64},{16,80},{32,96},{48,112},{64,0},{80,16},{96,32},{112,48},{1... | collective-permute-start | bytes 221192 | tf_op jit(solution)/shard_map/ppermute | solution.py:604
  193.0 4.4 %collective-permute-start.26 = (f32[9,8,256]{2,1,0:T(8,128)S(1)}, f32[9,8,256]{2,1,0:T(8,128)S(1)}, u32[]{:S(2)}, u32[]{:S(2)}) collective-permute-start(f32[9,8,256]{2,1,0:T(8,128)S(1)} %get-tuple-element.112.refs_0_), channel_id=1, source_target_pairs={{0,32},{16,48},{32,64},{48,80},{64,96},{80,112},{96,0},{112,16},{1... | collective-permute-start | bytes 221192 | tf_op jit(solution)/shard_map/ppermute | solution.py:604
  196.2 2.8 %copy-start.5 = (f32[2,32,1024]{2,1,0:T(8,128)}, f32[2,32,1024]{2,1,0:T(8,128)S(1)}, u32[]{:S(2)}) copy-start(f32[2,32,1024]{2,1,0:T(8,128)S(1)} %collective-permute-done.29.refs_4_.refs_6_) | copy-start | bytes 786436
  196.3 2.8 %copy-start.6 = (f32[2,32,1024]{2,1,0:T(8,128)}, f32[2,32,1024]{2,1,0:T(8,128)S(1)}, u32[]{:S(2)}) copy-start(f32[2,32,1024]{2,1,0:T(8,128)S(1)} %collective-permute-done.30.refs_5_.refs_7_) | copy-start | bytes 786436
  202.7 6.2 %copy-start.16 = (f32[2,2,32,256]{3,2,1,0:T(8,128)S(1)}, f32[2,2,32,256]{3,2,1,0:T(8,128)}, u32[]{:S(2)}) copy-start(f32[2,2,32,256]{3,2,1,0:T(8,128)} %get-tuple-element.121) | copy-start | bytes 393220
  202.7 7.8 %copy-start.15 = (f32[2,2,32,256]{3,2,1,0:T(8,128)S(1)}, f32[2,2,32,256]{3,2,1,0:T(8,128)}, u32[]{:S(2)}) copy-start(f32[2,2,32,256]{3,2,1,0:T(8,128)} %get-tuple-element.122) | copy-start | bytes 393220
  202.7 9.4 %copy-start.14 = (f32[2,2,32,256]{3,2,1,0:T(8,128)S(1)}, f32[2,2,32,256]{3,2,1,0:T(8,128)}, u32[]{:S(2)}) copy-start(f32[2,2,32,256]{3,2,1,0:T(8,128)} %get-tuple-element.123) | copy-start | bytes 393220
  202.7 21.8 %copy-start.8 = (f32[2,256,256]{2,1,0:T(8,128)S(1)}, f32[2,256,256]{2,1,0:T(8,128)}, u32[]{:S(2)}) copy-start(f32[2,256,256]{2,1,0:T(8,128)} %get-tuple-element.124.refs_7_) | copy-start | bytes 1572868
  202.8 25.0 %all-to-all-start.5 = ((f32[16,8,8,256]{3,2,1,0:T(8,128)}), f32[16,8,8,256]{3,2,1,0:T(8,128)S(1)}, u32[]{:S(2)}, u32[]{:S(2)}) async-start(f32[16,8,8,256]{3,2,1,0:T(8,128)} %get-tuple-element.117), calls=%async_computation.5 | async-start | bytes 2097152 | tf_op jit(solution)/shard_map/all_to_all | solution.py:744
  208.9 5.1 %collective-permute-start.31 = (f32[2,2,32,256]{3,2,1,0:T(8,128)S(1)}, f32[2,2,32,256]{3,2,1,0:T(8,128)S(1)}, u32[]{:S(2)}, u32[]{:S(2)}) collective-permute-start(f32[2,2,32,256]{3,2,1,0:T(8,128)S(1)} %copy-done.16), channel_id=1, source_target_pairs={{0,32},{16,48},{32,64},{48,80},{64,96},{80,112},{96,0},{112,16},{1... | collective-permute-start | bytes 393224 | tf_op jit(solution)/shard_map/ppermute | solution.py:604
  210.5 5.6 %collective-permute-start.32 = (f32[2,2,32,256]{3,2,1,0:T(8,128)S(1)}, f32[2,2,32,256]{3,2,1,0:T(8,128)S(1)}, u32[]{:S(2)}, u32[]{:S(2)}) collective-permute-start(f32[2,2,32,256]{3,2,1,0:T(8,128)S(1)} %copy-done.15), channel_id=1, source_target_pairs={{0,64},{16,80},{32,96},{48,112},{64,0},{80,16},{96,32},{112,48},{1... | collective-permute-start | bytes 393224 | tf_op jit(solution)/shard_map/ppermute | solution.py:604
  212.1 4.9 %collective-permute-start.33 = (f32[2,2,32,256]{3,2,1,0:T(8,128)S(1)}, f32[2,2,32,256]{3,2,1,0:T(8,128)S(1)}, u32[]{:S(2)}, u32[]{:S(2)}) collective-permute-start(f32[2,2,32,256]{3,2,1,0:T(8,128)S(1)} %copy-done.14), channel_id=1, source_target_pairs={{0,96},{16,112},{32,0},{48,16},{64,32},{80,48},{96,64},{112,80},{1... | collective-permute-start | bytes 393224 | tf_op jit(solution)/shard_map/ppermute | solution.py:604
  217.1 7.4 %collective-permute-start.34 = (f32[4,2,32,256]{3,2,1,0:T(8,128)S(1)}, f32[4,2,32,256]{3,2,1,0:T(8,128)S(1)}, u32[]{:S(2)}, u32[]{:S(2)}) collective-permute-start(f32[4,2,32,256]{3,2,1,0:T(8,128)S(1)} %stack_kernel.3), channel_id=1, source_target_pairs={{0,16},{16,0},{32,48},{48,32},{64,80},{80,64},{96,112},{112,96},{1... | collective-permute-start | bytes 786440 | tf_op jit(solution)/shard_map/ppermute | solution.py:608
  226.1 1.6 collective-permute-start.35
  231.9 19.9 %copy-start.1 = (f32[8,128,256]{2,1,0:T(8,128)}, f32[8,128,256]{2,1,0:T(8,128)S(1)}, u32[]{:S(2)}) copy-start(f32[8,128,256]{2,1,0:T(8,128)S(1)} %relay_kernel.3.dmine) | copy-start | bytes 3145732
  231.9 19.9 %collective-permute-start.36 = (f32[8,128,256]{2,1,0:T(8,128)S(1)}, f32[8,128,256]{2,1,0:T(8,128)S(1)}, u32[]{:S(2)}, u32[]{:S(2)}) collective-permute-start(f32[8,128,256]{2,1,0:T(8,128)S(1)} %relay_kernel.3.dmine), channel_id=1, source_target_pairs={{0,16},{16,0},{32,48},{48,32},{64,80},{80,64},{96,112},{112,96},{1... | collective-permute-start | bytes 3145736 | tf_op jit(solution)/shard_map/ppermute | solution.py:608
  232.3 19.4 %all-to-all-start.6 = ((f32[128,1,128]{2,1,0:T(1,128)}), f32[128,1,128]{2,1,0:T(1,128)S(1)}, u32[]{:S(2)}, u32[]{:S(2)}) async-start(f32[128,1,128]{2,1,0:T(1,128)} %bitcast.12), calls=%async_computation.6 | async-start | bytes 131072 | tf_op jit(solution)/shard_map/all_to_all | solution.py:785
  (3 other events, 2.8 us)
Sparse Core Ops, SparseCore 0:
  131.1 26.5 all-gather.4
  202.9 27.8 all-gather.6

commit v3 on v2

--- a/solution.py
+++ b/solution.py
@@ -101,22 +101,23 @@
     return pltpu.roll(rows, lax.rem(384 - shift, 384), axis=1)[:, :N]
 
 
-def prepare_kernel(where, here, near, measured, swap, field, out, base, token):
+def prepare_kernel(where, here, measured, swap, field, out, base, window, sem):
+    e0 = here[0, 0] - where[3]
+    block, shift = window_of(here)
+    copy = pltpu.make_async_copy(field.at[:, :, pl.ds(block, 384)], window, sem)
+    copy.start()
     high, mid, low = thirds(measured[...])
     across, down_rows = swap[0], swap[1]
     high, mid, low = thirds(dot(high, across) + dot(mid, across) + dot(low, across))
     value = dot(down_rows, high) + dot(down_rows, mid) + dot(down_rows, low)
     out[0] = value[:H]
     out[1] = value[H:]
-    e0 = here[0, 0] - where[3]
-    block, shift = window_of(here)
     row = lax.broadcasted_iota(jnp.int32, (N, N), 0) + e0
     inside = (row >= H) & (row < H + N)
+    copy.wait()
     for part in range(2):
-        rows = field[part, :, pl.ds(block, 384)]
-        rows = jnp.concatenate([rows[H:], rows[:H]], axis=0)
+        rows = jnp.concatenate([window[part, H:], window[part, :H]], axis=0)
         base[part] = jnp.where(inside, cut(rows, e0, shift), 0.0)
-    token[0, 0] = 0.0
 
 
 def edge_kernel(where, field, top_rows, low_rows, sems):
@@ -132,28 +133,23 @@
 
 
 def edges(where, field):
-    rows = pltpu.HBM((H, field.shape[2]), F32)
-    hbm = pl.BlockSpec(memory_space=pltpu.HBM)
+    rows = pltpu.VMEM((H, field.shape[2]), F32)
     return pl.pallas_call(
         edge_kernel,
         out_shape=[rows, rows],
         in_specs=[SMEM, ANY],
-        out_specs=[hbm, hbm],
+        out_specs=[VMEM, VMEM],
         scratch_shapes=[pltpu.SemaphoreType.DMA((2,))],
-        compiler_params=pltpu.CompilerParams(vmem_limit_bytes=2**20),
+        compiler_params=pltpu.CompilerParams(vmem_limit_bytes=2 * 2**20),
     )(where, field)
 
 
-def announce_kernel(here, above, below, out):
+def announce_kernel(here, out):
     lane = lax.broadcasted_iota(jnp.int32, (8, 128), 1)
-    value = jnp.zeros((8, 128), jnp.int32)
-    for at, place in enumerate((here, above, below)):
-        value = jnp.where(lane == 2 * at, place[0, 0], value)
-        value = jnp.where(lane == 2 * at + 1, place[0, 1], value)
-    out[...] = value
-
-
-def side_kernel(where, near, token, above, below, own, far):
+    out[...] = jnp.where(lane == 0, here[0, 0], here[0, 1])
+
+
+def side_kernel(where, near, base, above, below, own, far):
     y, c, top = where[0], where[1], where[3]
     own_row = near[2 * y + c, 0] - top
     far_row = near[2 * y + 1 - c, 0] - top
@@ -173,21 +169,21 @@
         patch[part] = jnp.where(outside, rows, base[part])
 
 
-def patterns_kernel(first, ready, *refs):
+def patterns_kernel(first, ready, leave, *refs):
     if first:
         where, here, base, own_side, far_side, probe_now, measured, tab = refs[:8]
-        patch_now, keep, send, mine, other, power, token, psi, model, obj = refs[8:]
-        token[0, 0] = 0.0
+        patch_now, keep, send, mine, other, power, psi, model, obj = refs[8:]
         add_side(where, here, base, own_side, far_side, patch_now)
     else:
         where, here, everyone, patch, probe, measured, tab, dirp, dmine, doth = refs[:10]
-        patch_now, probe_now = refs[10:12]
-        keep, send, mine, other, power, psi, model, obj = refs[12:]
+        patch_now, probe_now = refs[13:15]
+        keep, send, mine, other, power, psi, model, obj = refs[15:]
         object_step, probe_step = map(twice, step_sizes(everyone))
         ready(3)
         ready(7)
         for part in range(2):
             patch_now[part] = patch[part] + object_step * dirp[part]
+        leave(0)
     y, c = where[0], where[1]
     e0 = here[0, 0] - where[3]
     first_core = c == 0
@@ -200,15 +196,13 @@
         obj[plane, 1] += value[:, H:]
 
     def forward(k):
-        if first:
-            ready(5, k)
-        else:
-            ready(4, k)
+        if not first:
+            for index in (4, 8, 9):
+                ready(index, k)
             for part in range(2):
-                ready(8, 2 * k + part)
-                ready(9, 2 * k + part)
                 moved = probe_step * joined(first_core, dmine, doth, 2 * k + part)
                 probe_now[k, part] = probe[k, part] + moved
+            leave(1, k)
         pr, pi = probe_now[k, 0], probe_now[k, 1]
         orr, oi = patch_now[0], patch_now[1]
         power[...] += pr * pr + pi * pi
@@ -230,10 +224,12 @@
             psi[k, row] = far
             model[row] += far[:H] * far[:H] + far[H:] * far[H:]
 
-    ready(7 if first else 6)
+    if not first:
+        ready(6)
     for k in range(4):
         forward(k)
-    ready(6 if first else 5)
+    if not first:
+        ready(5)
     for row in range(2):
         model[row] = jnp.sqrt(measured[row] / jnp.maximum(model[row], FLOOR)) - 1.0
 
@@ -277,9 +273,9 @@
                     dest[s, plane, :, half * H : half * H + H] = rows
 
 
-def place_of(where, places, owner, pattern, band=0):
-    e0 = places[pattern, 2 * band] - where[3]
-    col = places[pattern, 2 * band + 1]
+def place_of(where, places, owner, pattern):
+    e0 = places[pattern, 0] - where[3]
+    col = places[pattern, 1]
     start = lax.rem(owner - e0 + 1024, 8)
     row = lax.shift_right_logical(e0 + 256 + start - owner, 3)
     base = pl.multiple_of(lax.shift_right_logical(row, 3) * 8, 8)
@@ -293,30 +289,20 @@
     acc[pl.ds(base, 40), pl.ds(block, 384)] += wide
 
 
-def illum_kernel(where, near, token, total, out, power, acc):
+def illum_kernel(where, near, total, out, power, acc):
     owner = 2 * where[0] + where[1]
     acc[...] = jnp.zeros_like(acc)
     power[0] = total[:, :H]
     power[1] = total[:, H:]
-
-    def from_band(band):
-        def one(pattern, carry):
-            start, base, turn, block, shift = place_of(where, near, owner, pattern, band)
-            rows = pl.ds(start, 32, stride=8)
-            piece = jnp.concatenate([power[0, rows, :], power[1, rows, :]], axis=1)
-            place(acc, piece, base, turn, block, shift)
-            return carry
-
-        return one
-
-    tile = where[2]
-    lax.fori_loop(0, 8, from_band(0), 0)
-    lax.fori_loop(0, jnp.where(tile == 0, 0, 8), from_band(1), 0)
-    lax.fori_loop(0, jnp.where(tile == 15, 0, 8), from_band(2), 0)
-    out[...] = acc[32:96, :1024]
-
-
-def place_kernel(where, near, b0, b1, b2, b3, low, high, token, acc):
+    for pattern in range(8):
+        start, base, turn, block, shift = place_of(where, near, owner, pattern)
+        rows = pl.ds(start, 32, stride=8)
+        piece = jnp.concatenate([power[0, rows, :], power[1, rows, :]], axis=1)
+        place(acc, piece, base - 32, turn, block, shift)
+    out[...] = acc[:64, :1024]
+
+
+def place_kernel(where, near, light, b0, b1, b2, b3, low, high, token, acc):
     token[0, 0] = 0.0
     y, c = where[0], where[1]
     owner = 2 * y + c
@@ -328,12 +314,14 @@
             for plane in range(2):
                 piece = (b0, b1, b2, b3)[s][which, plane]
                 place(acc.at[plane], piece, base - 32, turn, block, shift)
-    low[...] = acc[:, :32, :1024]
-    high[...] = acc[:, 32:64, :1024]
+    low[:2] = acc[:, :32, :1024]
+    high[:2] = acc[:, 32:64, :1024]
+    low[2] = light[:32]
+    high[2] = light[32:]
 
 
 def direction_kernel(
-    where, near, token, illum, low, high, above, below, band, sums, r0, r1, r2, r3, wide
+    where, near, token, low, high, above, below, band, sums, r0, r1, r2, r3, wide
 ):
     y, c = where[0], where[1]
     owner = 2 * y + c
@@ -342,7 +330,7 @@
     total_n = jnp.zeros((16, 1024), F32)
     for at, (own, came) in enumerate(((low, above), (high, below))):
         rows = slice(32 * at, 32 * at + 32)
-        light = illum[rows]
+        light = own[2] + came[2]
         scale = 1.0 / (light + RIDGE)
         real = (own[0] + came[0]) * scale
         imag = (own[1] + came[1]) * scale
@@ -406,7 +394,7 @@
     token[0, 0] = 0.0
 
 
-def share_kernel(own, a, b, d, above, below, light, spread_out, sums):
+def share_kernel(own, a, b, d, above, below, spread_out, sums):
     total = own[...] + a[...] + b[...] + d[...]
     illum = total[8]
     value = total[:8] * (1.0 / (illum + RIDGE))
@@ -445,64 +433,50 @@
     out[...] = message
 
 
-def finish_kernel(
-    where, one, two, field, band1, band2, probe, dmine, doth, field_out, probe_out, steps, lanes
-):
-    at = pl.program_id(0)
-
-    @pl.when(at == 0)
-    def _():
-        steps[0:1] = step_sizes(one)[0]
-        object_step, probe_step = step_sizes(two)
-        steps[1:2] = object_step
-        steps[2:3] = probe_step
-
-    first = jnp.concatenate([steps[0:1]] * 8, axis=1)
-    second = jnp.concatenate([steps[1:2]] * 8, axis=1)
-    probe_step = twice(steps[2:3])
-    for part in range(2):
-        for owner in range(8):
-            rows = pl.ds(owner, 8, stride=8)
-            moved = first * band1[owner, part] + second * band2[owner, part]
+def combine_kernel(ready, leave, one, two, *refs):
+    bands, out = refs[:8], refs[8]
+    first = jnp.concatenate([step_sizes(one)[0]] * 8, axis=1)
+    second = jnp.concatenate([step_sizes(two)[0]] * 8, axis=1)
+    for s in range(4):
+        ready(2 + s)
+        ready(6 + s)
+        for part in range(2):
+            out[s, part] = first * bands[s][part] + second * bands[4 + s][part]
+        leave(0, s)
+
+
+def probe_kernel(ready, leave, where, two, probe, dmine, doth, probe_out):
+    probe_step = twice(step_sizes(two)[1])
+    first_core = where[1] == 0
+    for k in range(4):
+        for index in (2, 3, 4):
+            ready(index, k)
+        for part in range(2):
+            moved = probe_step * joined(first_core, dmine, doth, 2 * k + part)
+            probe_out[k, part] = probe[k, part] + moved
+        leave(0, k)
+
+
+def object_kernel(ready, leave, where, field, mine, other, out, lanes):
+    y, c = where[0], where[1]
+    for block in range(4):
+        for index in (1, 2, 3):
+            ready(index, block)
+        own = slice(8 * block, 8 * block + 8)
+        for s in range(4):
+            for which, change in ((c, mine), (1 - c, other)):
+                owner = 2 * lax.rem(y - s + 4, 4) + which
+                rows = pl.ds(64 * block + owner, 8, stride=8)
+                for part in range(2):
+                    moved = change[s, part, own]
+                    for column in range(8):
+                        lanes[part, column, rows, :] = moved[:, column * H : column * H + H]
+        for part in range(2):
+            rows = slice(64 * block, 64 * block + 64)
             for column in range(8):
-                lanes[part, column, rows, :] = moved[:, column * H : column * H + H]
-        for column in range(8):
-            here = slice(column * H, column * H + H)
-            field_out[part, :, here] = field[part, :, here] + lanes[part, column]
-    local = lax.shift_right_logical(at, 1) == where[1]
-    for k in range(4):
-        for part in range(2):
-            plane = 2 * k + part
-            value = jnp.where(local, dmine[plane], doth[plane])
-            probe_out[k, part] = probe[k, part] + probe_step * value
-
-
-def finish(where, one, two, field, band1, band2, probe, dmine, doth):
-    rows = pl.BlockSpec((2, 64, 1024), lambda i: (0, i, 0))
-    classes = pl.BlockSpec((8, 2, 8, 1024), lambda i: (0, 0, i, 0))
-    modes = pl.BlockSpec((4, 2, 64, N), lambda i: (0, 0, i, 0))
-    gathered = pl.BlockSpec((8, 64, N), lambda i: (0, lax.rem(i, 2), 0))
-    whole = pl.BlockSpec((128, 128), lambda i: (0, 0))
-    return pl.pallas_call(
-        finish_kernel,
-        grid=(4,),
-        out_shape=[
-            jax.ShapeDtypeStruct(field.shape, F32),
-            jax.ShapeDtypeStruct(probe.shape, F32),
-        ],
-        in_specs=[SMEM, whole, whole, rows, classes, classes, modes, gathered, gathered],
-        out_specs=[rows, modes],
-        scratch_shapes=[pltpu.VMEM((8, 128), F32), pltpu.VMEM((2, 8, 64, H), F32)],
-        compiler_params=pltpu.CompilerParams(vmem_limit_bytes=14 * 2**20),
-    )(
-        where,
-        one,
-        two,
-        *[
-            pltpu.with_memory_space_constraint(a, pltpu.HBM)
-            for a in (field, band1, band2, probe, dmine, doth)
-        ],
-    )
+                here = slice(column * H, column * H + H)
+                out[part, rows, here] = field[part, rows, here] + lanes[part, column, rows]
+        leave(0, block)
 
 
 def call(
@@ -517,6 +491,7 @@
     hbm_in=(),
     any_in=(),
     lazy=False,
+    cheap=False,
     flops=0,
     room=12,
     name=None,
@@ -531,6 +506,7 @@
         for i, out in enumerate(outs)
     ]
     hbm_in = hbm_in if isinstance(hbm_in, dict) else {index: 1 for index in hbm_in}
+    hbm_out = hbm_out if isinstance(hbm_out, dict) else {index: 1 for index in hbm_out}
     moved = 4 * (sum(math.prod(out[0]) for out in outs) + sum(a.size for a in args))
     stage_in = [pltpu.VMEM(args[i].shape, args[i].dtype) for i in hbm_in]
     stage_out = [pltpu.VMEM(*outs[i]) for i in hbm_out]
@@ -539,41 +515,55 @@
         for i, a in enumerate(args)
     ]
     first, last = len(args), len(args) + len(outs)
-    pieces = sum(hbm_in.values())
+
+    def cuts(ref, count):
+        if count == 1:
+            return [ref]
+        count, axis = count if isinstance(count, tuple) else (count, 0)
+        size = ref.shape[axis] // count
+        return [
+            ref.at[(slice(None),) * axis + (pl.ds(size * piece, size),)] for piece in range(count)
+        ]
+
+    def number(count):
+        return count[0] if isinstance(count, tuple) else count
 
     def run(*refs):
         given, results = list(refs[:first]), list(refs[first:last])
         rest = refs[last:]
         staged = rest[len(scratch) : len(scratch) + len(stage_in) + len(stage_out)]
         sems = rest[-1] if staged else None
-        arrivals, at = {}, 0
+        arrivals, departures, at = {}, {}, 0
         for slot, (index, count) in enumerate(hbm_in.items()):
             stage, source = staged[slot], given[index]
-            for piece in range(count):
-                pair = (source, stage) if count == 1 else (source.at[piece], stage.at[piece])
+            for piece, pair in enumerate(zip(cuts(source, count), cuts(stage, count))):
                 copy = pltpu.make_async_copy(*pair, sems.at[at])
                 copy.start()
                 arrivals[index, piece] = copy
                 at += 1
             given[index] = stage
-        departures = []
-        for slot, index in enumerate(hbm_out):
+        for slot, (index, count) in enumerate(hbm_out.items()):
             stage = staged[len(stage_in) + slot]
-            departures.append(pltpu.make_async_copy(stage, results[index], sems.at[at + slot]))
+            for piece, pair in enumerate(zip(cuts(stage, count), cuts(results[index], count))):
+                departures[index, piece] = pltpu.make_async_copy(*pair, sems.at[at])
+                at += 1
             results[index] = stage
 
         def ready(index, piece=0):
             arrivals[index, piece].wait()
 
+        def leave(index, piece=0):
+            departures[index, piece].start()
+
         if lazy:
-            kernel(ready, *given, *results, *rest[: len(scratch)])
+            kernel(ready, leave, *given, *results, *rest[: len(scratch)])
         else:
             for copy in arrivals.values():
                 copy.wait()
             kernel(*given, *results, *rest[: len(scratch)])
-        for copy in departures:
-            copy.start()
-        for copy in departures:
+            for copy in departures.values():
+                copy.start()
+        for copy in departures.values():
             copy.wait()
 
     def space(index, smem, hbm):
@@ -581,7 +571,8 @@
 
     extra = stage_in + stage_out
     if extra:
-        extra.append(pltpu.SemaphoreType.DMA((pieces + len(stage_out),)))
+        count = sum(number(n) for n in (*hbm_in.values(), *hbm_out.values()))
+        extra.append(pltpu.SemaphoreType.DMA((count,)))
     hbm = pl.BlockSpec(memory_space=pltpu.HBM)
     return pl.pallas_call(
         run,
@@ -596,7 +587,9 @@
         + extra,
         name=name or kernel.__name__,
         compiler_params=pltpu.CompilerParams(vmem_limit_bytes=room * 2**20),
-        cost_estimate=pl.CostEstimate(flops=flops, bytes_accessed=moved, transcendentals=0),
+        cost_estimate=pl.CostEstimate(
+            flops=flops, bytes_accessed=0 if cheap else moved, transcendentals=0
+        ),
     )(*args)
 
 
@@ -633,36 +626,27 @@
     y, c = pat // 2, pat % 2
     top = tile * N - H
     where = jnp.stack([y, c, tile, top]).astype(jnp.int32)
-    neighbours = up(positions), down(positions)
-    top_rows, low_rows = edges(where, object_init)
+    top_rows, low_rows = edges(where, pltpu.with_memory_space_constraint(object_init, pltpu.HBM))
     from_above, from_below = up(low_rows), down(top_rows)
-    (news,) = call(
-        announce_kernel, (((8, 128), jnp.int32),), (positions, *neighbours), (0, 1, 2), room=1
-    )
+    (news,) = call(announce_kernel, (((8, 128), jnp.int32),), (positions,), (0,), room=1)
     near = lax.all_to_all(news, "pat", 0, 0)
     table = jnp.asarray(real_tables())
-    measured, base, token = call(
+    field = pltpu.with_memory_space_constraint(object_init, pltpu.HBM)
+    measured, base = call(
         prepare_kernel,
-        ((2, H, N), (2, N, N), (1, 1)),
-        (
-            where,
-            positions,
-            near,
-            intensity[0],
-            jnp.asarray(one_hot()),
-            object_init,
-        ),
-        (0, 1, 2),
-        hbm_in=(3, 4, 5),
-        smem_out=(2,),
-        hbm_out=(0,),
-        room=16,
+        ((2, H, N), (2, N, N)),
+        (where, positions, intensity[0], jnp.asarray(one_hot()), field),
+        (0, 1),
+        ((2, N, 384), None),
+        any_in=(4,),
+        room=8,
     )
     own_side, far_side = call(
         side_kernel,
         ((H, 1024), (H, 1024)),
-        (where, near, token, from_above, from_below),
-        (0, 1, 2),
+        (where, near, base, from_above, from_below),
+        (0, 1),
+        any_in=(2,),
         room=4,
     )
     far_side = partner(far_side)
@@ -676,15 +660,22 @@
 
     for iteration in range(ITERS):
         if iteration == 0:
-            patch, keep, send, mine, other, power, token = call(
+            patch, keep, send, mine, other, power = call(
                 lambda *refs: patterns_kernel(True, *refs),
-                ((2, N, N),) + outs + ((1, 1),),
-                (where, positions, base, own_side, far_side, probe, measured, table),
+                ((2, N, N),) + outs,
+                (
+                    where,
+                    positions,
+                    base,
+                    own_side,
+                    far_side,
+                    probe,
+                    measured,
+                    table,
+                ),
                 (0, 1),
                 scratch,
-                hbm_in={5: 4, 6: 1, 7: 1},
                 lazy=True,
-                smem_out=(6,),
                 flops=6 * 10**9,
                 room=28,
                 name="patterns",
@@ -693,12 +684,25 @@
             patch, probe, keep, send, mine, other, power = call(
                 lambda *refs: patterns_kernel(False, *refs),
                 ((2, N, N), (4, 2, N, N)) + outs,
-                (where, positions, messages[-1], patch, probe, measured, table, dirp, dmine, doth),
+                (
+                    where,
+                    positions,
+                    messages[-1],
+                    patch,
+                    probe,
+                    measured,
+                    table,
+                    dirp,
+                    dmine,
+                    doth,
+                    *bands[0][1:],
+                ),
                 (0, 1),
                 scratch,
-                hbm_in={3: 1, 4: 4, 5: 1, 6: 1, 7: 1, 8: 8, 9: 8},
+                hbm_in={3: 1, 7: 1, 6: 1, 4: 4, 8: 4, 9: 4, 5: 1},
                 lazy=True,
-                hbm_out=(0, 1),
+                hbm_out={0: 1, 1: 4},
+                any_in=(10, 11, 12),
                 flops=6 * 10**9,
                 room=30,
                 name="patterns",
@@ -711,10 +715,17 @@
             hbm_out=(0, 2, 3, 4),
         )
         came = [b0, along_y(b1, 1), along_y(b2, 2), along_y(b3, 3)]
+        (illum,) = call(
+            illum_kernel,
+            ((64, 1024),),
+            (where, near, power),
+            (0, 1),
+            ((2, N, H), (72, 1152)),
+        )
         low, high, token = call(
             place_kernel,
-            ((2, 32, 1024), (2, 32, 1024), (1, 1)),
-            (where, near, *came),
+            ((3, 32, 1024), (3, 32, 1024), (1, 1)),
+            (where, near, illum, *came),
             (0, 1),
             ((2, 72, 1152),),
             smem_out=(2,),
@@ -725,42 +736,37 @@
         share, token = call(
             sum_kernel, ((9, 8, N), (1, 1)), (token, shares), (0,), smem_out=(1,)
         )
-        (illum,) = call(
-            illum_kernel,
-            ((64, 1024),),
-            (where, near, token, power),
-            (0, 1, 2),
-            ((2, N, H), (136, 1152)),
-        )
         probe_dir, df = call(
             share_kernel,
             ((16, 8, 8, N), (1, 2)),
-            (share, *[along_y(share, s) for s in range(1, 4)], above, below, illum),
+            (share, *[along_y(share, s) for s in range(1, 4)], above, below),
             (),
             smem_out=(1,),
             hbm_out=(0,),
-            any_in=(4, 5, 6),
+            any_in=(4, 5),
         )
         gathered = lax.all_to_all(probe_dir, "tile", 0, 0)
         band, ae, r0, r1, r2, r3 = call(
             direction_kernel,
             ((2, 32, 1024), (1, 2)) + ((2, 2, 32, N),) * 4,
-            (where, near, df, illum, low, high, above, below),
+            (where, near, df, low, high, above, below),
             (0, 1, 2),
             ((2, 72, 1152),),
             smem_out=(1,),
-            hbm_out=(0, 3, 4, 5),
-            hbm_in=(4, 5, 6, 7),
-        )
-        bands.append(lax.all_gather(band, "pat"))
+            hbm_out=(0,),
+            hbm_in=(3, 4, 5, 6),
+            cheap=True,
+        )
+        bands.append([band] + [along_y(band, s) for s in range(1, 4)])
         back = [r0] + [along_y(r, s) for s, r in ((1, r1), (2, r2), (3, r3))]
-        (oth,) = call(stack_kernel, ((4, 2, 32, N),), back, (), room=4)
+        (oth,) = call(stack_kernel, ((4, 2, 32, N),), back, (), room=4, cheap=True)
         dirp, kept, sent_mixed = call(
             patch_kernel,
             ((2, N, N), (2, H, N), (2, H, N)),
             (where, near, *back, partner(oth), patch),
             (0, 1),
             ((2, 2, N, H),),
+            cheap=True,
         )
         message, token = call(
             message_kernel,
@@ -783,7 +789,38 @@
         (dmine,) = call(relay_kernel, ((8, H, N),), (token, gathered), (0,))
         doth = partner(dmine)
         messages.append(lax.all_to_all(message, BOTH, 0, 0))
-    return finish(where, *messages, object_init, *bands, probe, dmine, doth)
+    (change,) = call(
+        combine_kernel,
+        ((4, 2, 32, 1024),),
+        (*messages, *bands[0], *bands[1]),
+        (),
+        hbm_in={index: 1 for index in range(2, 10)},
+        hbm_out={0: 4},
+        lazy=True,
+    )
+    change_far = partner(change)
+    (probe_out,) = call(
+        probe_kernel,
+        (probe_init.shape,),
+        (where, messages[1], probe, dmine, doth),
+        (0,),
+        hbm_in={2: 4, 3: 4, 4: 4},
+        hbm_out={0: 4},
+        lazy=True,
+        flops=10**9,
+    )
+    (object_out,) = call(
+        object_kernel,
+        (object_init.shape,),
+        (where, object_init, change, change_far),
+        (0,),
+        ((2, 8, N, H),),
+        hbm_in={1: (4, 1), 2: (4, 2), 3: (4, 2)},
+        hbm_out={0: (4, 1)},
+        lazy=True,
+        room=16,
+    )
+    return object_out, probe_out
 
 
 def solution(mesh):

time: 268 us -> 245 us (0.914)
  blocking collectives: 29.3 us -> 0 us
  starting transfers between devices: 89 us -> 107 us
  between operations: 14.7 us -> 1.52 us
  waiting for transfers between devices: 56.9 us -> 64.4 us
  Pallas kernels: 72.3 us -> 67.4 us
    all_to_all x2 -> x0, blocking collectives: 29.3 us -> none  [the longest x1 18.6 us: body(): messages.append(lax.all_to_all(message, BOTH, 0, 0))]
    ppermute x18 -> x24, starting transfers between devices: 18.6 us -> 28.7 us  [along_y(): return lax.ppermute(value, 'pat', [(i, (i + 2 * s) % 8) for i in range(8)])]
    all_to_all x1 -> x2, starting transfers between devices: 9.69 us -> 19.6 us  [body(): messages.append(lax.all_to_all(message, BOTH, 0, 0))]
    pallas_call x1 -> x0, Pallas kernels: 7.16 us -> none  [finish(): pl.pallas_call(finish_kernel, grid=(4,), out_shape=[jax.ShapeDtypeStruct(...]
    all_to_all x0 -> x1, starting transfers between devices: none -> 5.42 us  [body(): near = lax.all_to_all(news, 'pat', 0, 0)]
    all_to_all x1 -> x2, waiting for transfers between devices: 9.68 us -> 14.9 us  [body(): messages.append(lax.all_to_all(message, BOTH, 0, 0))]
    ppermute x4 -> x3, starting transfers between devices: 14.4 us -> 9.82 us  [up(): return lax.ppermute(value, 'tile', [(i, i + 1) for i in range(15)])]
    ppermute x18 -> x24, waiting for transfers between devices: 22.1 us -> 26.4 us  [along_y(): return lax.ppermute(value, 'pat', [(i, (i + 2 * s) % 8) for i in range(8)])]
  transfers between devices with their start and end apart: 44 -> 49, of which waited for: 27 -> 29; matrix products, arithmetic and copies ran while one was open for 0% -> 0% of each run, Pallas kernels for 17% -> 13%
where the time goes in v3:
time: 245 us; the launch traced here: 244 us
  starting transfers between devices  107 us (44%)
  Pallas kernels  67.4 us (28%)
  waiting for transfers between devices  64.4 us (26%)
  local copies, waits for them, and re-layouts  3.73 us (2%)
    pallas_call x28, Pallas kernels, call(): pl.pallas_call(run, out_shape=shapes, in_specs=[space(i, smem_in, hbm_in)...  64.6 us
    ppermute x24, starting transfers between devices, along_y(): return lax.ppermute(value, 'pat', [(i, (i + 2 * s) % 8) for i in range(8)])  28.7 us
    ppermute x24, waiting for transfers between devices, along_y(): return lax.ppermute(value, 'pat', [(i, (i + 2 * s) % 8) for i in range(8)])  26.4 us
    all_to_all x2, starting transfers between devices, body(): messages.append(lax.all_to_all(message, BOTH, 0, 0))  19.6 us
    all_to_all x2, waiting for transfers between devices, body(): messages.append(lax.all_to_all(message, BOTH, 0, 0))  14.9 us
    ppermute x12, starting transfers between devices, partner(): return lax.ppermute(value, 'pat', [(i, i ^ 1) for i in range(8)])  13.5 us
    all_to_all x2, starting transfers between devices, body(): shares = lax.all_to_all(chip, 'tile', 0, 0)  13.3 us
    all_to_all x2, starting transfers between devices, body(): gathered = lax.all_to_all(probe_dir, 'tile', 0, 0)  12.6 us
  transfers between devices with their start and end apart: 49, of which 29 were waited for; matrix products, arithmetic and copies ran while one was open for 0% of the time, Pallas kernels for 13%

profile of v3, /device:TPU:1, one launch (start us, length us, event | category | flops | bytes accessed | tf_op | source)
XLA Modules:
  0.0 244.1 jit_solution(16891074089751322198)
XLA Ops:
  0.7 2.7 %shard_map.77 = (f32[128,1024]{1,0:T(8,128)}, f32[128,1024]{1,0:T(8,128)}) custom-call(s32[4]{0:T(128)S(1)} %pad_add_fusion.refs_0_.where, f32[2,256,1024]{2,1,0:T(8,128)} %refs_1_.7), custom_call_target="tpu_custom_call" | custom-call | tf_op jit(solution)/shard_map/pallas_call | solution.py:137
  3.5 4.0 %collective-permute-start = (f32[128,1024]{1,0:T(8,128)}, f32[128,1024]{1,0:T(8,128)S(1)}, u32[]{:S(2)}, u32[]{:S(2)}) collective-permute-start(f32[128,1024]{1,0:T(8,128)} %get-tuple-element.65), channel_id=1, source_target_pairs={{0,1},{1,2},{2,3},{3,4},{4,5},{5,6},{6,7},{7,8},{8,9},{9,10},{10,1... | collective-permute-start | bytes 1572872 | tf_op jit(solution)/shard_map/ppermute | solution.py:605
  7.5 1.3 collective-permute-start.1
  9.9 5.4 %all-to-all-start = ((s32[8,1,128]{2,1,0:T(1,128)}), s32[8,1,128]{2,1,0:T(1,128)S(1)}, u32[]{:S(2)}, u32[]{:S(2)}) async-start(s32[8,1,128]{2,1,0:T(1,128)} %bitcast.5), calls=%async_computation | async-start | bytes 8192 | tf_op jit(solution)/shard_map/all_to_all | solution.py:632
  16.3 2.5 %prepare_kernel.1 = (f32[2,128,256]{2,1,0:T(8,128)S(1)}, f32[2,256,256]{2,1,0:T(8,128)S(1)}) custom-call(s32[4]{0:T(128)S(1)} %pad_add_fusion.refs_0_.where, s32[1,2]{1,0:T(1,128)S(1)} %copy-done.15, f32[256,256]{1,0:T(8,128)S(1)} %bitcast.28, bf16[2,256,256]{2,1,0:T(8,128)(2,1)S(1)} %copy-done.14, f32[2,256,1024]{2,1,0:T(8,128)} %refs_1_.7), custom_call_target="tpu_custom_call" | custom-call | bytes 3670040 | tf_op jit(solution)/shard_map/prepare_kernel/pallas_call | solution.py:577
  19.9 2.2 collective-permute-done.1.refs_4_
  23.3 1.9 collective-permute-start.2
  25.3 1.5 collective-permute-done.2.refs_4_
  26.8 6.7 %patterns.2 = (f32[2,256,256]{2,1,0:T(8,128)S(1)}, f32[16,9,8,256]{3,2,1,0:T(8,128)S(1)}, f32[16,9,8,256]{3,2,1,0:T(8,128)S(1)}, f32[4,2,32,256]{3,2,1,0:T(8,128...) custom-call(s32[4]{0:T(128)S(1)} %pad_add_fusion.refs_0_.where, s32[1,2]{1,0:T(1,128)S(1)} %copy-done.15, ...), custom_call_target="tpu_custom_call" | custom-call | flops 6000000000 | bytes 9699352 | tf_op jit(solution)/shard_map/patterns/pallas_call | solution.py:577
  34.1 2.7 %collective-permute-done.4.refs_3_ = f32[4,2,32,256]{3,2,1,0:T(8,128)S(1)} collective-permute-done((f32[4,2,32,256]{3,2,1,0:T(8,128)S(1)}, f32[4,2,32,256]{3,2,1,0:T(8,128)S(1)}, u32[]{:S(2)}, u32[]{:S(2)}) %collective-permute-start.4) | collective-permute-done | bytes 262176 | tf_op jit(solution)/shard_map/ppermute | solution.py:601
  36.8 1.3 pack_kernel.2
  38.2 9.4 %all-to-all-start.1 = ((f32[16,9,8,256]{3,2,1,0:T(8,128)}), f32[16,9,8,256]{3,2,1,0:T(8,128)S(1)}, u32[]{:S(2)}, u32[]{:S(2)}) async-start(f32[16,9,8,256]{3,2,1,0:T(8,128)} %get-tuple-element.80), calls=%async_computation.1 | async-start | bytes 2359296 | tf_op jit(solution)/shard_map/all_to_all | solution.py:735
  47.6 1.4 collective-permute-start.5
  49.0 2.6 %collective-permute-start.6 = (f32[2,2,32,256]{3,2,1,0:T(8,128)S(1)}, f32[2,2,32,256]{3,2,1,0:T(8,128)S(1)}, u32[]{:S(2)}, u32[]{:S(2)}) collective-permute-start(f32[2,2,32,256]{3,2,1,0:T(8,128)S(1)} %copy-done.29), channel_id=1, source_target_pairs={{0,64},{16,80},{32,96},{48,112},{64,0},{80,16},{96,32},{112,48},{1... | collective-permute-start | bytes 393224 | tf_op jit(solution)/shard_map/ppermute | solution.py:597
  53.6 3.8 %collective-permute-done.6.refs_5_ = f32[2,2,32,256]{3,2,1,0:T(8,128)S(1)} collective-permute-done((f32[2,2,32,256]{3,2,1,0:T(8,128)S(1)}, f32[2,2,32,256]{3,2,1,0:T(8,128)S(1)}, u32[]{:S(2)}, u32[]{:S(2)}) %collective-permute-start.6) | collective-permute-done | bytes 131104 | tf_op jit(solution)/shard_map/ppermute | solution.py:597
  57.3 2.4 place_kernel.2
  59.8 3.0 %collective-permute-start.11 = (f32[3,32,1024]{2,1,0:T(8,128)}, f32[3,32,1024]{2,1,0:T(8,128)S(1)}, u32[]{:S(2)}, u32[]{:S(2)}) collective-permute-start(f32[3,32,1024]{2,1,0:T(8,128)} %get-tuple-element.82.refs_4_), channel_id=1, source_target_pairs={{0,1},{1,2},{2,3},{3,4},{4,5},{5,6},{6,7},{7,8},{8,9},{9,10},{10,1... | collective-permute-start | bytes 1179656 | tf_op jit(solution)/shard_map/ppermute | solution.py:605
  62.8 1.3 collective-permute-start.12
  64.1 1.5 all-to-all-done.1.refs_1_
  65.5 1.2 sum_kernel.2
  66.7 2.8 %collective-permute-start.10 = (f32[9,8,256]{2,1,0:T(8,128)S(1)}, f32[9,8,256]{2,1,0:T(8,128)S(1)}, u32[]{:S(2)}, u32[]{:S(2)}) collective-permute-start(f32[9,8,256]{2,1,0:T(8,128)S(1)} %get-tuple-element.81.refs_0_), channel_id=1, source_target_pairs={{0,96},{16,112},{32,0},{48,16},{64,32},{80,48},{96,64},{112,80},{1... | collective-permute-start | bytes 221192 | tf_op jit(solution)/shard_map/ppermute | solution.py:597
  70.6 2.8 %collective-permute-done.12.refs_5_.refs_6_ = f32[3,32,1024]{2,1,0:T(8,128)S(1)} collective-permute-done((f32[3,32,1024]{2,1,0:T(8,128)}, f32[3,32,1024]{2,1,0:T(8,128)S(1)}, u32[]{:S(2)}, u32[]{:S(2)}) %collective-permute-start.12) | collective-permute-done | bytes 393248 | tf_op jit(solution)/shard_map/ppermute | solution.py:609
  75.0 1.7 share_kernel.2
  76.7 6.4 %all-to-all-start.2 = ((f32[16,8,8,256]{3,2,1,0:T(8,128)}), f32[16,8,8,256]{3,2,1,0:T(8,128)S(1)}, u32[]{:S(2)}, u32[]{:S(2)}) async-start(f32[16,8,8,256]{3,2,1,0:T(8,128)} %get-tuple-element.84), calls=%async_computation.2 | async-start | bytes 2097152 | tf_op jit(solution)/shard_map/all_to_all | solution.py:748
  83.1 3.6 %direction_kernel.2 = (f32[2,32,1024]{2,1,0:T(8,128)}, f32[1,2]{1,0:T(1,128)S(1)}, f32[2,2,32,256]{3,2,1,0:T(8,128)S(1)}, f32[2,2,32,256]{3,2,1,0:T(8,128)S(1)},...) custom-call(s32[4]{0:T(128)S(1)} %pad_add_fusion.refs_0_.where, s32[8,128]{1,0:T(8,128)S(1)} %bitcast.22, ...), custom_call_target="tpu_custom_call" | custom-call | tf_op jit(solution)/shard_map/direction_kernel/pallas_call | solution.py:577
  86.7 1.2 collective-permute-start.13
  88.0 2.8 %collective-permute-start.14 = (f32[2,2,32,256]{3,2,1,0:T(8,128)S(1)}, f32[2,2,32,256]{3,2,1,0:T(8,128)S(1)}, u32[]{:S(2)}, u32[]{:S(2)}) collective-permute-start(f32[2,2,32,256]{3,2,1,0:T(8,128)S(1)} %get-tuple-element.88), channel_id=1, source_target_pairs={{0,64},{16,80},{32,96},{48,112},{64,0},{80,16},{96,32},{112,48},{1... | collective-permute-start | bytes 393224 | tf_op jit(solution)/shard_map/ppermute | solution.py:597
  90.8 1.5 collective-permute-done.13.refs_1_.refs_3_
  92.2 2.6 %collective-permute-done.14.refs_2_.refs_4_ = f32[2,2,32,256]{3,2,1,0:T(8,128)S(1)} collective-permute-done((f32[2,2,32,256]{3,2,1,0:T(8,128)S(1)}, f32[2,2,32,256]{3,2,1,0:T(8,128)S(1)}, u32[]{:S(2)}, u32[]{:S(2)}) %collective-permute-start.14) | collective-permute-done | bytes 131104 | tf_op jit(solution)/shard_map/ppermute | solution.py:597
  94.9 4.4 %collective-permute-start.16 = (f32[4,2,32,256]{3,2,1,0:T(8,128)S(1)}, f32[4,2,32,256]{3,2,1,0:T(8,128)S(1)}, u32[]{:S(2)}, u32[]{:S(2)}) collective-permute-start(f32[4,2,32,256]{3,2,1,0:T(8,128)S(1)} %stack_kernel.2), channel_id=1, source_target_pairs={{0,16},{16,0},{32,48},{48,32},{64,80},{80,64},{96,112},{112,96},{1... | collective-permute-start | bytes 786440 | tf_op jit(solution)/shard_map/ppermute | solution.py:601
  103.0 3.4 %message_kernel.2 = (f32[128,128]{1,0:T(8,128)}, f32[1,1]{1,0:T(1,128)}) custom-call(s32[4]{0:T(128)S(1)} %pad_add_fusion.refs_0_.where, f32[16,8,8,256]{3,2,1,0:T(8,128)S(1)} %all-to-all-done.2.refs_1_, f32[4,2,256,256]{3,2,1,0:T(8,128)} %refs_4_.3, f32[2,128,256]{2,1,0:T(8,128)S(1)} %get-tuple-element.91.refs_3_, ...), custom_call_target="tpu_custom_call" | custom-call | bytes 3735588 | tf_op jit(solution)/shard_map/message_kernel/pallas_call | solution.py:577
  107.7 1.7 collective-permute-start.21
  110.2 10.1 %all-to-all-start.3 = ((f32[128,1,128]{2,1,0:T(1,128)}), f32[128,1,128]{2,1,0:T(1,128)S(1)}, u32[]{:S(2)}, u32[]{:S(2)}) async-start(f32[128,1,128]{2,1,0:T(1,128)} %bitcast.9), calls=%async_computation.3 | async-start | bytes 131072 | tf_op jit(solution)/shard_map/all_to_all | solution.py:791
  120.3 4.5 %collective-permute-done.19.refs_10_.refs_3_ = f32[2,32,1024]{2,1,0:T(8,128)S(1)} collective-permute-done((f32[2,32,1024]{2,1,0:T(8,128)S(1)}, f32[2,32,1024]{2,1,0:T(8,128)S(1)}, u32[]{:S(2)}, u32[]{:S(2)}) %collective-permute-start.19) | collective-permute-done | bytes 262176 | tf_op jit(solution)/shard_map/ppermute | solution.py:597
  124.8 5.2 %all-to-all-done.3 = f32[128,1,128]{2,1,0:T(1,128)S(1)} async-done(((f32[128,1,128]{2,1,0:T(1,128)}), f32[128,1,128]{2,1,0:T(1,128)S(1)}, u32[]{:S(2)}, u32[]{:S(2)}) %all-to-all-start.3) | async-done | bytes 65568 | tf_op jit(solution)/shard_map/all_to_all | solution.py:791
  130.0 9.8 %patterns.3 = (f32[2,256,256]{2,1,0:T(8,128)}, f32[4,2,256,256]{3,2,1,0:T(8,128)}, f32[16,9,8,256]{3,2,1,0:T(8,128)S(1)}, f32[16,9,8,256]{3,2,1,0:T(8,128)S(1)},...) custom-call(s32[4]{0:T(128)S(1)} %pad_add_fusion.refs_0_.where, ...), custom_call_target="tpu_custom_call" | custom-call | flops 6000000000 | bytes 14221336 | tf_op jit(solution)/shard_map/patterns/pallas_call | solution.py:577
  140.8 2.8 %collective-permute-done.23.refs_3_ = f32[4,2,32,256]{3,2,1,0:T(8,128)S(1)} collective-permute-done((f32[4,2,32,256]{3,2,1,0:T(8,128)S(1)}, f32[4,2,32,256]{3,2,1,0:T(8,128)S(1)}, u32[]{:S(2)}, u32[]{:S(2)}) %collective-permute-start.23) | collective-permute-done | bytes 262176 | tf_op jit(solution)/shard_map/ppermute | solution.py:601
  143.5 1.3 pack_kernel.3
  144.9 3.8 %all-to-all-start.4 = ((f32[16,9,8,256]{3,2,1,0:T(8,128)}), f32[16,9,8,256]{3,2,1,0:T(8,128)S(1)}, u32[]{:S(2)}, u32[]{:S(2)}) async-start(f32[16,9,8,256]{3,2,1,0:T(8,128)} %get-tuple-element.108), calls=%async_computation.4 | async-start | bytes 2359296 | tf_op jit(solution)/shard_map/all_to_all | solution.py:735
  149.2 1.7 collective-permute-start.25
  152.5 2.8 %collective-permute-done.24.refs_4_ = f32[2,2,32,256]{3,2,1,0:T(8,128)S(1)} collective-permute-done((f32[2,2,32,256]{3,2,1,0:T(8,128)S(1)}, f32[2,2,32,256]{3,2,1,0:T(8,128)S(1)}, u32[]{:S(2)}, u32[]{:S(2)}) %collective-permute-start.24) | collective-permute-done | bytes 131104 | tf_op jit(solution)/shard_map/ppermute | solution.py:597
  155.4 1.5 collective-permute-done.25.refs_5_
  157.9 2.4 place_kernel.3
  160.3 2.8 %collective-permute-start.30 = (f32[3,32,1024]{2,1,0:T(8,128)}, f32[3,32,1024]{2,1,0:T(8,128)S(1)}, u32[]{:S(2)}, u32[]{:S(2)}) collective-permute-start(f32[3,32,1024]{2,1,0:T(8,128)} %get-tuple-element.110.refs_4_), channel_id=1, source_target_pairs={{0,1},{1,2},{2,3},{3,4},{4,5},{5,6},{6,7},{7,8},{8,9},{9,10},{10,1... | collective-permute-start | bytes 1179656 | tf_op jit(solution)/shard_map/ppermute | solution.py:605
  163.1 1.5 collective-permute-start.31
  164.7 3.3 %all-to-all-done.4.refs_1_ = f32[16,9,8,256]{3,2,1,0:T(8,128)S(1)} async-done(((f32[16,9,8,256]{3,2,1,0:T(8,128)}), f32[16,9,8,256]{3,2,1,0:T(8,128)S(1)}, u32[]{:S(2)}, u32[]{:S(2)}) %all-to-all-start.4) | async-done | bytes 1179680 | tf_op jit(solution)/shard_map/all_to_all | solution.py:735
  170.0 1.3 collective-permute-start.28
  171.4 2.4 collective-permute-done.31.refs_5_.refs_6_
  175.8 1.7 share_kernel.3
  177.5 6.2 %all-to-all-start.5 = ((f32[16,8,8,256]{3,2,1,0:T(8,128)}), f32[16,8,8,256]{3,2,1,0:T(8,128)S(1)}, u32[]{:S(2)}, u32[]{:S(2)}) async-start(f32[16,8,8,256]{3,2,1,0:T(8,128)} %get-tuple-element.112), calls=%async_computation.5 | async-start | bytes 2097152 | tf_op jit(solution)/shard_map/all_to_all | solution.py:748
  183.7 3.6 %direction_kernel.3 = (f32[2,32,1024]{2,1,0:T(8,128)}, f32[1,2]{1,0:T(1,128)S(1)}, f32[2,2,32,256]{3,2,1,0:T(8,128)S(1)}, f32[2,2,32,256]{3,2,1,0:T(8,128)S(1)},...) custom-call(s32[4]{0:T(128)S(1)} %pad_add_fusion.refs_0_.where, s32[8,128]{1,0:T(8,128)S(1)} %bitcast.26, ...), custom_call_target="tpu_custom_call" | custom-call | tf_op jit(solution)/shard_map/direction_kernel/pallas_call | solution.py:577
  187.3 1.3 collective-permute-start.32
  188.6 4.5 %collective-permute-start.33 = (f32[2,2,32,256]{3,2,1,0:T(8,128)S(1)}, f32[2,2,32,256]{3,2,1,0:T(8,128)S(1)}, u32[]{:S(2)}, u32[]{:S(2)}) collective-permute-start(f32[2,2,32,256]{3,2,1,0:T(8,128)S(1)} %get-tuple-element.117), channel_id=1, source_target_pairs={{0,64},{16,80},{32,96},{48,112},{64,0},{80,16},{96,32},{112,48},{1... | collective-permute-start | bytes 393224 | tf_op jit(solution)/shard_map/ppermute | solution.py:597
  193.1 1.5 collective-permute-done.32.refs_1_.refs_3_
  194.5 2.9 %collective-permute-done.33.refs_2_.refs_4_ = f32[2,2,32,256]{3,2,1,0:T(8,128)S(1)} collective-permute-done((f32[2,2,32,256]{3,2,1,0:T(8,128)S(1)}, f32[2,2,32,256]{3,2,1,0:T(8,128)S(1)}, u32[]{:S(2)}, u32[]{:S(2)}) %collective-permute-start.33) | collective-permute-done | bytes 131104 | tf_op jit(solution)/shard_map/ppermute | solution.py:597
  198.1 2.7 %collective-permute-start.35 = (f32[4,2,32,256]{3,2,1,0:T(8,128)S(1)}, f32[4,2,32,256]{3,2,1,0:T(8,128)S(1)}, u32[]{:S(2)}, u32[]{:S(2)}) collective-permute-start(f32[4,2,32,256]{3,2,1,0:T(8,128)S(1)} %stack_kernel.3), channel_id=1, source_target_pairs={{0,16},{16,0},{32,48},{48,32},{64,80},{80,64},{96,112},{112,96},{1... | collective-permute-start | bytes 786440 | tf_op jit(solution)/shard_map/ppermute | solution.py:601
  201.9 1.7 patch_kernel.3
  204.0 1.8 collective-permute-start.39
  206.3 3.4 %message_kernel.3 = (f32[128,128]{1,0:T(8,128)}, f32[1,1]{1,0:T(1,128)}) custom-call(s32[4]{0:T(128)S(1)} %pad_add_fusion.refs_0_.where, f32[16,8,8,256]{3,2,1,0:T(8,128)S(1)} %all-to-all-done.5.refs_1_, f32[4,2,256,256]{3,2,1,0:T(8,128)} %get-tuple-element.113.refs_2_, f32[2,128,256]{2,1,0:T(8,128)S(1)} %get-tuple-element.120.refs_3_, ...), custom_call_target="tpu_custom_call" | custom-call | bytes 3735588 | tf_op jit(solution)/shard_map/message_kernel/pallas_call | solution.py:577
  211.3 9.5 %all-to-all-start.6 = ((f32[128,1,128]{2,1,0:T(1,128)}), f32[128,1,128]{2,1,0:T(1,128)S(1)}, u32[]{:S(2)}, u32[]{:S(2)}) async-start(f32[128,1,128]{2,1,0:T(1,128)} %bitcast.12), calls=%async_computation.6 | async-start | bytes 131072 | tf_op jit(solution)/shard_map/all_to_all | solution.py:791
  220.8 9.7 %all-to-all-done.6 = f32[128,1,128]{2,1,0:T(1,128)S(1)} async-done(((f32[128,1,128]{2,1,0:T(1,128)}), f32[128,1,128]{2,1,0:T(1,128)S(1)}, u32[]{:S(2)}, u32[]{:S(2)}) %all-to-all-start.6) | async-done | bytes 65568 | tf_op jit(solution)/shard_map/all_to_all | solution.py:791
  230.5 2.4 combine_kernel.1.refs_2_
  234.8 3.9 %probe_kernel.1 = f32[4,2,256,256]{3,2,1,0:T(8,128)} custom-call(s32[4]{0:T(128)S(1)} %pad_add_fusion.refs_0_.where, f32[128,128]{1,0:T(8,128)S(1)} %bitcast.18, f32[4,2,256,256]{3,2,1,0:T(8,128)} %get-tuple-element.113.refs_2_, f32[8,128,256]{2,1,0:T(8,128)} %copy-done, f32[8,128,256]{2,1,0:T(8,128)} %copy-done.20), custom_call_target="tpu_custom_call" | custom-call | flops 1000000000 | bytes 6357008 | tf_op jit(solution)/shard_map/probe_kernel/pallas_call | solution.py:577
  239.7 4.2 %object_kernel.1 = f32[2,256,1024]{2,1,0:T(8,128)} custom-call(s32[4]{0:T(128)S(1)} %pad_add_fusion.refs_0_.where, f32[2,256,1024]{2,1,0:T(8,128)} %refs_1_.7, f32[4,2,32,1024]{3,2,1,0:T(8,128)} %combine_kernel.1.refs_2_, f32[4,2,32,1024]{3,2,1,0:T(8,128)} %copy-done.21), custom_call_target="tpu_custom_call" | custom-call | bytes 6291472 | tf_op jit(solution)/shard_map/object_kernel/pallas_call | solution.py:577
  (130 shorter events, 30.9 us)
Async XLA Ops:
  0.6 14.7 %copy-start.10 = (f32[1,256,256]{2,1,0:T(8,128)S(1)}, f32[1,256,256]{2,1,0:T(8,128)}, u32[]{:S(2)}) copy-start(f32[1,256,256]{2,1,0:T(8,128)} %param.6) | copy-start | bytes 786436
  3.5 16.4 %collective-permute-start = (f32[128,1024]{1,0:T(8,128)}, f32[128,1024]{1,0:T(8,128)S(1)}, u32[]{:S(2)}, u32[]{:S(2)}) collective-permute-start(f32[128,1024]{1,0:T(8,128)} %get-tuple-element.65), channel_id=1, source_target_pairs={{0,1},{1,2},{2,3},{3,4},{4,5},{5,6},{6,7},{7,8},{8,9},{9,10},{10,1... | collective-permute-start | bytes 1572872 | tf_op jit(solution)/shard_map/ppermute | solution.py:605
  7.5 14.7 %collective-permute-start.1 = (f32[128,1024]{1,0:T(8,128)}, f32[128,1024]{1,0:T(8,128)}, u32[]{:S(2)}, u32[]{:S(2)}) collective-permute-start(f32[128,1024]{1,0:T(8,128)} %get-tuple-element.66), channel_id=1, source_target_pairs={{1,0},{2,1},{3,2},{4,3},{5,4},{6,5},{7,6},{8,7},{9,8},{10,9},{11,1... | collective-permute-start | bytes 1572872 | tf_op jit(solution)/shard_map/ppermute | solution.py:609
  9.9 10.0 %all-to-all-start = ((s32[8,1,128]{2,1,0:T(1,128)}), s32[8,1,128]{2,1,0:T(1,128)S(1)}, u32[]{:S(2)}, u32[]{:S(2)}) async-start(s32[8,1,128]{2,1,0:T(1,128)} %bitcast.5), calls=%async_computation | async-start | bytes 8192 | tf_op jit(solution)/shard_map/all_to_all | solution.py:632
  16.3 10.5 %copy-start.1 = (f32[4,2,256,256]{3,2,1,0:T(8,128)S(1)}, f32[4,2,256,256]{3,2,1,0:T(8,128)}, u32[]{:S(2)}) copy-start(f32[4,2,256,256]{3,2,1,0:T(8,128)} %refs_4_.3) | copy-start | bytes 6291460
  23.3 3.5 %collective-permute-start.2 = (f32[128,1024]{1,0:T(8,128)S(1)}, f32[128,1024]{1,0:T(8,128)S(1)}, u32[]{:S(2)}, u32[]{:S(2)}) collective-permute-start(f32[128,1024]{1,0:T(8,128)S(1)} %get-tuple-element.68), channel_id=1, source_target_pairs={{0,16},{16,0},{32,48},{48,32},{64,80},{80,64},{96,112},{112,96},{1... | collective-permute-start | bytes 1572872 | tf_op jit(solution)/shard_map/ppermute | solution.py:601
  33.5 3.3 %collective-permute-start.3 = (f32[16,9,8,256]{3,2,1,0:T(8,128)S(1)}, f32[16,9,8,256]{3,2,1,0:T(8,128)S(1)}, u32[]{:S(2)}, u32[]{:S(2)}) collective-permute-start(f32[16,9,8,256]{3,2,1,0:T(8,128)S(1)} %get-tuple-element.72), channel_id=1, source_target_pairs={{0,16},{16,0},{32,48},{48,32},{64,80},{80,64},{96,112},{112,96},{1... | collective-permute-start | bytes 3538952 | tf_op jit(solution)/shard_map/ppermute | solution.py:601
  34.0 2.8 %collective-permute-start.4 = (f32[4,2,32,256]{3,2,1,0:T(8,128)S(1)}, f32[4,2,32,256]{3,2,1,0:T(8,128)S(1)}, u32[]{:S(2)}, u32[]{:S(2)}) collective-permute-start(f32[4,2,32,256]{3,2,1,0:T(8,128)S(1)} %get-tuple-element.74), channel_id=1, source_target_pairs={{0,16},{16,0},{32,48},{48,32},{64,80},{80,64},{96,112},{112,96},{1... | collective-permute-start | bytes 786440 | tf_op jit(solution)/shard_map/ppermute | solution.py:601
  38.1 10.9 %copy-start.29 = (f32[2,2,32,256]{3,2,1,0:T(8,128)S(1)}, f32[2,2,32,256]{3,2,1,0:T(8,128)}, u32[]{:S(2)}) copy-start(f32[2,2,32,256]{3,2,1,0:T(8,128)} %get-tuple-element.77) | copy-start | bytes 393220
  38.1 13.5 %copy-start.27 = (f32[2,2,32,256]{3,2,1,0:T(8,128)S(1)}, f32[2,2,32,256]{3,2,1,0:T(8,128)}, u32[]{:S(2)}) copy-start(f32[2,2,32,256]{3,2,1,0:T(8,128)} %get-tuple-element.78) | copy-start | bytes 393220
  38.2 27.4 %all-to-all-start.1 = ((f32[16,9,8,256]{3,2,1,0:T(8,128)}), f32[16,9,8,256]{3,2,1,0:T(8,128)S(1)}, u32[]{:S(2)}, u32[]{:S(2)}) async-start(f32[16,9,8,256]{3,2,1,0:T(8,128)} %get-tuple-element.80), calls=%async_computation.1 | async-start | bytes 2359296 | tf_op jit(solution)/shard_map/all_to_all | solution.py:735
  47.6 6.0 %collective-permute-start.5 = (f32[2,2,32,256]{3,2,1,0:T(8,128)S(1)}, f32[2,2,32,256]{3,2,1,0:T(8,128)S(1)}, u32[]{:S(2)}, u32[]{:S(2)}) collective-permute-start(f32[2,2,32,256]{3,2,1,0:T(8,128)S(1)} %copy-done.31), channel_id=1, source_target_pairs={{0,32},{16,48},{32,64},{48,80},{64,96},{80,112},{96,0},{112,16},{1... | collective-permute-start | bytes 393224 | tf_op jit(solution)/shard_map/ppermute | solution.py:597
  49.0 8.3 %collective-permute-start.6 = (f32[2,2,32,256]{3,2,1,0:T(8,128)S(1)}, f32[2,2,32,256]{3,2,1,0:T(8,128)S(1)}, u32[]{:S(2)}, u32[]{:S(2)}) collective-permute-start(f32[2,2,32,256]{3,2,1,0:T(8,128)S(1)} %copy-done.29), channel_id=1, source_target_pairs={{0,64},{16,80},{32,96},{48,112},{64,0},{80,16},{96,32},{112,48},{1... | collective-permute-start | bytes 393224 | tf_op jit(solution)/shard_map/ppermute | solution.py:597
  51.6 5.7 %collective-permute-start.7 = (f32[2,2,32,256]{3,2,1,0:T(8,128)S(1)}, f32[2,2,32,256]{3,2,1,0:T(8,128)S(1)}, u32[]{:S(2)}, u32[]{:S(2)}) collective-permute-start(f32[2,2,32,256]{3,2,1,0:T(8,128)S(1)} %copy-done.27), channel_id=1, source_target_pairs={{0,96},{16,112},{32,0},{48,16},{64,32},{80,48},{96,64},{112,80},{1... | collective-permute-start | bytes 393224 | tf_op jit(solution)/shard_map/ppermute | solution.py:597
  59.8 10.8 %collective-permute-start.11 = (f32[3,32,1024]{2,1,0:T(8,128)}, f32[3,32,1024]{2,1,0:T(8,128)S(1)}, u32[]{:S(2)}, u32[]{:S(2)}) collective-permute-start(f32[3,32,1024]{2,1,0:T(8,128)} %get-tuple-element.82.refs_4_), channel_id=1, source_target_pairs={{0,1},{1,2},{2,3},{3,4},{4,5},{5,6},{6,7},{7,8},{8,9},{9,10},{10,1... | collective-permute-start | bytes 1179656 | tf_op jit(solution)/shard_map/ppermute | solution.py:605
  62.8 10.6 %collective-permute-start.12 = (f32[3,32,1024]{2,1,0:T(8,128)}, f32[3,32,1024]{2,1,0:T(8,128)S(1)}, u32[]{:S(2)}, u32[]{:S(2)}) collective-permute-start(f32[3,32,1024]{2,1,0:T(8,128)} %get-tuple-element.83.refs_3_), channel_id=1, source_target_pairs={{1,0},{2,1},{3,2},{4,3},{5,4},{6,5},{7,6},{8,7},{9,8},{10,9},{11,1... | collective-permute-start | bytes 1179656 | tf_op jit(solution)/shard_map/ppermute | solution.py:609
  66.7 6.7 %collective-permute-start.10 = (f32[9,8,256]{2,1,0:T(8,128)S(1)}, f32[9,8,256]{2,1,0:T(8,128)S(1)}, u32[]{:S(2)}, u32[]{:S(2)}) collective-permute-start(f32[9,8,256]{2,1,0:T(8,128)S(1)} %get-tuple-element.81.refs_0_), channel_id=1, source_target_pairs={{0,96},{16,112},{32,0},{48,16},{64,32},{80,48},{96,64},{112,80},{1... | collective-permute-start | bytes 221192 | tf_op jit(solution)/shard_map/ppermute | solution.py:597
  69.5 4.8 %collective-permute-start.9 = (f32[9,8,256]{2,1,0:T(8,128)S(1)}, f32[9,8,256]{2,1,0:T(8,128)S(1)}, u32[]{:S(2)}, u32[]{:S(2)}) collective-permute-start(f32[9,8,256]{2,1,0:T(8,128)S(1)} %get-tuple-element.81.refs_0_), channel_id=1, source_target_pairs={{0,64},{16,80},{32,96},{48,112},{64,0},{80,16},{96,32},{112,48},{1... | collective-permute-start | bytes 221192 | tf_op jit(solution)/shard_map/ppermute | solution.py:597
  69.9 5.1 %collective-permute-start.8 = (f32[9,8,256]{2,1,0:T(8,128)S(1)}, f32[9,8,256]{2,1,0:T(8,128)S(1)}, u32[]{:S(2)}, u32[]{:S(2)}) collective-permute-start(f32[9,8,256]{2,1,0:T(8,128)S(1)} %get-tuple-element.81.refs_0_), channel_id=1, source_target_pairs={{0,32},{16,48},{32,64},{48,80},{64,96},{80,112},{96,0},{112,16},{1... | collective-permute-start | bytes 221192 | tf_op jit(solution)/shard_map/ppermute | solution.py:597
  76.7 26.3 %all-to-all-start.2 = ((f32[16,8,8,256]{3,2,1,0:T(8,128)}), f32[16,8,8,256]{3,2,1,0:T(8,128)S(1)}, u32[]{:S(2)}, u32[]{:S(2)}) async-start(f32[16,8,8,256]{3,2,1,0:T(8,128)} %get-tuple-element.84), calls=%async_computation.2 | async-start | bytes 2097152 | tf_op jit(solution)/shard_map/all_to_all | solution.py:748
  83.1 17.4 %copy-start.8 = (f32[2,256,256]{2,1,0:T(8,128)S(1)}, f32[2,256,256]{2,1,0:T(8,128)}, u32[]{:S(2)}) copy-start(f32[2,256,256]{2,1,0:T(8,128)} %copy-done.7) | copy-start | bytes 1572868
  86.7 5.5 %collective-permute-start.13 = (f32[2,2,32,256]{3,2,1,0:T(8,128)S(1)}, f32[2,2,32,256]{3,2,1,0:T(8,128)S(1)}, u32[]{:S(2)}, u32[]{:S(2)}) collective-permute-start(f32[2,2,32,256]{3,2,1,0:T(8,128)S(1)} %get-tuple-element.87), channel_id=1, source_target_pairs={{0,32},{16,48},{32,64},{48,80},{64,96},{80,112},{96,0},{112,16},{1... | collective-permute-start | bytes 393224 | tf_op jit(solution)/shard_map/ppermute | solution.py:597
  88.0 6.8 %collective-permute-start.14 = (f32[2,2,32,256]{3,2,1,0:T(8,128)S(1)}, f32[2,2,32,256]{3,2,1,0:T(8,128)S(1)}, u32[]{:S(2)}, u32[]{:S(2)}) collective-permute-start(f32[2,2,32,256]{3,2,1,0:T(8,128)S(1)} %get-tuple-element.88), channel_id=1, source_target_pairs={{0,64},{16,80},{32,96},{48,112},{64,0},{80,16},{96,32},{112,48},{1... | collective-permute-start | bytes 393224 | tf_op jit(solution)/shard_map/ppermute | solution.py:597
  90.8 4.1 %collective-permute-start.15 = (f32[2,2,32,256]{3,2,1,0:T(8,128)S(1)}, f32[2,2,32,256]{3,2,1,0:T(8,128)S(1)}, u32[]{:S(2)}, u32[]{:S(2)}) collective-permute-start(f32[2,2,32,256]{3,2,1,0:T(8,128)S(1)} %get-tuple-element.89), channel_id=1, source_target_pairs={{0,96},{16,112},{32,0},{48,16},{64,32},{80,48},{96,64},{112,80},{1... | collective-permute-start | bytes 393224 | tf_op jit(solution)/shard_map/ppermute | solution.py:597
  94.9 5.6 %collective-permute-start.16 = (f32[4,2,32,256]{3,2,1,0:T(8,128)S(1)}, f32[4,2,32,256]{3,2,1,0:T(8,128)S(1)}, u32[]{:S(2)}, u32[]{:S(2)}) collective-permute-start(f32[4,2,32,256]{3,2,1,0:T(8,128)S(1)} %stack_kernel.2), channel_id=1, source_target_pairs={{0,16},{16,0},{32,48},{48,32},{64,80},{80,64},{96,112},{112,96},{1... | collective-permute-start | bytes 786440 | tf_op jit(solution)/shard_map/ppermute | solution.py:601
  101.4 1.6 collective-permute-start.17
  107.2 22.8 %copy-start.6 = (f32[8,128,256]{2,1,0:T(8,128)}, f32[8,128,256]{2,1,0:T(8,128)S(1)}, u32[]{:S(2)}) copy-start(f32[8,128,256]{2,1,0:T(8,128)S(1)} %relay_kernel.2.refs_8_) | copy-start | bytes 3145732
  107.2 22.8 %collective-permute-start.18 = (f32[8,128,256]{2,1,0:T(8,128)S(1)}, f32[8,128,256]{2,1,0:T(8,128)}, u32[]{:S(2)}, u32[]{:S(2)}) collective-permute-start(f32[8,128,256]{2,1,0:T(8,128)S(1)} %relay_kernel.2.refs_8_), channel_id=1, source_target_pairs={{0,16},{16,0},{32,48},{48,32},{64,80},{80,64},{96,112},{112,96},{1... | collective-permute-start | bytes 3145736 | tf_op jit(solution)/shard_map/ppermute | solution.py:601
  107.7 12.6 %collective-permute-start.21 = (f32[2,32,1024]{2,1,0:T(8,128)S(1)}, f32[2,32,1024]{2,1,0:T(8,128)S(1)}, u32[]{:S(2)}, u32[]{:S(2)}) collective-permute-start(f32[2,32,1024]{2,1,0:T(8,128)S(1)} %copy-done.22), channel_id=1, source_target_pairs={{0,96},{16,112},{32,0},{48,16},{64,32},{80,48},{96,64},{112,80},{1... | collective-permute-start | bytes 786440 | tf_op jit(solution)/shard_map/ppermute | solution.py:597
  109.4 10.9 %collective-permute-start.20 = (f32[2,32,1024]{2,1,0:T(8,128)S(1)}, f32[2,32,1024]{2,1,0:T(8,128)S(1)}, u32[]{:S(2)}, u32[]{:S(2)}) collective-permute-start(f32[2,32,1024]{2,1,0:T(8,128)S(1)} %copy-done.22), channel_id=1, source_target_pairs={{0,64},{16,80},{32,96},{48,112},{64,0},{80,16},{96,32},{112,48},{1... | collective-permute-start | bytes 786440 | tf_op jit(solution)/shard_map/ppermute | solution.py:597
  110.2 14.6 %collective-permute-start.19 = (f32[2,32,1024]{2,1,0:T(8,128)S(1)}, f32[2,32,1024]{2,1,0:T(8,128)S(1)}, u32[]{:S(2)}, u32[]{:S(2)}) collective-permute-start(f32[2,32,1024]{2,1,0:T(8,128)S(1)} %copy-done.22), channel_id=1, source_target_pairs={{0,32},{16,48},{32,64},{48,80},{64,96},{80,112},{96,0},{112,16},{1... | collective-permute-start | bytes 786440 | tf_op jit(solution)/shard_map/ppermute | solution.py:597
  110.2 19.8 %all-to-all-start.3 = ((f32[128,1,128]{2,1,0:T(1,128)}), f32[128,1,128]{2,1,0:T(1,128)S(1)}, u32[]{:S(2)}, u32[]{:S(2)}) async-start(f32[128,1,128]{2,1,0:T(1,128)} %bitcast.9), calls=%async_computation.3 | async-start | bytes 131072 | tf_op jit(solution)/shard_map/all_to_all | solution.py:791
  120.3 19.5 %copy-start.11 = (f32[2,32,1024]{2,1,0:T(8,128)}, f32[2,32,1024]{2,1,0:T(8,128)S(1)}, u32[]{:S(2)}) copy-start(f32[2,32,1024]{2,1,0:T(8,128)S(1)} %collective-permute-done.21.refs_12_.refs_5_) | copy-start | bytes 786436
  120.3 19.5 %copy-start.12 = (f32[2,32,1024]{2,1,0:T(8,128)}, f32[2,32,1024]{2,1,0:T(8,128)S(1)}, u32[]{:S(2)}) copy-start(f32[2,32,1024]{2,1,0:T(8,128)S(1)} %collective-permute-done.20.refs_11_.refs_4_) | copy-start | bytes 786436
  124.8 15.0 %copy-start.13 = (f32[2,32,1024]{2,1,0:T(8,128)}, f32[2,32,1024]{2,1,0:T(8,128)S(1)}, u32[]{:S(2)}) copy-start(f32[2,32,1024]{2,1,0:T(8,128)S(1)} %collective-permute-done.19.refs_10_.refs_3_) | copy-start | bytes 786436
  139.8 3.7 %collective-permute-start.22 = (f32[16,9,8,256]{3,2,1,0:T(8,128)S(1)}, f32[16,9,8,256]{3,2,1,0:T(8,128)S(1)}, u32[]{:S(2)}, u32[]{:S(2)}) collective-permute-start(f32[16,9,8,256]{3,2,1,0:T(8,128)S(1)} %get-tuple-element.100), channel_id=1, source_target_pairs={{0,16},{16,0},{32,48},{48,32},{64,80},{80,64},{96,112},{112,96},{1... | collective-permute-start | bytes 3538952 | tf_op jit(solution)/shard_map/ppermute | solution.py:601
  140.7 2.8 %collective-permute-start.23 = (f32[4,2,32,256]{3,2,1,0:T(8,128)S(1)}, f32[4,2,32,256]{3,2,1,0:T(8,128)S(1)}, u32[]{:S(2)}, u32[]{:S(2)}) collective-permute-start(f32[4,2,32,256]{3,2,1,0:T(8,128)S(1)} %get-tuple-element.102), channel_id=1, source_target_pairs={{0,16},{16,0},{32,48},{48,32},{64,80},{80,64},{96,112},{112,96},{1... | collective-permute-start | bytes 786440 | tf_op jit(solution)/shard_map/ppermute | solution.py:601
  144.9 23.1 %all-to-all-start.4 = ((f32[16,9,8,256]{3,2,1,0:T(8,128)}), f32[16,9,8,256]{3,2,1,0:T(8,128)S(1)}, u32[]{:S(2)}, u32[]{:S(2)}) async-start(f32[16,9,8,256]{3,2,1,0:T(8,128)} %get-tuple-element.108), calls=%async_computation.4 | async-start | bytes 2359296 | tf_op jit(solution)/shard_map/all_to_all | solution.py:735
  148.7 6.6 %collective-permute-start.24 = (f32[2,2,32,256]{3,2,1,0:T(8,128)S(1)}, f32[2,2,32,256]{3,2,1,0:T(8,128)S(1)}, u32[]{:S(2)}, u32[]{:S(2)}) collective-permute-start(f32[2,2,32,256]{3,2,1,0:T(8,128)S(1)} %copy-done.32), channel_id=1, source_target_pairs={{0,32},{16,48},{32,64},{48,80},{64,96},{80,112},{96,0},{112,16},{1... | collective-permute-start | bytes 393224 | tf_op jit(solution)/shard_map/ppermute | solution.py:597
  149.2 7.8 %collective-permute-start.25 = (f32[2,2,32,256]{3,2,1,0:T(8,128)S(1)}, f32[2,2,32,256]{3,2,1,0:T(8,128)S(1)}, u32[]{:S(2)}, u32[]{:S(2)}) collective-permute-start(f32[2,2,32,256]{3,2,1,0:T(8,128)S(1)} %copy-done.30), channel_id=1, source_target_pairs={{0,64},{16,80},{32,96},{48,112},{64,0},{80,16},{96,32},{112,48},{1... | collective-permute-start | bytes 393224 | tf_op jit(solution)/shard_map/ppermute | solution.py:597
  150.8 7.1 %collective-permute-start.26 = (f32[2,2,32,256]{3,2,1,0:T(8,128)S(1)}, f32[2,2,32,256]{3,2,1,0:T(8,128)S(1)}, u32[]{:S(2)}, u32[]{:S(2)}) collective-permute-start(f32[2,2,32,256]{3,2,1,0:T(8,128)S(1)} %copy-done.28), channel_id=1, source_target_pairs={{0,96},{16,112},{32,0},{48,16},{64,32},{80,48},{96,64},{112,80},{1... | collective-permute-start | bytes 393224 | tf_op jit(solution)/shard_map/ppermute | solution.py:597
  160.3 11.1 %collective-permute-start.30 = (f32[3,32,1024]{2,1,0:T(8,128)}, f32[3,32,1024]{2,1,0:T(8,128)S(1)}, u32[]{:S(2)}, u32[]{:S(2)}) collective-permute-start(f32[3,32,1024]{2,1,0:T(8,128)} %get-tuple-element.110.refs_4_), channel_id=1, source_target_pairs={{0,1},{1,2},{2,3},{3,4},{4,5},{5,6},{6,7},{7,8},{8,9},{9,10},{10,1... | collective-permute-start | bytes 1179656 | tf_op jit(solution)/shard_map/ppermute | solution.py:605
  163.1 10.6 %collective-permute-start.31 = (f32[3,32,1024]{2,1,0:T(8,128)}, f32[3,32,1024]{2,1,0:T(8,128)S(1)}, u32[]{:S(2)}, u32[]{:S(2)}) collective-permute-start(f32[3,32,1024]{2,1,0:T(8,128)} %get-tuple-element.111.refs_3_), channel_id=1, source_target_pairs={{1,0},{2,1},{3,2},{4,3},{5,4},{6,5},{7,6},{8,7},{9,8},{10,9},{11,1... | collective-permute-start | bytes 1179656 | tf_op jit(solution)/shard_map/ppermute | solution.py:609
  169.1 4.6 %collective-permute-start.29 = (f32[9,8,256]{2,1,0:T(8,128)S(1)}, f32[9,8,256]{2,1,0:T(8,128)S(1)}, u32[]{:S(2)}, u32[]{:S(2)}) collective-permute-start(f32[9,8,256]{2,1,0:T(8,128)S(1)} %get-tuple-element.109.refs_0_), channel_id=1, source_target_pairs={{0,96},{16,112},{32,0},{48,16},{64,32},{80,48},{96,64},{112,80},{1... | collective-permute-start | bytes 221192 | tf_op jit(solution)/shard_map/ppermute | solution.py:597
  170.0 4.7 %collective-permute-start.28 = (f32[9,8,256]{2,1,0:T(8,128)S(1)}, f32[9,8,256]{2,1,0:T(8,128)S(1)}, u32[]{:S(2)}, u32[]{:S(2)}) collective-permute-start(f32[9,8,256]{2,1,0:T(8,128)S(1)} %get-tuple-element.109.refs_0_), channel_id=1, source_target_pairs={{0,64},{16,80},{32,96},{48,112},{64,0},{80,16},{96,32},{112,48},{1... | collective-permute-start | bytes 221192 | tf_op jit(solution)/shard_map/ppermute | solution.py:597
  171.4 4.4 %collective-permute-start.27 = (f32[9,8,256]{2,1,0:T(8,128)S(1)}, f32[9,8,256]{2,1,0:T(8,128)S(1)}, u32[]{:S(2)}, u32[]{:S(2)}) collective-permute-start(f32[9,8,256]{2,1,0:T(8,128)S(1)} %get-tuple-element.109.refs_0_), channel_id=1, source_target_pairs={{0,32},{16,48},{32,64},{48,80},{64,96},{80,112},{96,0},{112,16},{1... | collective-permute-start | bytes 221192 | tf_op jit(solution)/shard_map/ppermute | solution.py:597
  177.5 28.9 %all-to-all-start.5 = ((f32[16,8,8,256]{3,2,1,0:T(8,128)}), f32[16,8,8,256]{3,2,1,0:T(8,128)S(1)}, u32[]{:S(2)}, u32[]{:S(2)}) async-start(f32[16,8,8,256]{3,2,1,0:T(8,128)} %get-tuple-element.112), calls=%async_computation.5 | async-start | bytes 2097152 | tf_op jit(solution)/shard_map/all_to_all | solution.py:748
  183.7 18.3 %copy-start.9 = (f32[2,256,256]{2,1,0:T(8,128)S(1)}, f32[2,256,256]{2,1,0:T(8,128)}, u32[]{:S(2)}) copy-start(f32[2,256,256]{2,1,0:T(8,128)} %get-tuple-element.119.refs_7_) | copy-start | bytes 1572868
  187.3 16.7 %copy-start.23 = (f32[2,32,1024]{2,1,0:T(8,128)S(1)}, f32[2,32,1024]{2,1,0:T(8,128)}, u32[]{:S(2)}) copy-start(f32[2,32,1024]{2,1,0:T(8,128)} %get-tuple-element.124.refs_6_) | copy-start | bytes 786436
  187.3 7.2 %collective-permute-start.32 = (f32[2,2,32,256]{3,2,1,0:T(8,128)S(1)}, f32[2,2,32,256]{3,2,1,0:T(8,128)S(1)}, u32[]{:S(2)}, u32[]{:S(2)}) collective-permute-start(f32[2,2,32,256]{3,2,1,0:T(8,128)S(1)} %get-tuple-element.116), channel_id=1, source_target_pairs={{0,32},{16,48},{32,64},{48,80},{64,96},{80,112},{96,0},{112,16},{1... | collective-permute-start | bytes 393224 | tf_op jit(solution)/shard_map/ppermute | solution.py:597
  188.6 8.8 %collective-permute-start.33 = (f32[2,2,32,256]{3,2,1,0:T(8,128)S(1)}, f32[2,2,32,256]{3,2,1,0:T(8,128)S(1)}, u32[]{:S(2)}, u32[]{:S(2)}) collective-permute-start(f32[2,2,32,256]{3,2,1,0:T(8,128)S(1)} %get-tuple-element.117), channel_id=1, source_target_pairs={{0,64},{16,80},{32,96},{48,112},{64,0},{80,16},{96,32},{112,48},{1... | collective-permute-start | bytes 393224 | tf_op jit(solution)/shard_map/ppermute | solution.py:597
  193.1 5.0 %collective-permute-start.34 = (f32[2,2,32,256]{3,2,1,0:T(8,128)S(1)}, f32[2,2,32,256]{3,2,1,0:T(8,128)S(1)}, u32[]{:S(2)}, u32[]{:S(2)}) collective-permute-start(f32[2,2,32,256]{3,2,1,0:T(8,128)S(1)} %get-tuple-element.118), channel_id=1, source_target_pairs={{0,96},{16,112},{32,0},{48,16},{64,32},{80,48},{96,64},{112,80},{1... | collective-permute-start | bytes 393224 | tf_op jit(solution)/shard_map/ppermute | solution.py:597
  198.1 3.8 %collective-permute-start.35 = (f32[4,2,32,256]{3,2,1,0:T(8,128)S(1)}, f32[4,2,32,256]{3,2,1,0:T(8,128)S(1)}, u32[]{:S(2)}, u32[]{:S(2)}) collective-permute-start(f32[4,2,32,256]{3,2,1,0:T(8,128)S(1)} %stack_kernel.3), channel_id=1, source_target_pairs={{0,16},{16,0},{32,48},{48,32},{64,80},{80,64},{96,112},{112,96},{1... | collective-permute-start | bytes 786440 | tf_op jit(solution)/shard_map/ppermute | solution.py:601
  203.6 2.7 %collective-permute-start.36 = (f32[2,128,256]{2,1,0:T(8,128)S(1)}, f32[2,128,256]{2,1,0:T(8,128)S(1)}, u32[]{:S(2)}, u32[]{:S(2)}) collective-permute-start(f32[2,128,256]{2,1,0:T(8,128)S(1)} %get-tuple-element.121), channel_id=1, source_target_pairs={{0,16},{16,0},{32,48},{48,32},{64,80},{80,64},{96,112},{112,96},{1... | collective-permute-start | bytes 786440 | tf_op jit(solution)/shard_map/ppermute | solution.py:601
  204.0 16.8 %collective-permute-start.39 = (f32[2,32,1024]{2,1,0:T(8,128)S(1)}, f32[2,32,1024]{2,1,0:T(8,128)S(1)}, u32[]{:S(2)}, u32[]{:S(2)}) collective-permute-start(f32[2,32,1024]{2,1,0:T(8,128)S(1)} %copy-done.23), channel_id=1, source_target_pairs={{0,96},{16,112},{32,0},{48,16},{64,32},{80,48},{96,64},{112,80},{1... | collective-permute-start | bytes 786440 | tf_op jit(solution)/shard_map/ppermute | solution.py:597
  205.7 15.1 %collective-permute-start.38 = (f32[2,32,1024]{2,1,0:T(8,128)S(1)}, f32[2,32,1024]{2,1,0:T(8,128)S(1)}, u32[]{:S(2)}, u32[]{:S(2)}) collective-permute-start(f32[2,32,1024]{2,1,0:T(8,128)S(1)} %copy-done.23), channel_id=1, source_target_pairs={{0,64},{16,80},{32,96},{48,112},{64,0},{80,16},{96,32},{112,48},{1... | collective-permute-start | bytes 786440 | tf_op jit(solution)/shard_map/ppermute | solution.py:597
  205.7 15.1 %collective-permute-start.37 = (f32[2,32,1024]{2,1,0:T(8,128)S(1)}, f32[2,32,1024]{2,1,0:T(8,128)S(1)}, u32[]{:S(2)}, u32[]{:S(2)}) collective-permute-start(f32[2,32,1024]{2,1,0:T(8,128)S(1)} %copy-done.23), channel_id=1, source_target_pairs={{0,32},{16,48},{32,64},{48,80},{64,96},{80,112},{96,0},{112,16},{1... | collective-permute-start | bytes 786440 | tf_op jit(solution)/shard_map/ppermute | solution.py:597
  210.5 22.5 %copy-start = (f32[8,128,256]{2,1,0:T(8,128)}, f32[8,128,256]{2,1,0:T(8,128)S(1)}, u32[]{:S(2)}) copy-start(f32[8,128,256]{2,1,0:T(8,128)S(1)} %relay_kernel.3.refs_3_) | copy-start | bytes 3145732
  210.5 23.3 %collective-permute-start.41 = (f32[8,128,256]{2,1,0:T(8,128)S(1)}, f32[8,128,256]{2,1,0:T(8,128)S(1)}, u32[]{:S(2)}, u32[]{:S(2)}) collective-permute-start(f32[8,128,256]{2,1,0:T(8,128)S(1)} %relay_kernel.3.refs_3_), channel_id=1, source_target_pairs={{0,16},{16,0},{32,48},{48,32},{64,80},{80,64},{96,112},{112,96},{1... | collective-permute-start | bytes 3145736 | tf_op jit(solution)/shard_map/ppermute | solution.py:601
  211.3 19.2 %all-to-all-start.6 = ((f32[128,1,128]{2,1,0:T(1,128)}), f32[128,1,128]{2,1,0:T(1,128)S(1)}, u32[]{:S(2)}, u32[]{:S(2)}) async-start(f32[128,1,128]{2,1,0:T(1,128)} %bitcast.12), calls=%async_computation.6 | async-start | bytes 131072 | tf_op jit(solution)/shard_map/all_to_all | solution.py:791
  220.8 9.7 %copy-start.24 = (f32[2,32,1024]{2,1,0:T(8,128)}, f32[2,32,1024]{2,1,0:T(8,128)S(1)}, u32[]{:S(2)}) copy-start(f32[2,32,1024]{2,1,0:T(8,128)S(1)} %collective-permute-done.39.refs_9_) | copy-start | bytes 786436
  220.8 9.7 %copy-start.25 = (f32[2,32,1024]{2,1,0:T(8,128)}, f32[2,32,1024]{2,1,0:T(8,128)S(1)}, u32[]{:S(2)}) copy-start(f32[2,32,1024]{2,1,0:T(8,128)S(1)} %collective-permute-done.38.refs_8_) | copy-start | bytes 786436
  220.8 9.7 %copy-start.26 = (f32[2,32,1024]{2,1,0:T(8,128)}, f32[2,32,1024]{2,1,0:T(8,128)S(1)}, u32[]{:S(2)}) copy-start(f32[2,32,1024]{2,1,0:T(8,128)S(1)} %collective-permute-done.37.refs_7_) | copy-start | bytes 786436
  233.0 5.8 %collective-permute-start.40 = (f32[4,2,32,1024]{3,2,1,0:T(8,128)}, f32[4,2,32,1024]{3,2,1,0:T(8,128)S(1)}, u32[]{:S(2)}, u32[]{:S(2)}) collective-permute-start(f32[4,2,32,1024]{3,2,1,0:T(8,128)} %combine_kernel.1.refs_2_), channel_id=1, source_target_pairs={{0,16},{16,0},{32,48},{48,32},{64,80},{80,64},{96,112},{112,96},{1... | collective-permute-start | bytes 3145736 | tf_op jit(solution)/shard_map/ppermute | solution.py:601
  (18 other events, 79.3 us)

commit v4 on v3

--- a/solution.py
+++ b/solution.py
@@ -50,12 +50,14 @@
 
 def times_table(value, table):
     high, low = halves(value)
-    return dot(high, table[0]) + (dot(low, table[0]) + dot(high, table[1]))
+    both = dot(jnp.concatenate([high, low], axis=0), table[0])
+    return both[:N] + (both[N:] + dot(high, table[1]))
 
 
 def table_times(table, value):
     high, low = halves(value)
-    return dot(table[0], high) + (dot(table[0], low) + dot(table[1], high))
+    both = dot(jnp.concatenate([table[0], table[1]], axis=0), high)
+    return both[:N] + (both[N:] + dot(table[0], low))
 
 
 def thirds(value):
@@ -172,21 +174,23 @@
 def patterns_kernel(first, ready, leave, *refs):
     if first:
         where, here, base, own_side, far_side, probe_now, measured, tab = refs[:8]
-        patch_now, keep, send, mine, other, power, psi, model, obj = refs[8:]
+        patch_now, keep, send, mine, other, power, near_rows, psi, model, obj = refs[8:]
         add_side(where, here, base, own_side, far_side, patch_now)
     else:
         where, here, everyone, patch, probe, measured, tab, dirp, dmine, doth = refs[:10]
         patch_now, probe_now = refs[13:15]
-        keep, send, mine, other, power, psi, model, obj = refs[15:]
+        keep, send, mine, other, power, near_rows, psi, model, obj = refs[15:]
         object_step, probe_step = map(twice, step_sizes(everyone))
         ready(3)
         ready(7)
+        ready.more()
         for part in range(2):
             patch_now[part] = patch[part] + object_step * dirp[part]
         leave(0)
     y, c = where[0], where[1]
     e0 = here[0, 0] - where[3]
     first_core = c == 0
+    rows_at = pl.multiple_of(H * c + 8 * where[2], 8)
     model[...] = jnp.zeros_like(model)
     obj[...] = jnp.zeros_like(obj)
     power[...] = jnp.zeros_like(power)
@@ -206,6 +210,8 @@
         pr, pi = probe_now[k, 0], probe_now[k, 1]
         orr, oi = patch_now[0], patch_now[1]
         power[...] += pr * pr + pi * pi
+        for part in range(2):
+            near_rows[2 * k + part] = probe_now[k, part, pl.ds(rows_at, 8), :]
         xr = pr * orr - pi * oi
         xi = pr * oi + pi * orr
         even = times_table(
@@ -394,36 +400,29 @@
     token[0, 0] = 0.0
 
 
-def share_kernel(own, a, b, d, above, below, spread_out, sums):
+def share_kernel(own, a, b, d, above, below, near_rows, spread_out, sums):
     total = own[...] + a[...] + b[...] + d[...]
     illum = total[8]
     value = total[:8] * (1.0 / (illum + RIDGE))
-    spread_out[...] = jnp.broadcast_to(value[None], (16, 8, 8, N))
+    inner_real = jnp.zeros((8, N), F32)
+    inner_imag = jnp.zeros((8, N), F32)
+    for k in range(4):
+        pr, pi = near_rows[2 * k], near_rows[2 * k + 1]
+        inner_real += pr * value[2 * k] + pi * value[2 * k + 1]
+        inner_imag += pr * value[2 * k + 1] - pi * value[2 * k]
+    value_out = jnp.concatenate([value, inner_real[None], inner_imag[None]], axis=0)
+    spread_out[...] = jnp.broadcast_to(value_out[None], (16, 10, 8, N))
     size = jnp.sum(value * value, axis=0)
     sums[0, 0] = jnp.sum(size * illum)
     sums[0, 1] = jnp.sum(size)
 
 
-def relay_kernel(token, gathered, out):
+def message_kernel(where, gathered, kept, came, ae, df, out, planes):
     for plane in range(8):
-        out[plane] = gathered[:, plane].reshape(H, N)
-
-
-def message_kernel(where, gathered, probe, kept, came, ae, df, out, token, half, sem):
-    token[0, 0] = 0.0
-    rows = pl.ds(pl.multiple_of(where[1] * H, H), H)
-    copy = pltpu.make_async_copy(probe.at[:, :, rows, :], half, sem)
-    copy.start()
-    total = jnp.zeros((H, N), F32)
-    mixed_real = kept[0] + came[0]
-    mixed_imag = kept[1] + came[1]
-    copy.wait()
-    for k in range(4):
-        dr = gathered[:, 2 * k].reshape(H, N)
-        di = gathered[:, 2 * k + 1].reshape(H, N)
-        pr, pi = half[k, 0], half[k, 1]
-        total += mixed_real * (pr * dr + pi * di) - mixed_imag * (pr * di - pi * dr)
-    cross = jnp.sum(total)
+        planes[plane] = gathered[:, plane].reshape(H, N)
+    inner_real = gathered[:, 8].reshape(H, N)
+    inner_imag = gathered[:, 9].reshape(H, N)
+    cross = jnp.sum((kept[0] + came[0]) * inner_real - (kept[1] + came[1]) * inner_imag)
     d_sum = 0.25 * df[0, 0]
     values = (ae[0, 0], cross, d_sum, ae[0, 0] + ae[0, 1], d_sum + 0.25 * df[0, 1])
     lane = lax.broadcasted_iota(jnp.int32, (128, 128), 1)
@@ -442,15 +441,13 @@
         ready(6 + s)
         for part in range(2):
             out[s, part] = first * bands[s][part] + second * bands[4 + s][part]
-        leave(0, s)
 
 
 def probe_kernel(ready, leave, where, two, probe, dmine, doth, probe_out):
     probe_step = twice(step_sizes(two)[1])
     first_core = where[1] == 0
     for k in range(4):
-        for index in (2, 3, 4):
-            ready(index, k)
+        ready(2, k)
         for part in range(2):
             moved = probe_step * joined(first_core, dmine, doth, 2 * k + part)
             probe_out[k, part] = probe[k, part] + moved
@@ -460,8 +457,7 @@
 def object_kernel(ready, leave, where, field, mine, other, out, lanes):
     y, c = where[0], where[1]
     for block in range(4):
-        for index in (1, 2, 3):
-            ready(index, block)
+        ready(1, block)
         own = slice(8 * block, 8 * block + 8)
         for s in range(4):
             for which, change in ((c, mine), (1 - c, other)):
@@ -491,6 +487,7 @@
     hbm_in=(),
     any_in=(),
     lazy=False,
+    staged_in=False,
     cheap=False,
     flops=0,
     room=12,
@@ -538,7 +535,8 @@
             stage, source = staged[slot], given[index]
             for piece, pair in enumerate(zip(cuts(source, count), cuts(stage, count))):
                 copy = pltpu.make_async_copy(*pair, sems.at[at])
-                copy.start()
+                if piece < 2 or not staged_in:
+                    copy.start()
                 arrivals[index, piece] = copy
                 at += 1
             given[index] = stage
@@ -551,6 +549,13 @@
 
         def ready(index, piece=0):
             arrivals[index, piece].wait()
+
+        def more():
+            for (index, piece), copy in arrivals.items():
+                if piece >= 2:
+                    copy.start()
+
+        ready.more = more
 
         def leave(index, piece=0):
             departures[index, piece].start()
@@ -655,12 +660,12 @@
     sent = (16, 9, 8, N)
     pieces = (4, 2, 32, N)
     scratch = ((4, 2, N, N), (2, H, N), (2, 2, N, H))
-    outs = (sent, sent, pieces, pieces, (N, N))
+    outs = (sent, sent, pieces, pieces, (N, N), (8, 8, N))
     messages, bands = [], []
 
     for iteration in range(ITERS):
         if iteration == 0:
-            patch, keep, send, mine, other, power = call(
+            patch, keep, send, mine, other, power, near_rows = call(
                 lambda *refs: patterns_kernel(True, *refs),
                 ((2, N, N),) + outs,
                 (
@@ -681,7 +686,7 @@
                 name="patterns",
             )
         else:
-            patch, probe, keep, send, mine, other, power = call(
+            patch, probe, keep, send, mine, other, power, near_rows = call(
                 lambda *refs: patterns_kernel(False, *refs),
                 ((2, N, N), (4, 2, N, N)) + outs,
                 (
@@ -700,6 +705,7 @@
                 (0, 1),
                 scratch,
                 hbm_in={3: 1, 7: 1, 6: 1, 4: 4, 8: 4, 9: 4, 5: 1},
+                staged_in=True,
                 lazy=True,
                 hbm_out={0: 1, 1: 4},
                 any_in=(10, 11, 12),
@@ -712,7 +718,7 @@
             (sent,) + ((2, 2, 32, N),) * 4,
             (keep, partner(send), mine, partner(other)),
             (),
-            hbm_out=(0, 2, 3, 4),
+            hbm_out=(0,),
         )
         came = [b0, along_y(b1, 1), along_y(b2, 2), along_y(b3, 3)]
         (illum,) = call(
@@ -729,7 +735,6 @@
             (0, 1),
             ((2, 72, 1152),),
             smem_out=(2,),
-            hbm_out=(0, 1),
         )
         above, below = up(high), down(low)
         shares = lax.all_to_all(chip, "tile", 0, 0)
@@ -738,8 +743,8 @@
         )
         probe_dir, df = call(
             share_kernel,
-            ((16, 8, 8, N), (1, 2)),
-            (share, *[along_y(share, s) for s in range(1, 4)], above, below),
+            ((16, 10, 8, N), (1, 2)),
+            (share, *[along_y(share, s) for s in range(1, 4)], above, below, near_rows),
             (),
             smem_out=(1,),
             hbm_out=(0,),
@@ -753,8 +758,6 @@
             (0, 1, 2),
             ((2, 72, 1152),),
             smem_out=(1,),
-            hbm_out=(0,),
-            hbm_in=(3, 4, 5, 6),
             cheap=True,
         )
         bands.append([band] + [along_y(band, s) for s in range(1, 4)])
@@ -768,25 +771,13 @@
             ((2, 2, N, H),),
             cheap=True,
         )
-        message, token = call(
+        message, dmine = call(
             message_kernel,
-            ((128, 128), (1, 1)),
-            (
-                where,
-                gathered,
-                pltpu.with_memory_space_constraint(probe, pltpu.HBM),
-                kept,
-                partner(sent_mixed),
-                ae,
-                df,
-            ),
-            (0, 5, 6),
-            ((4, 2, H, N), None),
-            any_in=(2,),
-            smem_out=(1,),
+            ((128, 128), (8, H, N)),
+            (where, gathered, kept, partner(sent_mixed), ae, df),
+            (0, 4, 5),
             hbm_out=(0,),
         )
-        (dmine,) = call(relay_kernel, ((8, H, N),), (token, gathered), (0,))
         doth = partner(dmine)
         messages.append(lax.all_to_all(message, BOTH, 0, 0))
     (change,) = call(
@@ -795,7 +786,6 @@
         (*messages, *bands[0], *bands[1]),
         (),
         hbm_in={index: 1 for index in range(2, 10)},
-        hbm_out={0: 4},
         lazy=True,
     )
     change_far = partner(change)
@@ -804,7 +794,7 @@
         (probe_init.shape,),
         (where, messages[1], probe, dmine, doth),
         (0,),
-        hbm_in={2: 4, 3: 4, 4: 4},
+        hbm_in={2: 4},
         hbm_out={0: 4},
         lazy=True,
         flops=10**9,
@@ -815,7 +805,7 @@
         (where, object_init, change, change_far),
         (0,),
         ((2, 8, N, H),),
-        hbm_in={1: (4, 1), 2: (4, 2), 3: (4, 2)},
+        hbm_in={1: (4, 1)},
         hbm_out={0: (4, 1)},
         lazy=True,
         room=16,

time: 245 us -> 230 us (0.939)
  Pallas kernels: 67.4 us -> 52.4 us
  waiting for transfers between devices: 64.4 us -> 68.1 us
  starting transfers between devices: 107 us -> 104 us
    pallas_call x28 -> x26, Pallas kernels: 64.6 us -> 50.6 us  [call(): pl.pallas_call(run, out_shape=shapes, in_specs=[space(i, smem_in, hbm_in)...]
    ppermute x24, waiting for transfers between devices: 26.4 us -> 34.7 us  [along_y(): return lax.ppermute(value, 'pat', [(i, (i + 2 * s) % 8) for i in range(8)])]
    all_to_all x2, waiting for transfers between devices: 14.9 us -> 9.14 us  [body(): messages.append(lax.all_to_all(message, BOTH, 0, 0))]
    all_to_all x2, starting transfers between devices: 19.6 us -> 16.3 us  [body(): messages.append(lax.all_to_all(message, BOTH, 0, 0))]
    ppermute x3, waiting for transfers between devices: 7.45 us -> 4.35 us  [down(): return lax.ppermute(value, 'tile', [(i + 1, i) for i in range(15)])]
    all_to_all x2, starting transfers between devices: 12.6 us -> 9.92 us  [body(): gathered = lax.all_to_all(probe_dir, 'tile', 0, 0)]
    ppermute x12, starting transfers between devices: 13.5 us -> 15.9 us  [partner(): return lax.ppermute(value, 'pat', [(i, i ^ 1) for i in range(8)])]
  transfers between devices with their start and end apart: 49 -> 49, of which waited for: 29 -> 33; matrix products, arithmetic and copies ran while one was open for 0% -> 0% of each run, Pallas kernels for 13% -> 10%
where the time goes in v4:
time: 230 us; the launch traced here: 229 us
  starting transfers between devices  104 us (45%)
  waiting for transfers between devices  68.1 us (30%)
  Pallas kernels  52.4 us (23%)
  local copies, waits for them, and re-layouts  4.09 us (2%)
    pallas_call x26, Pallas kernels, call(): pl.pallas_call(run, out_shape=shapes, in_specs=[space(i, smem_in, hbm_in)...  50.6 us
    ppermute x24, waiting for transfers between devices, along_y(): return lax.ppermute(value, 'pat', [(i, (i + 2 * s) % 8) for i in range(8)])  34.7 us
    ppermute x24, starting transfers between devices, along_y(): return lax.ppermute(value, 'pat', [(i, (i + 2 * s) % 8) for i in range(8)])  29.4 us
    all_to_all x2, starting transfers between devices, body(): messages.append(lax.all_to_all(message, BOTH, 0, 0))  16.3 us
    ppermute x12, starting transfers between devices, partner(): return lax.ppermute(value, 'pat', [(i, i ^ 1) for i in range(8)])  15.9 us
    all_to_all x2, starting transfers between devices, body(): shares = lax.all_to_all(chip, 'tile', 0, 0)  13 us
    ppermute x12, waiting for transfers between devices, partner(): return lax.ppermute(value, 'pat', [(i, i ^ 1) for i in range(8)])  10.5 us
    all_to_all x2, starting transfers between devices, body(): gathered = lax.all_to_all(probe_dir, 'tile', 0, 0)  9.92 us
  transfers between devices with their start and end apart: 49, of which 33 were waited for; matrix products, arithmetic and copies ran while one was open for 0% of the time, Pallas kernels for 10%

profile of v4, /device:TPU:1, one launch (start us, length us, event | category | flops | bytes accessed | tf_op | source)
XLA Modules:
  0.0 229.5 jit_solution(6694642987090463274)
XLA Ops:
  0.8 1.8 shard_map.77
  2.5 4.0 %collective-permute-start = (f32[128,1024]{1,0:T(8,128)S(1)}, f32[128,1024]{1,0:T(8,128)S(1)}, u32[]{:S(2)}, u32[]{:S(2)}) collective-permute-start(f32[128,1024]{1,0:T(8,128)S(1)} %get-tuple-element.67), channel_id=1, source_target_pairs={{0,1},{1,2},{2,3},{3,4},{4,5},{5,6},{6,7},{7,8},{8,9},{9,10},{10,1... | collective-permute-start | bytes 1572872 | tf_op jit(solution)/shard_map/ppermute | solution.py:610
  6.5 1.3 collective-permute-start.1
  9.0 5.4 %all-to-all-start = ((s32[8,1,128]{2,1,0:T(1,128)}), s32[8,1,128]{2,1,0:T(1,128)S(1)}, u32[]{:S(2)}, u32[]{:S(2)}) async-start(s32[8,1,128]{2,1,0:T(1,128)} %bitcast.5), calls=%async_computation | async-start | bytes 8192 | tf_op jit(solution)/shard_map/all_to_all | solution.py:637
  14.4 2.5 %prepare_kernel.1 = (f32[2,128,256]{2,1,0:T(8,128)S(1)}, f32[2,256,256]{2,1,0:T(8,128)S(1)}) custom-call(s32[4]{0:T(128)S(1)} %pad_add_fusion.refs_0_.where, s32[1,2]{1,0:T(1,128)S(1)} %copy-done.12, f32[256,256]{1,0:T(8,128)S(1)} %bitcast.28, bf16[2,256,256]{2,1,0:T(8,128)(2,1)S(1)} %copy-done.9, f32[2,256,1024]{2,1,0:T(8,128)} %refs_1_.7), custom_call_target="tpu_custom_call" | custom-call | bytes 3670040 | tf_op jit(solution)/shard_map/prepare_kernel/pallas_call | solution.py:582
  16.9 2.0 all-to-all-done
  18.9 2.0 collective-permute-done.1.refs_4_
  21.6 1.9 collective-permute-start.2
  23.5 1.5 collective-permute-done.2.refs_4_
  25.1 1.6 copy-done.13
  26.7 6.5 %patterns.2 = (f32[2,256,256]{2,1,0:T(8,128)S(1)}, f32[16,9,8,256]{3,2,1,0:T(8,128)S(1)}, f32[16,9,8,256]{3,2,1,0:T(8,128)S(1)}, f32[4,2,32,256]{3,2,1,0:T(8,128...) custom-call(s32[4]{0:T(128)S(1)} %pad_add_fusion.refs_0_.where, ...), custom_call_target="tpu_custom_call" | custom-call | flops 6000000000 | bytes 9764888 | tf_op jit(solution)/shard_map/patterns/pallas_call | solution.py:582
  33.8 2.7 %collective-permute-done.4.refs_3_ = f32[4,2,32,256]{3,2,1,0:T(8,128)S(1)} collective-permute-done((f32[4,2,32,256]{3,2,1,0:T(8,128)S(1)}, f32[4,2,32,256]{3,2,1,0:T(8,128)S(1)}, u32[]{:S(2)}, u32[]{:S(2)}) %collective-permute-start.4) | collective-permute-done | bytes 262176 | tf_op jit(solution)/shard_map/ppermute | solution.py:606
  37.8 9.3 %all-to-all-start.1 = ((f32[16,9,8,256]{3,2,1,0:T(8,128)}), f32[16,9,8,256]{3,2,1,0:T(8,128)S(1)}, u32[]{:S(2)}, u32[]{:S(2)}) async-start(f32[16,9,8,256]{3,2,1,0:T(8,128)} %get-tuple-element.82), calls=%async_computation.1 | async-start | bytes 2359296 | tf_op jit(solution)/shard_map/all_to_all | solution.py:740
  47.1 1.4 collective-permute-start.5
  48.4 2.6 %collective-permute-start.6 = (f32[2,2,32,256]{3,2,1,0:T(8,128)S(1)}, f32[2,2,32,256]{3,2,1,0:T(8,128)S(1)}, u32[]{:S(2)}, u32[]{:S(2)}) collective-permute-start(f32[2,2,32,256]{3,2,1,0:T(8,128)S(1)} %get-tuple-element.79), channel_id=1, source_target_pairs={{0,64},{16,80},{32,96},{48,112},{64,0},{80,16},{96,32},{112,48},{1... | collective-permute-start | bytes 393224 | tf_op jit(solution)/shard_map/ppermute | solution.py:602
  53.0 3.7 %collective-permute-done.6.refs_5_ = f32[2,2,32,256]{3,2,1,0:T(8,128)S(1)} collective-permute-done((f32[2,2,32,256]{3,2,1,0:T(8,128)S(1)}, f32[2,2,32,256]{3,2,1,0:T(8,128)S(1)}, u32[]{:S(2)}, u32[]{:S(2)}) %collective-permute-start.6) | collective-permute-done | bytes 131104 | tf_op jit(solution)/shard_map/ppermute | solution.py:602
  56.8 1.4 place_kernel.2
  58.2 2.9 %collective-permute-start.11 = (f32[3,32,1024]{2,1,0:T(8,128)S(1)}, f32[3,32,1024]{2,1,0:T(8,128)S(1)}, u32[]{:S(2)}, u32[]{:S(2)}) collective-permute-start(f32[3,32,1024]{2,1,0:T(8,128)S(1)} %get-tuple-element.84.refs_4_), channel_id=1, source_target_pairs={{0,1},{1,2},{2,3},{3,4},{4,5},{5,6},{6,7},{7,8},{8,9},{9,10},{10,1... | collective-permute-start | bytes 1179656 | tf_op jit(solution)/shard_map/ppermute | solution.py:610
  61.2 1.3 collective-permute-start.12
  62.5 2.6 %all-to-all-done.1.refs_1_ = f32[16,9,8,256]{3,2,1,0:T(8,128)S(1)} async-done(((f32[16,9,8,256]{3,2,1,0:T(8,128)}), f32[16,9,8,256]{3,2,1,0:T(8,128)S(1)}, u32[]{:S(2)}, u32[]{:S(2)}) %all-to-all-start.1) | async-done | bytes 1179680 | tf_op jit(solution)/shard_map/all_to_all | solution.py:740
  66.2 2.8 %collective-permute-start.10 = (f32[9,8,256]{2,1,0:T(8,128)S(1)}, f32[9,8,256]{2,1,0:T(8,128)S(1)}, u32[]{:S(2)}, u32[]{:S(2)}) collective-permute-start(f32[9,8,256]{2,1,0:T(8,128)S(1)} %get-tuple-element.83.refs_0_), channel_id=1, source_target_pairs={{0,96},{16,112},{32,0},{48,16},{64,32},{80,48},{96,64},{112,80},{1... | collective-permute-start | bytes 221192 | tf_op jit(solution)/shard_map/ppermute | solution.py:602
  70.1 1.5 collective-permute-done.12.refs_5_.refs_6_
  71.6 2.3 collective-permute-done.9.refs_2_
  74.5 1.8 share_kernel.2
  76.3 5.0 %all-to-all-start.2 = ((f32[16,10,8,256]{3,2,1,0:T(8,128)}), f32[16,10,8,256]{3,2,1,0:T(8,128)S(1)}, u32[]{:S(2)}, u32[]{:S(2)}) async-start(f32[16,10,8,256]{3,2,1,0:T(8,128)} %get-tuple-element.87), calls=%async_computation.2 | async-start | bytes 2621440 | tf_op jit(solution)/shard_map/all_to_all | solution.py:753
  81.3 1.6 direction_kernel.2
  84.7 2.9 %collective-permute-start.14 = (f32[2,2,32,256]{3,2,1,0:T(8,128)S(1)}, f32[2,2,32,256]{3,2,1,0:T(8,128)S(1)}, u32[]{:S(2)}, u32[]{:S(2)}) collective-permute-start(f32[2,2,32,256]{3,2,1,0:T(8,128)S(1)} %get-tuple-element.91), channel_id=1, source_target_pairs={{0,64},{16,80},{32,96},{48,112},{64,0},{80,16},{96,32},{112,48},{1... | collective-permute-start | bytes 393224 | tf_op jit(solution)/shard_map/ppermute | solution.py:602
  88.7 2.9 %collective-permute-done.14.refs_2_.refs_4_ = f32[2,2,32,256]{3,2,1,0:T(8,128)S(1)} collective-permute-done((f32[2,2,32,256]{3,2,1,0:T(8,128)S(1)}, f32[2,2,32,256]{3,2,1,0:T(8,128)S(1)}, u32[]{:S(2)}, u32[]{:S(2)}) %collective-permute-start.14) | collective-permute-done | bytes 131104 | tf_op jit(solution)/shard_map/ppermute | solution.py:602
  91.7 4.4 %collective-permute-start.16 = (f32[4,2,32,256]{3,2,1,0:T(8,128)S(1)}, f32[4,2,32,256]{3,2,1,0:T(8,128)S(1)}, u32[]{:S(2)}, u32[]{:S(2)}) collective-permute-start(f32[4,2,32,256]{3,2,1,0:T(8,128)S(1)} %stack_kernel.2), channel_id=1, source_target_pairs={{0,16},{16,0},{32,48},{48,32},{64,80},{80,64},{96,112},{112,96},{1... | collective-permute-start | bytes 786440 | tf_op jit(solution)/shard_map/ppermute | solution.py:606
  100.6 2.4 %message_kernel.2 = (f32[128,128]{1,0:T(8,128)}, f32[8,128,256]{2,1,0:T(8,128)}) custom-call(s32[4]{0:T(128)S(1)} %pad_add_fusion.refs_0_.where, f32[16,10,8,256]{3,2,1,0:T(8,128)S(1)} %all-to-all-done.2.refs_1_, f32[2,128,256]{2,1,0:T(8,128)S(1)} %get-tuple-element.94.refs_2_, f32[2,128,256]{2,1,0:T(8,128)S(1)} %collective-permute-done.17.refs_3_, ...), custom_call_target="tpu_custom_call" | custom-call | bytes 2949152 | tf_op jit(solution)/shard_map/message_kernel/pallas_call | solution.py:582
  103.0 2.5 %collective-permute-start.18 = (f32[8,128,256]{2,1,0:T(8,128)}, f32[8,128,256]{2,1,0:T(8,128)S(1)}, u32[]{:S(2)}, u32[]{:S(2)}) collective-permute-start(f32[8,128,256]{2,1,0:T(8,128)} %get-tuple-element.99.refs_8_), channel_id=1, source_target_pairs={{0,16},{16,0},{32,48},{48,32},{64,80},{80,64},{96,112},{112,96},{1... | collective-permute-start | bytes 3145736 | tf_op jit(solution)/shard_map/ppermute | solution.py:606
  105.5 2.8 %collective-permute-start.21 = (f32[2,32,1024]{2,1,0:T(8,128)S(1)}, f32[2,32,1024]{2,1,0:T(8,128)S(1)}, u32[]{:S(2)}, u32[]{:S(2)}) collective-permute-start(f32[2,32,1024]{2,1,0:T(8,128)S(1)} %copy-done.4), channel_id=1, source_target_pairs={{0,96},{16,112},{32,0},{48,16},{64,32},{80,48},{96,64},{112,80},{1... | collective-permute-start | bytes 786440 | tf_op jit(solution)/shard_map/ppermute | solution.py:602
  108.9 7.2 %all-to-all-start.3 = ((f32[128,1,128]{2,1,0:T(1,128)}), f32[128,1,128]{2,1,0:T(1,128)S(1)}, u32[]{:S(2)}, u32[]{:S(2)}) async-start(f32[128,1,128]{2,1,0:T(1,128)} %bitcast.31), calls=%async_computation.3 | async-start | bytes 131072 | tf_op jit(solution)/shard_map/all_to_all | solution.py:782
  116.0 3.9 %collective-permute-done.21.refs_12_.refs_5_ = f32[2,32,1024]{2,1,0:T(8,128)S(1)} collective-permute-done((f32[2,32,1024]{2,1,0:T(8,128)S(1)}, f32[2,32,1024]{2,1,0:T(8,128)S(1)}, u32[]{:S(2)}, u32[]{:S(2)}) %collective-permute-start.21) | collective-permute-done | bytes 262176 | tf_op jit(solution)/shard_map/ppermute | solution.py:602
  119.9 3.8 %collective-permute-done.19.refs_10_.refs_3_ = f32[2,32,1024]{2,1,0:T(8,128)S(1)} collective-permute-done((f32[2,32,1024]{2,1,0:T(8,128)S(1)}, f32[2,32,1024]{2,1,0:T(8,128)S(1)}, u32[]{:S(2)}, u32[]{:S(2)}) %collective-permute-start.19) | collective-permute-done | bytes 262176 | tf_op jit(solution)/shard_map/ppermute | solution.py:602
  123.7 2.0 all-to-all-done.3
  126.7 9.5 %patterns.3 = (f32[2,256,256]{2,1,0:T(8,128)}, f32[4,2,256,256]{3,2,1,0:T(8,128)}, f32[16,9,8,256]{3,2,1,0:T(8,128)S(1)}, f32[16,9,8,256]{3,2,1,0:T(8,128)S(1)},...) custom-call(s32[4]{0:T(128)S(1)} %pad_add_fusion.refs_0_.where, ...), custom_call_target="tpu_custom_call" | custom-call | flops 6000000000 | bytes 14286872 | tf_op jit(solution)/shard_map/patterns/pallas_call | solution.py:582
  137.2 2.8 %collective-permute-done.23.refs_3_ = f32[4,2,32,256]{3,2,1,0:T(8,128)S(1)} collective-permute-done((f32[4,2,32,256]{3,2,1,0:T(8,128)S(1)}, f32[4,2,32,256]{3,2,1,0:T(8,128)S(1)}, u32[]{:S(2)}, u32[]{:S(2)}) %collective-permute-start.23) | collective-permute-done | bytes 262176 | tf_op jit(solution)/shard_map/ppermute | solution.py:606
  141.1 3.7 %all-to-all-start.4 = ((f32[16,9,8,256]{3,2,1,0:T(8,128)}), f32[16,9,8,256]{3,2,1,0:T(8,128)S(1)}, u32[]{:S(2)}, u32[]{:S(2)}) async-start(f32[16,9,8,256]{3,2,1,0:T(8,128)} %get-tuple-element.111), calls=%async_computation.4 | async-start | bytes 2359296 | tf_op jit(solution)/shard_map/all_to_all | solution.py:740
  145.3 1.7 collective-permute-start.25
  148.6 2.9 %collective-permute-done.24.refs_4_ = f32[2,2,32,256]{3,2,1,0:T(8,128)S(1)} collective-permute-done((f32[2,2,32,256]{3,2,1,0:T(8,128)S(1)}, f32[2,2,32,256]{3,2,1,0:T(8,128)S(1)}, u32[]{:S(2)}, u32[]{:S(2)}) %collective-permute-start.24) | collective-permute-done | bytes 131104 | tf_op jit(solution)/shard_map/ppermute | solution.py:602
  151.5 1.5 collective-permute-done.25.refs_5_
  154.0 1.4 place_kernel.3
  155.4 2.8 %collective-permute-start.30 = (f32[3,32,1024]{2,1,0:T(8,128)S(1)}, f32[3,32,1024]{2,1,0:T(8,128)S(1)}, u32[]{:S(2)}, u32[]{:S(2)}) collective-permute-start(f32[3,32,1024]{2,1,0:T(8,128)S(1)} %get-tuple-element.113.refs_4_), channel_id=1, source_target_pairs={{0,1},{1,2},{2,3},{3,4},{4,5},{5,6},{6,7},{7,8},{8,9},{9,10},{10,1... | collective-permute-start | bytes 1179656 | tf_op jit(solution)/shard_map/ppermute | solution.py:610
  158.2 1.3 collective-permute-start.31
  159.5 4.6 %all-to-all-done.4.refs_1_ = f32[16,9,8,256]{3,2,1,0:T(8,128)S(1)} async-done(((f32[16,9,8,256]{3,2,1,0:T(8,128)}), f32[16,9,8,256]{3,2,1,0:T(8,128)S(1)}, u32[]{:S(2)}, u32[]{:S(2)}) %all-to-all-start.4) | async-done | bytes 1179680 | tf_op jit(solution)/shard_map/all_to_all | solution.py:740
  166.2 1.3 collective-permute-start.28
  168.9 2.0 collective-permute-done.28.refs_2_
  171.9 1.8 share_kernel.3
  173.7 4.9 %all-to-all-start.5 = ((f32[16,10,8,256]{3,2,1,0:T(8,128)}), f32[16,10,8,256]{3,2,1,0:T(8,128)S(1)}, u32[]{:S(2)}, u32[]{:S(2)}) async-start(f32[16,10,8,256]{3,2,1,0:T(8,128)} %get-tuple-element.116), calls=%async_computation.5 | async-start | bytes 2621440 | tf_op jit(solution)/shard_map/all_to_all | solution.py:753
  178.6 1.5 direction_kernel.3
  181.4 4.5 %collective-permute-start.33 = (f32[2,2,32,256]{3,2,1,0:T(8,128)S(1)}, f32[2,2,32,256]{3,2,1,0:T(8,128)S(1)}, u32[]{:S(2)}, u32[]{:S(2)}) collective-permute-start(f32[2,2,32,256]{3,2,1,0:T(8,128)S(1)} %get-tuple-element.120), channel_id=1, source_target_pairs={{0,64},{16,80},{32,96},{48,112},{64,0},{80,16},{96,32},{112,48},{1... | collective-permute-start | bytes 393224 | tf_op jit(solution)/shard_map/ppermute | solution.py:602
  185.8 1.5 collective-permute-done.32.refs_1_.refs_3_
  187.3 2.8 %collective-permute-done.33.refs_2_.refs_4_ = f32[2,2,32,256]{3,2,1,0:T(8,128)S(1)} collective-permute-done((f32[2,2,32,256]{3,2,1,0:T(8,128)S(1)}, f32[2,2,32,256]{3,2,1,0:T(8,128)S(1)}, u32[]{:S(2)}, u32[]{:S(2)}) %collective-permute-start.33) | collective-permute-done | bytes 131104 | tf_op jit(solution)/shard_map/ppermute | solution.py:602
  190.9 2.7 %collective-permute-start.35 = (f32[4,2,32,256]{3,2,1,0:T(8,128)S(1)}, f32[4,2,32,256]{3,2,1,0:T(8,128)S(1)}, u32[]{:S(2)}, u32[]{:S(2)}) collective-permute-start(f32[4,2,32,256]{3,2,1,0:T(8,128)S(1)} %stack_kernel.3), channel_id=1, source_target_pairs={{0,16},{16,0},{32,48},{48,32},{64,80},{80,64},{96,112},{112,96},{1... | collective-permute-start | bytes 786440 | tf_op jit(solution)/shard_map/ppermute | solution.py:606
  194.8 1.6 patch_kernel.3
  196.8 1.8 collective-permute-start.39
  199.1 1.4 message_kernel.3
  201.8 9.1 %all-to-all-start.6 = ((f32[128,1,128]{2,1,0:T(1,128)}), f32[128,1,128]{2,1,0:T(1,128)S(1)}, u32[]{:S(2)}, u32[]{:S(2)}) async-start(f32[128,1,128]{2,1,0:T(1,128)} %bitcast.32), calls=%async_computation.6 | async-start | bytes 131072 | tf_op jit(solution)/shard_map/all_to_all | solution.py:782
  210.9 2.5 %collective-permute-done.37.refs_7_ = f32[2,32,1024]{2,1,0:T(8,128)} collective-permute-done((f32[2,32,1024]{2,1,0:T(8,128)S(1)}, f32[2,32,1024]{2,1,0:T(8,128)}, u32[]{:S(2)}, u32[]{:S(2)}) %collective-permute-start.37) | collective-permute-done | bytes 262176 | tf_op jit(solution)/shard_map/ppermute | solution.py:602
  213.4 7.1 %all-to-all-done.6 = f32[128,1,128]{2,1,0:T(1,128)S(1)} async-done(((f32[128,1,128]{2,1,0:T(1,128)}), f32[128,1,128]{2,1,0:T(1,128)S(1)}, u32[]{:S(2)}, u32[]{:S(2)}) %all-to-all-start.6) | async-done | bytes 65568 | tf_op jit(solution)/shard_map/all_to_all | solution.py:782
  220.6 1.6 combine_kernel.1.refs_2_
  223.0 3.0 %probe_kernel.1 = f32[4,2,256,256]{3,2,1,0:T(8,128)} custom-call(s32[4]{0:T(128)S(1)} %pad_add_fusion.refs_0_.where, f32[128,128]{1,0:T(8,128)S(1)} %bitcast.18, f32[4,2,256,256]{3,2,1,0:T(8,128)} %get-tuple-element.128.refs_2_, f32[8,128,256]{2,1,0:T(8,128)S(1)} %get-tuple-element.129.refs_3_, f32[8,128,256]{2,1,0:T(8,128)S(1)} %collective-permute-done.41.refs_4_), custom_call_target="tpu_custom_call" | custom-call | flops 1000000000 | bytes 6357008 | tf_op jit(solution)/shard_map/probe_kernel/pallas_call | solution.py:582
  226.1 3.2 %object_kernel.1 = f32[2,256,1024]{2,1,0:T(8,128)} custom-call(s32[4]{0:T(128)S(1)} %pad_add_fusion.refs_0_.where, f32[2,256,1024]{2,1,0:T(8,128)} %refs_1_.7, f32[4,2,32,1024]{3,2,1,0:T(8,128)S(1)} %combine_kernel.1.refs_2_, f32[4,2,32,1024]{3,2,1,0:T(8,128)S(1)} %collective-permute-done.40.refs_3_), custom_call_target="tpu_custom_call" | custom-call | bytes 6291472 | tf_op jit(solution)/shard_map/object_kernel/pallas_call | solution.py:582
  (98 shorter events, 33.4 us)
Async XLA Ops:
  0.6 13.8 %copy-start.9 = (bf16[2,256,256]{2,1,0:T(8,128)(2,1)S(1)}, bf16[2,256,256]{2,1,0:T(8,128)(2,1)}, u32[]{:S(2)}) copy-start(bf16[2,256,256]{2,1,0:T(8,128)(2,1)} %constant.43.clone.refs_3_) | copy-start | bytes 786436
  0.6 7.2 %copy-start.12 = (s32[1,2]{1,0:T(1,128)S(1)}, s32[1,2]{1,0:T(1,128)}, u32[]{:S(2)}) copy-start(s32[1,2]{1,0:T(1,128)} %refs_1_.6) | copy-start | bytes 28
  0.7 13.7 %copy-start.2 = (f32[1,256,256]{2,1,0:T(8,128)S(1)}, f32[1,256,256]{2,1,0:T(8,128)}, u32[]{:S(2)}) copy-start(f32[1,256,256]{2,1,0:T(8,128)} %param.6) | copy-start | bytes 786436
  2.5 16.4 %collective-permute-start = (f32[128,1024]{1,0:T(8,128)S(1)}, f32[128,1024]{1,0:T(8,128)S(1)}, u32[]{:S(2)}, u32[]{:S(2)}) collective-permute-start(f32[128,1024]{1,0:T(8,128)S(1)} %get-tuple-element.67), channel_id=1, source_target_pairs={{0,1},{1,2},{2,3},{3,4},{4,5},{5,6},{6,7},{7,8},{8,9},{9,10},{10,1... | collective-permute-start | bytes 1572872 | tf_op jit(solution)/shard_map/ppermute | solution.py:610
  6.5 14.4 %collective-permute-start.1 = (f32[128,1024]{1,0:T(8,128)S(1)}, f32[128,1024]{1,0:T(8,128)S(1)}, u32[]{:S(2)}, u32[]{:S(2)}) collective-permute-start(f32[128,1024]{1,0:T(8,128)S(1)} %get-tuple-element.68), channel_id=1, source_target_pairs={{1,0},{2,1},{3,2},{4,3},{5,4},{6,5},{7,6},{8,7},{9,8},{10,9},{11,1... | collective-permute-start | bytes 1572872 | tf_op jit(solution)/shard_map/ppermute | solution.py:614
  9.0 9.9 %all-to-all-start = ((s32[8,1,128]{2,1,0:T(1,128)}), s32[8,1,128]{2,1,0:T(1,128)S(1)}, u32[]{:S(2)}, u32[]{:S(2)}) async-start(s32[8,1,128]{2,1,0:T(1,128)} %bitcast.5), calls=%async_computation | async-start | bytes 8192 | tf_op jit(solution)/shard_map/all_to_all | solution.py:637
  16.9 16.4 %copy-start.15 = (f32[2,128,256]{2,1,0:T(8,128)}, f32[2,128,256]{2,1,0:T(8,128)S(1)}, u32[]{:S(2)}) copy-start(f32[2,128,256]{2,1,0:T(8,128)S(1)} %get-tuple-element.71.refs_6_.refs_5_) | copy-start | bytes 786436
  18.9 6.2 %copy-start.16 = (bf16[4,2,256,256]{3,2,1,0:T(8,128)(2,1)S(1)}, bf16[4,2,256,256]{3,2,1,0:T(8,128)(2,1)}, u32[]{:S(2)}) copy-start(bf16[4,2,256,256]{3,2,1,0:T(8,128)(2,1)} %constant.42.clone.refs_7_.refs_6_) | copy-start | bytes 3145732
  21.6 3.5 %collective-permute-start.2 = (f32[128,1024]{1,0:T(8,128)S(1)}, f32[128,1024]{1,0:T(8,128)S(1)}, u32[]{:S(2)}, u32[]{:S(2)}) collective-permute-start(f32[128,1024]{1,0:T(8,128)S(1)} %get-tuple-element.70), channel_id=1, source_target_pairs={{0,16},{16,0},{32,48},{48,32},{64,80},{80,64},{96,112},{112,96},{1... | collective-permute-start | bytes 1572872 | tf_op jit(solution)/shard_map/ppermute | solution.py:606
  25.1 1.6 copy-start.13
  33.2 4.5 %copy-start.10 = (f32[8,8,256]{2,1,0:T(8,128)}, f32[8,8,256]{2,1,0:T(8,128)S(1)}, u32[]{:S(2)}) copy-start(f32[8,8,256]{2,1,0:T(8,128)S(1)} %get-tuple-element.86.refs_6_) | copy-start | bytes 196612
  33.2 64.0 %copy-start = (f32[2,256,256]{2,1,0:T(8,128)}, f32[2,256,256]{2,1,0:T(8,128)S(1)}, u32[]{:S(2)}) copy-start(f32[2,256,256]{2,1,0:T(8,128)S(1)} %get-tuple-element.93.refs_7_.refs_3_) | copy-start | bytes 1572868
  33.3 3.3 %collective-permute-start.3 = (f32[16,9,8,256]{3,2,1,0:T(8,128)S(1)}, f32[16,9,8,256]{3,2,1,0:T(8,128)S(1)}, u32[]{:S(2)}, u32[]{:S(2)}) collective-permute-start(f32[16,9,8,256]{3,2,1,0:T(8,128)S(1)} %get-tuple-element.74), channel_id=1, source_target_pairs={{0,16},{16,0},{32,48},{48,32},{64,80},{80,64},{96,112},{112,96},{1... | collective-permute-start | bytes 3538952 | tf_op jit(solution)/shard_map/ppermute | solution.py:606
  33.7 2.8 %collective-permute-start.4 = (f32[4,2,32,256]{3,2,1,0:T(8,128)S(1)}, f32[4,2,32,256]{3,2,1,0:T(8,128)S(1)}, u32[]{:S(2)}, u32[]{:S(2)}) collective-permute-start(f32[4,2,32,256]{3,2,1,0:T(8,128)S(1)} %get-tuple-element.76), channel_id=1, source_target_pairs={{0,16},{16,0},{32,48},{48,32},{64,80},{80,64},{96,112},{112,96},{1... | collective-permute-start | bytes 786440 | tf_op jit(solution)/shard_map/ppermute | solution.py:606
  37.8 27.3 %all-to-all-start.1 = ((f32[16,9,8,256]{3,2,1,0:T(8,128)}), f32[16,9,8,256]{3,2,1,0:T(8,128)S(1)}, u32[]{:S(2)}, u32[]{:S(2)}) async-start(f32[16,9,8,256]{3,2,1,0:T(8,128)} %get-tuple-element.82), calls=%async_computation.1 | async-start | bytes 2359296 | tf_op jit(solution)/shard_map/all_to_all | solution.py:740
  47.1 6.0 %collective-permute-start.5 = (f32[2,2,32,256]{3,2,1,0:T(8,128)S(1)}, f32[2,2,32,256]{3,2,1,0:T(8,128)S(1)}, u32[]{:S(2)}, u32[]{:S(2)}) collective-permute-start(f32[2,2,32,256]{3,2,1,0:T(8,128)S(1)} %get-tuple-element.78), channel_id=1, source_target_pairs={{0,32},{16,48},{32,64},{48,80},{64,96},{80,112},{96,0},{112,16},{1... | collective-permute-start | bytes 393224 | tf_op jit(solution)/shard_map/ppermute | solution.py:602
  48.4 8.3 %collective-permute-start.6 = (f32[2,2,32,256]{3,2,1,0:T(8,128)S(1)}, f32[2,2,32,256]{3,2,1,0:T(8,128)S(1)}, u32[]{:S(2)}, u32[]{:S(2)}) collective-permute-start(f32[2,2,32,256]{3,2,1,0:T(8,128)S(1)} %get-tuple-element.79), channel_id=1, source_target_pairs={{0,64},{16,80},{32,96},{48,112},{64,0},{80,16},{96,32},{112,48},{1... | collective-permute-start | bytes 393224 | tf_op jit(solution)/shard_map/ppermute | solution.py:602
  51.1 5.7 %collective-permute-start.7 = (f32[2,2,32,256]{3,2,1,0:T(8,128)S(1)}, f32[2,2,32,256]{3,2,1,0:T(8,128)S(1)}, u32[]{:S(2)}, u32[]{:S(2)}) collective-permute-start(f32[2,2,32,256]{3,2,1,0:T(8,128)S(1)} %get-tuple-element.80), channel_id=1, source_target_pairs={{0,96},{16,112},{32,0},{48,16},{64,32},{80,48},{96,64},{112,80},{1... | collective-permute-start | bytes 393224 | tf_op jit(solution)/shard_map/ppermute | solution.py:602
  53.0 21.5 %copy-start.11 = (f32[8,8,256]{2,1,0:T(8,128)S(1)}, f32[8,8,256]{2,1,0:T(8,128)}, u32[]{:S(2)}) copy-start(f32[8,8,256]{2,1,0:T(8,128)} %copy-done.10) | copy-start | bytes 196612
  58.2 11.8 %collective-permute-start.11 = (f32[3,32,1024]{2,1,0:T(8,128)S(1)}, f32[3,32,1024]{2,1,0:T(8,128)S(1)}, u32[]{:S(2)}, u32[]{:S(2)}) collective-permute-start(f32[3,32,1024]{2,1,0:T(8,128)S(1)} %get-tuple-element.84.refs_4_), channel_id=1, source_target_pairs={{0,1},{1,2},{2,3},{3,4},{4,5},{5,6},{6,7},{7,8},{8,9},{9,10},{10,1... | collective-permute-start | bytes 1179656 | tf_op jit(solution)/shard_map/ppermute | solution.py:610
  61.2 10.4 %collective-permute-start.12 = (f32[3,32,1024]{2,1,0:T(8,128)S(1)}, f32[3,32,1024]{2,1,0:T(8,128)S(1)}, u32[]{:S(2)}, u32[]{:S(2)}) collective-permute-start(f32[3,32,1024]{2,1,0:T(8,128)S(1)} %get-tuple-element.85.refs_3_), channel_id=1, source_target_pairs={{1,0},{2,1},{3,2},{4,3},{5,4},{6,5},{7,6},{8,7},{9,8},{10,9},{11,1... | collective-permute-start | bytes 1179656 | tf_op jit(solution)/shard_map/ppermute | solution.py:614
  66.2 5.3 %collective-permute-start.10 = (f32[9,8,256]{2,1,0:T(8,128)S(1)}, f32[9,8,256]{2,1,0:T(8,128)S(1)}, u32[]{:S(2)}, u32[]{:S(2)}) collective-permute-start(f32[9,8,256]{2,1,0:T(8,128)S(1)} %get-tuple-element.83.refs_0_), channel_id=1, source_target_pairs={{0,96},{16,112},{32,0},{48,16},{64,32},{80,48},{96,64},{112,80},{1... | collective-permute-start | bytes 221192 | tf_op jit(solution)/shard_map/ppermute | solution.py:602
  69.0 4.8 %collective-permute-start.9 = (f32[9,8,256]{2,1,0:T(8,128)S(1)}, f32[9,8,256]{2,1,0:T(8,128)S(1)}, u32[]{:S(2)}, u32[]{:S(2)}) collective-permute-start(f32[9,8,256]{2,1,0:T(8,128)S(1)} %get-tuple-element.83.refs_0_), channel_id=1, source_target_pairs={{0,64},{16,80},{32,96},{48,112},{64,0},{80,16},{96,32},{112,48},{1... | collective-permute-start | bytes 221192 | tf_op jit(solution)/shard_map/ppermute | solution.py:602
  69.4 5.1 %collective-permute-start.8 = (f32[9,8,256]{2,1,0:T(8,128)S(1)}, f32[9,8,256]{2,1,0:T(8,128)S(1)}, u32[]{:S(2)}, u32[]{:S(2)}) collective-permute-start(f32[9,8,256]{2,1,0:T(8,128)S(1)} %get-tuple-element.83.refs_0_), channel_id=1, source_target_pairs={{0,32},{16,48},{32,64},{48,80},{64,96},{80,112},{96,0},{112,16},{1... | collective-permute-start | bytes 221192 | tf_op jit(solution)/shard_map/ppermute | solution.py:602
  76.3 24.2 %all-to-all-start.2 = ((f32[16,10,8,256]{3,2,1,0:T(8,128)}), f32[16,10,8,256]{3,2,1,0:T(8,128)S(1)}, u32[]{:S(2)}, u32[]{:S(2)}) async-start(f32[16,10,8,256]{3,2,1,0:T(8,128)} %get-tuple-element.87), calls=%async_computation.2 | async-start | bytes 2621440 | tf_op jit(solution)/shard_map/all_to_all | solution.py:753
  83.6 5.2 %collective-permute-start.13 = (f32[2,2,32,256]{3,2,1,0:T(8,128)S(1)}, f32[2,2,32,256]{3,2,1,0:T(8,128)S(1)}, u32[]{:S(2)}, u32[]{:S(2)}) collective-permute-start(f32[2,2,32,256]{3,2,1,0:T(8,128)S(1)} %get-tuple-element.90), channel_id=1, source_target_pairs={{0,32},{16,48},{32,64},{48,80},{64,96},{80,112},{96,0},{112,16},{1... | collective-permute-start | bytes 393224 | tf_op jit(solution)/shard_map/ppermute | solution.py:602
  84.7 7.0 %collective-permute-start.14 = (f32[2,2,32,256]{3,2,1,0:T(8,128)S(1)}, f32[2,2,32,256]{3,2,1,0:T(8,128)S(1)}, u32[]{:S(2)}, u32[]{:S(2)}) collective-permute-start(f32[2,2,32,256]{3,2,1,0:T(8,128)S(1)} %get-tuple-element.91), channel_id=1, source_target_pairs={{0,64},{16,80},{32,96},{48,112},{64,0},{80,16},{96,32},{112,48},{1... | collective-permute-start | bytes 393224 | tf_op jit(solution)/shard_map/ppermute | solution.py:602
  87.6 4.1 %collective-permute-start.15 = (f32[2,2,32,256]{3,2,1,0:T(8,128)S(1)}, f32[2,2,32,256]{3,2,1,0:T(8,128)S(1)}, u32[]{:S(2)}, u32[]{:S(2)}) collective-permute-start(f32[2,2,32,256]{3,2,1,0:T(8,128)S(1)} %get-tuple-element.92), channel_id=1, source_target_pairs={{0,96},{16,112},{32,0},{48,16},{64,32},{80,48},{96,64},{112,80},{1... | collective-permute-start | bytes 393224 | tf_op jit(solution)/shard_map/ppermute | solution.py:602
  91.7 5.6 %collective-permute-start.16 = (f32[4,2,32,256]{3,2,1,0:T(8,128)S(1)}, f32[4,2,32,256]{3,2,1,0:T(8,128)S(1)}, u32[]{:S(2)}, u32[]{:S(2)}) collective-permute-start(f32[4,2,32,256]{3,2,1,0:T(8,128)S(1)} %stack_kernel.2), channel_id=1, source_target_pairs={{0,16},{16,0},{32,48},{48,32},{64,80},{80,64},{96,112},{112,96},{1... | collective-permute-start | bytes 786440 | tf_op jit(solution)/shard_map/ppermute | solution.py:606
  99.0 6.5 %copy-start.4 = (f32[2,32,1024]{2,1,0:T(8,128)S(1)}, f32[2,32,1024]{2,1,0:T(8,128)}, u32[]{:S(2)}) copy-start(f32[2,32,1024]{2,1,0:T(8,128)} %copy-done.3) | copy-start | bytes 786436
  99.0 1.5 collective-permute-start.17
  103.0 22.8 %collective-permute-start.18 = (f32[8,128,256]{2,1,0:T(8,128)}, f32[8,128,256]{2,1,0:T(8,128)S(1)}, u32[]{:S(2)}, u32[]{:S(2)}) collective-permute-start(f32[8,128,256]{2,1,0:T(8,128)} %get-tuple-element.99.refs_8_), channel_id=1, source_target_pairs={{0,16},{16,0},{32,48},{48,32},{64,80},{80,64},{96,112},{112,96},{1... | collective-permute-start | bytes 3145736 | tf_op jit(solution)/shard_map/ppermute | solution.py:606
  105.5 14.4 %collective-permute-start.21 = (f32[2,32,1024]{2,1,0:T(8,128)S(1)}, f32[2,32,1024]{2,1,0:T(8,128)S(1)}, u32[]{:S(2)}, u32[]{:S(2)}) collective-permute-start(f32[2,32,1024]{2,1,0:T(8,128)S(1)} %copy-done.4), channel_id=1, source_target_pairs={{0,96},{16,112},{32,0},{48,16},{64,32},{80,48},{96,64},{112,80},{1... | collective-permute-start | bytes 786440 | tf_op jit(solution)/shard_map/ppermute | solution.py:602
  108.3 11.6 %collective-permute-start.20 = (f32[2,32,1024]{2,1,0:T(8,128)S(1)}, f32[2,32,1024]{2,1,0:T(8,128)S(1)}, u32[]{:S(2)}, u32[]{:S(2)}) collective-permute-start(f32[2,32,1024]{2,1,0:T(8,128)S(1)} %copy-done.4), channel_id=1, source_target_pairs={{0,64},{16,80},{32,96},{48,112},{64,0},{80,16},{96,32},{112,48},{1... | collective-permute-start | bytes 786440 | tf_op jit(solution)/shard_map/ppermute | solution.py:602
  108.4 15.4 %collective-permute-start.19 = (f32[2,32,1024]{2,1,0:T(8,128)S(1)}, f32[2,32,1024]{2,1,0:T(8,128)S(1)}, u32[]{:S(2)}, u32[]{:S(2)}) collective-permute-start(f32[2,32,1024]{2,1,0:T(8,128)S(1)} %copy-done.4), channel_id=1, source_target_pairs={{0,32},{16,48},{32,64},{48,80},{64,96},{80,112},{96,0},{112,16},{1... | collective-permute-start | bytes 786440 | tf_op jit(solution)/shard_map/ppermute | solution.py:602
  108.9 16.9 %all-to-all-start.3 = ((f32[128,1,128]{2,1,0:T(1,128)}), f32[128,1,128]{2,1,0:T(1,128)S(1)}, u32[]{:S(2)}, u32[]{:S(2)}) async-start(f32[128,1,128]{2,1,0:T(1,128)} %bitcast.31), calls=%async_computation.3 | async-start | bytes 131072 | tf_op jit(solution)/shard_map/all_to_all | solution.py:782
  119.9 16.3 %copy-start.5 = (f32[2,32,1024]{2,1,0:T(8,128)}, f32[2,32,1024]{2,1,0:T(8,128)S(1)}, u32[]{:S(2)}) copy-start(f32[2,32,1024]{2,1,0:T(8,128)S(1)} %collective-permute-done.21.refs_12_.refs_5_) | copy-start | bytes 786436
  119.9 16.3 %copy-start.6 = (f32[2,32,1024]{2,1,0:T(8,128)}, f32[2,32,1024]{2,1,0:T(8,128)S(1)}, u32[]{:S(2)}) copy-start(f32[2,32,1024]{2,1,0:T(8,128)S(1)} %collective-permute-done.20.refs_11_.refs_4_) | copy-start | bytes 786436
  123.7 12.5 %copy-start.7 = (f32[2,32,1024]{2,1,0:T(8,128)}, f32[2,32,1024]{2,1,0:T(8,128)S(1)}, u32[]{:S(2)}) copy-start(f32[2,32,1024]{2,1,0:T(8,128)S(1)} %collective-permute-done.19.refs_10_.refs_3_) | copy-start | bytes 786436
  136.2 3.7 %collective-permute-start.22 = (f32[16,9,8,256]{3,2,1,0:T(8,128)S(1)}, f32[16,9,8,256]{3,2,1,0:T(8,128)S(1)}, u32[]{:S(2)}, u32[]{:S(2)}) collective-permute-start(f32[16,9,8,256]{3,2,1,0:T(8,128)S(1)} %get-tuple-element.103), channel_id=1, source_target_pairs={{0,16},{16,0},{32,48},{48,32},{64,80},{80,64},{96,112},{112,96},{1... | collective-permute-start | bytes 3538952 | tf_op jit(solution)/shard_map/ppermute | solution.py:606
  137.1 2.8 %collective-permute-start.23 = (f32[4,2,32,256]{3,2,1,0:T(8,128)S(1)}, f32[4,2,32,256]{3,2,1,0:T(8,128)S(1)}, u32[]{:S(2)}, u32[]{:S(2)}) collective-permute-start(f32[4,2,32,256]{3,2,1,0:T(8,128)S(1)} %get-tuple-element.105), channel_id=1, source_target_pairs={{0,16},{16,0},{32,48},{48,32},{64,80},{80,64},{96,112},{112,96},{1... | collective-permute-start | bytes 786440 | tf_op jit(solution)/shard_map/ppermute | solution.py:606
  141.1 23.0 %all-to-all-start.4 = ((f32[16,9,8,256]{3,2,1,0:T(8,128)}), f32[16,9,8,256]{3,2,1,0:T(8,128)S(1)}, u32[]{:S(2)}, u32[]{:S(2)}) async-start(f32[16,9,8,256]{3,2,1,0:T(8,128)} %get-tuple-element.111), calls=%async_computation.4 | async-start | bytes 2359296 | tf_op jit(solution)/shard_map/all_to_all | solution.py:740
  144.8 6.7 %collective-permute-start.24 = (f32[2,2,32,256]{3,2,1,0:T(8,128)S(1)}, f32[2,2,32,256]{3,2,1,0:T(8,128)S(1)}, u32[]{:S(2)}, u32[]{:S(2)}) collective-permute-start(f32[2,2,32,256]{3,2,1,0:T(8,128)S(1)} %get-tuple-element.107), channel_id=1, source_target_pairs={{0,32},{16,48},{32,64},{48,80},{64,96},{80,112},{96,0},{112,16},{1... | collective-permute-start | bytes 393224 | tf_op jit(solution)/shard_map/ppermute | solution.py:602
  145.3 7.8 %collective-permute-start.25 = (f32[2,2,32,256]{3,2,1,0:T(8,128)S(1)}, f32[2,2,32,256]{3,2,1,0:T(8,128)S(1)}, u32[]{:S(2)}, u32[]{:S(2)}) collective-permute-start(f32[2,2,32,256]{3,2,1,0:T(8,128)S(1)} %get-tuple-element.108), channel_id=1, source_target_pairs={{0,64},{16,80},{32,96},{48,112},{64,0},{80,16},{96,32},{112,48},{1... | collective-permute-start | bytes 393224 | tf_op jit(solution)/shard_map/ppermute | solution.py:602
  146.9 7.1 %collective-permute-start.26 = (f32[2,2,32,256]{3,2,1,0:T(8,128)S(1)}, f32[2,2,32,256]{3,2,1,0:T(8,128)S(1)}, u32[]{:S(2)}, u32[]{:S(2)}) collective-permute-start(f32[2,2,32,256]{3,2,1,0:T(8,128)S(1)} %get-tuple-element.109), channel_id=1, source_target_pairs={{0,96},{16,112},{32,0},{48,16},{64,32},{80,48},{96,64},{112,80},{1... | collective-permute-start | bytes 393224 | tf_op jit(solution)/shard_map/ppermute | solution.py:602
  155.4 12.3 %collective-permute-start.30 = (f32[3,32,1024]{2,1,0:T(8,128)S(1)}, f32[3,32,1024]{2,1,0:T(8,128)S(1)}, u32[]{:S(2)}, u32[]{:S(2)}) collective-permute-start(f32[3,32,1024]{2,1,0:T(8,128)S(1)} %get-tuple-element.113.refs_4_), channel_id=1, source_target_pairs={{0,1},{1,2},{2,3},{3,4},{4,5},{5,6},{6,7},{7,8},{8,9},{9,10},{10,1... | collective-permute-start | bytes 1179656 | tf_op jit(solution)/shard_map/ppermute | solution.py:610
  158.2 10.4 %collective-permute-start.31 = (f32[3,32,1024]{2,1,0:T(8,128)S(1)}, f32[3,32,1024]{2,1,0:T(8,128)S(1)}, u32[]{:S(2)}, u32[]{:S(2)}) collective-permute-start(f32[3,32,1024]{2,1,0:T(8,128)S(1)} %get-tuple-element.114.refs_3_), channel_id=1, source_target_pairs={{1,0},{2,1},{3,2},{4,3},{5,4},{6,5},{7,6},{8,7},{9,8},{10,9},{11,1... | collective-permute-start | bytes 1179656 | tf_op jit(solution)/shard_map/ppermute | solution.py:614
  165.3 3.6 %collective-permute-start.29 = (f32[9,8,256]{2,1,0:T(8,128)S(1)}, f32[9,8,256]{2,1,0:T(8,128)S(1)}, u32[]{:S(2)}, u32[]{:S(2)}) collective-permute-start(f32[9,8,256]{2,1,0:T(8,128)S(1)} %get-tuple-element.112.refs_0_), channel_id=1, source_target_pairs={{0,96},{16,112},{32,0},{48,16},{64,32},{80,48},{96,64},{112,80},{1... | collective-permute-start | bytes 221192 | tf_op jit(solution)/shard_map/ppermute | solution.py:602
  166.2 4.7 %collective-permute-start.28 = (f32[9,8,256]{2,1,0:T(8,128)S(1)}, f32[9,8,256]{2,1,0:T(8,128)S(1)}, u32[]{:S(2)}, u32[]{:S(2)}) collective-permute-start(f32[9,8,256]{2,1,0:T(8,128)S(1)} %get-tuple-element.112.refs_0_), channel_id=1, source_target_pairs={{0,64},{16,80},{32,96},{48,112},{64,0},{80,16},{96,32},{112,48},{1... | collective-permute-start | bytes 221192 | tf_op jit(solution)/shard_map/ppermute | solution.py:602
  167.5 4.4 %collective-permute-start.27 = (f32[9,8,256]{2,1,0:T(8,128)S(1)}, f32[9,8,256]{2,1,0:T(8,128)S(1)}, u32[]{:S(2)}, u32[]{:S(2)}) collective-permute-start(f32[9,8,256]{2,1,0:T(8,128)S(1)} %get-tuple-element.112.refs_0_), channel_id=1, source_target_pairs={{0,32},{16,48},{32,64},{48,80},{64,96},{80,112},{96,0},{112,16},{1... | collective-permute-start | bytes 221192 | tf_op jit(solution)/shard_map/ppermute | solution.py:602
  173.7 25.4 %all-to-all-start.5 = ((f32[16,10,8,256]{3,2,1,0:T(8,128)}), f32[16,10,8,256]{3,2,1,0:T(8,128)S(1)}, u32[]{:S(2)}, u32[]{:S(2)}) async-start(f32[16,10,8,256]{3,2,1,0:T(8,128)} %get-tuple-element.116), calls=%async_computation.5 | async-start | bytes 2621440 | tf_op jit(solution)/shard_map/all_to_all | solution.py:753
  178.6 16.2 %copy-start.1 = (f32[2,256,256]{2,1,0:T(8,128)S(1)}, f32[2,256,256]{2,1,0:T(8,128)}, u32[]{:S(2)}) copy-start(f32[2,256,256]{2,1,0:T(8,128)} %get-tuple-element.122.refs_7_) | copy-start | bytes 1572868
  180.1 20.4 %copy-start.8 = (f32[2,32,1024]{2,1,0:T(8,128)}, f32[2,32,1024]{2,1,0:T(8,128)S(1)}, u32[]{:S(2)}) copy-start(f32[2,32,1024]{2,1,0:T(8,128)S(1)} %get-tuple-element.127.refs_6_) | copy-start | bytes 786436
  180.2 7.2 %collective-permute-start.32 = (f32[2,2,32,256]{3,2,1,0:T(8,128)S(1)}, f32[2,2,32,256]{3,2,1,0:T(8,128)S(1)}, u32[]{:S(2)}, u32[]{:S(2)}) collective-permute-start(f32[2,2,32,256]{3,2,1,0:T(8,128)S(1)} %get-tuple-element.119), channel_id=1, source_target_pairs={{0,32},{16,48},{32,64},{48,80},{64,96},{80,112},{96,0},{112,16},{1... | collective-permute-start | bytes 393224 | tf_op jit(solution)/shard_map/ppermute | solution.py:602
  181.4 8.8 %collective-permute-start.33 = (f32[2,2,32,256]{3,2,1,0:T(8,128)S(1)}, f32[2,2,32,256]{3,2,1,0:T(8,128)S(1)}, u32[]{:S(2)}, u32[]{:S(2)}) collective-permute-start(f32[2,2,32,256]{3,2,1,0:T(8,128)S(1)} %get-tuple-element.120), channel_id=1, source_target_pairs={{0,64},{16,80},{32,96},{48,112},{64,0},{80,16},{96,32},{112,48},{1... | collective-permute-start | bytes 393224 | tf_op jit(solution)/shard_map/ppermute | solution.py:602
  185.8 5.0 %collective-permute-start.34 = (f32[2,2,32,256]{3,2,1,0:T(8,128)S(1)}, f32[2,2,32,256]{3,2,1,0:T(8,128)S(1)}, u32[]{:S(2)}, u32[]{:S(2)}) collective-permute-start(f32[2,2,32,256]{3,2,1,0:T(8,128)S(1)} %get-tuple-element.121), channel_id=1, source_target_pairs={{0,96},{16,112},{32,0},{48,16},{64,32},{80,48},{96,64},{112,80},{1... | collective-permute-start | bytes 393224 | tf_op jit(solution)/shard_map/ppermute | solution.py:602
  190.9 3.9 %collective-permute-start.35 = (f32[4,2,32,256]{3,2,1,0:T(8,128)S(1)}, f32[4,2,32,256]{3,2,1,0:T(8,128)S(1)}, u32[]{:S(2)}, u32[]{:S(2)}) collective-permute-start(f32[4,2,32,256]{3,2,1,0:T(8,128)S(1)} %stack_kernel.3), channel_id=1, source_target_pairs={{0,16},{16,0},{32,48},{48,32},{64,80},{80,64},{96,112},{112,96},{1... | collective-permute-start | bytes 786440 | tf_op jit(solution)/shard_map/ppermute | solution.py:606
  196.4 2.7 %collective-permute-start.36 = (f32[2,128,256]{2,1,0:T(8,128)S(1)}, f32[2,128,256]{2,1,0:T(8,128)S(1)}, u32[]{:S(2)}, u32[]{:S(2)}) collective-permute-start(f32[2,128,256]{2,1,0:T(8,128)S(1)} %get-tuple-element.124), channel_id=1, source_target_pairs={{0,16},{16,0},{32,48},{48,32},{64,80},{80,64},{96,112},{112,96},{1... | collective-permute-start | bytes 786440 | tf_op jit(solution)/shard_map/ppermute | solution.py:606
  196.8 14.1 %collective-permute-start.39 = (f32[2,32,1024]{2,1,0:T(8,128)S(1)}, f32[2,32,1024]{2,1,0:T(8,128)}, u32[]{:S(2)}, u32[]{:S(2)}) collective-permute-start(f32[2,32,1024]{2,1,0:T(8,128)S(1)} %get-tuple-element.127.refs_6_), channel_id=1, source_target_pairs={{0,96},{16,112},{32,0},{48,16},{64,32},{80,48},{96,64},{112,80},{1... | collective-permute-start | bytes 786440 | tf_op jit(solution)/shard_map/ppermute | solution.py:602
  198.5 12.3 %collective-permute-start.38 = (f32[2,32,1024]{2,1,0:T(8,128)S(1)}, f32[2,32,1024]{2,1,0:T(8,128)}, u32[]{:S(2)}, u32[]{:S(2)}) collective-permute-start(f32[2,32,1024]{2,1,0:T(8,128)S(1)} %get-tuple-element.127.refs_6_), channel_id=1, source_target_pairs={{0,64},{16,80},{32,96},{48,112},{64,0},{80,16},{96,32},{112,48},{1... | collective-permute-start | bytes 786440 | tf_op jit(solution)/shard_map/ppermute | solution.py:602
  198.5 14.9 %collective-permute-start.37 = (f32[2,32,1024]{2,1,0:T(8,128)S(1)}, f32[2,32,1024]{2,1,0:T(8,128)}, u32[]{:S(2)}, u32[]{:S(2)}) collective-permute-start(f32[2,32,1024]{2,1,0:T(8,128)S(1)} %get-tuple-element.127.refs_6_), channel_id=1, source_target_pairs={{0,32},{16,48},{32,64},{48,80},{64,96},{80,112},{96,0},{112,16},{1... | collective-permute-start | bytes 786440 | tf_op jit(solution)/shard_map/ppermute | solution.py:602
  200.6 22.5 %collective-permute-start.41 = (f32[8,128,256]{2,1,0:T(8,128)S(1)}, f32[8,128,256]{2,1,0:T(8,128)S(1)}, u32[]{:S(2)}, u32[]{:S(2)}) collective-permute-start(f32[8,128,256]{2,1,0:T(8,128)S(1)} %get-tuple-element.129.refs_3_), channel_id=1, source_target_pairs={{0,16},{16,0},{32,48},{48,32},{64,80},{80,64},{96,112},{112,96},{1... | collective-permute-start | bytes 3145736 | tf_op jit(solution)/shard_map/ppermute | solution.py:606
  201.8 18.8 %all-to-all-start.6 = ((f32[128,1,128]{2,1,0:T(1,128)}), f32[128,1,128]{2,1,0:T(1,128)S(1)}, u32[]{:S(2)}, u32[]{:S(2)}) async-start(f32[128,1,128]{2,1,0:T(1,128)} %bitcast.32), calls=%async_computation.6 | async-start | bytes 131072 | tf_op jit(solution)/shard_map/all_to_all | solution.py:782
  222.2 3.9 %collective-permute-start.40 = (f32[4,2,32,1024]{3,2,1,0:T(8,128)S(1)}, f32[4,2,32,1024]{3,2,1,0:T(8,128)S(1)}, u32[]{:S(2)}, u32[]{:S(2)}) collective-permute-start(f32[4,2,32,1024]{3,2,1,0:T(8,128)S(1)} %combine_kernel.1.refs_2_), channel_id=1, source_target_pairs={{0,16},{16,0},{32,48},{48,32},{64,80},{80,64},{96,112},{112,96},{1... | collective-permute-start | bytes 3145736 | tf_op jit(solution)/shard_map/ppermute | solution.py:606
  (3 other events, 2.5 us)

commit v5 on v4

--- a/solution.py
+++ b/solution.py
@@ -201,8 +201,7 @@
 
     def forward(k):
         if not first:
-            for index in (4, 8, 9):
-                ready(index, k)
+            ready(4, k)
             for part in range(2):
                 moved = probe_step * joined(first_core, dmine, doth, 2 * k + part)
                 probe_now[k, part] = probe[k, part] + moved
@@ -336,10 +335,12 @@
     total_n = jnp.zeros((16, 1024), F32)
     for at, (own, came) in enumerate(((low, above), (high, below))):
         rows = slice(32 * at, 32 * at + 32)
-        light = own[2] + came[2]
+        inside = where[2] != 15 * at
+        total = own[...] + jnp.where(inside, came[...], 0.0)
+        light = total[2]
         scale = 1.0 / (light + RIDGE)
-        real = (own[0] + came[0]) * scale
-        imag = (own[1] + came[1]) * scale
+        real = total[0] * scale
+        imag = total[1] * scale
         wide[0, rows, :1024] = real
         wide[1, rows, :1024] = imag
         inner = slice(16, 32) if at == 0 else slice(0, 16)
@@ -607,11 +608,11 @@
 
 
 def up(value):
-    return lax.ppermute(value, "tile", [(i, i + 1) for i in range(15)])
+    return lax.ppermute(value, "tile", [(i, (i + 1) % 16) for i in range(16)])
 
 
 def down(value):
-    return lax.ppermute(value, "tile", [(i + 1, i) for i in range(15)])
+    return lax.ppermute(value, "tile", [((i + 1) % 16, i) for i in range(16)])
 
 
 def spread(value, axes, count):
@@ -704,7 +705,7 @@
                 ),
                 (0, 1),
                 scratch,
-                hbm_in={3: 1, 7: 1, 6: 1, 4: 4, 8: 4, 9: 4, 5: 1},
+                hbm_in={3: 1, 7: 1, 6: 1, 4: 4, 5: 1},
                 staged_in=True,
                 lazy=True,
                 hbm_out={0: 1, 1: 4},

time: 230 us -> 223 us (0.970)
  waiting for transfers between devices: 68.1 us -> 63.8 us
  starting transfers between devices: 104 us -> 101 us
    ppermute x24, waiting for transfers between devices: 34.7 us -> 28.3 us  [along_y(): return lax.ppermute(value, 'pat', [(i, (i + 2 * s) % 8) for i in range(8)])]
    ppermute x6, waiting for transfers between devices: 4.62 us -> 8.54 us  [the longest x3 8.53 us: up(): return lax.ppermute(value, 'tile', [(i, (i + 1) % 16) for i in range(16)])]
    ppermute x6, starting transfers between devices: 13.6 us -> 16.6 us  [the longest x3 12.7 us: down(): return lax.ppermute(value, 'tile', [((i + 1) % 16, i) for i in range(16)])]
    all_to_all x2, starting transfers between devices: 13 us -> 9.96 us  [body(): shares = lax.all_to_all(chip, 'tile', 0, 0)]
    ppermute x12, starting transfers between devices: 15.9 us -> 18.9 us  [partner(): return lax.ppermute(value, 'pat', [(i, i ^ 1) for i in range(8)])]
    ppermute x24, starting transfers between devices: 29.4 us -> 27 us  [along_y(): return lax.ppermute(value, 'pat', [(i, (i + 2 * s) % 8) for i in range(8)])]
  transfers between devices with their start and end apart: 49 -> 49, of which waited for: 33 -> 28; matrix products, arithmetic and copies ran while one was open for 0% -> 0% of each run, Pallas kernels for 10% -> 10%
where the time goes in v5:
time: 223 us; the launch traced here: 222 us
  starting transfers between devices  101 us (45%)
  waiting for transfers between devices  63.8 us (29%)
  Pallas kernels  52.5 us (24%)
  local copies, waits for them, and re-layouts  3.15 us (1%)
    pallas_call x26, Pallas kernels, call(): pl.pallas_call(run, out_shape=shapes, in_specs=[space(i, smem_in, hbm_in)...  50.8 us
    ppermute x24, waiting for transfers between devices, along_y(): return lax.ppermute(value, 'pat', [(i, (i + 2 * s) % 8) for i in range(8)])  28.3 us
    ppermute x24, starting transfers between devices, along_y(): return lax.ppermute(value, 'pat', [(i, (i + 2 * s) % 8) for i in range(8)])  27 us
    ppermute x12, starting transfers between devices, partner(): return lax.ppermute(value, 'pat', [(i, i ^ 1) for i in range(8)])  18.9 us
    all_to_all x2, starting transfers between devices, body(): messages.append(lax.all_to_all(message, BOTH, 0, 0))  14.9 us
    ppermute x3, starting transfers between devices, down(): return lax.ppermute(value, 'tile', [((i + 1) % 16, i) for i in range(16)])  12.7 us
    ppermute x12, waiting for transfers between devices, partner(): return lax.ppermute(value, 'pat', [(i, i ^ 1) for i in range(8)])  10.5 us
    all_to_all x2, starting transfers between devices, body(): shares = lax.all_to_all(chip, 'tile', 0, 0)  9.96 us
  transfers between devices with their start and end apart: 49, of which 28 were waited for; matrix products, arithmetic and copies ran while one was open for 0% of the time, Pallas kernels for 10%

profile of v5, /device:TPU:1, one launch (start us, length us, event | category | flops | bytes accessed | tf_op | source)
XLA Modules:
  0.0 222.3 jit_solution(13379239207832806619)
XLA Ops:
  0.8 1.8 shard_map.77
  2.5 2.1 collective-permute-start
  4.6 4.8 %collective-permute-start.1 = (f32[128,1024]{1,0:T(8,128)S(1)}, f32[128,1024]{1,0:T(8,128)S(1)}, u32[]{:S(2)}, u32[]{:S(2)}) collective-permute-start(f32[128,1024]{1,0:T(8,128)S(1)} %get-tuple-element.68), channel_id=1, source_target_pairs={{1,0},{2,1},{3,2},{4,3},{5,4},{6,5},{7,6},{8,7},{9,8},{10,9},{11,1... | collective-permute-start | bytes 1572872 | tf_op jit(solution)/shard_map/ppermute | solution.py:615
  10.6 5.4 %all-to-all-start = ((s32[8,1,128]{2,1,0:T(1,128)}), s32[8,1,128]{2,1,0:T(1,128)S(1)}, u32[]{:S(2)}, u32[]{:S(2)}) async-start(s32[8,1,128]{2,1,0:T(1,128)} %bitcast.5), calls=%async_computation | async-start | bytes 8192 | tf_op jit(solution)/shard_map/all_to_all | solution.py:638
  16.0 2.5 %prepare_kernel.1 = (f32[2,128,256]{2,1,0:T(8,128)S(1)}, f32[2,256,256]{2,1,0:T(8,128)S(1)}) custom-call(s32[4]{0:T(128)S(1)} %pad_add_fusion.refs_0_.where, s32[1,2]{1,0:T(1,128)S(1)} %copy-done.12, f32[256,256]{1,0:T(8,128)S(1)} %bitcast.28, bf16[2,256,256]{2,1,0:T(8,128)(2,1)S(1)} %copy-done.9, f32[2,256,1024]{2,1,0:T(8,128)} %refs_1_.7), custom_call_target="tpu_custom_call" | custom-call | bytes 3670040 | tf_op jit(solution)/shard_map/prepare_kernel/pallas_call | solution.py:583
  18.5 2.3 %all-to-all-done = s32[8,1,128]{2,1,0:T(1,128)S(1)} async-done(((s32[8,1,128]{2,1,0:T(1,128)}), s32[8,1,128]{2,1,0:T(1,128)S(1)}, u32[]{:S(2)}, u32[]{:S(2)}) %all-to-all-start) | async-done | bytes 4128 | tf_op jit(solution)/shard_map/all_to_all | solution.py:638
  21.8 1.3 collective-permute-start.2
  23.1 1.5 collective-permute-done.2.refs_4_
  24.6 1.6 copy-done.13
  26.2 6.5 %patterns.2 = (f32[2,256,256]{2,1,0:T(8,128)S(1)}, f32[16,9,8,256]{3,2,1,0:T(8,128)S(1)}, f32[16,9,8,256]{3,2,1,0:T(8,128)S(1)}, f32[4,2,32,256]{3,2,1,0:T(8,128...) custom-call(s32[4]{0:T(128)S(1)} %pad_add_fusion.refs_0_.where, ...), custom_call_target="tpu_custom_call" | custom-call | flops 6000000000 | bytes 9764888 | tf_op jit(solution)/shard_map/patterns/pallas_call | solution.py:583
  33.4 2.7 %collective-permute-done.4.refs_3_ = f32[4,2,32,256]{3,2,1,0:T(8,128)S(1)} collective-permute-done((f32[4,2,32,256]{3,2,1,0:T(8,128)S(1)}, f32[4,2,32,256]{3,2,1,0:T(8,128)S(1)}, u32[]{:S(2)}, u32[]{:S(2)}) %collective-permute-start.4) | collective-permute-done | bytes 262176 | tf_op jit(solution)/shard_map/ppermute | solution.py:607
  36.1 1.2 pack_kernel.2
  37.3 6.2 %all-to-all-start.1 = ((f32[16,9,8,256]{3,2,1,0:T(8,128)}), f32[16,9,8,256]{3,2,1,0:T(8,128)S(1)}, u32[]{:S(2)}, u32[]{:S(2)}) async-start(f32[16,9,8,256]{3,2,1,0:T(8,128)} %get-tuple-element.82), calls=%async_computation.1 | async-start | bytes 2359296 | tf_op jit(solution)/shard_map/all_to_all | solution.py:741
  43.5 1.4 collective-permute-start.5
  44.9 2.6 %collective-permute-start.6 = (f32[2,2,32,256]{3,2,1,0:T(8,128)S(1)}, f32[2,2,32,256]{3,2,1,0:T(8,128)S(1)}, u32[]{:S(2)}, u32[]{:S(2)}) collective-permute-start(f32[2,2,32,256]{3,2,1,0:T(8,128)S(1)} %get-tuple-element.79), channel_id=1, source_target_pairs={{0,64},{16,80},{32,96},{48,112},{64,0},{80,16},{96,32},{112,48},{1... | collective-permute-start | bytes 393224 | tf_op jit(solution)/shard_map/ppermute | solution.py:603
  49.5 3.8 %collective-permute-done.6.refs_5_ = f32[2,2,32,256]{3,2,1,0:T(8,128)S(1)} collective-permute-done((f32[2,2,32,256]{3,2,1,0:T(8,128)S(1)}, f32[2,2,32,256]{3,2,1,0:T(8,128)S(1)}, u32[]{:S(2)}, u32[]{:S(2)}) %collective-permute-start.6) | collective-permute-done | bytes 131104 | tf_op jit(solution)/shard_map/ppermute | solution.py:603
  53.3 1.4 place_kernel.2
  55.7 3.8 %collective-permute-start.12 = (f32[3,32,1024]{2,1,0:T(8,128)S(1)}, f32[3,32,1024]{2,1,0:T(8,128)S(1)}, u32[]{:S(2)}, u32[]{:S(2)}) collective-permute-start(f32[3,32,1024]{2,1,0:T(8,128)S(1)} %get-tuple-element.85.refs_3_), channel_id=1, source_target_pairs={{1,0},{2,1},{3,2},{4,3},{5,4},{6,5},{7,6},{8,7},{9,8},{10,9},{11,1... | collective-permute-start | bytes 1179656 | tf_op jit(solution)/shard_map/ppermute | solution.py:615
  59.5 1.9 all-to-all-done.1.refs_1_
  61.5 1.2 sum_kernel.2
  62.7 2.8 %collective-permute-start.10 = (f32[9,8,256]{2,1,0:T(8,128)S(1)}, f32[9,8,256]{2,1,0:T(8,128)S(1)}, u32[]{:S(2)}, u32[]{:S(2)}) collective-permute-start(f32[9,8,256]{2,1,0:T(8,128)S(1)} %get-tuple-element.83.refs_0_), channel_id=1, source_target_pairs={{0,96},{16,112},{32,0},{48,16},{64,32},{80,48},{96,64},{112,80},{1... | collective-permute-start | bytes 221192 | tf_op jit(solution)/shard_map/ppermute | solution.py:603
  66.6 3.7 %collective-permute-done.11.refs_4_.refs_5_ = f32[3,32,1024]{2,1,0:T(8,128)S(1)} collective-permute-done((f32[3,32,1024]{2,1,0:T(8,128)S(1)}, f32[3,32,1024]{2,1,0:T(8,128)S(1)}, u32[]{:S(2)}, u32[]{:S(2)}) %collective-permute-start.11) | collective-permute-done | bytes 393248 | tf_op jit(solution)/shard_map/ppermute | solution.py:611
  71.1 1.8 share_kernel.2
  72.9 4.5 %all-to-all-start.2 = ((f32[16,10,8,256]{3,2,1,0:T(8,128)}), f32[16,10,8,256]{3,2,1,0:T(8,128)S(1)}, u32[]{:S(2)}, u32[]{:S(2)}) async-start(f32[16,10,8,256]{3,2,1,0:T(8,128)} %get-tuple-element.87), calls=%async_computation.2 | async-start | bytes 2621440 | tf_op jit(solution)/shard_map/all_to_all | solution.py:754
  77.4 1.5 direction_kernel.2
  79.8 2.8 %collective-permute-start.14 = (f32[2,2,32,256]{3,2,1,0:T(8,128)S(1)}, f32[2,2,32,256]{3,2,1,0:T(8,128)S(1)}, u32[]{:S(2)}, u32[]{:S(2)}) collective-permute-start(f32[2,2,32,256]{3,2,1,0:T(8,128)S(1)} %get-tuple-element.91), channel_id=1, source_target_pairs={{0,64},{16,80},{32,96},{48,112},{64,0},{80,16},{96,32},{112,48},{1... | collective-permute-start | bytes 393224 | tf_op jit(solution)/shard_map/ppermute | solution.py:603
  84.7 1.7 collective-permute-done.14.refs_2_.refs_4_
  87.0 5.1 %collective-permute-start.16 = (f32[4,2,32,256]{3,2,1,0:T(8,128)S(1)}, f32[4,2,32,256]{3,2,1,0:T(8,128)S(1)}, u32[]{:S(2)}, u32[]{:S(2)}) collective-permute-start(f32[4,2,32,256]{3,2,1,0:T(8,128)S(1)} %stack_kernel.2), channel_id=1, source_target_pairs={{0,16},{16,0},{32,48},{48,32},{64,80},{80,64},{96,112},{112,96},{1... | collective-permute-start | bytes 786440 | tf_op jit(solution)/shard_map/ppermute | solution.py:607
  96.5 2.4 %message_kernel.2 = (f32[128,128]{1,0:T(8,128)}, f32[8,128,256]{2,1,0:T(8,128)}) custom-call(s32[4]{0:T(128)S(1)} %pad_add_fusion.refs_0_.where, f32[16,10,8,256]{3,2,1,0:T(8,128)S(1)} %all-to-all-done.2.refs_1_, f32[2,128,256]{2,1,0:T(8,128)S(1)} %get-tuple-element.94.refs_2_, f32[2,128,256]{2,1,0:T(8,128)S(1)} %collective-permute-done.17.refs_3_, ...), custom_call_target="tpu_custom_call" | custom-call | bytes 2949152 | tf_op jit(solution)/shard_map/message_kernel/pallas_call | solution.py:583
  98.9 2.7 %collective-permute-start.18 = (f32[8,128,256]{2,1,0:T(8,128)}, f32[8,128,256]{2,1,0:T(8,128)S(1)}, u32[]{:S(2)}, u32[]{:S(2)}) collective-permute-start(f32[8,128,256]{2,1,0:T(8,128)} %get-tuple-element.99.refs_8_), channel_id=1, source_target_pairs={{0,16},{16,0},{32,48},{48,32},{64,80},{80,64},{96,112},{112,96},{1... | collective-permute-start | bytes 3145736 | tf_op jit(solution)/shard_map/ppermute | solution.py:607
  101.6 1.3 collective-permute-start.21
  104.2 7.4 %all-to-all-start.3 = ((f32[128,1,128]{2,1,0:T(1,128)}), f32[128,1,128]{2,1,0:T(1,128)S(1)}, u32[]{:S(2)}, u32[]{:S(2)}) async-start(f32[128,1,128]{2,1,0:T(1,128)} %bitcast.31), calls=%async_computation.3 | async-start | bytes 131072 | tf_op jit(solution)/shard_map/all_to_all | solution.py:783
  112.0 6.8 %collective-permute-done.19.refs_10_.refs_3_ = f32[2,32,1024]{2,1,0:T(8,128)S(1)} collective-permute-done((f32[2,32,1024]{2,1,0:T(8,128)S(1)}, f32[2,32,1024]{2,1,0:T(8,128)S(1)}, u32[]{:S(2)}, u32[]{:S(2)}) %collective-permute-start.19) | collective-permute-done | bytes 262176 | tf_op jit(solution)/shard_map/ppermute | solution.py:603
  118.9 2.4 %all-to-all-done.3 = f32[128,1,128]{2,1,0:T(1,128)S(1)} async-done(((f32[128,1,128]{2,1,0:T(1,128)}), f32[128,1,128]{2,1,0:T(1,128)S(1)}, u32[]{:S(2)}, u32[]{:S(2)}) %all-to-all-start.3) | async-done | bytes 65568 | tf_op jit(solution)/shard_map/all_to_all | solution.py:783
  121.3 9.8 %patterns.3 = (f32[2,256,256]{2,1,0:T(8,128)}, f32[4,2,256,256]{3,2,1,0:T(8,128)}, f32[16,9,8,256]{3,2,1,0:T(8,128)S(1)}, f32[16,9,8,256]{3,2,1,0:T(8,128)S(1)},...) custom-call(s32[4]{0:T(128)S(1)} %pad_add_fusion.refs_0_.where, ...), custom_call_target="tpu_custom_call" | custom-call | flops 6000000000 | bytes 14286872 | tf_op jit(solution)/shard_map/patterns/pallas_call | solution.py:583
  132.1 2.8 %collective-permute-done.23.refs_3_ = f32[4,2,32,256]{3,2,1,0:T(8,128)S(1)} collective-permute-done((f32[4,2,32,256]{3,2,1,0:T(8,128)S(1)}, f32[4,2,32,256]{3,2,1,0:T(8,128)S(1)}, u32[]{:S(2)}, u32[]{:S(2)}) %collective-permute-start.23) | collective-permute-done | bytes 262176 | tf_op jit(solution)/shard_map/ppermute | solution.py:607
  134.8 1.2 pack_kernel.3
  136.0 3.7 %all-to-all-start.4 = ((f32[16,9,8,256]{3,2,1,0:T(8,128)}), f32[16,9,8,256]{3,2,1,0:T(8,128)S(1)}, u32[]{:S(2)}, u32[]{:S(2)}) async-start(f32[16,9,8,256]{3,2,1,0:T(8,128)} %get-tuple-element.111), calls=%async_computation.4 | async-start | bytes 2359296 | tf_op jit(solution)/shard_map/all_to_all | solution.py:741
  140.2 1.7 collective-permute-start.25
  143.5 2.7 %collective-permute-done.24.refs_4_ = f32[2,2,32,256]{3,2,1,0:T(8,128)S(1)} collective-permute-done((f32[2,2,32,256]{3,2,1,0:T(8,128)S(1)}, f32[2,2,32,256]{3,2,1,0:T(8,128)S(1)}, u32[]{:S(2)}, u32[]{:S(2)}) %collective-permute-start.24) | collective-permute-done | bytes 131104 | tf_op jit(solution)/shard_map/ppermute | solution.py:603
  146.2 1.7 collective-permute-done.25.refs_5_
  148.8 1.4 place_kernel.3
  151.0 4.0 %collective-permute-start.31 = (f32[3,32,1024]{2,1,0:T(8,128)S(1)}, f32[3,32,1024]{2,1,0:T(8,128)S(1)}, u32[]{:S(2)}, u32[]{:S(2)}) collective-permute-start(f32[3,32,1024]{2,1,0:T(8,128)S(1)} %get-tuple-element.114.refs_3_), channel_id=1, source_target_pairs={{1,0},{2,1},{3,2},{4,3},{5,4},{6,5},{7,6},{8,7},{9,8},{10,9},{11,1... | collective-permute-start | bytes 1179656 | tf_op jit(solution)/shard_map/ppermute | solution.py:615
  155.1 3.2 %all-to-all-done.4.refs_1_ = f32[16,9,8,256]{3,2,1,0:T(8,128)S(1)} async-done(((f32[16,9,8,256]{3,2,1,0:T(8,128)}), f32[16,9,8,256]{3,2,1,0:T(8,128)S(1)}, u32[]{:S(2)}, u32[]{:S(2)}) %all-to-all-start.4) | async-done | bytes 1179680 | tf_op jit(solution)/shard_map/all_to_all | solution.py:741
  158.3 1.2 sum_kernel.3
  159.5 1.6 collective-permute-start.29
  161.1 1.3 collective-permute-start.28
  162.4 4.7 %collective-permute-done.30.refs_4_.refs_5_ = f32[3,32,1024]{2,1,0:T(8,128)S(1)} collective-permute-done((f32[3,32,1024]{2,1,0:T(8,128)S(1)}, f32[3,32,1024]{2,1,0:T(8,128)S(1)}, u32[]{:S(2)}, u32[]{:S(2)}) %collective-permute-start.30) | collective-permute-done | bytes 393248 | tf_op jit(solution)/shard_map/ppermute | solution.py:611
  167.1 1.8 share_kernel.3
  168.9 4.2 %all-to-all-start.5 = ((f32[16,10,8,256]{3,2,1,0:T(8,128)}), f32[16,10,8,256]{3,2,1,0:T(8,128)S(1)}, u32[]{:S(2)}, u32[]{:S(2)}) async-start(f32[16,10,8,256]{3,2,1,0:T(8,128)} %get-tuple-element.116), calls=%async_computation.5 | async-start | bytes 2621440 | tf_op jit(solution)/shard_map/all_to_all | solution.py:754
  173.1 1.5 direction_kernel.3
  174.6 2.6 %collective-permute-start.33 = (f32[2,2,32,256]{3,2,1,0:T(8,128)S(1)}, f32[2,2,32,256]{3,2,1,0:T(8,128)S(1)}, u32[]{:S(2)}, u32[]{:S(2)}) collective-permute-start(f32[2,2,32,256]{3,2,1,0:T(8,128)S(1)} %get-tuple-element.120), channel_id=1, source_target_pairs={{0,64},{16,80},{32,96},{48,112},{64,0},{80,16},{96,32},{112,48},{1... | collective-permute-start | bytes 393224 | tf_op jit(solution)/shard_map/ppermute | solution.py:603
  177.3 3.8 %collective-permute-done.32.refs_1_.refs_3_ = f32[2,2,32,256]{3,2,1,0:T(8,128)S(1)} collective-permute-done((f32[2,2,32,256]{3,2,1,0:T(8,128)S(1)}, f32[2,2,32,256]{3,2,1,0:T(8,128)S(1)}, u32[]{:S(2)}, u32[]{:S(2)}) %collective-permute-start.32) | collective-permute-done | bytes 131104 | tf_op jit(solution)/shard_map/ppermute | solution.py:603
  182.0 4.4 %collective-permute-start.35 = (f32[4,2,32,256]{3,2,1,0:T(8,128)S(1)}, f32[4,2,32,256]{3,2,1,0:T(8,128)S(1)}, u32[]{:S(2)}, u32[]{:S(2)}) collective-permute-start(f32[4,2,32,256]{3,2,1,0:T(8,128)S(1)} %stack_kernel.3), channel_id=1, source_target_pairs={{0,16},{16,0},{32,48},{48,32},{64,80},{80,64},{96,112},{112,96},{1... | collective-permute-start | bytes 786440 | tf_op jit(solution)/shard_map/ppermute | solution.py:607
  187.6 1.7 patch_kernel.3
  189.6 2.4 %collective-permute-start.39 = (f32[2,32,1024]{2,1,0:T(8,128)S(1)}, f32[2,32,1024]{2,1,0:T(8,128)}, u32[]{:S(2)}, u32[]{:S(2)}) collective-permute-start(f32[2,32,1024]{2,1,0:T(8,128)S(1)} %get-tuple-element.127.refs_6_), channel_id=1, source_target_pairs={{0,96},{16,112},{32,0},{48,16},{64,32},{80,48},{96,64},{112,80},{1... | collective-permute-start | bytes 786440 | tf_op jit(solution)/shard_map/ppermute | solution.py:603
  192.6 1.4 message_kernel.3
  194.0 2.2 collective-permute-start.41
  196.2 7.5 %all-to-all-start.6 = ((f32[128,1,128]{2,1,0:T(1,128)}), f32[128,1,128]{2,1,0:T(1,128)S(1)}, u32[]{:S(2)}, u32[]{:S(2)}) async-start(f32[128,1,128]{2,1,0:T(1,128)} %bitcast.32), calls=%async_computation.6 | async-start | bytes 131072 | tf_op jit(solution)/shard_map/all_to_all | solution.py:783
  203.7 3.2 %collective-permute-done.37.refs_7_ = f32[2,32,1024]{2,1,0:T(8,128)} collective-permute-done((f32[2,32,1024]{2,1,0:T(8,128)S(1)}, f32[2,32,1024]{2,1,0:T(8,128)}, u32[]{:S(2)}, u32[]{:S(2)}) %collective-permute-start.37) | collective-permute-done | bytes 262176 | tf_op jit(solution)/shard_map/ppermute | solution.py:603
  206.9 6.5 %all-to-all-done.6 = f32[128,1,128]{2,1,0:T(1,128)S(1)} async-done(((f32[128,1,128]{2,1,0:T(1,128)}), f32[128,1,128]{2,1,0:T(1,128)S(1)}, u32[]{:S(2)}, u32[]{:S(2)}) %all-to-all-start.6) | async-done | bytes 65568 | tf_op jit(solution)/shard_map/all_to_all | solution.py:783
  213.4 1.6 combine_kernel.1.refs_2_
  215.9 3.0 %probe_kernel.1 = f32[4,2,256,256]{3,2,1,0:T(8,128)} custom-call(s32[4]{0:T(128)S(1)} %pad_add_fusion.refs_0_.where, f32[128,128]{1,0:T(8,128)S(1)} %bitcast.18, f32[4,2,256,256]{3,2,1,0:T(8,128)} %get-tuple-element.128.refs_2_, f32[8,128,256]{2,1,0:T(8,128)S(1)} %get-tuple-element.129.refs_3_, f32[8,128,256]{2,1,0:T(8,128)S(1)} %collective-permute-done.41.refs_4_), custom_call_target="tpu_custom_call" | custom-call | flops 1000000000 | bytes 6357008 | tf_op jit(solution)/shard_map/probe_kernel/pallas_call | solution.py:583
  218.9 3.2 %object_kernel.1 = f32[2,256,1024]{2,1,0:T(8,128)} custom-call(s32[4]{0:T(128)S(1)} %pad_add_fusion.refs_0_.where, f32[2,256,1024]{2,1,0:T(8,128)} %refs_1_.7, f32[4,2,32,1024]{3,2,1,0:T(8,128)S(1)} %combine_kernel.1.refs_2_, f32[4,2,32,1024]{3,2,1,0:T(8,128)S(1)} %collective-permute-done.40.refs_3_), custom_call_target="tpu_custom_call" | custom-call | bytes 6291472 | tf_op jit(solution)/shard_map/object_kernel/pallas_call | solution.py:583
  (96 shorter events, 26.2 us)
Async XLA Ops:
  0.6 15.4 %copy-start.9 = (bf16[2,256,256]{2,1,0:T(8,128)(2,1)S(1)}, bf16[2,256,256]{2,1,0:T(8,128)(2,1)}, u32[]{:S(2)}) copy-start(bf16[2,256,256]{2,1,0:T(8,128)(2,1)} %constant.43.clone.refs_3_) | copy-start | bytes 786436
  0.6 8.8 %copy-start.12 = (s32[1,2]{1,0:T(1,128)S(1)}, s32[1,2]{1,0:T(1,128)}, u32[]{:S(2)}) copy-start(s32[1,2]{1,0:T(1,128)} %refs_1_.6) | copy-start | bytes 28
  0.7 15.4 %copy-start.2 = (f32[1,256,256]{2,1,0:T(8,128)S(1)}, f32[1,256,256]{2,1,0:T(8,128)}, u32[]{:S(2)}) copy-start(f32[1,256,256]{2,1,0:T(8,128)} %param.6) | copy-start | bytes 786436
  2.5 18.5 %collective-permute-start = (f32[128,1024]{1,0:T(8,128)S(1)}, f32[128,1024]{1,0:T(8,128)S(1)}, u32[]{:S(2)}, u32[]{:S(2)}) collective-permute-start(f32[128,1024]{1,0:T(8,128)S(1)} %get-tuple-element.67), channel_id=1, source_target_pairs={{0,1},{1,2},{2,3},{3,4},{4,5},{5,6},{6,7},{7,8},{8,9},{9,10},{10,1... | collective-permute-start | bytes 1572872 | tf_op jit(solution)/shard_map/ppermute | solution.py:611
  4.6 16.4 %collective-permute-start.1 = (f32[128,1024]{1,0:T(8,128)S(1)}, f32[128,1024]{1,0:T(8,128)S(1)}, u32[]{:S(2)}, u32[]{:S(2)}) collective-permute-start(f32[128,1024]{1,0:T(8,128)S(1)} %get-tuple-element.68), channel_id=1, source_target_pairs={{1,0},{2,1},{3,2},{4,3},{5,4},{6,5},{7,6},{8,7},{9,8},{10,9},{11,1... | collective-permute-start | bytes 1572872 | tf_op jit(solution)/shard_map/ppermute | solution.py:615
  10.6 10.2 %all-to-all-start = ((s32[8,1,128]{2,1,0:T(1,128)}), s32[8,1,128]{2,1,0:T(1,128)S(1)}, u32[]{:S(2)}, u32[]{:S(2)}) async-start(s32[8,1,128]{2,1,0:T(1,128)} %bitcast.5), calls=%async_computation | async-start | bytes 8192 | tf_op jit(solution)/shard_map/all_to_all | solution.py:638
  18.5 14.2 %copy-start.15 = (f32[2,128,256]{2,1,0:T(8,128)}, f32[2,128,256]{2,1,0:T(8,128)S(1)}, u32[]{:S(2)}) copy-start(f32[2,128,256]{2,1,0:T(8,128)S(1)} %get-tuple-element.71.refs_6_.refs_5_) | copy-start | bytes 786436
  20.8 3.8 %copy-start.16 = (bf16[4,2,256,256]{3,2,1,0:T(8,128)(2,1)S(1)}, bf16[4,2,256,256]{3,2,1,0:T(8,128)(2,1)}, u32[]{:S(2)}) copy-start(bf16[4,2,256,256]{3,2,1,0:T(8,128)(2,1)} %constant.42.clone.refs_7_.refs_6_) | copy-start | bytes 3145732
  21.8 2.8 %collective-permute-start.2 = (f32[128,1024]{1,0:T(8,128)S(1)}, f32[128,1024]{1,0:T(8,128)S(1)}, u32[]{:S(2)}, u32[]{:S(2)}) collective-permute-start(f32[128,1024]{1,0:T(8,128)S(1)} %get-tuple-element.70), channel_id=1, source_target_pairs={{0,16},{16,0},{32,48},{48,32},{64,80},{80,64},{96,112},{112,96},{1... | collective-permute-start | bytes 1572872 | tf_op jit(solution)/shard_map/ppermute | solution.py:607
  24.6 1.6 copy-start.13
  32.8 4.5 %copy-start.10 = (f32[8,8,256]{2,1,0:T(8,128)}, f32[8,8,256]{2,1,0:T(8,128)S(1)}, u32[]{:S(2)}) copy-start(f32[8,8,256]{2,1,0:T(8,128)S(1)} %get-tuple-element.86.refs_6_) | copy-start | bytes 196612
  32.8 60.5 %copy-start = (f32[2,256,256]{2,1,0:T(8,128)}, f32[2,256,256]{2,1,0:T(8,128)S(1)}, u32[]{:S(2)}) copy-start(f32[2,256,256]{2,1,0:T(8,128)S(1)} %get-tuple-element.93.refs_7_.refs_3_) | copy-start | bytes 1572868
  32.8 3.3 %collective-permute-start.3 = (f32[16,9,8,256]{3,2,1,0:T(8,128)S(1)}, f32[16,9,8,256]{3,2,1,0:T(8,128)S(1)}, u32[]{:S(2)}, u32[]{:S(2)}) collective-permute-start(f32[16,9,8,256]{3,2,1,0:T(8,128)S(1)} %get-tuple-element.74), channel_id=1, source_target_pairs={{0,16},{16,0},{32,48},{48,32},{64,80},{80,64},{96,112},{112,96},{1... | collective-permute-start | bytes 3538952 | tf_op jit(solution)/shard_map/ppermute | solution.py:607
  33.2 2.9 %collective-permute-start.4 = (f32[4,2,32,256]{3,2,1,0:T(8,128)S(1)}, f32[4,2,32,256]{3,2,1,0:T(8,128)S(1)}, u32[]{:S(2)}, u32[]{:S(2)}) collective-permute-start(f32[4,2,32,256]{3,2,1,0:T(8,128)S(1)} %get-tuple-element.76), channel_id=1, source_target_pairs={{0,16},{16,0},{32,48},{48,32},{64,80},{80,64},{96,112},{112,96},{1... | collective-permute-start | bytes 786440 | tf_op jit(solution)/shard_map/ppermute | solution.py:607
  37.3 24.2 %all-to-all-start.1 = ((f32[16,9,8,256]{3,2,1,0:T(8,128)}), f32[16,9,8,256]{3,2,1,0:T(8,128)S(1)}, u32[]{:S(2)}, u32[]{:S(2)}) async-start(f32[16,9,8,256]{3,2,1,0:T(8,128)} %get-tuple-element.82), calls=%async_computation.1 | async-start | bytes 2359296 | tf_op jit(solution)/shard_map/all_to_all | solution.py:741
  43.5 6.0 %collective-permute-start.5 = (f32[2,2,32,256]{3,2,1,0:T(8,128)S(1)}, f32[2,2,32,256]{3,2,1,0:T(8,128)S(1)}, u32[]{:S(2)}, u32[]{:S(2)}) collective-permute-start(f32[2,2,32,256]{3,2,1,0:T(8,128)S(1)} %get-tuple-element.78), channel_id=1, source_target_pairs={{0,32},{16,48},{32,64},{48,80},{64,96},{80,112},{96,0},{112,16},{1... | collective-permute-start | bytes 393224 | tf_op jit(solution)/shard_map/ppermute | solution.py:603
  44.9 8.4 %collective-permute-start.6 = (f32[2,2,32,256]{3,2,1,0:T(8,128)S(1)}, f32[2,2,32,256]{3,2,1,0:T(8,128)S(1)}, u32[]{:S(2)}, u32[]{:S(2)}) collective-permute-start(f32[2,2,32,256]{3,2,1,0:T(8,128)S(1)} %get-tuple-element.79), channel_id=1, source_target_pairs={{0,64},{16,80},{32,96},{48,112},{64,0},{80,16},{96,32},{112,48},{1... | collective-permute-start | bytes 393224 | tf_op jit(solution)/shard_map/ppermute | solution.py:603
  47.5 5.7 %collective-permute-start.7 = (f32[2,2,32,256]{3,2,1,0:T(8,128)S(1)}, f32[2,2,32,256]{3,2,1,0:T(8,128)S(1)}, u32[]{:S(2)}, u32[]{:S(2)}) collective-permute-start(f32[2,2,32,256]{3,2,1,0:T(8,128)S(1)} %get-tuple-element.80), channel_id=1, source_target_pairs={{0,96},{16,112},{32,0},{48,16},{64,32},{80,48},{96,64},{112,80},{1... | collective-permute-start | bytes 393224 | tf_op jit(solution)/shard_map/ppermute | solution.py:603
  49.5 21.6 %copy-start.11 = (f32[8,8,256]{2,1,0:T(8,128)S(1)}, f32[8,8,256]{2,1,0:T(8,128)}, u32[]{:S(2)}) copy-start(f32[8,8,256]{2,1,0:T(8,128)} %copy-done.10) | copy-start | bytes 196612
  54.7 15.6 %collective-permute-start.11 = (f32[3,32,1024]{2,1,0:T(8,128)S(1)}, f32[3,32,1024]{2,1,0:T(8,128)S(1)}, u32[]{:S(2)}, u32[]{:S(2)}) collective-permute-start(f32[3,32,1024]{2,1,0:T(8,128)S(1)} %get-tuple-element.84.refs_4_), channel_id=1, source_target_pairs={{0,1},{1,2},{2,3},{3,4},{4,5},{5,6},{6,7},{7,8},{8,9},{9,10},{10,1... | collective-permute-start | bytes 1179656 | tf_op jit(solution)/shard_map/ppermute | solution.py:611
  55.7 14.5 %collective-permute-start.12 = (f32[3,32,1024]{2,1,0:T(8,128)S(1)}, f32[3,32,1024]{2,1,0:T(8,128)S(1)}, u32[]{:S(2)}, u32[]{:S(2)}) collective-permute-start(f32[3,32,1024]{2,1,0:T(8,128)S(1)} %get-tuple-element.85.refs_3_), channel_id=1, source_target_pairs={{1,0},{2,1},{3,2},{4,3},{5,4},{6,5},{7,6},{8,7},{9,8},{10,9},{11,1... | collective-permute-start | bytes 1179656 | tf_op jit(solution)/shard_map/ppermute | solution.py:615
  62.7 7.6 %collective-permute-start.10 = (f32[9,8,256]{2,1,0:T(8,128)S(1)}, f32[9,8,256]{2,1,0:T(8,128)S(1)}, u32[]{:S(2)}, u32[]{:S(2)}) collective-permute-start(f32[9,8,256]{2,1,0:T(8,128)S(1)} %get-tuple-element.83.refs_0_), channel_id=1, source_target_pairs={{0,96},{16,112},{32,0},{48,16},{64,32},{80,48},{96,64},{112,80},{1... | collective-permute-start | bytes 221192 | tf_op jit(solution)/shard_map/ppermute | solution.py:603
  65.5 5.0 %collective-permute-start.9 = (f32[9,8,256]{2,1,0:T(8,128)S(1)}, f32[9,8,256]{2,1,0:T(8,128)S(1)}, u32[]{:S(2)}, u32[]{:S(2)}) collective-permute-start(f32[9,8,256]{2,1,0:T(8,128)S(1)} %get-tuple-element.83.refs_0_), channel_id=1, source_target_pairs={{0,64},{16,80},{32,96},{48,112},{64,0},{80,16},{96,32},{112,48},{1... | collective-permute-start | bytes 221192 | tf_op jit(solution)/shard_map/ppermute | solution.py:603
  65.9 5.2 %collective-permute-start.8 = (f32[9,8,256]{2,1,0:T(8,128)S(1)}, f32[9,8,256]{2,1,0:T(8,128)S(1)}, u32[]{:S(2)}, u32[]{:S(2)}) collective-permute-start(f32[9,8,256]{2,1,0:T(8,128)S(1)} %get-tuple-element.83.refs_0_), channel_id=1, source_target_pairs={{0,32},{16,48},{32,64},{48,80},{64,96},{80,112},{96,0},{112,16},{1... | collective-permute-start | bytes 221192 | tf_op jit(solution)/shard_map/ppermute | solution.py:603
  72.9 23.6 %all-to-all-start.2 = ((f32[16,10,8,256]{3,2,1,0:T(8,128)}), f32[16,10,8,256]{3,2,1,0:T(8,128)S(1)}, u32[]{:S(2)}, u32[]{:S(2)}) async-start(f32[16,10,8,256]{3,2,1,0:T(8,128)} %get-tuple-element.87), calls=%async_computation.2 | async-start | bytes 2621440 | tf_op jit(solution)/shard_map/all_to_all | solution.py:754
  79.6 5.0 %collective-permute-start.13 = (f32[2,2,32,256]{3,2,1,0:T(8,128)S(1)}, f32[2,2,32,256]{3,2,1,0:T(8,128)S(1)}, u32[]{:S(2)}, u32[]{:S(2)}) collective-permute-start(f32[2,2,32,256]{3,2,1,0:T(8,128)S(1)} %get-tuple-element.90), channel_id=1, source_target_pairs={{0,32},{16,48},{32,64},{48,80},{64,96},{80,112},{96,0},{112,16},{1... | collective-permute-start | bytes 393224 | tf_op jit(solution)/shard_map/ppermute | solution.py:603
  79.8 6.5 %collective-permute-start.14 = (f32[2,2,32,256]{3,2,1,0:T(8,128)S(1)}, f32[2,2,32,256]{3,2,1,0:T(8,128)S(1)}, u32[]{:S(2)}, u32[]{:S(2)}) collective-permute-start(f32[2,2,32,256]{3,2,1,0:T(8,128)S(1)} %get-tuple-element.91), channel_id=1, source_target_pairs={{0,64},{16,80},{32,96},{48,112},{64,0},{80,16},{96,32},{112,48},{1... | collective-permute-start | bytes 393224 | tf_op jit(solution)/shard_map/ppermute | solution.py:603
  82.6 4.4 %collective-permute-start.15 = (f32[2,2,32,256]{3,2,1,0:T(8,128)S(1)}, f32[2,2,32,256]{3,2,1,0:T(8,128)S(1)}, u32[]{:S(2)}, u32[]{:S(2)}) collective-permute-start(f32[2,2,32,256]{3,2,1,0:T(8,128)S(1)} %get-tuple-element.92), channel_id=1, source_target_pairs={{0,96},{16,112},{32,0},{48,16},{64,32},{80,48},{96,64},{112,80},{1... | collective-permute-start | bytes 393224 | tf_op jit(solution)/shard_map/ppermute | solution.py:603
  87.0 6.3 %collective-permute-start.16 = (f32[4,2,32,256]{3,2,1,0:T(8,128)S(1)}, f32[4,2,32,256]{3,2,1,0:T(8,128)S(1)}, u32[]{:S(2)}, u32[]{:S(2)}) collective-permute-start(f32[4,2,32,256]{3,2,1,0:T(8,128)S(1)} %stack_kernel.2), channel_id=1, source_target_pairs={{0,16},{16,0},{32,48},{48,32},{64,80},{80,64},{96,112},{112,96},{1... | collective-permute-start | bytes 786440 | tf_op jit(solution)/shard_map/ppermute | solution.py:607
  94.9 6.7 %copy-start.4 = (f32[2,32,1024]{2,1,0:T(8,128)S(1)}, f32[2,32,1024]{2,1,0:T(8,128)}, u32[]{:S(2)}) copy-start(f32[2,32,1024]{2,1,0:T(8,128)} %copy-done.3) | copy-start | bytes 786436
  94.9 1.5 collective-permute-start.17
  98.9 22.4 %collective-permute-start.18 = (f32[8,128,256]{2,1,0:T(8,128)}, f32[8,128,256]{2,1,0:T(8,128)S(1)}, u32[]{:S(2)}, u32[]{:S(2)}) collective-permute-start(f32[8,128,256]{2,1,0:T(8,128)} %get-tuple-element.99.refs_8_), channel_id=1, source_target_pairs={{0,16},{16,0},{32,48},{48,32},{64,80},{80,64},{96,112},{112,96},{1... | collective-permute-start | bytes 3145736 | tf_op jit(solution)/shard_map/ppermute | solution.py:607
  101.6 10.0 %collective-permute-start.21 = (f32[2,32,1024]{2,1,0:T(8,128)S(1)}, f32[2,32,1024]{2,1,0:T(8,128)S(1)}, u32[]{:S(2)}, u32[]{:S(2)}) collective-permute-start(f32[2,32,1024]{2,1,0:T(8,128)S(1)} %copy-done.4), channel_id=1, source_target_pairs={{0,96},{16,112},{32,0},{48,16},{64,32},{80,48},{96,64},{112,80},{1... | collective-permute-start | bytes 786440 | tf_op jit(solution)/shard_map/ppermute | solution.py:603
  102.9 9.1 %collective-permute-start.20 = (f32[2,32,1024]{2,1,0:T(8,128)S(1)}, f32[2,32,1024]{2,1,0:T(8,128)S(1)}, u32[]{:S(2)}, u32[]{:S(2)}) collective-permute-start(f32[2,32,1024]{2,1,0:T(8,128)S(1)} %copy-done.4), channel_id=1, source_target_pairs={{0,64},{16,80},{32,96},{48,112},{64,0},{80,16},{96,32},{112,48},{1... | collective-permute-start | bytes 786440 | tf_op jit(solution)/shard_map/ppermute | solution.py:603
  103.3 15.5 %collective-permute-start.19 = (f32[2,32,1024]{2,1,0:T(8,128)S(1)}, f32[2,32,1024]{2,1,0:T(8,128)S(1)}, u32[]{:S(2)}, u32[]{:S(2)}) collective-permute-start(f32[2,32,1024]{2,1,0:T(8,128)S(1)} %copy-done.4), channel_id=1, source_target_pairs={{0,32},{16,48},{32,64},{48,80},{64,96},{80,112},{96,0},{112,16},{1... | collective-permute-start | bytes 786440 | tf_op jit(solution)/shard_map/ppermute | solution.py:603
  104.2 17.2 %all-to-all-start.3 = ((f32[128,1,128]{2,1,0:T(1,128)}), f32[128,1,128]{2,1,0:T(1,128)S(1)}, u32[]{:S(2)}, u32[]{:S(2)}) async-start(f32[128,1,128]{2,1,0:T(1,128)} %bitcast.31), calls=%async_computation.3 | async-start | bytes 131072 | tf_op jit(solution)/shard_map/all_to_all | solution.py:783
  111.6 19.5 %copy-start.5 = (f32[2,32,1024]{2,1,0:T(8,128)}, f32[2,32,1024]{2,1,0:T(8,128)S(1)}, u32[]{:S(2)}) copy-start(f32[2,32,1024]{2,1,0:T(8,128)S(1)} %collective-permute-done.21.refs_12_.refs_5_) | copy-start | bytes 786436
  112.0 19.1 %copy-start.6 = (f32[2,32,1024]{2,1,0:T(8,128)}, f32[2,32,1024]{2,1,0:T(8,128)S(1)}, u32[]{:S(2)}) copy-start(f32[2,32,1024]{2,1,0:T(8,128)S(1)} %collective-permute-done.20.refs_11_.refs_4_) | copy-start | bytes 786436
  118.9 12.3 %copy-start.7 = (f32[2,32,1024]{2,1,0:T(8,128)}, f32[2,32,1024]{2,1,0:T(8,128)S(1)}, u32[]{:S(2)}) copy-start(f32[2,32,1024]{2,1,0:T(8,128)S(1)} %collective-permute-done.19.refs_10_.refs_3_) | copy-start | bytes 786436
  131.1 3.7 %collective-permute-start.22 = (f32[16,9,8,256]{3,2,1,0:T(8,128)S(1)}, f32[16,9,8,256]{3,2,1,0:T(8,128)S(1)}, u32[]{:S(2)}, u32[]{:S(2)}) collective-permute-start(f32[16,9,8,256]{3,2,1,0:T(8,128)S(1)} %get-tuple-element.103), channel_id=1, source_target_pairs={{0,16},{16,0},{32,48},{48,32},{64,80},{80,64},{96,112},{112,96},{1... | collective-permute-start | bytes 3538952 | tf_op jit(solution)/shard_map/ppermute | solution.py:607
  132.0 2.8 %collective-permute-start.23 = (f32[4,2,32,256]{3,2,1,0:T(8,128)S(1)}, f32[4,2,32,256]{3,2,1,0:T(8,128)S(1)}, u32[]{:S(2)}, u32[]{:S(2)}) collective-permute-start(f32[4,2,32,256]{3,2,1,0:T(8,128)S(1)} %get-tuple-element.105), channel_id=1, source_target_pairs={{0,16},{16,0},{32,48},{48,32},{64,80},{80,64},{96,112},{112,96},{1... | collective-permute-start | bytes 786440 | tf_op jit(solution)/shard_map/ppermute | solution.py:607
  136.0 22.3 %all-to-all-start.4 = ((f32[16,9,8,256]{3,2,1,0:T(8,128)}), f32[16,9,8,256]{3,2,1,0:T(8,128)S(1)}, u32[]{:S(2)}, u32[]{:S(2)}) async-start(f32[16,9,8,256]{3,2,1,0:T(8,128)} %get-tuple-element.111), calls=%async_computation.4 | async-start | bytes 2359296 | tf_op jit(solution)/shard_map/all_to_all | solution.py:741
  139.7 6.5 %collective-permute-start.24 = (f32[2,2,32,256]{3,2,1,0:T(8,128)S(1)}, f32[2,2,32,256]{3,2,1,0:T(8,128)S(1)}, u32[]{:S(2)}, u32[]{:S(2)}) collective-permute-start(f32[2,2,32,256]{3,2,1,0:T(8,128)S(1)} %get-tuple-element.107), channel_id=1, source_target_pairs={{0,32},{16,48},{32,64},{48,80},{64,96},{80,112},{96,0},{112,16},{1... | collective-permute-start | bytes 393224 | tf_op jit(solution)/shard_map/ppermute | solution.py:603
  140.2 7.8 %collective-permute-start.25 = (f32[2,2,32,256]{3,2,1,0:T(8,128)S(1)}, f32[2,2,32,256]{3,2,1,0:T(8,128)S(1)}, u32[]{:S(2)}, u32[]{:S(2)}) collective-permute-start(f32[2,2,32,256]{3,2,1,0:T(8,128)S(1)} %get-tuple-element.108), channel_id=1, source_target_pairs={{0,64},{16,80},{32,96},{48,112},{64,0},{80,16},{96,32},{112,48},{1... | collective-permute-start | bytes 393224 | tf_op jit(solution)/shard_map/ppermute | solution.py:603
  141.8 7.0 %collective-permute-start.26 = (f32[2,2,32,256]{3,2,1,0:T(8,128)S(1)}, f32[2,2,32,256]{3,2,1,0:T(8,128)S(1)}, u32[]{:S(2)}, u32[]{:S(2)}) collective-permute-start(f32[2,2,32,256]{3,2,1,0:T(8,128)S(1)} %get-tuple-element.109), channel_id=1, source_target_pairs={{0,96},{16,112},{32,0},{48,16},{64,32},{80,48},{96,64},{112,80},{1... | collective-permute-start | bytes 393224 | tf_op jit(solution)/shard_map/ppermute | solution.py:603
  150.2 16.8 %collective-permute-start.30 = (f32[3,32,1024]{2,1,0:T(8,128)S(1)}, f32[3,32,1024]{2,1,0:T(8,128)S(1)}, u32[]{:S(2)}, u32[]{:S(2)}) collective-permute-start(f32[3,32,1024]{2,1,0:T(8,128)S(1)} %get-tuple-element.113.refs_4_), channel_id=1, source_target_pairs={{0,1},{1,2},{2,3},{3,4},{4,5},{5,6},{6,7},{7,8},{8,9},{9,10},{10,1... | collective-permute-start | bytes 1179656 | tf_op jit(solution)/shard_map/ppermute | solution.py:611
  151.0 16.0 %collective-permute-start.31 = (f32[3,32,1024]{2,1,0:T(8,128)S(1)}, f32[3,32,1024]{2,1,0:T(8,128)S(1)}, u32[]{:S(2)}, u32[]{:S(2)}) collective-permute-start(f32[3,32,1024]{2,1,0:T(8,128)S(1)} %get-tuple-element.114.refs_3_), channel_id=1, source_target_pairs={{1,0},{2,1},{3,2},{4,3},{5,4},{6,5},{7,6},{8,7},{9,8},{10,9},{11,1... | collective-permute-start | bytes 1179656 | tf_op jit(solution)/shard_map/ppermute | solution.py:615
  159.5 7.5 %collective-permute-start.29 = (f32[9,8,256]{2,1,0:T(8,128)S(1)}, f32[9,8,256]{2,1,0:T(8,128)S(1)}, u32[]{:S(2)}, u32[]{:S(2)}) collective-permute-start(f32[9,8,256]{2,1,0:T(8,128)S(1)} %get-tuple-element.112.refs_0_), channel_id=1, source_target_pairs={{0,96},{16,112},{32,0},{48,16},{64,32},{80,48},{96,64},{112,80},{1... | collective-permute-start | bytes 221192 | tf_op jit(solution)/shard_map/ppermute | solution.py:603
  161.1 6.0 %collective-permute-start.28 = (f32[9,8,256]{2,1,0:T(8,128)S(1)}, f32[9,8,256]{2,1,0:T(8,128)S(1)}, u32[]{:S(2)}, u32[]{:S(2)}) collective-permute-start(f32[9,8,256]{2,1,0:T(8,128)S(1)} %get-tuple-element.112.refs_0_), channel_id=1, source_target_pairs={{0,64},{16,80},{32,96},{48,112},{64,0},{80,16},{96,32},{112,48},{1... | collective-permute-start | bytes 221192 | tf_op jit(solution)/shard_map/ppermute | solution.py:603
  162.4 4.7 %collective-permute-start.27 = (f32[9,8,256]{2,1,0:T(8,128)S(1)}, f32[9,8,256]{2,1,0:T(8,128)S(1)}, u32[]{:S(2)}, u32[]{:S(2)}) collective-permute-start(f32[9,8,256]{2,1,0:T(8,128)S(1)} %get-tuple-element.112.refs_0_), channel_id=1, source_target_pairs={{0,32},{16,48},{32,64},{48,80},{64,96},{80,112},{96,0},{112,16},{1... | collective-permute-start | bytes 221192 | tf_op jit(solution)/shard_map/ppermute | solution.py:603
  168.9 23.7 %all-to-all-start.5 = ((f32[16,10,8,256]{3,2,1,0:T(8,128)}), f32[16,10,8,256]{3,2,1,0:T(8,128)S(1)}, u32[]{:S(2)}, u32[]{:S(2)}) async-start(f32[16,10,8,256]{3,2,1,0:T(8,128)} %get-tuple-element.116), calls=%async_computation.5 | async-start | bytes 2621440 | tf_op jit(solution)/shard_map/all_to_all | solution.py:754
  173.0 14.5 %copy-start.1 = (f32[2,256,256]{2,1,0:T(8,128)S(1)}, f32[2,256,256]{2,1,0:T(8,128)}, u32[]{:S(2)}) copy-start(f32[2,256,256]{2,1,0:T(8,128)} %get-tuple-element.122.refs_7_) | copy-start | bytes 1572868
  174.5 19.5 %copy-start.8 = (f32[2,32,1024]{2,1,0:T(8,128)}, f32[2,32,1024]{2,1,0:T(8,128)S(1)}, u32[]{:S(2)}) copy-start(f32[2,32,1024]{2,1,0:T(8,128)S(1)} %get-tuple-element.127.refs_6_) | copy-start | bytes 786436
  174.6 6.6 %collective-permute-start.32 = (f32[2,2,32,256]{3,2,1,0:T(8,128)S(1)}, f32[2,2,32,256]{3,2,1,0:T(8,128)S(1)}, u32[]{:S(2)}, u32[]{:S(2)}) collective-permute-start(f32[2,2,32,256]{3,2,1,0:T(8,128)S(1)} %get-tuple-element.119), channel_id=1, source_target_pairs={{0,32},{16,48},{32,64},{48,80},{64,96},{80,112},{96,0},{112,16},{1... | collective-permute-start | bytes 393224 | tf_op jit(solution)/shard_map/ppermute | solution.py:603
  174.6 6.6 %collective-permute-start.33 = (f32[2,2,32,256]{3,2,1,0:T(8,128)S(1)}, f32[2,2,32,256]{3,2,1,0:T(8,128)S(1)}, u32[]{:S(2)}, u32[]{:S(2)}) collective-permute-start(f32[2,2,32,256]{3,2,1,0:T(8,128)S(1)} %get-tuple-element.120), channel_id=1, source_target_pairs={{0,64},{16,80},{32,96},{48,112},{64,0},{80,16},{96,32},{112,48},{1... | collective-permute-start | bytes 393224 | tf_op jit(solution)/shard_map/ppermute | solution.py:603
  177.2 4.8 %collective-permute-start.34 = (f32[2,2,32,256]{3,2,1,0:T(8,128)S(1)}, f32[2,2,32,256]{3,2,1,0:T(8,128)S(1)}, u32[]{:S(2)}, u32[]{:S(2)}) collective-permute-start(f32[2,2,32,256]{3,2,1,0:T(8,128)S(1)} %get-tuple-element.121), channel_id=1, source_target_pairs={{0,96},{16,112},{32,0},{48,16},{64,32},{80,48},{96,64},{112,80},{1... | collective-permute-start | bytes 393224 | tf_op jit(solution)/shard_map/ppermute | solution.py:603
  182.0 5.6 %collective-permute-start.35 = (f32[4,2,32,256]{3,2,1,0:T(8,128)S(1)}, f32[4,2,32,256]{3,2,1,0:T(8,128)S(1)}, u32[]{:S(2)}, u32[]{:S(2)}) collective-permute-start(f32[4,2,32,256]{3,2,1,0:T(8,128)S(1)} %stack_kernel.3), channel_id=1, source_target_pairs={{0,16},{16,0},{32,48},{48,32},{64,80},{80,64},{96,112},{112,96},{1... | collective-permute-start | bytes 786440 | tf_op jit(solution)/shard_map/ppermute | solution.py:607
  189.2 3.4 %collective-permute-start.36 = (f32[2,128,256]{2,1,0:T(8,128)S(1)}, f32[2,128,256]{2,1,0:T(8,128)S(1)}, u32[]{:S(2)}, u32[]{:S(2)}) collective-permute-start(f32[2,128,256]{2,1,0:T(8,128)S(1)} %get-tuple-element.124), channel_id=1, source_target_pairs={{0,16},{16,0},{32,48},{48,32},{64,80},{80,64},{96,112},{112,96},{1... | collective-permute-start | bytes 786440 | tf_op jit(solution)/shard_map/ppermute | solution.py:607
  189.6 14.1 %collective-permute-start.39 = (f32[2,32,1024]{2,1,0:T(8,128)S(1)}, f32[2,32,1024]{2,1,0:T(8,128)}, u32[]{:S(2)}, u32[]{:S(2)}) collective-permute-start(f32[2,32,1024]{2,1,0:T(8,128)S(1)} %get-tuple-element.127.refs_6_), channel_id=1, source_target_pairs={{0,96},{16,112},{32,0},{48,16},{64,32},{80,48},{96,64},{112,80},{1... | collective-permute-start | bytes 786440 | tf_op jit(solution)/shard_map/ppermute | solution.py:603
  192.0 11.7 %collective-permute-start.38 = (f32[2,32,1024]{2,1,0:T(8,128)S(1)}, f32[2,32,1024]{2,1,0:T(8,128)}, u32[]{:S(2)}, u32[]{:S(2)}) collective-permute-start(f32[2,32,1024]{2,1,0:T(8,128)S(1)} %get-tuple-element.127.refs_6_), channel_id=1, source_target_pairs={{0,64},{16,80},{32,96},{48,112},{64,0},{80,16},{96,32},{112,48},{1... | collective-permute-start | bytes 786440 | tf_op jit(solution)/shard_map/ppermute | solution.py:603
  192.0 14.9 %collective-permute-start.37 = (f32[2,32,1024]{2,1,0:T(8,128)S(1)}, f32[2,32,1024]{2,1,0:T(8,128)}, u32[]{:S(2)}, u32[]{:S(2)}) collective-permute-start(f32[2,32,1024]{2,1,0:T(8,128)S(1)} %get-tuple-element.127.refs_6_), channel_id=1, source_target_pairs={{0,32},{16,48},{32,64},{48,80},{64,96},{80,112},{96,0},{112,16},{1... | collective-permute-start | bytes 786440 | tf_op jit(solution)/shard_map/ppermute | solution.py:603
  194.0 21.8 %collective-permute-start.41 = (f32[8,128,256]{2,1,0:T(8,128)S(1)}, f32[8,128,256]{2,1,0:T(8,128)S(1)}, u32[]{:S(2)}, u32[]{:S(2)}) collective-permute-start(f32[8,128,256]{2,1,0:T(8,128)S(1)} %get-tuple-element.129.refs_3_), channel_id=1, source_target_pairs={{0,16},{16,0},{32,48},{48,32},{64,80},{80,64},{96,112},{112,96},{1... | collective-permute-start | bytes 3145736 | tf_op jit(solution)/shard_map/ppermute | solution.py:607
  196.2 17.2 %all-to-all-start.6 = ((f32[128,1,128]{2,1,0:T(1,128)}), f32[128,1,128]{2,1,0:T(1,128)S(1)}, u32[]{:S(2)}, u32[]{:S(2)}) async-start(f32[128,1,128]{2,1,0:T(1,128)} %bitcast.32), calls=%async_computation.6 | async-start | bytes 131072 | tf_op jit(solution)/shard_map/all_to_all | solution.py:783
  215.0 3.9 %collective-permute-start.40 = (f32[4,2,32,1024]{3,2,1,0:T(8,128)S(1)}, f32[4,2,32,1024]{3,2,1,0:T(8,128)S(1)}, u32[]{:S(2)}, u32[]{:S(2)}) collective-permute-start(f32[4,2,32,1024]{3,2,1,0:T(8,128)S(1)} %combine_kernel.1.refs_2_), channel_id=1, source_target_pairs={{0,16},{16,0},{32,48},{48,32},{64,80},{80,64},{96,112},{112,96},{1... | collective-permute-start | bytes 3145736 | tf_op jit(solution)/shard_map/ppermute | solution.py:607
  (2 other events, 1.5 us)

commit v6 on v5

--- a/solution.py
+++ b/solution.py
@@ -200,7 +200,9 @@
         obj[plane, 1] += value[:, H:]
 
     def forward(k):
-        if not first:
+        if first:
+            ready(5, k)
+        else:
             ready(4, k)
             for part in range(2):
                 moved = probe_step * joined(first_core, dmine, doth, 2 * k + part)
@@ -389,8 +391,11 @@
         dest[1] = dr * oi - di * orr
 
 
-def pack_kernel(keep, came, mine, part, chip, b0, b1, b2, b3):
-    chip[...] = keep[...] + came[...]
+def pack_kernel(ready, leave, keep, came, mine, part, chip, b0, b1, b2, b3):
+    for piece in range(4):
+        tiles = slice(4 * piece, 4 * piece + 4)
+        chip[tiles] = keep[tiles] + came[tiles]
+        leave(0, piece)
     for s, dest in enumerate((b0, b1, b2, b3)):
         dest[0] = mine[s]
         dest[1] = part[s]
@@ -401,7 +406,7 @@
     token[0, 0] = 0.0
 
 
-def share_kernel(own, a, b, d, above, below, near_rows, spread_out, sums):
+def share_kernel(own, a, b, d, above, below, near_rows, spread_out, sums, block, sems):
     total = own[...] + a[...] + b[...] + d[...]
     illum = total[8]
     value = total[:8] * (1.0 / (illum + RIDGE))
@@ -411,11 +416,17 @@
         pr, pi = near_rows[2 * k], near_rows[2 * k + 1]
         inner_real += pr * value[2 * k] + pi * value[2 * k + 1]
         inner_imag += pr * value[2 * k + 1] - pi * value[2 * k]
-    value_out = jnp.concatenate([value, inner_real[None], inner_imag[None]], axis=0)
-    spread_out[...] = jnp.broadcast_to(value_out[None], (16, 10, 8, N))
+    block[:8] = value
+    block[8] = inner_real
+    block[9] = inner_imag
+    copies = [pltpu.make_async_copy(block, spread_out.at[i], sems.at[i]) for i in range(16)]
+    for copy in copies:
+        copy.start()
     size = jnp.sum(value * value, axis=0)
     sums[0, 0] = jnp.sum(size * illum)
     sums[0, 1] = jnp.sum(size)
+    for copy in copies:
+        copy.wait()
 
 
 def message_kernel(where, gathered, kept, came, ae, df, out, planes):
@@ -487,6 +498,7 @@
     vmem_out=(),
     hbm_in=(),
     any_in=(),
+    raw_out=(),
     lazy=False,
     staged_in=False,
     cheap=False,
@@ -497,7 +509,7 @@
     outs = [out if isinstance(out[0], tuple) else (out, F32) for out in outs]
     shapes = [
         pltpu.HBM(*out)
-        if i in hbm_out
+        if i in hbm_out or i in raw_out
         else pltpu.VMEM(*out)
         if i in vmem_out
         else jax.ShapeDtypeStruct(*out)
@@ -585,10 +597,13 @@
         out_shape=shapes,
         in_specs=[space(i, smem_in, hbm_in) for i in range(len(args))],
         out_specs=[
-            hbm if i in hbm_out else SMEM if i in smem_out else VMEM for i in range(len(outs))
+            hbm if i in hbm_out or i in raw_out else SMEM if i in smem_out else VMEM for i in range(len(outs))
         ],
         scratch_shapes=[
-            pltpu.VMEM(shape, F32) if shape else pltpu.SemaphoreType.DMA for shape in scratch
+            pltpu.VMEM(shape, F32)
+            if isinstance(shape, tuple)
+            else pltpu.SemaphoreType.DMA((shape,) if shape else ())
+            for shape in scratch
         ]
         + extra,
         name=name or kernel.__name__,
@@ -681,6 +696,7 @@
                 ),
                 (0, 1),
                 scratch,
+                hbm_in={5: 4},
                 lazy=True,
                 flops=6 * 10**9,
                 room=28,
@@ -719,7 +735,8 @@
             (sent,) + ((2, 2, 32, N),) * 4,
             (keep, partner(send), mine, partner(other)),
             (),
-            hbm_out=(0,),
+            hbm_out={0: 4},
+            lazy=True,
         )
         came = [b0, along_y(b1, 1), along_y(b2, 2), along_y(b3, 3)]
         (illum,) = call(
@@ -747,8 +764,9 @@
             ((16, 10, 8, N), (1, 2)),
             (share, *[along_y(share, s) for s in range(1, 4)], above, below, near_rows),
             (),
+            ((10, 8, N), 16),
             smem_out=(1,),
-            hbm_out=(0,),
+            raw_out=(0,),
             any_in=(4, 5),
         )
         gathered = lax.all_to_all(probe_dir, "tile", 0, 0)

time: 223 us -> 223 us (level)
  transfers between devices with their start and end apart: 49 -> 49, of which waited for: 28 -> 29; matrix products, arithmetic and copies ran while one was open for 0% -> 0% of each run, Pallas kernels for 10% -> 10%
where the time goes in v6:
time: 223 us; the launch traced here: 222 us
  starting transfers between devices  102 us (46%)
  waiting for transfers between devices  63.8 us (29%)
  Pallas kernels  53.8 us (24%)
    pallas_call x26, Pallas kernels, call(): pl.pallas_call(run, out_shape=shapes, in_specs=[space(i, smem_in, hbm_in)...  52 us
    ppermute x24, waiting for transfers between devices, along_y(): return lax.ppermute(value, 'pat', [(i, (i + 2 * s) % 8) for i in range(8)])  28.3 us
    ppermute x24, starting transfers between devices, along_y(): return lax.ppermute(value, 'pat', [(i, (i + 2 * s) % 8) for i in range(8)])  27.3 us
    ppermute x12, starting transfers between devices, partner(): return lax.ppermute(value, 'pat', [(i, i ^ 1) for i in range(8)])  18.9 us
    all_to_all x2, starting transfers between devices, body(): messages.append(lax.all_to_all(message, BOTH, 0, 0))  14.9 us
    ppermute x3, starting transfers between devices, down(): return lax.ppermute(value, 'tile', [((i + 1) % 16, i) for i in range(16)])  12.6 us
    ppermute x12, waiting for transfers between devices, partner(): return lax.ppermute(value, 'pat', [(i, i ^ 1) for i in range(8)])  10.5 us
    all_to_all x2, starting transfers between devices, body(): shares = lax.all_to_all(chip, 'tile', 0, 0)  9.96 us
  transfers between devices with their start and end apart: 49, of which 29 were waited for; matrix products, arithmetic and copies ran while one was open for 0% of the time, Pallas kernels for 10%

profile of v6, /device:TPU:1, one launch (start us, length us, event | category | flops | bytes accessed | tf_op | source)
XLA Modules:
  0.0 222.2 jit_solution(13700459103631120195)
XLA Ops:
  0.8 1.8 shard_map.77
  2.5 2.1 collective-permute-start
  4.6 4.8 %collective-permute-start.1 = (f32[128,1024]{1,0:T(8,128)S(1)}, f32[128,1024]{1,0:T(8,128)S(1)}, u32[]{:S(2)}, u32[]{:S(2)}) collective-permute-start(f32[128,1024]{1,0:T(8,128)S(1)} %get-tuple-element.68), channel_id=1, source_target_pairs={{1,0},{2,1},{3,2},{4,3},{5,4},{6,5},{7,6},{8,7},{9,8},{10,9},{11,1... | collective-permute-start | bytes 1572872 | tf_op jit(solution)/shard_map/ppermute | solution.py:630
  10.6 5.4 %all-to-all-start = ((s32[8,1,128]{2,1,0:T(1,128)}), s32[8,1,128]{2,1,0:T(1,128)S(1)}, u32[]{:S(2)}, u32[]{:S(2)}) async-start(s32[8,1,128]{2,1,0:T(1,128)} %bitcast.5), calls=%async_computation | async-start | bytes 8192 | tf_op jit(solution)/shard_map/all_to_all | solution.py:653
  16.0 2.5 %prepare_kernel.1 = (f32[2,128,256]{2,1,0:T(8,128)S(1)}, f32[2,256,256]{2,1,0:T(8,128)S(1)}) custom-call(s32[4]{0:T(128)S(1)} %pad_add_fusion.refs_0_.where, s32[1,2]{1,0:T(1,128)S(1)} %copy-done.12, f32[256,256]{1,0:T(8,128)S(1)} %bitcast.28, bf16[2,256,256]{2,1,0:T(8,128)(2,1)S(1)} %copy-done.9, f32[2,256,1024]{2,1,0:T(8,128)} %refs_1_.7), custom_call_target="tpu_custom_call" | custom-call | bytes 3670040 | tf_op jit(solution)/shard_map/prepare_kernel/pallas_call | solution.py:595
  18.5 2.3 %all-to-all-done = s32[8,1,128]{2,1,0:T(1,128)S(1)} async-done(((s32[8,1,128]{2,1,0:T(1,128)}), s32[8,1,128]{2,1,0:T(1,128)S(1)}, u32[]{:S(2)}, u32[]{:S(2)}) %all-to-all-start) | async-done | bytes 4128 | tf_op jit(solution)/shard_map/all_to_all | solution.py:653
  21.8 1.3 collective-permute-start.2
  23.1 1.5 collective-permute-done.2.refs_4_
  24.6 7.9 %patterns.2 = (f32[2,256,256]{2,1,0:T(8,128)S(1)}, f32[16,9,8,256]{3,2,1,0:T(8,128)S(1)}, f32[16,9,8,256]{3,2,1,0:T(8,128)S(1)}, f32[4,2,32,256]{3,2,1,0:T(8,128...) custom-call(s32[4]{0:T(128)S(1)} %pad_add_fusion.refs_0_.where, ...), custom_call_target="tpu_custom_call" | custom-call | flops 6000000000 | bytes 9764888 | tf_op jit(solution)/shard_map/patterns/pallas_call | solution.py:595
  33.2 2.7 %collective-permute-done.4.refs_3_ = f32[4,2,32,256]{3,2,1,0:T(8,128)S(1)} collective-permute-done((f32[4,2,32,256]{3,2,1,0:T(8,128)S(1)}, f32[4,2,32,256]{3,2,1,0:T(8,128)S(1)}, u32[]{:S(2)}, u32[]{:S(2)}) %collective-permute-start.4) | collective-permute-done | bytes 262176 | tf_op jit(solution)/shard_map/ppermute | solution.py:622
  37.0 6.3 %all-to-all-start.1 = ((f32[16,9,8,256]{3,2,1,0:T(8,128)}), f32[16,9,8,256]{3,2,1,0:T(8,128)S(1)}, u32[]{:S(2)}, u32[]{:S(2)}) async-start(f32[16,9,8,256]{3,2,1,0:T(8,128)} %get-tuple-element.82), calls=%async_computation.1 | async-start | bytes 2359296 | tf_op jit(solution)/shard_map/all_to_all | solution.py:758
  43.2 1.4 collective-permute-start.5
  44.6 2.6 %collective-permute-start.6 = (f32[2,2,32,256]{3,2,1,0:T(8,128)S(1)}, f32[2,2,32,256]{3,2,1,0:T(8,128)S(1)}, u32[]{:S(2)}, u32[]{:S(2)}) collective-permute-start(f32[2,2,32,256]{3,2,1,0:T(8,128)S(1)} %get-tuple-element.79), channel_id=1, source_target_pairs={{0,64},{16,80},{32,96},{48,112},{64,0},{80,16},{96,32},{112,48},{1... | collective-permute-start | bytes 393224 | tf_op jit(solution)/shard_map/ppermute | solution.py:618
  49.2 3.7 %collective-permute-done.6.refs_5_ = f32[2,2,32,256]{3,2,1,0:T(8,128)S(1)} collective-permute-done((f32[2,2,32,256]{3,2,1,0:T(8,128)S(1)}, f32[2,2,32,256]{3,2,1,0:T(8,128)S(1)}, u32[]{:S(2)}, u32[]{:S(2)}) %collective-permute-start.6) | collective-permute-done | bytes 131104 | tf_op jit(solution)/shard_map/ppermute | solution.py:618
  53.0 1.4 place_kernel.2
  55.4 3.8 %collective-permute-start.12 = (f32[3,32,1024]{2,1,0:T(8,128)S(1)}, f32[3,32,1024]{2,1,0:T(8,128)S(1)}, u32[]{:S(2)}, u32[]{:S(2)}) collective-permute-start(f32[3,32,1024]{2,1,0:T(8,128)S(1)} %get-tuple-element.85.refs_3_), channel_id=1, source_target_pairs={{1,0},{2,1},{3,2},{4,3},{5,4},{6,5},{7,6},{8,7},{9,8},{10,9},{11,1... | collective-permute-start | bytes 1179656 | tf_op jit(solution)/shard_map/ppermute | solution.py:630
  59.2 1.9 all-to-all-done.1.refs_1_
  61.2 1.2 sum_kernel.2
  62.4 2.8 %collective-permute-start.10 = (f32[9,8,256]{2,1,0:T(8,128)S(1)}, f32[9,8,256]{2,1,0:T(8,128)S(1)}, u32[]{:S(2)}, u32[]{:S(2)}) collective-permute-start(f32[9,8,256]{2,1,0:T(8,128)S(1)} %get-tuple-element.83.refs_0_), channel_id=1, source_target_pairs={{0,96},{16,112},{32,0},{48,16},{64,32},{80,48},{96,64},{112,80},{1... | collective-permute-start | bytes 221192 | tf_op jit(solution)/shard_map/ppermute | solution.py:618
  66.2 3.7 %collective-permute-done.11.refs_4_.refs_5_ = f32[3,32,1024]{2,1,0:T(8,128)S(1)} collective-permute-done((f32[3,32,1024]{2,1,0:T(8,128)S(1)}, f32[3,32,1024]{2,1,0:T(8,128)S(1)}, u32[]{:S(2)}, u32[]{:S(2)}) %collective-permute-start.11) | collective-permute-done | bytes 393248 | tf_op jit(solution)/shard_map/ppermute | solution.py:626
  70.8 1.8 share_kernel.2
  72.6 4.4 %all-to-all-start.2 = ((f32[16,10,8,256]{3,2,1,0:T(8,128)}), f32[16,10,8,256]{3,2,1,0:T(8,128)S(1)}, u32[]{:S(2)}, u32[]{:S(2)}) async-start(f32[16,10,8,256]{3,2,1,0:T(8,128)} %get-tuple-element.87), calls=%async_computation.2 | async-start | bytes 2621440 | tf_op jit(solution)/shard_map/all_to_all | solution.py:772
  77.1 1.5 direction_kernel.2
  79.5 2.8 %collective-permute-start.14 = (f32[2,2,32,256]{3,2,1,0:T(8,128)S(1)}, f32[2,2,32,256]{3,2,1,0:T(8,128)S(1)}, u32[]{:S(2)}, u32[]{:S(2)}) collective-permute-start(f32[2,2,32,256]{3,2,1,0:T(8,128)S(1)} %get-tuple-element.91), channel_id=1, source_target_pairs={{0,64},{16,80},{32,96},{48,112},{64,0},{80,16},{96,32},{112,48},{1... | collective-permute-start | bytes 393224 | tf_op jit(solution)/shard_map/ppermute | solution.py:618
  84.3 1.7 collective-permute-done.14.refs_2_.refs_4_
  86.6 5.1 %collective-permute-start.16 = (f32[4,2,32,256]{3,2,1,0:T(8,128)S(1)}, f32[4,2,32,256]{3,2,1,0:T(8,128)S(1)}, u32[]{:S(2)}, u32[]{:S(2)}) collective-permute-start(f32[4,2,32,256]{3,2,1,0:T(8,128)S(1)} %stack_kernel.2), channel_id=1, source_target_pairs={{0,16},{16,0},{32,48},{48,32},{64,80},{80,64},{96,112},{112,96},{1... | collective-permute-start | bytes 786440 | tf_op jit(solution)/shard_map/ppermute | solution.py:622
  91.7 1.2 collective-permute-done.16.refs_6_
  95.0 1.2 collective-permute-done.17.refs_3_
  96.2 2.4 %message_kernel.2 = (f32[128,128]{1,0:T(8,128)}, f32[8,128,256]{2,1,0:T(8,128)}) custom-call(s32[4]{0:T(128)S(1)} %pad_add_fusion.refs_0_.where, f32[16,10,8,256]{3,2,1,0:T(8,128)S(1)} %all-to-all-done.2.refs_1_, f32[2,128,256]{2,1,0:T(8,128)S(1)} %get-tuple-element.94.refs_2_, f32[2,128,256]{2,1,0:T(8,128)S(1)} %collective-permute-done.17.refs_3_, ...), custom_call_target="tpu_custom_call" | custom-call | bytes 2949152 | tf_op jit(solution)/shard_map/message_kernel/pallas_call | solution.py:595
  98.6 2.7 %collective-permute-start.18 = (f32[8,128,256]{2,1,0:T(8,128)}, f32[8,128,256]{2,1,0:T(8,128)S(1)}, u32[]{:S(2)}, u32[]{:S(2)}) collective-permute-start(f32[8,128,256]{2,1,0:T(8,128)} %get-tuple-element.99.refs_8_), channel_id=1, source_target_pairs={{0,16},{16,0},{32,48},{48,32},{64,80},{80,64},{96,112},{112,96},{1... | collective-permute-start | bytes 3145736 | tf_op jit(solution)/shard_map/ppermute | solution.py:622
  101.3 1.6 collective-permute-start.21
  104.1 7.4 %all-to-all-start.3 = ((f32[128,1,128]{2,1,0:T(1,128)}), f32[128,1,128]{2,1,0:T(1,128)S(1)}, u32[]{:S(2)}, u32[]{:S(2)}) async-start(f32[128,1,128]{2,1,0:T(1,128)} %bitcast.31), calls=%async_computation.3 | async-start | bytes 131072 | tf_op jit(solution)/shard_map/all_to_all | solution.py:801
  111.9 6.8 %collective-permute-done.19.refs_10_.refs_3_ = f32[2,32,1024]{2,1,0:T(8,128)S(1)} collective-permute-done((f32[2,32,1024]{2,1,0:T(8,128)S(1)}, f32[2,32,1024]{2,1,0:T(8,128)S(1)}, u32[]{:S(2)}, u32[]{:S(2)}) %collective-permute-start.19) | collective-permute-done | bytes 262176 | tf_op jit(solution)/shard_map/ppermute | solution.py:618
  118.8 2.4 %all-to-all-done.3 = f32[128,1,128]{2,1,0:T(1,128)S(1)} async-done(((f32[128,1,128]{2,1,0:T(1,128)}), f32[128,1,128]{2,1,0:T(1,128)S(1)}, u32[]{:S(2)}, u32[]{:S(2)}) %all-to-all-start.3) | async-done | bytes 65568 | tf_op jit(solution)/shard_map/all_to_all | solution.py:801
  121.2 9.8 %patterns.3 = (f32[2,256,256]{2,1,0:T(8,128)}, f32[4,2,256,256]{3,2,1,0:T(8,128)}, f32[16,9,8,256]{3,2,1,0:T(8,128)S(1)}, f32[16,9,8,256]{3,2,1,0:T(8,128)S(1)},...) custom-call(s32[4]{0:T(128)S(1)} %pad_add_fusion.refs_0_.where, ...), custom_call_target="tpu_custom_call" | custom-call | flops 6000000000 | bytes 14286872 | tf_op jit(solution)/shard_map/patterns/pallas_call | solution.py:595
  131.9 2.8 %collective-permute-done.23.refs_3_ = f32[4,2,32,256]{3,2,1,0:T(8,128)S(1)} collective-permute-done((f32[4,2,32,256]{3,2,1,0:T(8,128)S(1)}, f32[4,2,32,256]{3,2,1,0:T(8,128)S(1)}, u32[]{:S(2)}, u32[]{:S(2)}) %collective-permute-start.23) | collective-permute-done | bytes 262176 | tf_op jit(solution)/shard_map/ppermute | solution.py:622
  135.8 3.7 %all-to-all-start.4 = ((f32[16,9,8,256]{3,2,1,0:T(8,128)}), f32[16,9,8,256]{3,2,1,0:T(8,128)S(1)}, u32[]{:S(2)}, u32[]{:S(2)}) async-start(f32[16,9,8,256]{3,2,1,0:T(8,128)} %get-tuple-element.111), calls=%async_computation.4 | async-start | bytes 2359296 | tf_op jit(solution)/shard_map/all_to_all | solution.py:758
  139.9 1.7 collective-permute-start.25
  143.3 2.7 %collective-permute-done.24.refs_4_ = f32[2,2,32,256]{3,2,1,0:T(8,128)S(1)} collective-permute-done((f32[2,2,32,256]{3,2,1,0:T(8,128)S(1)}, f32[2,2,32,256]{3,2,1,0:T(8,128)S(1)}, u32[]{:S(2)}, u32[]{:S(2)}) %collective-permute-start.24) | collective-permute-done | bytes 131104 | tf_op jit(solution)/shard_map/ppermute | solution.py:618
  146.0 1.7 collective-permute-done.25.refs_5_
  148.6 1.4 place_kernel.3
  150.8 4.0 %collective-permute-start.31 = (f32[3,32,1024]{2,1,0:T(8,128)S(1)}, f32[3,32,1024]{2,1,0:T(8,128)S(1)}, u32[]{:S(2)}, u32[]{:S(2)}) collective-permute-start(f32[3,32,1024]{2,1,0:T(8,128)S(1)} %get-tuple-element.114.refs_3_), channel_id=1, source_target_pairs={{1,0},{2,1},{3,2},{4,3},{5,4},{6,5},{7,6},{8,7},{9,8},{10,9},{11,1... | collective-permute-start | bytes 1179656 | tf_op jit(solution)/shard_map/ppermute | solution.py:630
  154.8 3.2 %all-to-all-done.4.refs_1_ = f32[16,9,8,256]{3,2,1,0:T(8,128)S(1)} async-done(((f32[16,9,8,256]{3,2,1,0:T(8,128)}), f32[16,9,8,256]{3,2,1,0:T(8,128)S(1)}, u32[]{:S(2)}, u32[]{:S(2)}) %all-to-all-start.4) | async-done | bytes 1179680 | tf_op jit(solution)/shard_map/all_to_all | solution.py:758
  158.1 1.2 sum_kernel.3
  159.3 1.6 collective-permute-start.29
  160.8 1.3 collective-permute-start.28
  162.2 4.7 %collective-permute-done.30.refs_4_.refs_5_ = f32[3,32,1024]{2,1,0:T(8,128)S(1)} collective-permute-done((f32[3,32,1024]{2,1,0:T(8,128)S(1)}, f32[3,32,1024]{2,1,0:T(8,128)S(1)}, u32[]{:S(2)}, u32[]{:S(2)}) %collective-permute-start.30) | collective-permute-done | bytes 393248 | tf_op jit(solution)/shard_map/ppermute | solution.py:626
  166.9 1.8 share_kernel.3
  168.7 4.1 %all-to-all-start.5 = ((f32[16,10,8,256]{3,2,1,0:T(8,128)}), f32[16,10,8,256]{3,2,1,0:T(8,128)S(1)}, u32[]{:S(2)}, u32[]{:S(2)}) async-start(f32[16,10,8,256]{3,2,1,0:T(8,128)} %get-tuple-element.116), calls=%async_computation.5 | async-start | bytes 2621440 | tf_op jit(solution)/shard_map/all_to_all | solution.py:772
  172.8 1.5 direction_kernel.3
  174.4 2.6 %collective-permute-start.33 = (f32[2,2,32,256]{3,2,1,0:T(8,128)S(1)}, f32[2,2,32,256]{3,2,1,0:T(8,128)S(1)}, u32[]{:S(2)}, u32[]{:S(2)}) collective-permute-start(f32[2,2,32,256]{3,2,1,0:T(8,128)S(1)} %get-tuple-element.120), channel_id=1, source_target_pairs={{0,64},{16,80},{32,96},{48,112},{64,0},{80,16},{96,32},{112,48},{1... | collective-permute-start | bytes 393224 | tf_op jit(solution)/shard_map/ppermute | solution.py:618
  177.1 2.4 %collective-permute-done.32.refs_1_.refs_3_ = f32[2,2,32,256]{3,2,1,0:T(8,128)S(1)} collective-permute-done((f32[2,2,32,256]{3,2,1,0:T(8,128)S(1)}, f32[2,2,32,256]{3,2,1,0:T(8,128)S(1)}, u32[]{:S(2)}, u32[]{:S(2)}) %collective-permute-start.32) | collective-permute-done | bytes 131104 | tf_op jit(solution)/shard_map/ppermute | solution.py:618
  179.4 1.5 collective-permute-done.33.refs_2_.refs_4_
  181.8 4.5 %collective-permute-start.35 = (f32[4,2,32,256]{3,2,1,0:T(8,128)S(1)}, f32[4,2,32,256]{3,2,1,0:T(8,128)S(1)}, u32[]{:S(2)}, u32[]{:S(2)}) collective-permute-start(f32[4,2,32,256]{3,2,1,0:T(8,128)S(1)} %stack_kernel.3), channel_id=1, source_target_pairs={{0,16},{16,0},{32,48},{48,32},{64,80},{80,64},{96,112},{112,96},{1... | collective-permute-start | bytes 786440 | tf_op jit(solution)/shard_map/ppermute | solution.py:622
  187.4 1.7 patch_kernel.3
  189.4 2.4 %collective-permute-start.39 = (f32[2,32,1024]{2,1,0:T(8,128)S(1)}, f32[2,32,1024]{2,1,0:T(8,128)}, u32[]{:S(2)}, u32[]{:S(2)}) collective-permute-start(f32[2,32,1024]{2,1,0:T(8,128)S(1)} %get-tuple-element.127.refs_6_), channel_id=1, source_target_pairs={{0,96},{16,112},{32,0},{48,16},{64,32},{80,48},{96,64},{112,80},{1... | collective-permute-start | bytes 786440 | tf_op jit(solution)/shard_map/ppermute | solution.py:618
  192.4 1.4 message_kernel.3
  193.9 2.1 collective-permute-start.41
  196.0 7.5 %all-to-all-start.6 = ((f32[128,1,128]{2,1,0:T(1,128)}), f32[128,1,128]{2,1,0:T(1,128)S(1)}, u32[]{:S(2)}, u32[]{:S(2)}) async-start(f32[128,1,128]{2,1,0:T(1,128)} %bitcast.32), calls=%async_computation.6 | async-start | bytes 131072 | tf_op jit(solution)/shard_map/all_to_all | solution.py:801
  203.6 3.2 %collective-permute-done.37.refs_7_ = f32[2,32,1024]{2,1,0:T(8,128)} collective-permute-done((f32[2,32,1024]{2,1,0:T(8,128)S(1)}, f32[2,32,1024]{2,1,0:T(8,128)}, u32[]{:S(2)}, u32[]{:S(2)}) %collective-permute-start.37) | collective-permute-done | bytes 262176 | tf_op jit(solution)/shard_map/ppermute | solution.py:618
  206.7 6.5 %all-to-all-done.6 = f32[128,1,128]{2,1,0:T(1,128)S(1)} async-done(((f32[128,1,128]{2,1,0:T(1,128)}), f32[128,1,128]{2,1,0:T(1,128)S(1)}, u32[]{:S(2)}, u32[]{:S(2)}) %all-to-all-start.6) | async-done | bytes 65568 | tf_op jit(solution)/shard_map/all_to_all | solution.py:801
  213.2 1.6 combine_kernel.1.refs_2_
  215.7 3.0 %probe_kernel.1 = f32[4,2,256,256]{3,2,1,0:T(8,128)} custom-call(s32[4]{0:T(128)S(1)} %pad_add_fusion.refs_0_.where, f32[128,128]{1,0:T(8,128)S(1)} %bitcast.18, f32[4,2,256,256]{3,2,1,0:T(8,128)} %get-tuple-element.128.refs_2_, f32[8,128,256]{2,1,0:T(8,128)S(1)} %get-tuple-element.129.refs_3_, f32[8,128,256]{2,1,0:T(8,128)S(1)} %collective-permute-done.41.refs_4_), custom_call_target="tpu_custom_call" | custom-call | flops 1000000000 | bytes 6357008 | tf_op jit(solution)/shard_map/probe_kernel/pallas_call | solution.py:595
  218.8 3.2 %object_kernel.1 = f32[2,256,1024]{2,1,0:T(8,128)} custom-call(s32[4]{0:T(128)S(1)} %pad_add_fusion.refs_0_.where, f32[2,256,1024]{2,1,0:T(8,128)} %refs_1_.7, f32[4,2,32,1024]{3,2,1,0:T(8,128)S(1)} %combine_kernel.1.refs_2_, f32[4,2,32,1024]{3,2,1,0:T(8,128)S(1)} %collective-permute-done.40.refs_3_), custom_call_target="tpu_custom_call" | custom-call | bytes 6291472 | tf_op jit(solution)/shard_map/object_kernel/pallas_call | solution.py:595
  (94 shorter events, 25.9 us)
Async XLA Ops:
  0.6 15.4 %copy-start.9 = (bf16[2,256,256]{2,1,0:T(8,128)(2,1)S(1)}, bf16[2,256,256]{2,1,0:T(8,128)(2,1)}, u32[]{:S(2)}) copy-start(bf16[2,256,256]{2,1,0:T(8,128)(2,1)} %constant.43.clone.refs_3_) | copy-start | bytes 786436
  0.6 8.8 %copy-start.12 = (s32[1,2]{1,0:T(1,128)S(1)}, s32[1,2]{1,0:T(1,128)}, u32[]{:S(2)}) copy-start(s32[1,2]{1,0:T(1,128)} %refs_1_.6) | copy-start | bytes 28
  0.7 15.4 %copy-start.2 = (f32[1,256,256]{2,1,0:T(8,128)S(1)}, f32[1,256,256]{2,1,0:T(8,128)}, u32[]{:S(2)}) copy-start(f32[1,256,256]{2,1,0:T(8,128)} %param.6) | copy-start | bytes 786436
  2.5 18.5 %collective-permute-start = (f32[128,1024]{1,0:T(8,128)S(1)}, f32[128,1024]{1,0:T(8,128)S(1)}, u32[]{:S(2)}, u32[]{:S(2)}) collective-permute-start(f32[128,1024]{1,0:T(8,128)S(1)} %get-tuple-element.67), channel_id=1, source_target_pairs={{0,1},{1,2},{2,3},{3,4},{4,5},{5,6},{6,7},{7,8},{8,9},{9,10},{10,1... | collective-permute-start | bytes 1572872 | tf_op jit(solution)/shard_map/ppermute | solution.py:626
  4.6 16.4 %collective-permute-start.1 = (f32[128,1024]{1,0:T(8,128)S(1)}, f32[128,1024]{1,0:T(8,128)S(1)}, u32[]{:S(2)}, u32[]{:S(2)}) collective-permute-start(f32[128,1024]{1,0:T(8,128)S(1)} %get-tuple-element.68), channel_id=1, source_target_pairs={{1,0},{2,1},{3,2},{4,3},{5,4},{6,5},{7,6},{8,7},{9,8},{10,9},{11,1... | collective-permute-start | bytes 1572872 | tf_op jit(solution)/shard_map/ppermute | solution.py:630
  10.6 10.2 %all-to-all-start = ((s32[8,1,128]{2,1,0:T(1,128)}), s32[8,1,128]{2,1,0:T(1,128)S(1)}, u32[]{:S(2)}, u32[]{:S(2)}) async-start(s32[8,1,128]{2,1,0:T(1,128)} %bitcast.5), calls=%async_computation | async-start | bytes 8192 | tf_op jit(solution)/shard_map/all_to_all | solution.py:653
  18.5 14.0 %copy-start.14 = (f32[2,128,256]{2,1,0:T(8,128)}, f32[2,128,256]{2,1,0:T(8,128)S(1)}, u32[]{:S(2)}) copy-start(f32[2,128,256]{2,1,0:T(8,128)S(1)} %get-tuple-element.71.refs_6_.refs_5_) | copy-start | bytes 786436
  20.8 3.8 %copy-start.15 = (bf16[4,2,256,256]{3,2,1,0:T(8,128)(2,1)S(1)}, bf16[4,2,256,256]{3,2,1,0:T(8,128)(2,1)}, u32[]{:S(2)}) copy-start(bf16[4,2,256,256]{3,2,1,0:T(8,128)(2,1)} %constant.42.clone.refs_7_.refs_6_) | copy-start | bytes 3145732
  21.8 2.8 %collective-permute-start.2 = (f32[128,1024]{1,0:T(8,128)S(1)}, f32[128,1024]{1,0:T(8,128)S(1)}, u32[]{:S(2)}, u32[]{:S(2)}) collective-permute-start(f32[128,1024]{1,0:T(8,128)S(1)} %get-tuple-element.70), channel_id=1, source_target_pairs={{0,16},{16,0},{32,48},{48,32},{64,80},{80,64},{96,112},{112,96},{1... | collective-permute-start | bytes 1572872 | tf_op jit(solution)/shard_map/ppermute | solution.py:622
  32.5 4.4 %copy-start.10 = (f32[8,8,256]{2,1,0:T(8,128)}, f32[8,8,256]{2,1,0:T(8,128)S(1)}, u32[]{:S(2)}) copy-start(f32[8,8,256]{2,1,0:T(8,128)S(1)} %get-tuple-element.86.refs_6_) | copy-start | bytes 196612
  32.6 60.3 %copy-start = (f32[2,256,256]{2,1,0:T(8,128)}, f32[2,256,256]{2,1,0:T(8,128)S(1)}, u32[]{:S(2)}) copy-start(f32[2,256,256]{2,1,0:T(8,128)S(1)} %get-tuple-element.93.refs_7_.refs_3_) | copy-start | bytes 1572868
  32.6 3.3 %collective-permute-start.3 = (f32[16,9,8,256]{3,2,1,0:T(8,128)S(1)}, f32[16,9,8,256]{3,2,1,0:T(8,128)S(1)}, u32[]{:S(2)}, u32[]{:S(2)}) collective-permute-start(f32[16,9,8,256]{3,2,1,0:T(8,128)S(1)} %get-tuple-element.74), channel_id=1, source_target_pairs={{0,16},{16,0},{32,48},{48,32},{64,80},{80,64},{96,112},{112,96},{1... | collective-permute-start | bytes 3538952 | tf_op jit(solution)/shard_map/ppermute | solution.py:622
  33.0 2.8 %collective-permute-start.4 = (f32[4,2,32,256]{3,2,1,0:T(8,128)S(1)}, f32[4,2,32,256]{3,2,1,0:T(8,128)S(1)}, u32[]{:S(2)}, u32[]{:S(2)}) collective-permute-start(f32[4,2,32,256]{3,2,1,0:T(8,128)S(1)} %get-tuple-element.76), channel_id=1, source_target_pairs={{0,16},{16,0},{32,48},{48,32},{64,80},{80,64},{96,112},{112,96},{1... | collective-permute-start | bytes 786440 | tf_op jit(solution)/shard_map/ppermute | solution.py:622
  37.0 24.2 %all-to-all-start.1 = ((f32[16,9,8,256]{3,2,1,0:T(8,128)}), f32[16,9,8,256]{3,2,1,0:T(8,128)S(1)}, u32[]{:S(2)}, u32[]{:S(2)}) async-start(f32[16,9,8,256]{3,2,1,0:T(8,128)} %get-tuple-element.82), calls=%async_computation.1 | async-start | bytes 2359296 | tf_op jit(solution)/shard_map/all_to_all | solution.py:758
  43.2 6.0 %collective-permute-start.5 = (f32[2,2,32,256]{3,2,1,0:T(8,128)S(1)}, f32[2,2,32,256]{3,2,1,0:T(8,128)S(1)}, u32[]{:S(2)}, u32[]{:S(2)}) collective-permute-start(f32[2,2,32,256]{3,2,1,0:T(8,128)S(1)} %get-tuple-element.78), channel_id=1, source_target_pairs={{0,32},{16,48},{32,64},{48,80},{64,96},{80,112},{96,0},{112,16},{1... | collective-permute-start | bytes 393224 | tf_op jit(solution)/shard_map/ppermute | solution.py:618
  44.6 8.4 %collective-permute-start.6 = (f32[2,2,32,256]{3,2,1,0:T(8,128)S(1)}, f32[2,2,32,256]{3,2,1,0:T(8,128)S(1)}, u32[]{:S(2)}, u32[]{:S(2)}) collective-permute-start(f32[2,2,32,256]{3,2,1,0:T(8,128)S(1)} %get-tuple-element.79), channel_id=1, source_target_pairs={{0,64},{16,80},{32,96},{48,112},{64,0},{80,16},{96,32},{112,48},{1... | collective-permute-start | bytes 393224 | tf_op jit(solution)/shard_map/ppermute | solution.py:618
  47.2 5.7 %collective-permute-start.7 = (f32[2,2,32,256]{3,2,1,0:T(8,128)S(1)}, f32[2,2,32,256]{3,2,1,0:T(8,128)S(1)}, u32[]{:S(2)}, u32[]{:S(2)}) collective-permute-start(f32[2,2,32,256]{3,2,1,0:T(8,128)S(1)} %get-tuple-element.80), channel_id=1, source_target_pairs={{0,96},{16,112},{32,0},{48,16},{64,32},{80,48},{96,64},{112,80},{1... | collective-permute-start | bytes 393224 | tf_op jit(solution)/shard_map/ppermute | solution.py:618
  49.2 21.7 %copy-start.11 = (f32[8,8,256]{2,1,0:T(8,128)S(1)}, f32[8,8,256]{2,1,0:T(8,128)}, u32[]{:S(2)}) copy-start(f32[8,8,256]{2,1,0:T(8,128)} %copy-done.10) | copy-start | bytes 196612
  54.4 15.6 %collective-permute-start.11 = (f32[3,32,1024]{2,1,0:T(8,128)S(1)}, f32[3,32,1024]{2,1,0:T(8,128)S(1)}, u32[]{:S(2)}, u32[]{:S(2)}) collective-permute-start(f32[3,32,1024]{2,1,0:T(8,128)S(1)} %get-tuple-element.84.refs_4_), channel_id=1, source_target_pairs={{0,1},{1,2},{2,3},{3,4},{4,5},{5,6},{6,7},{7,8},{8,9},{9,10},{10,1... | collective-permute-start | bytes 1179656 | tf_op jit(solution)/shard_map/ppermute | solution.py:626
  55.4 14.5 %collective-permute-start.12 = (f32[3,32,1024]{2,1,0:T(8,128)S(1)}, f32[3,32,1024]{2,1,0:T(8,128)S(1)}, u32[]{:S(2)}, u32[]{:S(2)}) collective-permute-start(f32[3,32,1024]{2,1,0:T(8,128)S(1)} %get-tuple-element.85.refs_3_), channel_id=1, source_target_pairs={{1,0},{2,1},{3,2},{4,3},{5,4},{6,5},{7,6},{8,7},{9,8},{10,9},{11,1... | collective-permute-start | bytes 1179656 | tf_op jit(solution)/shard_map/ppermute | solution.py:630
  62.4 7.6 %collective-permute-start.10 = (f32[9,8,256]{2,1,0:T(8,128)S(1)}, f32[9,8,256]{2,1,0:T(8,128)S(1)}, u32[]{:S(2)}, u32[]{:S(2)}) collective-permute-start(f32[9,8,256]{2,1,0:T(8,128)S(1)} %get-tuple-element.83.refs_0_), channel_id=1, source_target_pairs={{0,96},{16,112},{32,0},{48,16},{64,32},{80,48},{96,64},{112,80},{1... | collective-permute-start | bytes 221192 | tf_op jit(solution)/shard_map/ppermute | solution.py:618
  65.2 5.0 %collective-permute-start.9 = (f32[9,8,256]{2,1,0:T(8,128)S(1)}, f32[9,8,256]{2,1,0:T(8,128)S(1)}, u32[]{:S(2)}, u32[]{:S(2)}) collective-permute-start(f32[9,8,256]{2,1,0:T(8,128)S(1)} %get-tuple-element.83.refs_0_), channel_id=1, source_target_pairs={{0,64},{16,80},{32,96},{48,112},{64,0},{80,16},{96,32},{112,48},{1... | collective-permute-start | bytes 221192 | tf_op jit(solution)/shard_map/ppermute | solution.py:618
  65.5 5.3 %collective-permute-start.8 = (f32[9,8,256]{2,1,0:T(8,128)S(1)}, f32[9,8,256]{2,1,0:T(8,128)S(1)}, u32[]{:S(2)}, u32[]{:S(2)}) collective-permute-start(f32[9,8,256]{2,1,0:T(8,128)S(1)} %get-tuple-element.83.refs_0_), channel_id=1, source_target_pairs={{0,32},{16,48},{32,64},{48,80},{64,96},{80,112},{96,0},{112,16},{1... | collective-permute-start | bytes 221192 | tf_op jit(solution)/shard_map/ppermute | solution.py:618
  72.6 23.5 %all-to-all-start.2 = ((f32[16,10,8,256]{3,2,1,0:T(8,128)}), f32[16,10,8,256]{3,2,1,0:T(8,128)S(1)}, u32[]{:S(2)}, u32[]{:S(2)}) async-start(f32[16,10,8,256]{3,2,1,0:T(8,128)} %get-tuple-element.87), calls=%async_computation.2 | async-start | bytes 2621440 | tf_op jit(solution)/shard_map/all_to_all | solution.py:772
  79.3 5.0 %collective-permute-start.13 = (f32[2,2,32,256]{3,2,1,0:T(8,128)S(1)}, f32[2,2,32,256]{3,2,1,0:T(8,128)S(1)}, u32[]{:S(2)}, u32[]{:S(2)}) collective-permute-start(f32[2,2,32,256]{3,2,1,0:T(8,128)S(1)} %get-tuple-element.90), channel_id=1, source_target_pairs={{0,32},{16,48},{32,64},{48,80},{64,96},{80,112},{96,0},{112,16},{1... | collective-permute-start | bytes 393224 | tf_op jit(solution)/shard_map/ppermute | solution.py:618
  79.5 6.6 %collective-permute-start.14 = (f32[2,2,32,256]{3,2,1,0:T(8,128)S(1)}, f32[2,2,32,256]{3,2,1,0:T(8,128)S(1)}, u32[]{:S(2)}, u32[]{:S(2)}) collective-permute-start(f32[2,2,32,256]{3,2,1,0:T(8,128)S(1)} %get-tuple-element.91), channel_id=1, source_target_pairs={{0,64},{16,80},{32,96},{48,112},{64,0},{80,16},{96,32},{112,48},{1... | collective-permute-start | bytes 393224 | tf_op jit(solution)/shard_map/ppermute | solution.py:618
  82.3 4.3 %collective-permute-start.15 = (f32[2,2,32,256]{3,2,1,0:T(8,128)S(1)}, f32[2,2,32,256]{3,2,1,0:T(8,128)S(1)}, u32[]{:S(2)}, u32[]{:S(2)}) collective-permute-start(f32[2,2,32,256]{3,2,1,0:T(8,128)S(1)} %get-tuple-element.92), channel_id=1, source_target_pairs={{0,96},{16,112},{32,0},{48,16},{64,32},{80,48},{96,64},{112,80},{1... | collective-permute-start | bytes 393224 | tf_op jit(solution)/shard_map/ppermute | solution.py:618
  86.6 6.3 %collective-permute-start.16 = (f32[4,2,32,256]{3,2,1,0:T(8,128)S(1)}, f32[4,2,32,256]{3,2,1,0:T(8,128)S(1)}, u32[]{:S(2)}, u32[]{:S(2)}) collective-permute-start(f32[4,2,32,256]{3,2,1,0:T(8,128)S(1)} %stack_kernel.2), channel_id=1, source_target_pairs={{0,16},{16,0},{32,48},{48,32},{64,80},{80,64},{96,112},{112,96},{1... | collective-permute-start | bytes 786440 | tf_op jit(solution)/shard_map/ppermute | solution.py:622
  93.8 0.8 copy-start.13
  94.6 6.7 %copy-start.4 = (f32[2,32,1024]{2,1,0:T(8,128)S(1)}, f32[2,32,1024]{2,1,0:T(8,128)}, u32[]{:S(2)}) copy-start(f32[2,32,1024]{2,1,0:T(8,128)} %copy-done.3) | copy-start | bytes 786436
  94.6 1.5 collective-permute-start.17
  98.6 22.6 %collective-permute-start.18 = (f32[8,128,256]{2,1,0:T(8,128)}, f32[8,128,256]{2,1,0:T(8,128)S(1)}, u32[]{:S(2)}, u32[]{:S(2)}) collective-permute-start(f32[8,128,256]{2,1,0:T(8,128)} %get-tuple-element.99.refs_8_), channel_id=1, source_target_pairs={{0,16},{16,0},{32,48},{48,32},{64,80},{80,64},{96,112},{112,96},{1... | collective-permute-start | bytes 3145736 | tf_op jit(solution)/shard_map/ppermute | solution.py:622
  101.3 10.2 %collective-permute-start.21 = (f32[2,32,1024]{2,1,0:T(8,128)S(1)}, f32[2,32,1024]{2,1,0:T(8,128)S(1)}, u32[]{:S(2)}, u32[]{:S(2)}) collective-permute-start(f32[2,32,1024]{2,1,0:T(8,128)S(1)} %copy-done.4), channel_id=1, source_target_pairs={{0,96},{16,112},{32,0},{48,16},{64,32},{80,48},{96,64},{112,80},{1... | collective-permute-start | bytes 786440 | tf_op jit(solution)/shard_map/ppermute | solution.py:618
  102.8 9.1 %collective-permute-start.20 = (f32[2,32,1024]{2,1,0:T(8,128)S(1)}, f32[2,32,1024]{2,1,0:T(8,128)S(1)}, u32[]{:S(2)}, u32[]{:S(2)}) collective-permute-start(f32[2,32,1024]{2,1,0:T(8,128)S(1)} %copy-done.4), channel_id=1, source_target_pairs={{0,64},{16,80},{32,96},{48,112},{64,0},{80,16},{96,32},{112,48},{1... | collective-permute-start | bytes 786440 | tf_op jit(solution)/shard_map/ppermute | solution.py:618
  103.2 15.6 %collective-permute-start.19 = (f32[2,32,1024]{2,1,0:T(8,128)S(1)}, f32[2,32,1024]{2,1,0:T(8,128)S(1)}, u32[]{:S(2)}, u32[]{:S(2)}) collective-permute-start(f32[2,32,1024]{2,1,0:T(8,128)S(1)} %copy-done.4), channel_id=1, source_target_pairs={{0,32},{16,48},{32,64},{48,80},{64,96},{80,112},{96,0},{112,16},{1... | collective-permute-start | bytes 786440 | tf_op jit(solution)/shard_map/ppermute | solution.py:618
  104.1 17.1 %all-to-all-start.3 = ((f32[128,1,128]{2,1,0:T(1,128)}), f32[128,1,128]{2,1,0:T(1,128)S(1)}, u32[]{:S(2)}, u32[]{:S(2)}) async-start(f32[128,1,128]{2,1,0:T(1,128)} %bitcast.31), calls=%async_computation.3 | async-start | bytes 131072 | tf_op jit(solution)/shard_map/all_to_all | solution.py:801
  111.5 19.5 %copy-start.5 = (f32[2,32,1024]{2,1,0:T(8,128)}, f32[2,32,1024]{2,1,0:T(8,128)S(1)}, u32[]{:S(2)}) copy-start(f32[2,32,1024]{2,1,0:T(8,128)S(1)} %collective-permute-done.21.refs_12_.refs_5_) | copy-start | bytes 786436
  111.9 19.1 %copy-start.6 = (f32[2,32,1024]{2,1,0:T(8,128)}, f32[2,32,1024]{2,1,0:T(8,128)S(1)}, u32[]{:S(2)}) copy-start(f32[2,32,1024]{2,1,0:T(8,128)S(1)} %collective-permute-done.20.refs_11_.refs_4_) | copy-start | bytes 786436
  118.8 12.2 %copy-start.7 = (f32[2,32,1024]{2,1,0:T(8,128)}, f32[2,32,1024]{2,1,0:T(8,128)S(1)}, u32[]{:S(2)}) copy-start(f32[2,32,1024]{2,1,0:T(8,128)S(1)} %collective-permute-done.19.refs_10_.refs_3_) | copy-start | bytes 786436
  131.0 3.7 %collective-permute-start.22 = (f32[16,9,8,256]{3,2,1,0:T(8,128)S(1)}, f32[16,9,8,256]{3,2,1,0:T(8,128)S(1)}, u32[]{:S(2)}, u32[]{:S(2)}) collective-permute-start(f32[16,9,8,256]{3,2,1,0:T(8,128)S(1)} %get-tuple-element.103), channel_id=1, source_target_pairs={{0,16},{16,0},{32,48},{48,32},{64,80},{80,64},{96,112},{112,96},{1... | collective-permute-start | bytes 3538952 | tf_op jit(solution)/shard_map/ppermute | solution.py:622
  131.8 2.8 %collective-permute-start.23 = (f32[4,2,32,256]{3,2,1,0:T(8,128)S(1)}, f32[4,2,32,256]{3,2,1,0:T(8,128)S(1)}, u32[]{:S(2)}, u32[]{:S(2)}) collective-permute-start(f32[4,2,32,256]{3,2,1,0:T(8,128)S(1)} %get-tuple-element.105), channel_id=1, source_target_pairs={{0,16},{16,0},{32,48},{48,32},{64,80},{80,64},{96,112},{112,96},{1... | collective-permute-start | bytes 786440 | tf_op jit(solution)/shard_map/ppermute | solution.py:622
  135.8 22.3 %all-to-all-start.4 = ((f32[16,9,8,256]{3,2,1,0:T(8,128)}), f32[16,9,8,256]{3,2,1,0:T(8,128)S(1)}, u32[]{:S(2)}, u32[]{:S(2)}) async-start(f32[16,9,8,256]{3,2,1,0:T(8,128)} %get-tuple-element.111), calls=%async_computation.4 | async-start | bytes 2359296 | tf_op jit(solution)/shard_map/all_to_all | solution.py:758
  139.5 6.5 %collective-permute-start.24 = (f32[2,2,32,256]{3,2,1,0:T(8,128)S(1)}, f32[2,2,32,256]{3,2,1,0:T(8,128)S(1)}, u32[]{:S(2)}, u32[]{:S(2)}) collective-permute-start(f32[2,2,32,256]{3,2,1,0:T(8,128)S(1)} %get-tuple-element.107), channel_id=1, source_target_pairs={{0,32},{16,48},{32,64},{48,80},{64,96},{80,112},{96,0},{112,16},{1... | collective-permute-start | bytes 393224 | tf_op jit(solution)/shard_map/ppermute | solution.py:618
  139.9 7.8 %collective-permute-start.25 = (f32[2,2,32,256]{3,2,1,0:T(8,128)S(1)}, f32[2,2,32,256]{3,2,1,0:T(8,128)S(1)}, u32[]{:S(2)}, u32[]{:S(2)}) collective-permute-start(f32[2,2,32,256]{3,2,1,0:T(8,128)S(1)} %get-tuple-element.108), channel_id=1, source_target_pairs={{0,64},{16,80},{32,96},{48,112},{64,0},{80,16},{96,32},{112,48},{1... | collective-permute-start | bytes 393224 | tf_op jit(solution)/shard_map/ppermute | solution.py:618
  141.6 7.0 %collective-permute-start.26 = (f32[2,2,32,256]{3,2,1,0:T(8,128)S(1)}, f32[2,2,32,256]{3,2,1,0:T(8,128)S(1)}, u32[]{:S(2)}, u32[]{:S(2)}) collective-permute-start(f32[2,2,32,256]{3,2,1,0:T(8,128)S(1)} %get-tuple-element.109), channel_id=1, source_target_pairs={{0,96},{16,112},{32,0},{48,16},{64,32},{80,48},{96,64},{112,80},{1... | collective-permute-start | bytes 393224 | tf_op jit(solution)/shard_map/ppermute | solution.py:618
  150.0 16.8 %collective-permute-start.30 = (f32[3,32,1024]{2,1,0:T(8,128)S(1)}, f32[3,32,1024]{2,1,0:T(8,128)S(1)}, u32[]{:S(2)}, u32[]{:S(2)}) collective-permute-start(f32[3,32,1024]{2,1,0:T(8,128)S(1)} %get-tuple-element.113.refs_4_), channel_id=1, source_target_pairs={{0,1},{1,2},{2,3},{3,4},{4,5},{5,6},{6,7},{7,8},{8,9},{9,10},{10,1... | collective-permute-start | bytes 1179656 | tf_op jit(solution)/shard_map/ppermute | solution.py:626
  150.8 16.0 %collective-permute-start.31 = (f32[3,32,1024]{2,1,0:T(8,128)S(1)}, f32[3,32,1024]{2,1,0:T(8,128)S(1)}, u32[]{:S(2)}, u32[]{:S(2)}) collective-permute-start(f32[3,32,1024]{2,1,0:T(8,128)S(1)} %get-tuple-element.114.refs_3_), channel_id=1, source_target_pairs={{1,0},{2,1},{3,2},{4,3},{5,4},{6,5},{7,6},{8,7},{9,8},{10,9},{11,1... | collective-permute-start | bytes 1179656 | tf_op jit(solution)/shard_map/ppermute | solution.py:630
  159.3 7.5 %collective-permute-start.29 = (f32[9,8,256]{2,1,0:T(8,128)S(1)}, f32[9,8,256]{2,1,0:T(8,128)S(1)}, u32[]{:S(2)}, u32[]{:S(2)}) collective-permute-start(f32[9,8,256]{2,1,0:T(8,128)S(1)} %get-tuple-element.112.refs_0_), channel_id=1, source_target_pairs={{0,96},{16,112},{32,0},{48,16},{64,32},{80,48},{96,64},{112,80},{1... | collective-permute-start | bytes 221192 | tf_op jit(solution)/shard_map/ppermute | solution.py:618
  160.8 6.0 %collective-permute-start.28 = (f32[9,8,256]{2,1,0:T(8,128)S(1)}, f32[9,8,256]{2,1,0:T(8,128)S(1)}, u32[]{:S(2)}, u32[]{:S(2)}) collective-permute-start(f32[9,8,256]{2,1,0:T(8,128)S(1)} %get-tuple-element.112.refs_0_), channel_id=1, source_target_pairs={{0,64},{16,80},{32,96},{48,112},{64,0},{80,16},{96,32},{112,48},{1... | collective-permute-start | bytes 221192 | tf_op jit(solution)/shard_map/ppermute | solution.py:618
  162.1 4.7 %collective-permute-start.27 = (f32[9,8,256]{2,1,0:T(8,128)S(1)}, f32[9,8,256]{2,1,0:T(8,128)S(1)}, u32[]{:S(2)}, u32[]{:S(2)}) collective-permute-start(f32[9,8,256]{2,1,0:T(8,128)S(1)} %get-tuple-element.112.refs_0_), channel_id=1, source_target_pairs={{0,32},{16,48},{32,64},{48,80},{64,96},{80,112},{96,0},{112,16},{1... | collective-permute-start | bytes 221192 | tf_op jit(solution)/shard_map/ppermute | solution.py:618
  168.7 23.8 %all-to-all-start.5 = ((f32[16,10,8,256]{3,2,1,0:T(8,128)}), f32[16,10,8,256]{3,2,1,0:T(8,128)S(1)}, u32[]{:S(2)}, u32[]{:S(2)}) async-start(f32[16,10,8,256]{3,2,1,0:T(8,128)} %get-tuple-element.116), calls=%async_computation.5 | async-start | bytes 2621440 | tf_op jit(solution)/shard_map/all_to_all | solution.py:772
  172.8 14.6 %copy-start.1 = (f32[2,256,256]{2,1,0:T(8,128)S(1)}, f32[2,256,256]{2,1,0:T(8,128)}, u32[]{:S(2)}) copy-start(f32[2,256,256]{2,1,0:T(8,128)} %get-tuple-element.122.refs_7_) | copy-start | bytes 1572868
  174.3 19.5 %copy-start.8 = (f32[2,32,1024]{2,1,0:T(8,128)}, f32[2,32,1024]{2,1,0:T(8,128)S(1)}, u32[]{:S(2)}) copy-start(f32[2,32,1024]{2,1,0:T(8,128)S(1)} %get-tuple-element.127.refs_6_) | copy-start | bytes 786436
  174.3 5.1 %collective-permute-start.32 = (f32[2,2,32,256]{3,2,1,0:T(8,128)S(1)}, f32[2,2,32,256]{3,2,1,0:T(8,128)S(1)}, u32[]{:S(2)}, u32[]{:S(2)}) collective-permute-start(f32[2,2,32,256]{3,2,1,0:T(8,128)S(1)} %get-tuple-element.119), channel_id=1, source_target_pairs={{0,32},{16,48},{32,64},{48,80},{64,96},{80,112},{96,0},{112,16},{1... | collective-permute-start | bytes 393224 | tf_op jit(solution)/shard_map/ppermute | solution.py:618
  174.4 6.6 %collective-permute-start.33 = (f32[2,2,32,256]{3,2,1,0:T(8,128)S(1)}, f32[2,2,32,256]{3,2,1,0:T(8,128)S(1)}, u32[]{:S(2)}, u32[]{:S(2)}) collective-permute-start(f32[2,2,32,256]{3,2,1,0:T(8,128)S(1)} %get-tuple-element.120), channel_id=1, source_target_pairs={{0,64},{16,80},{32,96},{48,112},{64,0},{80,16},{96,32},{112,48},{1... | collective-permute-start | bytes 393224 | tf_op jit(solution)/shard_map/ppermute | solution.py:618
  177.0 4.7 %collective-permute-start.34 = (f32[2,2,32,256]{3,2,1,0:T(8,128)S(1)}, f32[2,2,32,256]{3,2,1,0:T(8,128)S(1)}, u32[]{:S(2)}, u32[]{:S(2)}) collective-permute-start(f32[2,2,32,256]{3,2,1,0:T(8,128)S(1)} %get-tuple-element.121), channel_id=1, source_target_pairs={{0,96},{16,112},{32,0},{48,16},{64,32},{80,48},{96,64},{112,80},{1... | collective-permute-start | bytes 393224 | tf_op jit(solution)/shard_map/ppermute | solution.py:618
  181.8 5.6 %collective-permute-start.35 = (f32[4,2,32,256]{3,2,1,0:T(8,128)S(1)}, f32[4,2,32,256]{3,2,1,0:T(8,128)S(1)}, u32[]{:S(2)}, u32[]{:S(2)}) collective-permute-start(f32[4,2,32,256]{3,2,1,0:T(8,128)S(1)} %stack_kernel.3), channel_id=1, source_target_pairs={{0,16},{16,0},{32,48},{48,32},{64,80},{80,64},{96,112},{112,96},{1... | collective-permute-start | bytes 786440 | tf_op jit(solution)/shard_map/ppermute | solution.py:622
  189.1 3.4 %collective-permute-start.36 = (f32[2,128,256]{2,1,0:T(8,128)S(1)}, f32[2,128,256]{2,1,0:T(8,128)S(1)}, u32[]{:S(2)}, u32[]{:S(2)}) collective-permute-start(f32[2,128,256]{2,1,0:T(8,128)S(1)} %get-tuple-element.124), channel_id=1, source_target_pairs={{0,16},{16,0},{32,48},{48,32},{64,80},{80,64},{96,112},{112,96},{1... | collective-permute-start | bytes 786440 | tf_op jit(solution)/shard_map/ppermute | solution.py:622
  189.4 14.1 %collective-permute-start.39 = (f32[2,32,1024]{2,1,0:T(8,128)S(1)}, f32[2,32,1024]{2,1,0:T(8,128)}, u32[]{:S(2)}, u32[]{:S(2)}) collective-permute-start(f32[2,32,1024]{2,1,0:T(8,128)S(1)} %get-tuple-element.127.refs_6_), channel_id=1, source_target_pairs={{0,96},{16,112},{32,0},{48,16},{64,32},{80,48},{96,64},{112,80},{1... | collective-permute-start | bytes 786440 | tf_op jit(solution)/shard_map/ppermute | solution.py:618
  191.8 11.7 %collective-permute-start.38 = (f32[2,32,1024]{2,1,0:T(8,128)S(1)}, f32[2,32,1024]{2,1,0:T(8,128)}, u32[]{:S(2)}, u32[]{:S(2)}) collective-permute-start(f32[2,32,1024]{2,1,0:T(8,128)S(1)} %get-tuple-element.127.refs_6_), channel_id=1, source_target_pairs={{0,64},{16,80},{32,96},{48,112},{64,0},{80,16},{96,32},{112,48},{1... | collective-permute-start | bytes 786440 | tf_op jit(solution)/shard_map/ppermute | solution.py:618
  191.8 14.9 %collective-permute-start.37 = (f32[2,32,1024]{2,1,0:T(8,128)S(1)}, f32[2,32,1024]{2,1,0:T(8,128)}, u32[]{:S(2)}, u32[]{:S(2)}) collective-permute-start(f32[2,32,1024]{2,1,0:T(8,128)S(1)} %get-tuple-element.127.refs_6_), channel_id=1, source_target_pairs={{0,32},{16,48},{32,64},{48,80},{64,96},{80,112},{96,0},{112,16},{1... | collective-permute-start | bytes 786440 | tf_op jit(solution)/shard_map/ppermute | solution.py:618
  193.9 21.8 %collective-permute-start.41 = (f32[8,128,256]{2,1,0:T(8,128)S(1)}, f32[8,128,256]{2,1,0:T(8,128)S(1)}, u32[]{:S(2)}, u32[]{:S(2)}) collective-permute-start(f32[8,128,256]{2,1,0:T(8,128)S(1)} %get-tuple-element.129.refs_3_), channel_id=1, source_target_pairs={{0,16},{16,0},{32,48},{48,32},{64,80},{80,64},{96,112},{112,96},{1... | collective-permute-start | bytes 3145736 | tf_op jit(solution)/shard_map/ppermute | solution.py:622
  196.0 17.2 %all-to-all-start.6 = ((f32[128,1,128]{2,1,0:T(1,128)}), f32[128,1,128]{2,1,0:T(1,128)S(1)}, u32[]{:S(2)}, u32[]{:S(2)}) async-start(f32[128,1,128]{2,1,0:T(1,128)} %bitcast.32), calls=%async_computation.6 | async-start | bytes 131072 | tf_op jit(solution)/shard_map/all_to_all | solution.py:801
  214.9 3.9 %collective-permute-start.40 = (f32[4,2,32,1024]{3,2,1,0:T(8,128)S(1)}, f32[4,2,32,1024]{3,2,1,0:T(8,128)S(1)}, u32[]{:S(2)}, u32[]{:S(2)}) collective-permute-start(f32[4,2,32,1024]{3,2,1,0:T(8,128)S(1)} %combine_kernel.1.refs_2_), channel_id=1, source_target_pairs={{0,16},{16,0},{32,48},{48,32},{64,80},{80,64},{96,112},{112,96},{1... | collective-permute-start | bytes 3145736 | tf_op jit(solution)/shard_map/ppermute | solution.py:622
  (1 other events, 0.7 us)

commit v7 on v6

--- a/solution.py
+++ b/solution.py
@@ -196,8 +196,8 @@
     power[...] = jnp.zeros_like(power)
 
     def gather(plane, value):
-        obj[plane, 0] += value[:, :H]
-        obj[plane, 1] += value[:, H:]
+        obj[plane, 0, :N] += value[:, :H]
+        obj[plane, 1, :N] += value[:, H:]
 
     def forward(k):
         if first:
@@ -299,8 +299,8 @@
 def illum_kernel(where, near, total, out, power, acc):
     owner = 2 * where[0] + where[1]
     acc[...] = jnp.zeros_like(acc)
-    power[0] = total[:, :H]
-    power[1] = total[:, H:]
+    power[0, :N] = total[:, :H]
+    power[1, :N] = total[:, H:]
     for pattern in range(8):
         start, base, turn, block, shift = place_of(where, near, owner, pattern)
         rows = pl.ds(start, 32, stride=8)
@@ -382,7 +382,7 @@
                     lanes[part, half, rows, :] = piece[:, half * H : half * H + H]
     for part in range(2):
         for half in range(2):
-            dirp[part, :, half * H : half * H + H] = lanes[part, half]
+            dirp[part, :, half * H : half * H + H] = lanes[part, half, :N]
     for which, dest in ((c, kept), (1 - c, sent)):
         rows = pl.ds(pl.multiple_of(which * H, H), H)
         dr, di = dirp[0, rows, :], dirp[1, rows, :]
@@ -675,7 +675,7 @@
     probe = probe_init
     sent = (16, 9, 8, N)
     pieces = (4, 2, 32, N)
-    scratch = ((4, 2, N, N), (2, H, N), (2, 2, N, H))
+    scratch = ((4, 2, N, N), (2, H, N), (2, 2, N + 8, H))
     outs = (sent, sent, pieces, pieces, (N, N), (8, 8, N))
     messages, bands = [], []
 
@@ -744,7 +744,7 @@
             ((64, 1024),),
             (where, near, power),
             (0, 1),
-            ((2, N, H), (72, 1152)),
+            ((2, N + 8, H), (72, 1152)),
         )
         low, high, token = call(
             place_kernel,
@@ -787,7 +787,7 @@
             ((2, N, N), (2, H, N), (2, H, N)),
             (where, near, *back, partner(oth), patch),
             (0, 1),
-            ((2, 2, N, H),),
+            ((2, 2, N + 8, H),),
             cheap=True,
         )
         message, dmine = call(
@@ -823,7 +823,7 @@
         (object_init.shape,),
         (where, object_init, change, change_far),
         (0,),
-        ((2, 8, N, H),),
+        ((2, 8, N + 8, H),),
         hbm_in={1: (4, 1)},
         hbm_out={0: (4, 1)},
         lazy=True,

time: 223 us -> 223 us (level)
  transfers between devices with their start and end apart: 49 -> 49, of which waited for: 29 -> 28; matrix products, arithmetic and copies ran while one was open for 0% -> 0% of each run, Pallas kernels for 10% -> 10%
where the time goes in v7:
time: 223 us; the launch traced here: 222 us
  starting transfers between devices  102 us (46%)
  waiting for transfers between devices  63.9 us (29%)
  Pallas kernels  53.8 us (24%)
    pallas_call x26, Pallas kernels, call(): pl.pallas_call(run, out_shape=shapes, in_specs=[space(i, smem_in, hbm_in)...  52 us
    ppermute x24, waiting for transfers between devices, along_y(): return lax.ppermute(value, 'pat', [(i, (i + 2 * s) % 8) for i in range(8)])  28.3 us
    ppermute x24, starting transfers between devices, along_y(): return lax.ppermute(value, 'pat', [(i, (i + 2 * s) % 8) for i in range(8)])  27.2 us
    ppermute x12, starting transfers between devices, partner(): return lax.ppermute(value, 'pat', [(i, i ^ 1) for i in range(8)])  18.9 us
    all_to_all x2, starting transfers between devices, body(): messages.append(lax.all_to_all(message, BOTH, 0, 0))  14.9 us
    ppermute x3, starting transfers between devices, down(): return lax.ppermute(value, 'tile', [((i + 1) % 16, i) for i in range(16)])  12.7 us
    ppermute x12, waiting for transfers between devices, partner(): return lax.ppermute(value, 'pat', [(i, i ^ 1) for i in range(8)])  10.5 us
    all_to_all x2, starting transfers between devices, body(): shares = lax.all_to_all(chip, 'tile', 0, 0)  9.96 us
  transfers between devices with their start and end apart: 49, of which 28 were waited for; matrix products, arithmetic and copies ran while one was open for 0% of the time, Pallas kernels for 10%

profile of v7, /device:TPU:1, one launch (start us, length us, event | category | flops | bytes accessed | tf_op | source)
XLA Modules:
  0.0 222.1 jit_solution(9608843393207097201)
XLA Ops:
  0.8 1.8 shard_map.77
  2.5 2.1 collective-permute-start
  4.6 4.8 %collective-permute-start.1 = (f32[128,1024]{1,0:T(8,128)S(1)}, f32[128,1024]{1,0:T(8,128)S(1)}, u32[]{:S(2)}, u32[]{:S(2)}) collective-permute-start(f32[128,1024]{1,0:T(8,128)S(1)} %get-tuple-element.68), channel_id=1, source_target_pairs={{1,0},{2,1},{3,2},{4,3},{5,4},{6,5},{7,6},{8,7},{9,8},{10,9},{11,1... | collective-permute-start | bytes 1572872 | tf_op jit(solution)/shard_map/ppermute | solution.py:630
  10.6 5.4 %all-to-all-start = ((s32[8,1,128]{2,1,0:T(1,128)}), s32[8,1,128]{2,1,0:T(1,128)S(1)}, u32[]{:S(2)}, u32[]{:S(2)}) async-start(s32[8,1,128]{2,1,0:T(1,128)} %bitcast.5), calls=%async_computation | async-start | bytes 8192 | tf_op jit(solution)/shard_map/all_to_all | solution.py:653
  16.0 2.5 %prepare_kernel.1 = (f32[2,128,256]{2,1,0:T(8,128)S(1)}, f32[2,256,256]{2,1,0:T(8,128)S(1)}) custom-call(s32[4]{0:T(128)S(1)} %pad_add_fusion.refs_0_.where, s32[1,2]{1,0:T(1,128)S(1)} %copy-done.12, f32[256,256]{1,0:T(8,128)S(1)} %bitcast.28, bf16[2,256,256]{2,1,0:T(8,128)(2,1)S(1)} %copy-done.9, f32[2,256,1024]{2,1,0:T(8,128)} %refs_1_.7), custom_call_target="tpu_custom_call" | custom-call | bytes 3670040 | tf_op jit(solution)/shard_map/prepare_kernel/pallas_call | solution.py:595
  18.5 2.3 %all-to-all-done = s32[8,1,128]{2,1,0:T(1,128)S(1)} async-done(((s32[8,1,128]{2,1,0:T(1,128)}), s32[8,1,128]{2,1,0:T(1,128)S(1)}, u32[]{:S(2)}, u32[]{:S(2)}) %all-to-all-start) | async-done | bytes 4128 | tf_op jit(solution)/shard_map/all_to_all | solution.py:653
  21.8 1.3 collective-permute-start.2
  23.1 1.5 collective-permute-done.2.refs_4_
  24.6 7.9 %patterns.2 = (f32[2,256,256]{2,1,0:T(8,128)S(1)}, f32[16,9,8,256]{3,2,1,0:T(8,128)S(1)}, f32[16,9,8,256]{3,2,1,0:T(8,128)S(1)}, f32[4,2,32,256]{3,2,1,0:T(8,128...) custom-call(s32[4]{0:T(128)S(1)} %pad_add_fusion.refs_0_.where, ...), custom_call_target="tpu_custom_call" | custom-call | flops 6000000000 | bytes 9764888 | tf_op jit(solution)/shard_map/patterns/pallas_call | solution.py:595
  33.1 2.7 %collective-permute-done.4.refs_3_ = f32[4,2,32,256]{3,2,1,0:T(8,128)S(1)} collective-permute-done((f32[4,2,32,256]{3,2,1,0:T(8,128)S(1)}, f32[4,2,32,256]{3,2,1,0:T(8,128)S(1)}, u32[]{:S(2)}, u32[]{:S(2)}) %collective-permute-start.4) | collective-permute-done | bytes 262176 | tf_op jit(solution)/shard_map/ppermute | solution.py:622
  37.0 6.3 %all-to-all-start.1 = ((f32[16,9,8,256]{3,2,1,0:T(8,128)}), f32[16,9,8,256]{3,2,1,0:T(8,128)S(1)}, u32[]{:S(2)}, u32[]{:S(2)}) async-start(f32[16,9,8,256]{3,2,1,0:T(8,128)} %get-tuple-element.82), calls=%async_computation.1 | async-start | bytes 2359296 | tf_op jit(solution)/shard_map/all_to_all | solution.py:758
  43.2 1.4 collective-permute-start.5
  44.6 2.6 %collective-permute-start.6 = (f32[2,2,32,256]{3,2,1,0:T(8,128)S(1)}, f32[2,2,32,256]{3,2,1,0:T(8,128)S(1)}, u32[]{:S(2)}, u32[]{:S(2)}) collective-permute-start(f32[2,2,32,256]{3,2,1,0:T(8,128)S(1)} %get-tuple-element.79), channel_id=1, source_target_pairs={{0,64},{16,80},{32,96},{48,112},{64,0},{80,16},{96,32},{112,48},{1... | collective-permute-start | bytes 393224 | tf_op jit(solution)/shard_map/ppermute | solution.py:618
  49.2 3.7 %collective-permute-done.6.refs_5_ = f32[2,2,32,256]{3,2,1,0:T(8,128)S(1)} collective-permute-done((f32[2,2,32,256]{3,2,1,0:T(8,128)S(1)}, f32[2,2,32,256]{3,2,1,0:T(8,128)S(1)}, u32[]{:S(2)}, u32[]{:S(2)}) %collective-permute-start.6) | collective-permute-done | bytes 131104 | tf_op jit(solution)/shard_map/ppermute | solution.py:618
  53.0 1.4 place_kernel.2
  55.4 3.8 %collective-permute-start.12 = (f32[3,32,1024]{2,1,0:T(8,128)S(1)}, f32[3,32,1024]{2,1,0:T(8,128)S(1)}, u32[]{:S(2)}, u32[]{:S(2)}) collective-permute-start(f32[3,32,1024]{2,1,0:T(8,128)S(1)} %get-tuple-element.85.refs_3_), channel_id=1, source_target_pairs={{1,0},{2,1},{3,2},{4,3},{5,4},{6,5},{7,6},{8,7},{9,8},{10,9},{11,1... | collective-permute-start | bytes 1179656 | tf_op jit(solution)/shard_map/ppermute | solution.py:630
  59.2 1.9 all-to-all-done.1.refs_1_
  61.2 1.2 sum_kernel.2
  62.4 2.8 %collective-permute-start.10 = (f32[9,8,256]{2,1,0:T(8,128)S(1)}, f32[9,8,256]{2,1,0:T(8,128)S(1)}, u32[]{:S(2)}, u32[]{:S(2)}) collective-permute-start(f32[9,8,256]{2,1,0:T(8,128)S(1)} %get-tuple-element.83.refs_0_), channel_id=1, source_target_pairs={{0,96},{16,112},{32,0},{48,16},{64,32},{80,48},{96,64},{112,80},{1... | collective-permute-start | bytes 221192 | tf_op jit(solution)/shard_map/ppermute | solution.py:618
  66.2 3.7 %collective-permute-done.11.refs_4_.refs_5_ = f32[3,32,1024]{2,1,0:T(8,128)S(1)} collective-permute-done((f32[3,32,1024]{2,1,0:T(8,128)S(1)}, f32[3,32,1024]{2,1,0:T(8,128)S(1)}, u32[]{:S(2)}, u32[]{:S(2)}) %collective-permute-start.11) | collective-permute-done | bytes 393248 | tf_op jit(solution)/shard_map/ppermute | solution.py:626
  70.8 1.8 share_kernel.2
  72.6 4.4 %all-to-all-start.2 = ((f32[16,10,8,256]{3,2,1,0:T(8,128)}), f32[16,10,8,256]{3,2,1,0:T(8,128)S(1)}, u32[]{:S(2)}, u32[]{:S(2)}) async-start(f32[16,10,8,256]{3,2,1,0:T(8,128)} %get-tuple-element.87), calls=%async_computation.2 | async-start | bytes 2621440 | tf_op jit(solution)/shard_map/all_to_all | solution.py:772
  77.1 1.5 direction_kernel.2
  79.5 2.8 %collective-permute-start.14 = (f32[2,2,32,256]{3,2,1,0:T(8,128)S(1)}, f32[2,2,32,256]{3,2,1,0:T(8,128)S(1)}, u32[]{:S(2)}, u32[]{:S(2)}) collective-permute-start(f32[2,2,32,256]{3,2,1,0:T(8,128)S(1)} %get-tuple-element.91), channel_id=1, source_target_pairs={{0,64},{16,80},{32,96},{48,112},{64,0},{80,16},{96,32},{112,48},{1... | collective-permute-start | bytes 393224 | tf_op jit(solution)/shard_map/ppermute | solution.py:618
  84.3 1.7 collective-permute-done.14.refs_2_.refs_4_
  86.6 5.1 %collective-permute-start.16 = (f32[4,2,32,256]{3,2,1,0:T(8,128)S(1)}, f32[4,2,32,256]{3,2,1,0:T(8,128)S(1)}, u32[]{:S(2)}, u32[]{:S(2)}) collective-permute-start(f32[4,2,32,256]{3,2,1,0:T(8,128)S(1)} %stack_kernel.2), channel_id=1, source_target_pairs={{0,16},{16,0},{32,48},{48,32},{64,80},{80,64},{96,112},{112,96},{1... | collective-permute-start | bytes 786440 | tf_op jit(solution)/shard_map/ppermute | solution.py:622
  91.7 1.2 collective-permute-done.16.refs_6_
  95.0 1.2 collective-permute-done.17.refs_3_
  96.2 2.4 %message_kernel.2 = (f32[128,128]{1,0:T(8,128)}, f32[8,128,256]{2,1,0:T(8,128)}) custom-call(s32[4]{0:T(128)S(1)} %pad_add_fusion.refs_0_.where, f32[16,10,8,256]{3,2,1,0:T(8,128)S(1)} %all-to-all-done.2.refs_1_, f32[2,128,256]{2,1,0:T(8,128)S(1)} %get-tuple-element.94.refs_2_, f32[2,128,256]{2,1,0:T(8,128)S(1)} %collective-permute-done.17.refs_3_, ...), custom_call_target="tpu_custom_call" | custom-call | bytes 2949152 | tf_op jit(solution)/shard_map/message_kernel/pallas_call | solution.py:595
  98.6 2.7 %collective-permute-start.18 = (f32[8,128,256]{2,1,0:T(8,128)}, f32[8,128,256]{2,1,0:T(8,128)S(1)}, u32[]{:S(2)}, u32[]{:S(2)}) collective-permute-start(f32[8,128,256]{2,1,0:T(8,128)} %get-tuple-element.99.refs_8_), channel_id=1, source_target_pairs={{0,16},{16,0},{32,48},{48,32},{64,80},{80,64},{96,112},{112,96},{1... | collective-permute-start | bytes 3145736 | tf_op jit(solution)/shard_map/ppermute | solution.py:622
  101.3 1.6 collective-permute-start.21
  104.1 7.4 %all-to-all-start.3 = ((f32[128,1,128]{2,1,0:T(1,128)}), f32[128,1,128]{2,1,0:T(1,128)S(1)}, u32[]{:S(2)}, u32[]{:S(2)}) async-start(f32[128,1,128]{2,1,0:T(1,128)} %bitcast.31), calls=%async_computation.3 | async-start | bytes 131072 | tf_op jit(solution)/shard_map/all_to_all | solution.py:801
  111.9 6.8 %collective-permute-done.19.refs_10_.refs_3_ = f32[2,32,1024]{2,1,0:T(8,128)S(1)} collective-permute-done((f32[2,32,1024]{2,1,0:T(8,128)S(1)}, f32[2,32,1024]{2,1,0:T(8,128)S(1)}, u32[]{:S(2)}, u32[]{:S(2)}) %collective-permute-start.19) | collective-permute-done | bytes 262176 | tf_op jit(solution)/shard_map/ppermute | solution.py:618
  118.8 2.4 %all-to-all-done.3 = f32[128,1,128]{2,1,0:T(1,128)S(1)} async-done(((f32[128,1,128]{2,1,0:T(1,128)}), f32[128,1,128]{2,1,0:T(1,128)S(1)}, u32[]{:S(2)}, u32[]{:S(2)}) %all-to-all-start.3) | async-done | bytes 65568 | tf_op jit(solution)/shard_map/all_to_all | solution.py:801
  121.2 9.8 %patterns.3 = (f32[2,256,256]{2,1,0:T(8,128)}, f32[4,2,256,256]{3,2,1,0:T(8,128)}, f32[16,9,8,256]{3,2,1,0:T(8,128)S(1)}, f32[16,9,8,256]{3,2,1,0:T(8,128)S(1)},...) custom-call(s32[4]{0:T(128)S(1)} %pad_add_fusion.refs_0_.where, ...), custom_call_target="tpu_custom_call" | custom-call | flops 6000000000 | bytes 14286872 | tf_op jit(solution)/shard_map/patterns/pallas_call | solution.py:595
  131.9 2.8 %collective-permute-done.23.refs_3_ = f32[4,2,32,256]{3,2,1,0:T(8,128)S(1)} collective-permute-done((f32[4,2,32,256]{3,2,1,0:T(8,128)S(1)}, f32[4,2,32,256]{3,2,1,0:T(8,128)S(1)}, u32[]{:S(2)}, u32[]{:S(2)}) %collective-permute-start.23) | collective-permute-done | bytes 262176 | tf_op jit(solution)/shard_map/ppermute | solution.py:622
  135.8 3.7 %all-to-all-start.4 = ((f32[16,9,8,256]{3,2,1,0:T(8,128)}), f32[16,9,8,256]{3,2,1,0:T(8,128)S(1)}, u32[]{:S(2)}, u32[]{:S(2)}) async-start(f32[16,9,8,256]{3,2,1,0:T(8,128)} %get-tuple-element.111), calls=%async_computation.4 | async-start | bytes 2359296 | tf_op jit(solution)/shard_map/all_to_all | solution.py:758
  139.9 1.7 collective-permute-start.25
  143.3 2.7 %collective-permute-done.24.refs_4_ = f32[2,2,32,256]{3,2,1,0:T(8,128)S(1)} collective-permute-done((f32[2,2,32,256]{3,2,1,0:T(8,128)S(1)}, f32[2,2,32,256]{3,2,1,0:T(8,128)S(1)}, u32[]{:S(2)}, u32[]{:S(2)}) %collective-permute-start.24) | collective-permute-done | bytes 131104 | tf_op jit(solution)/shard_map/ppermute | solution.py:618
  146.0 1.7 collective-permute-done.25.refs_5_
  148.6 1.4 place_kernel.3
  150.8 4.0 %collective-permute-start.31 = (f32[3,32,1024]{2,1,0:T(8,128)S(1)}, f32[3,32,1024]{2,1,0:T(8,128)S(1)}, u32[]{:S(2)}, u32[]{:S(2)}) collective-permute-start(f32[3,32,1024]{2,1,0:T(8,128)S(1)} %get-tuple-element.114.refs_3_), channel_id=1, source_target_pairs={{1,0},{2,1},{3,2},{4,3},{5,4},{6,5},{7,6},{8,7},{9,8},{10,9},{11,1... | collective-permute-start | bytes 1179656 | tf_op jit(solution)/shard_map/ppermute | solution.py:630
  154.8 3.3 %all-to-all-done.4.refs_1_ = f32[16,9,8,256]{3,2,1,0:T(8,128)S(1)} async-done(((f32[16,9,8,256]{3,2,1,0:T(8,128)}), f32[16,9,8,256]{3,2,1,0:T(8,128)S(1)}, u32[]{:S(2)}, u32[]{:S(2)}) %all-to-all-start.4) | async-done | bytes 1179680 | tf_op jit(solution)/shard_map/all_to_all | solution.py:758
  158.1 1.2 sum_kernel.3
  159.3 1.5 collective-permute-start.29
  160.8 1.3 collective-permute-start.28
  162.1 4.7 %collective-permute-done.30.refs_4_.refs_5_ = f32[3,32,1024]{2,1,0:T(8,128)S(1)} collective-permute-done((f32[3,32,1024]{2,1,0:T(8,128)S(1)}, f32[3,32,1024]{2,1,0:T(8,128)S(1)}, u32[]{:S(2)}, u32[]{:S(2)}) %collective-permute-start.30) | collective-permute-done | bytes 393248 | tf_op jit(solution)/shard_map/ppermute | solution.py:626
  166.8 1.8 share_kernel.3
  168.7 4.2 %all-to-all-start.5 = ((f32[16,10,8,256]{3,2,1,0:T(8,128)}), f32[16,10,8,256]{3,2,1,0:T(8,128)S(1)}, u32[]{:S(2)}, u32[]{:S(2)}) async-start(f32[16,10,8,256]{3,2,1,0:T(8,128)} %get-tuple-element.116), calls=%async_computation.5 | async-start | bytes 2621440 | tf_op jit(solution)/shard_map/all_to_all | solution.py:772
  172.9 1.5 direction_kernel.3
  174.4 2.6 %collective-permute-start.33 = (f32[2,2,32,256]{3,2,1,0:T(8,128)S(1)}, f32[2,2,32,256]{3,2,1,0:T(8,128)S(1)}, u32[]{:S(2)}, u32[]{:S(2)}) collective-permute-start(f32[2,2,32,256]{3,2,1,0:T(8,128)S(1)} %get-tuple-element.120), channel_id=1, source_target_pairs={{0,64},{16,80},{32,96},{48,112},{64,0},{80,16},{96,32},{112,48},{1... | collective-permute-start | bytes 393224 | tf_op jit(solution)/shard_map/ppermute | solution.py:618
  177.1 3.9 %collective-permute-done.32.refs_1_.refs_3_ = f32[2,2,32,256]{3,2,1,0:T(8,128)S(1)} collective-permute-done((f32[2,2,32,256]{3,2,1,0:T(8,128)S(1)}, f32[2,2,32,256]{3,2,1,0:T(8,128)S(1)}, u32[]{:S(2)}, u32[]{:S(2)}) %collective-permute-start.32) | collective-permute-done | bytes 131104 | tf_op jit(solution)/shard_map/ppermute | solution.py:618
  181.8 4.4 %collective-permute-start.35 = (f32[4,2,32,256]{3,2,1,0:T(8,128)S(1)}, f32[4,2,32,256]{3,2,1,0:T(8,128)S(1)}, u32[]{:S(2)}, u32[]{:S(2)}) collective-permute-start(f32[4,2,32,256]{3,2,1,0:T(8,128)S(1)} %stack_kernel.3), channel_id=1, source_target_pairs={{0,16},{16,0},{32,48},{48,32},{64,80},{80,64},{96,112},{112,96},{1... | collective-permute-start | bytes 786440 | tf_op jit(solution)/shard_map/ppermute | solution.py:622
  186.2 1.2 collective-permute-done.35.refs_6_
  187.4 1.7 patch_kernel.3
  189.4 2.4 %collective-permute-start.39 = (f32[2,32,1024]{2,1,0:T(8,128)S(1)}, f32[2,32,1024]{2,1,0:T(8,128)}, u32[]{:S(2)}, u32[]{:S(2)}) collective-permute-start(f32[2,32,1024]{2,1,0:T(8,128)S(1)} %get-tuple-element.127.refs_6_), channel_id=1, source_target_pairs={{0,96},{16,112},{32,0},{48,16},{64,32},{80,48},{96,64},{112,80},{1... | collective-permute-start | bytes 786440 | tf_op jit(solution)/shard_map/ppermute | solution.py:618
  192.4 1.4 message_kernel.3
  193.9 2.2 collective-permute-start.41
  196.0 7.5 %all-to-all-start.6 = ((f32[128,1,128]{2,1,0:T(1,128)}), f32[128,1,128]{2,1,0:T(1,128)S(1)}, u32[]{:S(2)}, u32[]{:S(2)}) async-start(f32[128,1,128]{2,1,0:T(1,128)} %bitcast.32), calls=%async_computation.6 | async-start | bytes 131072 | tf_op jit(solution)/shard_map/all_to_all | solution.py:801
  203.5 3.2 %collective-permute-done.37.refs_7_ = f32[2,32,1024]{2,1,0:T(8,128)} collective-permute-done((f32[2,32,1024]{2,1,0:T(8,128)S(1)}, f32[2,32,1024]{2,1,0:T(8,128)}, u32[]{:S(2)}, u32[]{:S(2)}) %collective-permute-start.37) | collective-permute-done | bytes 262176 | tf_op jit(solution)/shard_map/ppermute | solution.py:618
  206.7 6.5 %all-to-all-done.6 = f32[128,1,128]{2,1,0:T(1,128)S(1)} async-done(((f32[128,1,128]{2,1,0:T(1,128)}), f32[128,1,128]{2,1,0:T(1,128)S(1)}, u32[]{:S(2)}, u32[]{:S(2)}) %all-to-all-start.6) | async-done | bytes 65568 | tf_op jit(solution)/shard_map/all_to_all | solution.py:801
  213.2 1.6 combine_kernel.1.refs_2_
  215.7 3.0 %probe_kernel.1 = f32[4,2,256,256]{3,2,1,0:T(8,128)} custom-call(s32[4]{0:T(128)S(1)} %pad_add_fusion.refs_0_.where, f32[128,128]{1,0:T(8,128)S(1)} %bitcast.18, f32[4,2,256,256]{3,2,1,0:T(8,128)} %get-tuple-element.128.refs_2_, f32[8,128,256]{2,1,0:T(8,128)S(1)} %get-tuple-element.129.refs_3_, f32[8,128,256]{2,1,0:T(8,128)S(1)} %collective-permute-done.41.refs_4_), custom_call_target="tpu_custom_call" | custom-call | flops 1000000000 | bytes 6357008 | tf_op jit(solution)/shard_map/probe_kernel/pallas_call | solution.py:595
  218.7 3.2 %object_kernel.1 = f32[2,256,1024]{2,1,0:T(8,128)} custom-call(s32[4]{0:T(128)S(1)} %pad_add_fusion.refs_0_.where, f32[2,256,1024]{2,1,0:T(8,128)} %refs_1_.7, f32[4,2,32,1024]{3,2,1,0:T(8,128)S(1)} %combine_kernel.1.refs_2_, f32[4,2,32,1024]{3,2,1,0:T(8,128)S(1)} %collective-permute-done.40.refs_3_), custom_call_target="tpu_custom_call" | custom-call | bytes 6291472 | tf_op jit(solution)/shard_map/object_kernel/pallas_call | solution.py:595
  (94 shorter events, 24.8 us)
Async XLA Ops:
  0.6 15.4 %copy-start.9 = (bf16[2,256,256]{2,1,0:T(8,128)(2,1)S(1)}, bf16[2,256,256]{2,1,0:T(8,128)(2,1)}, u32[]{:S(2)}) copy-start(bf16[2,256,256]{2,1,0:T(8,128)(2,1)} %constant.43.clone.refs_3_) | copy-start | bytes 786436
  0.6 8.8 %copy-start.12 = (s32[1,2]{1,0:T(1,128)S(1)}, s32[1,2]{1,0:T(1,128)}, u32[]{:S(2)}) copy-start(s32[1,2]{1,0:T(1,128)} %refs_1_.6) | copy-start | bytes 28
  0.7 15.4 %copy-start.2 = (f32[1,256,256]{2,1,0:T(8,128)S(1)}, f32[1,256,256]{2,1,0:T(8,128)}, u32[]{:S(2)}) copy-start(f32[1,256,256]{2,1,0:T(8,128)} %param.6) | copy-start | bytes 786436
  2.5 18.5 %collective-permute-start = (f32[128,1024]{1,0:T(8,128)S(1)}, f32[128,1024]{1,0:T(8,128)S(1)}, u32[]{:S(2)}, u32[]{:S(2)}) collective-permute-start(f32[128,1024]{1,0:T(8,128)S(1)} %get-tuple-element.67), channel_id=1, source_target_pairs={{0,1},{1,2},{2,3},{3,4},{4,5},{5,6},{6,7},{7,8},{8,9},{9,10},{10,1... | collective-permute-start | bytes 1572872 | tf_op jit(solution)/shard_map/ppermute | solution.py:626
  4.6 16.4 %collective-permute-start.1 = (f32[128,1024]{1,0:T(8,128)S(1)}, f32[128,1024]{1,0:T(8,128)S(1)}, u32[]{:S(2)}, u32[]{:S(2)}) collective-permute-start(f32[128,1024]{1,0:T(8,128)S(1)} %get-tuple-element.68), channel_id=1, source_target_pairs={{1,0},{2,1},{3,2},{4,3},{5,4},{6,5},{7,6},{8,7},{9,8},{10,9},{11,1... | collective-permute-start | bytes 1572872 | tf_op jit(solution)/shard_map/ppermute | solution.py:630
  10.6 10.2 %all-to-all-start = ((s32[8,1,128]{2,1,0:T(1,128)}), s32[8,1,128]{2,1,0:T(1,128)S(1)}, u32[]{:S(2)}, u32[]{:S(2)}) async-start(s32[8,1,128]{2,1,0:T(1,128)} %bitcast.5), calls=%async_computation | async-start | bytes 8192 | tf_op jit(solution)/shard_map/all_to_all | solution.py:653
  18.5 14.0 %copy-start.14 = (f32[2,128,256]{2,1,0:T(8,128)}, f32[2,128,256]{2,1,0:T(8,128)S(1)}, u32[]{:S(2)}) copy-start(f32[2,128,256]{2,1,0:T(8,128)S(1)} %get-tuple-element.71.refs_6_.refs_5_) | copy-start | bytes 786436
  20.8 3.8 %copy-start.15 = (bf16[4,2,256,256]{3,2,1,0:T(8,128)(2,1)S(1)}, bf16[4,2,256,256]{3,2,1,0:T(8,128)(2,1)}, u32[]{:S(2)}) copy-start(bf16[4,2,256,256]{3,2,1,0:T(8,128)(2,1)} %constant.42.clone.refs_7_.refs_6_) | copy-start | bytes 3145732
  21.8 2.8 %collective-permute-start.2 = (f32[128,1024]{1,0:T(8,128)S(1)}, f32[128,1024]{1,0:T(8,128)S(1)}, u32[]{:S(2)}, u32[]{:S(2)}) collective-permute-start(f32[128,1024]{1,0:T(8,128)S(1)} %get-tuple-element.70), channel_id=1, source_target_pairs={{0,16},{16,0},{32,48},{48,32},{64,80},{80,64},{96,112},{112,96},{1... | collective-permute-start | bytes 1572872 | tf_op jit(solution)/shard_map/ppermute | solution.py:622
  32.5 4.4 %copy-start.10 = (f32[8,8,256]{2,1,0:T(8,128)}, f32[8,8,256]{2,1,0:T(8,128)S(1)}, u32[]{:S(2)}) copy-start(f32[8,8,256]{2,1,0:T(8,128)S(1)} %get-tuple-element.86.refs_6_) | copy-start | bytes 196612
  32.5 60.3 %copy-start = (f32[2,256,256]{2,1,0:T(8,128)}, f32[2,256,256]{2,1,0:T(8,128)S(1)}, u32[]{:S(2)}) copy-start(f32[2,256,256]{2,1,0:T(8,128)S(1)} %get-tuple-element.93.refs_7_.refs_3_) | copy-start | bytes 1572868
  32.6 3.3 %collective-permute-start.3 = (f32[16,9,8,256]{3,2,1,0:T(8,128)S(1)}, f32[16,9,8,256]{3,2,1,0:T(8,128)S(1)}, u32[]{:S(2)}, u32[]{:S(2)}) collective-permute-start(f32[16,9,8,256]{3,2,1,0:T(8,128)S(1)} %get-tuple-element.74), channel_id=1, source_target_pairs={{0,16},{16,0},{32,48},{48,32},{64,80},{80,64},{96,112},{112,96},{1... | collective-permute-start | bytes 3538952 | tf_op jit(solution)/shard_map/ppermute | solution.py:622
  33.0 2.8 %collective-permute-start.4 = (f32[4,2,32,256]{3,2,1,0:T(8,128)S(1)}, f32[4,2,32,256]{3,2,1,0:T(8,128)S(1)}, u32[]{:S(2)}, u32[]{:S(2)}) collective-permute-start(f32[4,2,32,256]{3,2,1,0:T(8,128)S(1)} %get-tuple-element.76), channel_id=1, source_target_pairs={{0,16},{16,0},{32,48},{48,32},{64,80},{80,64},{96,112},{112,96},{1... | collective-permute-start | bytes 786440 | tf_op jit(solution)/shard_map/ppermute | solution.py:622
  37.0 24.2 %all-to-all-start.1 = ((f32[16,9,8,256]{3,2,1,0:T(8,128)}), f32[16,9,8,256]{3,2,1,0:T(8,128)S(1)}, u32[]{:S(2)}, u32[]{:S(2)}) async-start(f32[16,9,8,256]{3,2,1,0:T(8,128)} %get-tuple-element.82), calls=%async_computation.1 | async-start | bytes 2359296 | tf_op jit(solution)/shard_map/all_to_all | solution.py:758
  43.2 6.0 %collective-permute-start.5 = (f32[2,2,32,256]{3,2,1,0:T(8,128)S(1)}, f32[2,2,32,256]{3,2,1,0:T(8,128)S(1)}, u32[]{:S(2)}, u32[]{:S(2)}) collective-permute-start(f32[2,2,32,256]{3,2,1,0:T(8,128)S(1)} %get-tuple-element.78), channel_id=1, source_target_pairs={{0,32},{16,48},{32,64},{48,80},{64,96},{80,112},{96,0},{112,16},{1... | collective-permute-start | bytes 393224 | tf_op jit(solution)/shard_map/ppermute | solution.py:618
  44.6 8.4 %collective-permute-start.6 = (f32[2,2,32,256]{3,2,1,0:T(8,128)S(1)}, f32[2,2,32,256]{3,2,1,0:T(8,128)S(1)}, u32[]{:S(2)}, u32[]{:S(2)}) collective-permute-start(f32[2,2,32,256]{3,2,1,0:T(8,128)S(1)} %get-tuple-element.79), channel_id=1, source_target_pairs={{0,64},{16,80},{32,96},{48,112},{64,0},{80,16},{96,32},{112,48},{1... | collective-permute-start | bytes 393224 | tf_op jit(solution)/shard_map/ppermute | solution.py:618
  47.2 5.7 %collective-permute-start.7 = (f32[2,2,32,256]{3,2,1,0:T(8,128)S(1)}, f32[2,2,32,256]{3,2,1,0:T(8,128)S(1)}, u32[]{:S(2)}, u32[]{:S(2)}) collective-permute-start(f32[2,2,32,256]{3,2,1,0:T(8,128)S(1)} %get-tuple-element.80), channel_id=1, source_target_pairs={{0,96},{16,112},{32,0},{48,16},{64,32},{80,48},{96,64},{112,80},{1... | collective-permute-start | bytes 393224 | tf_op jit(solution)/shard_map/ppermute | solution.py:618
  49.2 21.7 %copy-start.11 = (f32[8,8,256]{2,1,0:T(8,128)S(1)}, f32[8,8,256]{2,1,0:T(8,128)}, u32[]{:S(2)}) copy-start(f32[8,8,256]{2,1,0:T(8,128)} %copy-done.10) | copy-start | bytes 196612
  54.4 15.6 %collective-permute-start.11 = (f32[3,32,1024]{2,1,0:T(8,128)S(1)}, f32[3,32,1024]{2,1,0:T(8,128)S(1)}, u32[]{:S(2)}, u32[]{:S(2)}) collective-permute-start(f32[3,32,1024]{2,1,0:T(8,128)S(1)} %get-tuple-element.84.refs_4_), channel_id=1, source_target_pairs={{0,1},{1,2},{2,3},{3,4},{4,5},{5,6},{6,7},{7,8},{8,9},{9,10},{10,1... | collective-permute-start | bytes 1179656 | tf_op jit(solution)/shard_map/ppermute | solution.py:626
  55.4 14.5 %collective-permute-start.12 = (f32[3,32,1024]{2,1,0:T(8,128)S(1)}, f32[3,32,1024]{2,1,0:T(8,128)S(1)}, u32[]{:S(2)}, u32[]{:S(2)}) collective-permute-start(f32[3,32,1024]{2,1,0:T(8,128)S(1)} %get-tuple-element.85.refs_3_), channel_id=1, source_target_pairs={{1,0},{2,1},{3,2},{4,3},{5,4},{6,5},{7,6},{8,7},{9,8},{10,9},{11,1... | collective-permute-start | bytes 1179656 | tf_op jit(solution)/shard_map/ppermute | solution.py:630
  62.4 7.6 %collective-permute-start.10 = (f32[9,8,256]{2,1,0:T(8,128)S(1)}, f32[9,8,256]{2,1,0:T(8,128)S(1)}, u32[]{:S(2)}, u32[]{:S(2)}) collective-permute-start(f32[9,8,256]{2,1,0:T(8,128)S(1)} %get-tuple-element.83.refs_0_), channel_id=1, source_target_pairs={{0,96},{16,112},{32,0},{48,16},{64,32},{80,48},{96,64},{112,80},{1... | collective-permute-start | bytes 221192 | tf_op jit(solution)/shard_map/ppermute | solution.py:618
  65.2 5.0 %collective-permute-start.9 = (f32[9,8,256]{2,1,0:T(8,128)S(1)}, f32[9,8,256]{2,1,0:T(8,128)S(1)}, u32[]{:S(2)}, u32[]{:S(2)}) collective-permute-start(f32[9,8,256]{2,1,0:T(8,128)S(1)} %get-tuple-element.83.refs_0_), channel_id=1, source_target_pairs={{0,64},{16,80},{32,96},{48,112},{64,0},{80,16},{96,32},{112,48},{1... | collective-permute-start | bytes 221192 | tf_op jit(solution)/shard_map/ppermute | solution.py:618
  65.5 5.3 %collective-permute-start.8 = (f32[9,8,256]{2,1,0:T(8,128)S(1)}, f32[9,8,256]{2,1,0:T(8,128)S(1)}, u32[]{:S(2)}, u32[]{:S(2)}) collective-permute-start(f32[9,8,256]{2,1,0:T(8,128)S(1)} %get-tuple-element.83.refs_0_), channel_id=1, source_target_pairs={{0,32},{16,48},{32,64},{48,80},{64,96},{80,112},{96,0},{112,16},{1... | collective-permute-start | bytes 221192 | tf_op jit(solution)/shard_map/ppermute | solution.py:618
  72.6 23.5 %all-to-all-start.2 = ((f32[16,10,8,256]{3,2,1,0:T(8,128)}), f32[16,10,8,256]{3,2,1,0:T(8,128)S(1)}, u32[]{:S(2)}, u32[]{:S(2)}) async-start(f32[16,10,8,256]{3,2,1,0:T(8,128)} %get-tuple-element.87), calls=%async_computation.2 | async-start | bytes 2621440 | tf_op jit(solution)/shard_map/all_to_all | solution.py:772
  79.3 5.0 %collective-permute-start.13 = (f32[2,2,32,256]{3,2,1,0:T(8,128)S(1)}, f32[2,2,32,256]{3,2,1,0:T(8,128)S(1)}, u32[]{:S(2)}, u32[]{:S(2)}) collective-permute-start(f32[2,2,32,256]{3,2,1,0:T(8,128)S(1)} %get-tuple-element.90), channel_id=1, source_target_pairs={{0,32},{16,48},{32,64},{48,80},{64,96},{80,112},{96,0},{112,16},{1... | collective-permute-start | bytes 393224 | tf_op jit(solution)/shard_map/ppermute | solution.py:618
  79.5 6.6 %collective-permute-start.14 = (f32[2,2,32,256]{3,2,1,0:T(8,128)S(1)}, f32[2,2,32,256]{3,2,1,0:T(8,128)S(1)}, u32[]{:S(2)}, u32[]{:S(2)}) collective-permute-start(f32[2,2,32,256]{3,2,1,0:T(8,128)S(1)} %get-tuple-element.91), channel_id=1, source_target_pairs={{0,64},{16,80},{32,96},{48,112},{64,0},{80,16},{96,32},{112,48},{1... | collective-permute-start | bytes 393224 | tf_op jit(solution)/shard_map/ppermute | solution.py:618
  82.3 4.3 %collective-permute-start.15 = (f32[2,2,32,256]{3,2,1,0:T(8,128)S(1)}, f32[2,2,32,256]{3,2,1,0:T(8,128)S(1)}, u32[]{:S(2)}, u32[]{:S(2)}) collective-permute-start(f32[2,2,32,256]{3,2,1,0:T(8,128)S(1)} %get-tuple-element.92), channel_id=1, source_target_pairs={{0,96},{16,112},{32,0},{48,16},{64,32},{80,48},{96,64},{112,80},{1... | collective-permute-start | bytes 393224 | tf_op jit(solution)/shard_map/ppermute | solution.py:618
  86.6 6.3 %collective-permute-start.16 = (f32[4,2,32,256]{3,2,1,0:T(8,128)S(1)}, f32[4,2,32,256]{3,2,1,0:T(8,128)S(1)}, u32[]{:S(2)}, u32[]{:S(2)}) collective-permute-start(f32[4,2,32,256]{3,2,1,0:T(8,128)S(1)} %stack_kernel.2), channel_id=1, source_target_pairs={{0,16},{16,0},{32,48},{48,32},{64,80},{80,64},{96,112},{112,96},{1... | collective-permute-start | bytes 786440 | tf_op jit(solution)/shard_map/ppermute | solution.py:622
  93.8 0.8 copy-start.13
  94.6 6.7 %copy-start.4 = (f32[2,32,1024]{2,1,0:T(8,128)S(1)}, f32[2,32,1024]{2,1,0:T(8,128)}, u32[]{:S(2)}) copy-start(f32[2,32,1024]{2,1,0:T(8,128)} %copy-done.3) | copy-start | bytes 786436
  94.6 1.5 collective-permute-start.17
  98.6 22.6 %collective-permute-start.18 = (f32[8,128,256]{2,1,0:T(8,128)}, f32[8,128,256]{2,1,0:T(8,128)S(1)}, u32[]{:S(2)}, u32[]{:S(2)}) collective-permute-start(f32[8,128,256]{2,1,0:T(8,128)} %get-tuple-element.99.refs_8_), channel_id=1, source_target_pairs={{0,16},{16,0},{32,48},{48,32},{64,80},{80,64},{96,112},{112,96},{1... | collective-permute-start | bytes 3145736 | tf_op jit(solution)/shard_map/ppermute | solution.py:622
  101.3 10.2 %collective-permute-start.21 = (f32[2,32,1024]{2,1,0:T(8,128)S(1)}, f32[2,32,1024]{2,1,0:T(8,128)S(1)}, u32[]{:S(2)}, u32[]{:S(2)}) collective-permute-start(f32[2,32,1024]{2,1,0:T(8,128)S(1)} %copy-done.4), channel_id=1, source_target_pairs={{0,96},{16,112},{32,0},{48,16},{64,32},{80,48},{96,64},{112,80},{1... | collective-permute-start | bytes 786440 | tf_op jit(solution)/shard_map/ppermute | solution.py:618
  102.8 9.1 %collective-permute-start.20 = (f32[2,32,1024]{2,1,0:T(8,128)S(1)}, f32[2,32,1024]{2,1,0:T(8,128)S(1)}, u32[]{:S(2)}, u32[]{:S(2)}) collective-permute-start(f32[2,32,1024]{2,1,0:T(8,128)S(1)} %copy-done.4), channel_id=1, source_target_pairs={{0,64},{16,80},{32,96},{48,112},{64,0},{80,16},{96,32},{112,48},{1... | collective-permute-start | bytes 786440 | tf_op jit(solution)/shard_map/ppermute | solution.py:618
  103.2 15.6 %collective-permute-start.19 = (f32[2,32,1024]{2,1,0:T(8,128)S(1)}, f32[2,32,1024]{2,1,0:T(8,128)S(1)}, u32[]{:S(2)}, u32[]{:S(2)}) collective-permute-start(f32[2,32,1024]{2,1,0:T(8,128)S(1)} %copy-done.4), channel_id=1, source_target_pairs={{0,32},{16,48},{32,64},{48,80},{64,96},{80,112},{96,0},{112,16},{1... | collective-permute-start | bytes 786440 | tf_op jit(solution)/shard_map/ppermute | solution.py:618
  104.1 17.1 %all-to-all-start.3 = ((f32[128,1,128]{2,1,0:T(1,128)}), f32[128,1,128]{2,1,0:T(1,128)S(1)}, u32[]{:S(2)}, u32[]{:S(2)}) async-start(f32[128,1,128]{2,1,0:T(1,128)} %bitcast.31), calls=%async_computation.3 | async-start | bytes 131072 | tf_op jit(solution)/shard_map/all_to_all | solution.py:801
  111.5 19.5 %copy-start.5 = (f32[2,32,1024]{2,1,0:T(8,128)}, f32[2,32,1024]{2,1,0:T(8,128)S(1)}, u32[]{:S(2)}) copy-start(f32[2,32,1024]{2,1,0:T(8,128)S(1)} %collective-permute-done.21.refs_12_.refs_5_) | copy-start | bytes 786436
  111.9 19.1 %copy-start.6 = (f32[2,32,1024]{2,1,0:T(8,128)}, f32[2,32,1024]{2,1,0:T(8,128)S(1)}, u32[]{:S(2)}) copy-start(f32[2,32,1024]{2,1,0:T(8,128)S(1)} %collective-permute-done.20.refs_11_.refs_4_) | copy-start | bytes 786436
  118.8 12.2 %copy-start.7 = (f32[2,32,1024]{2,1,0:T(8,128)}, f32[2,32,1024]{2,1,0:T(8,128)S(1)}, u32[]{:S(2)}) copy-start(f32[2,32,1024]{2,1,0:T(8,128)S(1)} %collective-permute-done.19.refs_10_.refs_3_) | copy-start | bytes 786436
  131.0 3.7 %collective-permute-start.22 = (f32[16,9,8,256]{3,2,1,0:T(8,128)S(1)}, f32[16,9,8,256]{3,2,1,0:T(8,128)S(1)}, u32[]{:S(2)}, u32[]{:S(2)}) collective-permute-start(f32[16,9,8,256]{3,2,1,0:T(8,128)S(1)} %get-tuple-element.103), channel_id=1, source_target_pairs={{0,16},{16,0},{32,48},{48,32},{64,80},{80,64},{96,112},{112,96},{1... | collective-permute-start | bytes 3538952 | tf_op jit(solution)/shard_map/ppermute | solution.py:622
  131.8 2.8 %collective-permute-start.23 = (f32[4,2,32,256]{3,2,1,0:T(8,128)S(1)}, f32[4,2,32,256]{3,2,1,0:T(8,128)S(1)}, u32[]{:S(2)}, u32[]{:S(2)}) collective-permute-start(f32[4,2,32,256]{3,2,1,0:T(8,128)S(1)} %get-tuple-element.105), channel_id=1, source_target_pairs={{0,16},{16,0},{32,48},{48,32},{64,80},{80,64},{96,112},{112,96},{1... | collective-permute-start | bytes 786440 | tf_op jit(solution)/shard_map/ppermute | solution.py:622
  135.8 22.3 %all-to-all-start.4 = ((f32[16,9,8,256]{3,2,1,0:T(8,128)}), f32[16,9,8,256]{3,2,1,0:T(8,128)S(1)}, u32[]{:S(2)}, u32[]{:S(2)}) async-start(f32[16,9,8,256]{3,2,1,0:T(8,128)} %get-tuple-element.111), calls=%async_computation.4 | async-start | bytes 2359296 | tf_op jit(solution)/shard_map/all_to_all | solution.py:758
  139.5 6.5 %collective-permute-start.24 = (f32[2,2,32,256]{3,2,1,0:T(8,128)S(1)}, f32[2,2,32,256]{3,2,1,0:T(8,128)S(1)}, u32[]{:S(2)}, u32[]{:S(2)}) collective-permute-start(f32[2,2,32,256]{3,2,1,0:T(8,128)S(1)} %get-tuple-element.107), channel_id=1, source_target_pairs={{0,32},{16,48},{32,64},{48,80},{64,96},{80,112},{96,0},{112,16},{1... | collective-permute-start | bytes 393224 | tf_op jit(solution)/shard_map/ppermute | solution.py:618
  139.9 7.8 %collective-permute-start.25 = (f32[2,2,32,256]{3,2,1,0:T(8,128)S(1)}, f32[2,2,32,256]{3,2,1,0:T(8,128)S(1)}, u32[]{:S(2)}, u32[]{:S(2)}) collective-permute-start(f32[2,2,32,256]{3,2,1,0:T(8,128)S(1)} %get-tuple-element.108), channel_id=1, source_target_pairs={{0,64},{16,80},{32,96},{48,112},{64,0},{80,16},{96,32},{112,48},{1... | collective-permute-start | bytes 393224 | tf_op jit(solution)/shard_map/ppermute | solution.py:618
  141.6 7.0 %collective-permute-start.26 = (f32[2,2,32,256]{3,2,1,0:T(8,128)S(1)}, f32[2,2,32,256]{3,2,1,0:T(8,128)S(1)}, u32[]{:S(2)}, u32[]{:S(2)}) collective-permute-start(f32[2,2,32,256]{3,2,1,0:T(8,128)S(1)} %get-tuple-element.109), channel_id=1, source_target_pairs={{0,96},{16,112},{32,0},{48,16},{64,32},{80,48},{96,64},{112,80},{1... | collective-permute-start | bytes 393224 | tf_op jit(solution)/shard_map/ppermute | solution.py:618
  150.0 16.8 %collective-permute-start.30 = (f32[3,32,1024]{2,1,0:T(8,128)S(1)}, f32[3,32,1024]{2,1,0:T(8,128)S(1)}, u32[]{:S(2)}, u32[]{:S(2)}) collective-permute-start(f32[3,32,1024]{2,1,0:T(8,128)S(1)} %get-tuple-element.113.refs_4_), channel_id=1, source_target_pairs={{0,1},{1,2},{2,3},{3,4},{4,5},{5,6},{6,7},{7,8},{8,9},{9,10},{10,1... | collective-permute-start | bytes 1179656 | tf_op jit(solution)/shard_map/ppermute | solution.py:626
  150.8 16.0 %collective-permute-start.31 = (f32[3,32,1024]{2,1,0:T(8,128)S(1)}, f32[3,32,1024]{2,1,0:T(8,128)S(1)}, u32[]{:S(2)}, u32[]{:S(2)}) collective-permute-start(f32[3,32,1024]{2,1,0:T(8,128)S(1)} %get-tuple-element.114.refs_3_), channel_id=1, source_target_pairs={{1,0},{2,1},{3,2},{4,3},{5,4},{6,5},{7,6},{8,7},{9,8},{10,9},{11,1... | collective-permute-start | bytes 1179656 | tf_op jit(solution)/shard_map/ppermute | solution.py:630
  159.3 7.5 %collective-permute-start.29 = (f32[9,8,256]{2,1,0:T(8,128)S(1)}, f32[9,8,256]{2,1,0:T(8,128)S(1)}, u32[]{:S(2)}, u32[]{:S(2)}) collective-permute-start(f32[9,8,256]{2,1,0:T(8,128)S(1)} %get-tuple-element.112.refs_0_), channel_id=1, source_target_pairs={{0,96},{16,112},{32,0},{48,16},{64,32},{80,48},{96,64},{112,80},{1... | collective-permute-start | bytes 221192 | tf_op jit(solution)/shard_map/ppermute | solution.py:618
  160.8 6.0 %collective-permute-start.28 = (f32[9,8,256]{2,1,0:T(8,128)S(1)}, f32[9,8,256]{2,1,0:T(8,128)S(1)}, u32[]{:S(2)}, u32[]{:S(2)}) collective-permute-start(f32[9,8,256]{2,1,0:T(8,128)S(1)} %get-tuple-element.112.refs_0_), channel_id=1, source_target_pairs={{0,64},{16,80},{32,96},{48,112},{64,0},{80,16},{96,32},{112,48},{1... | collective-permute-start | bytes 221192 | tf_op jit(solution)/shard_map/ppermute | solution.py:618
  162.1 4.7 %collective-permute-start.27 = (f32[9,8,256]{2,1,0:T(8,128)S(1)}, f32[9,8,256]{2,1,0:T(8,128)S(1)}, u32[]{:S(2)}, u32[]{:S(2)}) collective-permute-start(f32[9,8,256]{2,1,0:T(8,128)S(1)} %get-tuple-element.112.refs_0_), channel_id=1, source_target_pairs={{0,32},{16,48},{32,64},{48,80},{64,96},{80,112},{96,0},{112,16},{1... | collective-permute-start | bytes 221192 | tf_op jit(solution)/shard_map/ppermute | solution.py:618
  168.7 23.8 %all-to-all-start.5 = ((f32[16,10,8,256]{3,2,1,0:T(8,128)}), f32[16,10,8,256]{3,2,1,0:T(8,128)S(1)}, u32[]{:S(2)}, u32[]{:S(2)}) async-start(f32[16,10,8,256]{3,2,1,0:T(8,128)} %get-tuple-element.116), calls=%async_computation.5 | async-start | bytes 2621440 | tf_op jit(solution)/shard_map/all_to_all | solution.py:772
  172.8 14.5 %copy-start.1 = (f32[2,256,256]{2,1,0:T(8,128)S(1)}, f32[2,256,256]{2,1,0:T(8,128)}, u32[]{:S(2)}) copy-start(f32[2,256,256]{2,1,0:T(8,128)} %get-tuple-element.122.refs_7_) | copy-start | bytes 1572868
  174.3 19.5 %copy-start.8 = (f32[2,32,1024]{2,1,0:T(8,128)}, f32[2,32,1024]{2,1,0:T(8,128)S(1)}, u32[]{:S(2)}) copy-start(f32[2,32,1024]{2,1,0:T(8,128)S(1)} %get-tuple-element.127.refs_6_) | copy-start | bytes 786436
  174.4 6.6 %collective-permute-start.32 = (f32[2,2,32,256]{3,2,1,0:T(8,128)S(1)}, f32[2,2,32,256]{3,2,1,0:T(8,128)S(1)}, u32[]{:S(2)}, u32[]{:S(2)}) collective-permute-start(f32[2,2,32,256]{3,2,1,0:T(8,128)S(1)} %get-tuple-element.119), channel_id=1, source_target_pairs={{0,32},{16,48},{32,64},{48,80},{64,96},{80,112},{96,0},{112,16},{1... | collective-permute-start | bytes 393224 | tf_op jit(solution)/shard_map/ppermute | solution.py:618
  174.4 6.6 %collective-permute-start.33 = (f32[2,2,32,256]{3,2,1,0:T(8,128)S(1)}, f32[2,2,32,256]{3,2,1,0:T(8,128)S(1)}, u32[]{:S(2)}, u32[]{:S(2)}) collective-permute-start(f32[2,2,32,256]{3,2,1,0:T(8,128)S(1)} %get-tuple-element.120), channel_id=1, source_target_pairs={{0,64},{16,80},{32,96},{48,112},{64,0},{80,16},{96,32},{112,48},{1... | collective-permute-start | bytes 393224 | tf_op jit(solution)/shard_map/ppermute | solution.py:618
  177.0 4.8 %collective-permute-start.34 = (f32[2,2,32,256]{3,2,1,0:T(8,128)S(1)}, f32[2,2,32,256]{3,2,1,0:T(8,128)S(1)}, u32[]{:S(2)}, u32[]{:S(2)}) collective-permute-start(f32[2,2,32,256]{3,2,1,0:T(8,128)S(1)} %get-tuple-element.121), channel_id=1, source_target_pairs={{0,96},{16,112},{32,0},{48,16},{64,32},{80,48},{96,64},{112,80},{1... | collective-permute-start | bytes 393224 | tf_op jit(solution)/shard_map/ppermute | solution.py:618
  181.8 5.6 %collective-permute-start.35 = (f32[4,2,32,256]{3,2,1,0:T(8,128)S(1)}, f32[4,2,32,256]{3,2,1,0:T(8,128)S(1)}, u32[]{:S(2)}, u32[]{:S(2)}) collective-permute-start(f32[4,2,32,256]{3,2,1,0:T(8,128)S(1)} %stack_kernel.3), channel_id=1, source_target_pairs={{0,16},{16,0},{32,48},{48,32},{64,80},{80,64},{96,112},{112,96},{1... | collective-permute-start | bytes 786440 | tf_op jit(solution)/shard_map/ppermute | solution.py:622
  189.1 3.4 %collective-permute-start.36 = (f32[2,128,256]{2,1,0:T(8,128)S(1)}, f32[2,128,256]{2,1,0:T(8,128)S(1)}, u32[]{:S(2)}, u32[]{:S(2)}) collective-permute-start(f32[2,128,256]{2,1,0:T(8,128)S(1)} %get-tuple-element.124), channel_id=1, source_target_pairs={{0,16},{16,0},{32,48},{48,32},{64,80},{80,64},{96,112},{112,96},{1... | collective-permute-start | bytes 786440 | tf_op jit(solution)/shard_map/ppermute | solution.py:622
  189.4 14.1 %collective-permute-start.39 = (f32[2,32,1024]{2,1,0:T(8,128)S(1)}, f32[2,32,1024]{2,1,0:T(8,128)}, u32[]{:S(2)}, u32[]{:S(2)}) collective-permute-start(f32[2,32,1024]{2,1,0:T(8,128)S(1)} %get-tuple-element.127.refs_6_), channel_id=1, source_target_pairs={{0,96},{16,112},{32,0},{48,16},{64,32},{80,48},{96,64},{112,80},{1... | collective-permute-start | bytes 786440 | tf_op jit(solution)/shard_map/ppermute | solution.py:618
  191.8 11.7 %collective-permute-start.38 = (f32[2,32,1024]{2,1,0:T(8,128)S(1)}, f32[2,32,1024]{2,1,0:T(8,128)}, u32[]{:S(2)}, u32[]{:S(2)}) collective-permute-start(f32[2,32,1024]{2,1,0:T(8,128)S(1)} %get-tuple-element.127.refs_6_), channel_id=1, source_target_pairs={{0,64},{16,80},{32,96},{48,112},{64,0},{80,16},{96,32},{112,48},{1... | collective-permute-start | bytes 786440 | tf_op jit(solution)/shard_map/ppermute | solution.py:618
  191.8 14.9 %collective-permute-start.37 = (f32[2,32,1024]{2,1,0:T(8,128)S(1)}, f32[2,32,1024]{2,1,0:T(8,128)}, u32[]{:S(2)}, u32[]{:S(2)}) collective-permute-start(f32[2,32,1024]{2,1,0:T(8,128)S(1)} %get-tuple-element.127.refs_6_), channel_id=1, source_target_pairs={{0,32},{16,48},{32,64},{48,80},{64,96},{80,112},{96,0},{112,16},{1... | collective-permute-start | bytes 786440 | tf_op jit(solution)/shard_map/ppermute | solution.py:618
  193.9 21.8 %collective-permute-start.41 = (f32[8,128,256]{2,1,0:T(8,128)S(1)}, f32[8,128,256]{2,1,0:T(8,128)S(1)}, u32[]{:S(2)}, u32[]{:S(2)}) collective-permute-start(f32[8,128,256]{2,1,0:T(8,128)S(1)} %get-tuple-element.129.refs_3_), channel_id=1, source_target_pairs={{0,16},{16,0},{32,48},{48,32},{64,80},{80,64},{96,112},{112,96},{1... | collective-permute-start | bytes 3145736 | tf_op jit(solution)/shard_map/ppermute | solution.py:622
  196.0 17.2 %all-to-all-start.6 = ((f32[128,1,128]{2,1,0:T(1,128)}), f32[128,1,128]{2,1,0:T(1,128)S(1)}, u32[]{:S(2)}, u32[]{:S(2)}) async-start(f32[128,1,128]{2,1,0:T(1,128)} %bitcast.32), calls=%async_computation.6 | async-start | bytes 131072 | tf_op jit(solution)/shard_map/all_to_all | solution.py:801
  214.8 3.9 %collective-permute-start.40 = (f32[4,2,32,1024]{3,2,1,0:T(8,128)S(1)}, f32[4,2,32,1024]{3,2,1,0:T(8,128)S(1)}, u32[]{:S(2)}, u32[]{:S(2)}) collective-permute-start(f32[4,2,32,1024]{3,2,1,0:T(8,128)S(1)} %combine_kernel.1.refs_2_), channel_id=1, source_target_pairs={{0,16},{16,0},{32,48},{48,32},{64,80},{80,64},{96,112},{112,96},{1... | collective-permute-start | bytes 3145736 | tf_op jit(solution)/shard_map/ppermute | solution.py:622
  (1 other events, 0.7 us)

commit v8 on v7

--- a/solution.py
+++ b/solution.py
@@ -191,13 +191,11 @@
     e0 = here[0, 0] - where[3]
     first_core = c == 0
     rows_at = pl.multiple_of(H * c + 8 * where[2], 8)
-    model[...] = jnp.zeros_like(model)
-    obj[...] = jnp.zeros_like(obj)
-    power[...] = jnp.zeros_like(power)
-
-    def gather(plane, value):
-        obj[plane, 0, :N] += value[:, :H]
-        obj[plane, 1, :N] += value[:, H:]
+
+    def gather(k, plane, value):
+        for half in range(2):
+            part = value[:, half * H : half * H + H]
+            obj[plane, half, :N] = part if k == 0 else obj[plane, half, :N] + part
 
     def forward(k):
         if first:
@@ -210,7 +208,8 @@
             leave(1, k)
         pr, pi = probe_now[k, 0], probe_now[k, 1]
         orr, oi = patch_now[0], patch_now[1]
-        power[...] += pr * pr + pi * pi
+        size = pr * pr + pi * pi
+        power[...] = size if k == 0 else power[...] + size
         for part in range(2):
             near_rows[2 * k + part] = probe_now[k, part, pl.ds(rows_at, 8), :]
         xr = pr * orr - pi * oi
@@ -229,7 +228,8 @@
             )
             far = table_times(tab.at[2 + row], folded)
             psi[k, row] = far
-            model[row] += far[:H] * far[:H] + far[H:] * far[H:]
+            size = far[:H] * far[:H] + far[H:] * far[H:]
+            model[row] = size if k == 0 else model[row] + size
 
     if not first:
         ready(6)
@@ -261,8 +261,8 @@
         di = jnp.concatenate([even[:, H:] + odd[:, H:], even[:, H:] - odd[:, H:]], axis=1)
         pr, pi = probe_now[k, 0], probe_now[k, 1]
         orr, oi = patch_now[0], patch_now[1]
-        gather(0, pr * dr + pi * di)
-        gather(1, pr * di - pi * dr)
+        gather(k, 0, pr * dr + pi * di)
+        gather(k, 1, pr * di - pi * dr)
         put(2 * k, orr * dr + oi * di)
         put(2 * k + 1, orr * di - oi * dr)
 
@@ -399,6 +399,11 @@
     for s, dest in enumerate((b0, b1, b2, b3)):
         dest[0] = mine[s]
         dest[1] = part[s]
+
+
+def last_patch_kernel(*refs):
+    given, (kept, sent, lanes, dirp) = refs[:-4], refs[-4:]
+    patch_kernel(*given, dirp, kept, sent, lanes)
 
 
 def sum_kernel(before, shares, out, token):
@@ -782,14 +787,17 @@
         bands.append([band] + [along_y(band, s) for s in range(1, 4)])
         back = [r0] + [along_y(r, s) for s, r in ((1, r1), (2, r2), (3, r3))]
         (oth,) = call(stack_kernel, ((4, 2, 32, N),), back, (), room=4, cheap=True)
-        dirp, kept, sent_mixed = call(
-            patch_kernel,
-            ((2, N, N), (2, H, N), (2, H, N)),
+        last = iteration == ITERS - 1
+        halves_out = ((2, H, N), (2, H, N))
+        *dirps, kept, sent_mixed = call(
+            last_patch_kernel if last else patch_kernel,
+            halves_out if last else ((2, N, N),) + halves_out,
             (where, near, *back, partner(oth), patch),
             (0, 1),
-            ((2, 2, N + 8, H),),
+            ((2, 2, N + 8, H),) + (((2, N, N),) if last else ()),
             cheap=True,
         )
+        dirp = dirps[0] if dirps else None
         message, dmine = call(
             message_kernel,
             ((128, 128), (8, H, N)),

time: 223 us -> 222 us (level)
  no operation moved by 1% of the time
where the time goes in v8:
time: 222 us; the launch traced here: 221 us
  starting transfers between devices  102 us (46%)
  waiting for transfers between devices  63.8 us (29%)
  Pallas kernels  52.9 us (24%)
    pallas_call x26, Pallas kernels, call(): pl.pallas_call(run, out_shape=shapes, in_specs=[space(i, smem_in, hbm_in)...  51.2 us
    ppermute x24, waiting for transfers between devices, along_y(): return lax.ppermute(value, 'pat', [(i, (i + 2 * s) % 8) for i in range(8)])  28.3 us
    ppermute x24, starting transfers between devices, along_y(): return lax.ppermute(value, 'pat', [(i, (i + 2 * s) % 8) for i in range(8)])  27.3 us
    ppermute x12, starting transfers between devices, partner(): return lax.ppermute(value, 'pat', [(i, i ^ 1) for i in range(8)])  19.6 us
    all_to_all x2, starting transfers between devices, body(): messages.append(lax.all_to_all(message, BOTH, 0, 0))  14.2 us
    ppermute x3, starting transfers between devices, down(): return lax.ppermute(value, 'tile', [((i + 1) % 16, i) for i in range(16)])  12.7 us
    ppermute x12, waiting for transfers between devices, partner(): return lax.ppermute(value, 'pat', [(i, i ^ 1) for i in range(8)])  10.5 us
    all_to_all x2, starting transfers between devices, body(): shares = lax.all_to_all(chip, 'tile', 0, 0)  9.96 us
  transfers between devices with their start and end apart: 49, of which 28 were waited for; matrix products, arithmetic and copies ran while one was open for 0% of the time, Pallas kernels for 10%

profile of v8, /device:TPU:1, one launch (start us, length us, event | category | flops | bytes accessed | tf_op | source)
XLA Modules:
  0.0 221.4 jit_solution(10754109469753200486)
XLA Ops:
  0.8 1.8 shard_map.77
  2.5 2.1 collective-permute-start
  4.6 4.8 %collective-permute-start.1 = (f32[128,1024]{1,0:T(8,128)S(1)}, f32[128,1024]{1,0:T(8,128)S(1)}, u32[]{:S(2)}, u32[]{:S(2)}) collective-permute-start(f32[128,1024]{1,0:T(8,128)S(1)} %get-tuple-element.68), channel_id=1, source_target_pairs={{1,0},{2,1},{3,2},{4,3},{5,4},{6,5},{7,6},{8,7},{9,8},{10,9},{11,1... | collective-permute-start | bytes 1572872 | tf_op jit(solution)/shard_map/ppermute | solution.py:635
  9.5 1.1 announce_kernel.1
  10.6 5.4 %all-to-all-start = ((s32[8,1,128]{2,1,0:T(1,128)}), s32[8,1,128]{2,1,0:T(1,128)S(1)}, u32[]{:S(2)}, u32[]{:S(2)}) async-start(s32[8,1,128]{2,1,0:T(1,128)} %bitcast.5), calls=%async_computation | async-start | bytes 8192 | tf_op jit(solution)/shard_map/all_to_all | solution.py:658
  16.0 2.5 %prepare_kernel.1 = (f32[2,128,256]{2,1,0:T(8,128)S(1)}, f32[2,256,256]{2,1,0:T(8,128)S(1)}) custom-call(s32[4]{0:T(128)S(1)} %pad_add_fusion.refs_0_.where, s32[1,2]{1,0:T(1,128)S(1)} %copy-done.12, f32[256,256]{1,0:T(8,128)S(1)} %bitcast.28, bf16[2,256,256]{2,1,0:T(8,128)(2,1)S(1)} %copy-done.9, f32[2,256,1024]{2,1,0:T(8,128)} %refs_1_.7), custom_call_target="tpu_custom_call" | custom-call | bytes 3670040 | tf_op jit(solution)/shard_map/prepare_kernel/pallas_call | solution.py:600
  18.5 2.3 %all-to-all-done = s32[8,1,128]{2,1,0:T(1,128)S(1)} async-done(((s32[8,1,128]{2,1,0:T(1,128)}), s32[8,1,128]{2,1,0:T(1,128)S(1)}, u32[]{:S(2)}, u32[]{:S(2)}) %all-to-all-start) | async-done | bytes 4128 | tf_op jit(solution)/shard_map/all_to_all | solution.py:658
  21.8 1.3 collective-permute-start.2
  23.1 1.5 collective-permute-done.2.refs_4_
  24.6 7.9 %patterns.2 = (f32[2,256,256]{2,1,0:T(8,128)S(1)}, f32[16,9,8,256]{3,2,1,0:T(8,128)S(1)}, f32[16,9,8,256]{3,2,1,0:T(8,128)S(1)}, f32[4,2,32,256]{3,2,1,0:T(8,128...) custom-call(s32[4]{0:T(128)S(1)} %pad_add_fusion.refs_0_.where, ...), custom_call_target="tpu_custom_call" | custom-call | flops 6000000000 | bytes 9764888 | tf_op jit(solution)/shard_map/patterns/pallas_call | solution.py:600
  33.1 2.7 %collective-permute-done.4.refs_3_ = f32[4,2,32,256]{3,2,1,0:T(8,128)S(1)} collective-permute-done((f32[4,2,32,256]{3,2,1,0:T(8,128)S(1)}, f32[4,2,32,256]{3,2,1,0:T(8,128)S(1)}, u32[]{:S(2)}, u32[]{:S(2)}) %collective-permute-start.4) | collective-permute-done | bytes 262176 | tf_op jit(solution)/shard_map/ppermute | solution.py:627
  36.9 6.2 %all-to-all-start.1 = ((f32[16,9,8,256]{3,2,1,0:T(8,128)}), f32[16,9,8,256]{3,2,1,0:T(8,128)S(1)}, u32[]{:S(2)}, u32[]{:S(2)}) async-start(f32[16,9,8,256]{3,2,1,0:T(8,128)} %get-tuple-element.82), calls=%async_computation.1 | async-start | bytes 2359296 | tf_op jit(solution)/shard_map/all_to_all | solution.py:763
  43.2 1.4 collective-permute-start.5
  44.6 2.6 %collective-permute-start.6 = (f32[2,2,32,256]{3,2,1,0:T(8,128)S(1)}, f32[2,2,32,256]{3,2,1,0:T(8,128)S(1)}, u32[]{:S(2)}, u32[]{:S(2)}) collective-permute-start(f32[2,2,32,256]{3,2,1,0:T(8,128)S(1)} %get-tuple-element.79), channel_id=1, source_target_pairs={{0,64},{16,80},{32,96},{48,112},{64,0},{80,16},{96,32},{112,48},{1... | collective-permute-start | bytes 393224 | tf_op jit(solution)/shard_map/ppermute | solution.py:623
  49.2 3.8 %collective-permute-done.6.refs_5_ = f32[2,2,32,256]{3,2,1,0:T(8,128)S(1)} collective-permute-done((f32[2,2,32,256]{3,2,1,0:T(8,128)S(1)}, f32[2,2,32,256]{3,2,1,0:T(8,128)S(1)}, u32[]{:S(2)}, u32[]{:S(2)}) %collective-permute-start.6) | collective-permute-done | bytes 131104 | tf_op jit(solution)/shard_map/ppermute | solution.py:623
  52.9 1.4 place_kernel.2
  55.4 3.8 %collective-permute-start.12 = (f32[3,32,1024]{2,1,0:T(8,128)S(1)}, f32[3,32,1024]{2,1,0:T(8,128)S(1)}, u32[]{:S(2)}, u32[]{:S(2)}) collective-permute-start(f32[3,32,1024]{2,1,0:T(8,128)S(1)} %get-tuple-element.85.refs_3_), channel_id=1, source_target_pairs={{1,0},{2,1},{3,2},{4,3},{5,4},{6,5},{7,6},{8,7},{9,8},{10,9},{11,1... | collective-permute-start | bytes 1179656 | tf_op jit(solution)/shard_map/ppermute | solution.py:635
  59.2 1.9 all-to-all-done.1.refs_1_
  61.1 1.2 sum_kernel.2
  62.3 2.8 %collective-permute-start.10 = (f32[9,8,256]{2,1,0:T(8,128)S(1)}, f32[9,8,256]{2,1,0:T(8,128)S(1)}, u32[]{:S(2)}, u32[]{:S(2)}) collective-permute-start(f32[9,8,256]{2,1,0:T(8,128)S(1)} %get-tuple-element.83.refs_0_), channel_id=1, source_target_pairs={{0,96},{16,112},{32,0},{48,16},{64,32},{80,48},{96,64},{112,80},{1... | collective-permute-start | bytes 221192 | tf_op jit(solution)/shard_map/ppermute | solution.py:623
  66.2 3.7 %collective-permute-done.11.refs_4_.refs_5_ = f32[3,32,1024]{2,1,0:T(8,128)S(1)} collective-permute-done((f32[3,32,1024]{2,1,0:T(8,128)S(1)}, f32[3,32,1024]{2,1,0:T(8,128)S(1)}, u32[]{:S(2)}, u32[]{:S(2)}) %collective-permute-start.11) | collective-permute-done | bytes 393248 | tf_op jit(solution)/shard_map/ppermute | solution.py:631
  70.8 1.8 share_kernel.2
  72.6 4.5 %all-to-all-start.2 = ((f32[16,10,8,256]{3,2,1,0:T(8,128)}), f32[16,10,8,256]{3,2,1,0:T(8,128)S(1)}, u32[]{:S(2)}, u32[]{:S(2)}) async-start(f32[16,10,8,256]{3,2,1,0:T(8,128)} %get-tuple-element.87), calls=%async_computation.2 | async-start | bytes 2621440 | tf_op jit(solution)/shard_map/all_to_all | solution.py:777
  77.1 1.5 direction_kernel.2
  79.5 2.8 %collective-permute-start.14 = (f32[2,2,32,256]{3,2,1,0:T(8,128)S(1)}, f32[2,2,32,256]{3,2,1,0:T(8,128)S(1)}, u32[]{:S(2)}, u32[]{:S(2)}) collective-permute-start(f32[2,2,32,256]{3,2,1,0:T(8,128)S(1)} %get-tuple-element.91), channel_id=1, source_target_pairs={{0,64},{16,80},{32,96},{48,112},{64,0},{80,16},{96,32},{112,48},{1... | collective-permute-start | bytes 393224 | tf_op jit(solution)/shard_map/ppermute | solution.py:623
  84.3 1.7 collective-permute-done.14.refs_2_.refs_4_
  86.6 5.1 %collective-permute-start.16 = (f32[4,2,32,256]{3,2,1,0:T(8,128)S(1)}, f32[4,2,32,256]{3,2,1,0:T(8,128)S(1)}, u32[]{:S(2)}, u32[]{:S(2)}) collective-permute-start(f32[4,2,32,256]{3,2,1,0:T(8,128)S(1)} %stack_kernel.2), channel_id=1, source_target_pairs={{0,16},{16,0},{32,48},{48,32},{64,80},{80,64},{96,112},{112,96},{1... | collective-permute-start | bytes 786440 | tf_op jit(solution)/shard_map/ppermute | solution.py:627
  91.7 1.2 collective-permute-done.16.refs_6_
  95.0 1.2 collective-permute-done.17.refs_3_
  96.1 2.4 %message_kernel.2 = (f32[128,128]{1,0:T(8,128)}, f32[8,128,256]{2,1,0:T(8,128)}) custom-call(s32[4]{0:T(128)S(1)} %pad_add_fusion.refs_0_.where, f32[16,10,8,256]{3,2,1,0:T(8,128)S(1)} %all-to-all-done.2.refs_1_, f32[2,128,256]{2,1,0:T(8,128)S(1)} %get-tuple-element.94.refs_2_, f32[2,128,256]{2,1,0:T(8,128)S(1)} %collective-permute-done.17.refs_3_, ...), custom_call_target="tpu_custom_call" | custom-call | bytes 2949152 | tf_op jit(solution)/shard_map/message_kernel/pallas_call | solution.py:600
  98.5 2.7 %collective-permute-start.18 = (f32[8,128,256]{2,1,0:T(8,128)}, f32[8,128,256]{2,1,0:T(8,128)S(1)}, u32[]{:S(2)}, u32[]{:S(2)}) collective-permute-start(f32[8,128,256]{2,1,0:T(8,128)} %get-tuple-element.99.refs_8_), channel_id=1, source_target_pairs={{0,16},{16,0},{32,48},{48,32},{64,80},{80,64},{96,112},{112,96},{1... | collective-permute-start | bytes 3145736 | tf_op jit(solution)/shard_map/ppermute | solution.py:627
  101.3 1.6 collective-permute-start.21
  104.1 7.4 %all-to-all-start.3 = ((f32[128,1,128]{2,1,0:T(1,128)}), f32[128,1,128]{2,1,0:T(1,128)S(1)}, u32[]{:S(2)}, u32[]{:S(2)}) async-start(f32[128,1,128]{2,1,0:T(1,128)} %bitcast.31), calls=%async_computation.3 | async-start | bytes 131072 | tf_op jit(solution)/shard_map/all_to_all | solution.py:809
  111.9 6.8 %collective-permute-done.19.refs_10_.refs_3_ = f32[2,32,1024]{2,1,0:T(8,128)S(1)} collective-permute-done((f32[2,32,1024]{2,1,0:T(8,128)S(1)}, f32[2,32,1024]{2,1,0:T(8,128)S(1)}, u32[]{:S(2)}, u32[]{:S(2)}) %collective-permute-start.19) | collective-permute-done | bytes 262176 | tf_op jit(solution)/shard_map/ppermute | solution.py:623
  118.7 2.4 %all-to-all-done.3 = f32[128,1,128]{2,1,0:T(1,128)S(1)} async-done(((f32[128,1,128]{2,1,0:T(1,128)}), f32[128,1,128]{2,1,0:T(1,128)S(1)}, u32[]{:S(2)}, u32[]{:S(2)}) %all-to-all-start.3) | async-done | bytes 65568 | tf_op jit(solution)/shard_map/all_to_all | solution.py:809
  121.2 9.7 %patterns.3 = (f32[2,256,256]{2,1,0:T(8,128)}, f32[4,2,256,256]{3,2,1,0:T(8,128)}, f32[16,9,8,256]{3,2,1,0:T(8,128)S(1)}, f32[16,9,8,256]{3,2,1,0:T(8,128)S(1)},...) custom-call(s32[4]{0:T(128)S(1)} %pad_add_fusion.refs_0_.where, ...), custom_call_target="tpu_custom_call" | custom-call | flops 6000000000 | bytes 14286872 | tf_op jit(solution)/shard_map/patterns/pallas_call | solution.py:600
  131.9 2.8 %collective-permute-done.23.refs_3_ = f32[4,2,32,256]{3,2,1,0:T(8,128)S(1)} collective-permute-done((f32[4,2,32,256]{3,2,1,0:T(8,128)S(1)}, f32[4,2,32,256]{3,2,1,0:T(8,128)S(1)}, u32[]{:S(2)}, u32[]{:S(2)}) %collective-permute-start.23) | collective-permute-done | bytes 262176 | tf_op jit(solution)/shard_map/ppermute | solution.py:627
  135.7 3.7 %all-to-all-start.4 = ((f32[16,9,8,256]{3,2,1,0:T(8,128)}), f32[16,9,8,256]{3,2,1,0:T(8,128)S(1)}, u32[]{:S(2)}, u32[]{:S(2)}) async-start(f32[16,9,8,256]{3,2,1,0:T(8,128)} %get-tuple-element.111), calls=%async_computation.4 | async-start | bytes 2359296 | tf_op jit(solution)/shard_map/all_to_all | solution.py:763
  139.8 1.7 collective-permute-start.25
  143.2 2.7 %collective-permute-done.24.refs_4_ = f32[2,2,32,256]{3,2,1,0:T(8,128)S(1)} collective-permute-done((f32[2,2,32,256]{3,2,1,0:T(8,128)S(1)}, f32[2,2,32,256]{3,2,1,0:T(8,128)S(1)}, u32[]{:S(2)}, u32[]{:S(2)}) %collective-permute-start.24) | collective-permute-done | bytes 131104 | tf_op jit(solution)/shard_map/ppermute | solution.py:623
  145.9 1.7 collective-permute-done.25.refs_5_
  148.5 1.4 place_kernel.3
  150.7 4.0 %collective-permute-start.31 = (f32[3,32,1024]{2,1,0:T(8,128)S(1)}, f32[3,32,1024]{2,1,0:T(8,128)S(1)}, u32[]{:S(2)}, u32[]{:S(2)}) collective-permute-start(f32[3,32,1024]{2,1,0:T(8,128)S(1)} %get-tuple-element.114.refs_3_), channel_id=1, source_target_pairs={{1,0},{2,1},{3,2},{4,3},{5,4},{6,5},{7,6},{8,7},{9,8},{10,9},{11,1... | collective-permute-start | bytes 1179656 | tf_op jit(solution)/shard_map/ppermute | solution.py:635
  154.8 3.2 %all-to-all-done.4.refs_1_ = f32[16,9,8,256]{3,2,1,0:T(8,128)S(1)} async-done(((f32[16,9,8,256]{3,2,1,0:T(8,128)}), f32[16,9,8,256]{3,2,1,0:T(8,128)S(1)}, u32[]{:S(2)}, u32[]{:S(2)}) %all-to-all-start.4) | async-done | bytes 1179680 | tf_op jit(solution)/shard_map/all_to_all | solution.py:763
  158.0 1.2 sum_kernel.3
  159.2 1.5 collective-permute-start.29
  160.8 1.3 collective-permute-start.28
  162.1 4.7 %collective-permute-done.30.refs_4_.refs_5_ = f32[3,32,1024]{2,1,0:T(8,128)S(1)} collective-permute-done((f32[3,32,1024]{2,1,0:T(8,128)S(1)}, f32[3,32,1024]{2,1,0:T(8,128)S(1)}, u32[]{:S(2)}, u32[]{:S(2)}) %collective-permute-start.30) | collective-permute-done | bytes 393248 | tf_op jit(solution)/shard_map/ppermute | solution.py:631
  166.8 1.8 share_kernel.3
  168.6 4.2 %all-to-all-start.5 = ((f32[16,10,8,256]{3,2,1,0:T(8,128)}), f32[16,10,8,256]{3,2,1,0:T(8,128)S(1)}, u32[]{:S(2)}, u32[]{:S(2)}) async-start(f32[16,10,8,256]{3,2,1,0:T(8,128)} %get-tuple-element.116), calls=%async_computation.5 | async-start | bytes 2621440 | tf_op jit(solution)/shard_map/all_to_all | solution.py:777
  172.8 1.5 direction_kernel.3
  174.4 2.6 %collective-permute-start.33 = (f32[2,2,32,256]{3,2,1,0:T(8,128)S(1)}, f32[2,2,32,256]{3,2,1,0:T(8,128)S(1)}, u32[]{:S(2)}, u32[]{:S(2)}) collective-permute-start(f32[2,2,32,256]{3,2,1,0:T(8,128)S(1)} %get-tuple-element.120), channel_id=1, source_target_pairs={{0,64},{16,80},{32,96},{48,112},{64,0},{80,16},{96,32},{112,48},{1... | collective-permute-start | bytes 393224 | tf_op jit(solution)/shard_map/ppermute | solution.py:623
  177.0 3.9 %collective-permute-done.32.refs_1_.refs_3_ = f32[2,2,32,256]{3,2,1,0:T(8,128)S(1)} collective-permute-done((f32[2,2,32,256]{3,2,1,0:T(8,128)S(1)}, f32[2,2,32,256]{3,2,1,0:T(8,128)S(1)}, u32[]{:S(2)}, u32[]{:S(2)}) %collective-permute-start.32) | collective-permute-done | bytes 131104 | tf_op jit(solution)/shard_map/ppermute | solution.py:623
  181.7 4.4 %collective-permute-start.35 = (f32[4,2,32,256]{3,2,1,0:T(8,128)S(1)}, f32[4,2,32,256]{3,2,1,0:T(8,128)S(1)}, u32[]{:S(2)}, u32[]{:S(2)}) collective-permute-start(f32[4,2,32,256]{3,2,1,0:T(8,128)S(1)} %stack_kernel.3), channel_id=1, source_target_pairs={{0,16},{16,0},{32,48},{48,32},{64,80},{80,64},{96,112},{112,96},{1... | collective-permute-start | bytes 786440 | tf_op jit(solution)/shard_map/ppermute | solution.py:627
  186.2 1.2 collective-permute-done.35.refs_6_
  188.7 2.4 %collective-permute-start.39 = (f32[2,32,1024]{2,1,0:T(8,128)S(1)}, f32[2,32,1024]{2,1,0:T(8,128)}, u32[]{:S(2)}, u32[]{:S(2)}) collective-permute-start(f32[2,32,1024]{2,1,0:T(8,128)S(1)} %get-tuple-element.127.refs_6_), channel_id=1, source_target_pairs={{0,96},{16,112},{32,0},{48,16},{64,32},{80,48},{96,64},{112,80},{1... | collective-permute-start | bytes 786440 | tf_op jit(solution)/shard_map/ppermute | solution.py:623
  191.7 1.4 message_kernel.3
  193.1 2.8 %collective-permute-start.41 = (f32[8,128,256]{2,1,0:T(8,128)S(1)}, f32[8,128,256]{2,1,0:T(8,128)S(1)}, u32[]{:S(2)}, u32[]{:S(2)}) collective-permute-start(f32[8,128,256]{2,1,0:T(8,128)S(1)} %get-tuple-element.129.refs_3_), channel_id=1, source_target_pairs={{0,16},{16,0},{32,48},{48,32},{64,80},{80,64},{96,112},{112,96},{1... | collective-permute-start | bytes 3145736 | tf_op jit(solution)/shard_map/ppermute | solution.py:627
  196.0 6.8 %all-to-all-start.6 = ((f32[128,1,128]{2,1,0:T(1,128)}), f32[128,1,128]{2,1,0:T(1,128)S(1)}, u32[]{:S(2)}, u32[]{:S(2)}) async-start(f32[128,1,128]{2,1,0:T(1,128)} %bitcast.32), calls=%async_computation.6 | async-start | bytes 131072 | tf_op jit(solution)/shard_map/all_to_all | solution.py:809
  202.8 3.2 %collective-permute-done.37.refs_7_ = f32[2,32,1024]{2,1,0:T(8,128)} collective-permute-done((f32[2,32,1024]{2,1,0:T(8,128)S(1)}, f32[2,32,1024]{2,1,0:T(8,128)}, u32[]{:S(2)}, u32[]{:S(2)}) %collective-permute-start.37) | collective-permute-done | bytes 262176 | tf_op jit(solution)/shard_map/ppermute | solution.py:623
  206.0 6.5 %all-to-all-done.6 = f32[128,1,128]{2,1,0:T(1,128)S(1)} async-done(((f32[128,1,128]{2,1,0:T(1,128)}), f32[128,1,128]{2,1,0:T(1,128)S(1)}, u32[]{:S(2)}, u32[]{:S(2)}) %all-to-all-start.6) | async-done | bytes 65568 | tf_op jit(solution)/shard_map/all_to_all | solution.py:809
  212.5 1.6 combine_kernel.1.refs_2_
  215.0 3.0 %probe_kernel.1 = f32[4,2,256,256]{3,2,1,0:T(8,128)} custom-call(s32[4]{0:T(128)S(1)} %pad_add_fusion.refs_0_.where, f32[128,128]{1,0:T(8,128)S(1)} %bitcast.18, f32[4,2,256,256]{3,2,1,0:T(8,128)} %get-tuple-element.128.refs_2_, f32[8,128,256]{2,1,0:T(8,128)S(1)} %get-tuple-element.129.refs_3_, f32[8,128,256]{2,1,0:T(8,128)S(1)} %collective-permute-done.41.refs_4_), custom_call_target="tpu_custom_call" | custom-call | flops 1000000000 | bytes 6357008 | tf_op jit(solution)/shard_map/probe_kernel/pallas_call | solution.py:600
  218.0 3.2 %object_kernel.1 = f32[2,256,1024]{2,1,0:T(8,128)} custom-call(s32[4]{0:T(128)S(1)} %pad_add_fusion.refs_0_.where, f32[2,256,1024]{2,1,0:T(8,128)} %refs_1_.7, f32[4,2,32,1024]{3,2,1,0:T(8,128)S(1)} %combine_kernel.1.refs_2_, f32[4,2,32,1024]{3,2,1,0:T(8,128)S(1)} %collective-permute-done.40.refs_3_), custom_call_target="tpu_custom_call" | custom-call | bytes 6291472 | tf_op jit(solution)/shard_map/object_kernel/pallas_call | solution.py:600
  (94 shorter events, 24.6 us)
Async XLA Ops:
  0.6 15.4 %copy-start.9 = (bf16[2,256,256]{2,1,0:T(8,128)(2,1)S(1)}, bf16[2,256,256]{2,1,0:T(8,128)(2,1)}, u32[]{:S(2)}) copy-start(bf16[2,256,256]{2,1,0:T(8,128)(2,1)} %constant.43.clone.refs_3_) | copy-start | bytes 786436
  0.6 8.8 %copy-start.12 = (s32[1,2]{1,0:T(1,128)S(1)}, s32[1,2]{1,0:T(1,128)}, u32[]{:S(2)}) copy-start(s32[1,2]{1,0:T(1,128)} %refs_1_.6) | copy-start | bytes 28
  0.7 15.4 %copy-start.2 = (f32[1,256,256]{2,1,0:T(8,128)S(1)}, f32[1,256,256]{2,1,0:T(8,128)}, u32[]{:S(2)}) copy-start(f32[1,256,256]{2,1,0:T(8,128)} %param.6) | copy-start | bytes 786436
  2.5 18.5 %collective-permute-start = (f32[128,1024]{1,0:T(8,128)S(1)}, f32[128,1024]{1,0:T(8,128)S(1)}, u32[]{:S(2)}, u32[]{:S(2)}) collective-permute-start(f32[128,1024]{1,0:T(8,128)S(1)} %get-tuple-element.67), channel_id=1, source_target_pairs={{0,1},{1,2},{2,3},{3,4},{4,5},{5,6},{6,7},{7,8},{8,9},{9,10},{10,1... | collective-permute-start | bytes 1572872 | tf_op jit(solution)/shard_map/ppermute | solution.py:631
  4.6 16.4 %collective-permute-start.1 = (f32[128,1024]{1,0:T(8,128)S(1)}, f32[128,1024]{1,0:T(8,128)S(1)}, u32[]{:S(2)}, u32[]{:S(2)}) collective-permute-start(f32[128,1024]{1,0:T(8,128)S(1)} %get-tuple-element.68), channel_id=1, source_target_pairs={{1,0},{2,1},{3,2},{4,3},{5,4},{6,5},{7,6},{8,7},{9,8},{10,9},{11,1... | collective-permute-start | bytes 1572872 | tf_op jit(solution)/shard_map/ppermute | solution.py:635
  10.6 10.2 %all-to-all-start = ((s32[8,1,128]{2,1,0:T(1,128)}), s32[8,1,128]{2,1,0:T(1,128)S(1)}, u32[]{:S(2)}, u32[]{:S(2)}) async-start(s32[8,1,128]{2,1,0:T(1,128)} %bitcast.5), calls=%async_computation | async-start | bytes 8192 | tf_op jit(solution)/shard_map/all_to_all | solution.py:658
  18.5 14.0 %copy-start.14 = (f32[2,128,256]{2,1,0:T(8,128)}, f32[2,128,256]{2,1,0:T(8,128)S(1)}, u32[]{:S(2)}) copy-start(f32[2,128,256]{2,1,0:T(8,128)S(1)} %get-tuple-element.71.refs_6_.refs_5_) | copy-start | bytes 786436
  20.8 3.8 %copy-start.15 = (bf16[4,2,256,256]{3,2,1,0:T(8,128)(2,1)S(1)}, bf16[4,2,256,256]{3,2,1,0:T(8,128)(2,1)}, u32[]{:S(2)}) copy-start(bf16[4,2,256,256]{3,2,1,0:T(8,128)(2,1)} %constant.42.clone.refs_7_.refs_6_) | copy-start | bytes 3145732
  21.8 2.8 %collective-permute-start.2 = (f32[128,1024]{1,0:T(8,128)S(1)}, f32[128,1024]{1,0:T(8,128)S(1)}, u32[]{:S(2)}, u32[]{:S(2)}) collective-permute-start(f32[128,1024]{1,0:T(8,128)S(1)} %get-tuple-element.70), channel_id=1, source_target_pairs={{0,16},{16,0},{32,48},{48,32},{64,80},{80,64},{96,112},{112,96},{1... | collective-permute-start | bytes 1572872 | tf_op jit(solution)/shard_map/ppermute | solution.py:627
  32.5 4.4 %copy-start.10 = (f32[8,8,256]{2,1,0:T(8,128)}, f32[8,8,256]{2,1,0:T(8,128)S(1)}, u32[]{:S(2)}) copy-start(f32[8,8,256]{2,1,0:T(8,128)S(1)} %get-tuple-element.86.refs_6_) | copy-start | bytes 196612
  32.5 60.3 %copy-start = (f32[2,256,256]{2,1,0:T(8,128)}, f32[2,256,256]{2,1,0:T(8,128)S(1)}, u32[]{:S(2)}) copy-start(f32[2,256,256]{2,1,0:T(8,128)S(1)} %get-tuple-element.93.refs_7_.refs_3_) | copy-start | bytes 1572868
  32.5 3.3 %collective-permute-start.3 = (f32[16,9,8,256]{3,2,1,0:T(8,128)S(1)}, f32[16,9,8,256]{3,2,1,0:T(8,128)S(1)}, u32[]{:S(2)}, u32[]{:S(2)}) collective-permute-start(f32[16,9,8,256]{3,2,1,0:T(8,128)S(1)} %get-tuple-element.74), channel_id=1, source_target_pairs={{0,16},{16,0},{32,48},{48,32},{64,80},{80,64},{96,112},{112,96},{1... | collective-permute-start | bytes 3538952 | tf_op jit(solution)/shard_map/ppermute | solution.py:627
  33.0 2.8 %collective-permute-start.4 = (f32[4,2,32,256]{3,2,1,0:T(8,128)S(1)}, f32[4,2,32,256]{3,2,1,0:T(8,128)S(1)}, u32[]{:S(2)}, u32[]{:S(2)}) collective-permute-start(f32[4,2,32,256]{3,2,1,0:T(8,128)S(1)} %get-tuple-element.76), channel_id=1, source_target_pairs={{0,16},{16,0},{32,48},{48,32},{64,80},{80,64},{96,112},{112,96},{1... | collective-permute-start | bytes 786440 | tf_op jit(solution)/shard_map/ppermute | solution.py:627
  36.9 24.2 %all-to-all-start.1 = ((f32[16,9,8,256]{3,2,1,0:T(8,128)}), f32[16,9,8,256]{3,2,1,0:T(8,128)S(1)}, u32[]{:S(2)}, u32[]{:S(2)}) async-start(f32[16,9,8,256]{3,2,1,0:T(8,128)} %get-tuple-element.82), calls=%async_computation.1 | async-start | bytes 2359296 | tf_op jit(solution)/shard_map/all_to_all | solution.py:763
  43.2 6.0 %collective-permute-start.5 = (f32[2,2,32,256]{3,2,1,0:T(8,128)S(1)}, f32[2,2,32,256]{3,2,1,0:T(8,128)S(1)}, u32[]{:S(2)}, u32[]{:S(2)}) collective-permute-start(f32[2,2,32,256]{3,2,1,0:T(8,128)S(1)} %get-tuple-element.78), channel_id=1, source_target_pairs={{0,32},{16,48},{32,64},{48,80},{64,96},{80,112},{96,0},{112,16},{1... | collective-permute-start | bytes 393224 | tf_op jit(solution)/shard_map/ppermute | solution.py:623
  44.6 8.4 %collective-permute-start.6 = (f32[2,2,32,256]{3,2,1,0:T(8,128)S(1)}, f32[2,2,32,256]{3,2,1,0:T(8,128)S(1)}, u32[]{:S(2)}, u32[]{:S(2)}) collective-permute-start(f32[2,2,32,256]{3,2,1,0:T(8,128)S(1)} %get-tuple-element.79), channel_id=1, source_target_pairs={{0,64},{16,80},{32,96},{48,112},{64,0},{80,16},{96,32},{112,48},{1... | collective-permute-start | bytes 393224 | tf_op jit(solution)/shard_map/ppermute | solution.py:623
  47.2 5.7 %collective-permute-start.7 = (f32[2,2,32,256]{3,2,1,0:T(8,128)S(1)}, f32[2,2,32,256]{3,2,1,0:T(8,128)S(1)}, u32[]{:S(2)}, u32[]{:S(2)}) collective-permute-start(f32[2,2,32,256]{3,2,1,0:T(8,128)S(1)} %get-tuple-element.80), channel_id=1, source_target_pairs={{0,96},{16,112},{32,0},{48,16},{64,32},{80,48},{96,64},{112,80},{1... | collective-permute-start | bytes 393224 | tf_op jit(solution)/shard_map/ppermute | solution.py:623
  49.2 21.6 %copy-start.11 = (f32[8,8,256]{2,1,0:T(8,128)S(1)}, f32[8,8,256]{2,1,0:T(8,128)}, u32[]{:S(2)}) copy-start(f32[8,8,256]{2,1,0:T(8,128)} %copy-done.10) | copy-start | bytes 196612
  54.4 15.6 %collective-permute-start.11 = (f32[3,32,1024]{2,1,0:T(8,128)S(1)}, f32[3,32,1024]{2,1,0:T(8,128)S(1)}, u32[]{:S(2)}, u32[]{:S(2)}) collective-permute-start(f32[3,32,1024]{2,1,0:T(8,128)S(1)} %get-tuple-element.84.refs_4_), channel_id=1, source_target_pairs={{0,1},{1,2},{2,3},{3,4},{4,5},{5,6},{6,7},{7,8},{8,9},{9,10},{10,1... | collective-permute-start | bytes 1179656 | tf_op jit(solution)/shard_map/ppermute | solution.py:631
  55.4 14.5 %collective-permute-start.12 = (f32[3,32,1024]{2,1,0:T(8,128)S(1)}, f32[3,32,1024]{2,1,0:T(8,128)S(1)}, u32[]{:S(2)}, u32[]{:S(2)}) collective-permute-start(f32[3,32,1024]{2,1,0:T(8,128)S(1)} %get-tuple-element.85.refs_3_), channel_id=1, source_target_pairs={{1,0},{2,1},{3,2},{4,3},{5,4},{6,5},{7,6},{8,7},{9,8},{10,9},{11,1... | collective-permute-start | bytes 1179656 | tf_op jit(solution)/shard_map/ppermute | solution.py:635
  62.3 7.6 %collective-permute-start.10 = (f32[9,8,256]{2,1,0:T(8,128)S(1)}, f32[9,8,256]{2,1,0:T(8,128)S(1)}, u32[]{:S(2)}, u32[]{:S(2)}) collective-permute-start(f32[9,8,256]{2,1,0:T(8,128)S(1)} %get-tuple-element.83.refs_0_), channel_id=1, source_target_pairs={{0,96},{16,112},{32,0},{48,16},{64,32},{80,48},{96,64},{112,80},{1... | collective-permute-start | bytes 221192 | tf_op jit(solution)/shard_map/ppermute | solution.py:623
  65.2 5.0 %collective-permute-start.9 = (f32[9,8,256]{2,1,0:T(8,128)S(1)}, f32[9,8,256]{2,1,0:T(8,128)S(1)}, u32[]{:S(2)}, u32[]{:S(2)}) collective-permute-start(f32[9,8,256]{2,1,0:T(8,128)S(1)} %get-tuple-element.83.refs_0_), channel_id=1, source_target_pairs={{0,64},{16,80},{32,96},{48,112},{64,0},{80,16},{96,32},{112,48},{1... | collective-permute-start | bytes 221192 | tf_op jit(solution)/shard_map/ppermute | solution.py:623
  65.5 5.3 %collective-permute-start.8 = (f32[9,8,256]{2,1,0:T(8,128)S(1)}, f32[9,8,256]{2,1,0:T(8,128)S(1)}, u32[]{:S(2)}, u32[]{:S(2)}) collective-permute-start(f32[9,8,256]{2,1,0:T(8,128)S(1)} %get-tuple-element.83.refs_0_), channel_id=1, source_target_pairs={{0,32},{16,48},{32,64},{48,80},{64,96},{80,112},{96,0},{112,16},{1... | collective-permute-start | bytes 221192 | tf_op jit(solution)/shard_map/ppermute | solution.py:623
  72.6 23.5 %all-to-all-start.2 = ((f32[16,10,8,256]{3,2,1,0:T(8,128)}), f32[16,10,8,256]{3,2,1,0:T(8,128)S(1)}, u32[]{:S(2)}, u32[]{:S(2)}) async-start(f32[16,10,8,256]{3,2,1,0:T(8,128)} %get-tuple-element.87), calls=%async_computation.2 | async-start | bytes 2621440 | tf_op jit(solution)/shard_map/all_to_all | solution.py:777
  79.3 5.0 %collective-permute-start.13 = (f32[2,2,32,256]{3,2,1,0:T(8,128)S(1)}, f32[2,2,32,256]{3,2,1,0:T(8,128)S(1)}, u32[]{:S(2)}, u32[]{:S(2)}) collective-permute-start(f32[2,2,32,256]{3,2,1,0:T(8,128)S(1)} %get-tuple-element.90), channel_id=1, source_target_pairs={{0,32},{16,48},{32,64},{48,80},{64,96},{80,112},{96,0},{112,16},{1... | collective-permute-start | bytes 393224 | tf_op jit(solution)/shard_map/ppermute | solution.py:623
  79.5 6.6 %collective-permute-start.14 = (f32[2,2,32,256]{3,2,1,0:T(8,128)S(1)}, f32[2,2,32,256]{3,2,1,0:T(8,128)S(1)}, u32[]{:S(2)}, u32[]{:S(2)}) collective-permute-start(f32[2,2,32,256]{3,2,1,0:T(8,128)S(1)} %get-tuple-element.91), channel_id=1, source_target_pairs={{0,64},{16,80},{32,96},{48,112},{64,0},{80,16},{96,32},{112,48},{1... | collective-permute-start | bytes 393224 | tf_op jit(solution)/shard_map/ppermute | solution.py:623
  82.3 4.3 %collective-permute-start.15 = (f32[2,2,32,256]{3,2,1,0:T(8,128)S(1)}, f32[2,2,32,256]{3,2,1,0:T(8,128)S(1)}, u32[]{:S(2)}, u32[]{:S(2)}) collective-permute-start(f32[2,2,32,256]{3,2,1,0:T(8,128)S(1)} %get-tuple-element.92), channel_id=1, source_target_pairs={{0,96},{16,112},{32,0},{48,16},{64,32},{80,48},{96,64},{112,80},{1... | collective-permute-start | bytes 393224 | tf_op jit(solution)/shard_map/ppermute | solution.py:623
  86.6 6.3 %collective-permute-start.16 = (f32[4,2,32,256]{3,2,1,0:T(8,128)S(1)}, f32[4,2,32,256]{3,2,1,0:T(8,128)S(1)}, u32[]{:S(2)}, u32[]{:S(2)}) collective-permute-start(f32[4,2,32,256]{3,2,1,0:T(8,128)S(1)} %stack_kernel.2), channel_id=1, source_target_pairs={{0,16},{16,0},{32,48},{48,32},{64,80},{80,64},{96,112},{112,96},{1... | collective-permute-start | bytes 786440 | tf_op jit(solution)/shard_map/ppermute | solution.py:627
  93.8 0.8 copy-start.13
  94.6 6.7 %copy-start.4 = (f32[2,32,1024]{2,1,0:T(8,128)S(1)}, f32[2,32,1024]{2,1,0:T(8,128)}, u32[]{:S(2)}) copy-start(f32[2,32,1024]{2,1,0:T(8,128)} %copy-done.3) | copy-start | bytes 786436
  94.6 1.5 collective-permute-start.17
  98.5 22.6 %collective-permute-start.18 = (f32[8,128,256]{2,1,0:T(8,128)}, f32[8,128,256]{2,1,0:T(8,128)S(1)}, u32[]{:S(2)}, u32[]{:S(2)}) collective-permute-start(f32[8,128,256]{2,1,0:T(8,128)} %get-tuple-element.99.refs_8_), channel_id=1, source_target_pairs={{0,16},{16,0},{32,48},{48,32},{64,80},{80,64},{96,112},{112,96},{1... | collective-permute-start | bytes 3145736 | tf_op jit(solution)/shard_map/ppermute | solution.py:627
  101.3 10.2 %collective-permute-start.21 = (f32[2,32,1024]{2,1,0:T(8,128)S(1)}, f32[2,32,1024]{2,1,0:T(8,128)S(1)}, u32[]{:S(2)}, u32[]{:S(2)}) collective-permute-start(f32[2,32,1024]{2,1,0:T(8,128)S(1)} %copy-done.4), channel_id=1, source_target_pairs={{0,96},{16,112},{32,0},{48,16},{64,32},{80,48},{96,64},{112,80},{1... | collective-permute-start | bytes 786440 | tf_op jit(solution)/shard_map/ppermute | solution.py:623
  102.8 9.1 %collective-permute-start.20 = (f32[2,32,1024]{2,1,0:T(8,128)S(1)}, f32[2,32,1024]{2,1,0:T(8,128)S(1)}, u32[]{:S(2)}, u32[]{:S(2)}) collective-permute-start(f32[2,32,1024]{2,1,0:T(8,128)S(1)} %copy-done.4), channel_id=1, source_target_pairs={{0,64},{16,80},{32,96},{48,112},{64,0},{80,16},{96,32},{112,48},{1... | collective-permute-start | bytes 786440 | tf_op jit(solution)/shard_map/ppermute | solution.py:623
  103.2 15.6 %collective-permute-start.19 = (f32[2,32,1024]{2,1,0:T(8,128)S(1)}, f32[2,32,1024]{2,1,0:T(8,128)S(1)}, u32[]{:S(2)}, u32[]{:S(2)}) collective-permute-start(f32[2,32,1024]{2,1,0:T(8,128)S(1)} %copy-done.4), channel_id=1, source_target_pairs={{0,32},{16,48},{32,64},{48,80},{64,96},{80,112},{96,0},{112,16},{1... | collective-permute-start | bytes 786440 | tf_op jit(solution)/shard_map/ppermute | solution.py:623
  104.1 17.1 %all-to-all-start.3 = ((f32[128,1,128]{2,1,0:T(1,128)}), f32[128,1,128]{2,1,0:T(1,128)S(1)}, u32[]{:S(2)}, u32[]{:S(2)}) async-start(f32[128,1,128]{2,1,0:T(1,128)} %bitcast.31), calls=%async_computation.3 | async-start | bytes 131072 | tf_op jit(solution)/shard_map/all_to_all | solution.py:809
  111.5 19.4 %copy-start.5 = (f32[2,32,1024]{2,1,0:T(8,128)}, f32[2,32,1024]{2,1,0:T(8,128)S(1)}, u32[]{:S(2)}) copy-start(f32[2,32,1024]{2,1,0:T(8,128)S(1)} %collective-permute-done.21.refs_12_.refs_5_) | copy-start | bytes 786436
  111.9 19.0 %copy-start.6 = (f32[2,32,1024]{2,1,0:T(8,128)}, f32[2,32,1024]{2,1,0:T(8,128)S(1)}, u32[]{:S(2)}) copy-start(f32[2,32,1024]{2,1,0:T(8,128)S(1)} %collective-permute-done.20.refs_11_.refs_4_) | copy-start | bytes 786436
  118.7 12.2 %copy-start.7 = (f32[2,32,1024]{2,1,0:T(8,128)}, f32[2,32,1024]{2,1,0:T(8,128)S(1)}, u32[]{:S(2)}) copy-start(f32[2,32,1024]{2,1,0:T(8,128)S(1)} %collective-permute-done.19.refs_10_.refs_3_) | copy-start | bytes 786436
  130.9 3.7 %collective-permute-start.22 = (f32[16,9,8,256]{3,2,1,0:T(8,128)S(1)}, f32[16,9,8,256]{3,2,1,0:T(8,128)S(1)}, u32[]{:S(2)}, u32[]{:S(2)}) collective-permute-start(f32[16,9,8,256]{3,2,1,0:T(8,128)S(1)} %get-tuple-element.103), channel_id=1, source_target_pairs={{0,16},{16,0},{32,48},{48,32},{64,80},{80,64},{96,112},{112,96},{1... | collective-permute-start | bytes 3538952 | tf_op jit(solution)/shard_map/ppermute | solution.py:627
  131.8 2.8 %collective-permute-start.23 = (f32[4,2,32,256]{3,2,1,0:T(8,128)S(1)}, f32[4,2,32,256]{3,2,1,0:T(8,128)S(1)}, u32[]{:S(2)}, u32[]{:S(2)}) collective-permute-start(f32[4,2,32,256]{3,2,1,0:T(8,128)S(1)} %get-tuple-element.105), channel_id=1, source_target_pairs={{0,16},{16,0},{32,48},{48,32},{64,80},{80,64},{96,112},{112,96},{1... | collective-permute-start | bytes 786440 | tf_op jit(solution)/shard_map/ppermute | solution.py:627
  135.7 22.3 %all-to-all-start.4 = ((f32[16,9,8,256]{3,2,1,0:T(8,128)}), f32[16,9,8,256]{3,2,1,0:T(8,128)S(1)}, u32[]{:S(2)}, u32[]{:S(2)}) async-start(f32[16,9,8,256]{3,2,1,0:T(8,128)} %get-tuple-element.111), calls=%async_computation.4 | async-start | bytes 2359296 | tf_op jit(solution)/shard_map/all_to_all | solution.py:763
  139.4 6.5 %collective-permute-start.24 = (f32[2,2,32,256]{3,2,1,0:T(8,128)S(1)}, f32[2,2,32,256]{3,2,1,0:T(8,128)S(1)}, u32[]{:S(2)}, u32[]{:S(2)}) collective-permute-start(f32[2,2,32,256]{3,2,1,0:T(8,128)S(1)} %get-tuple-element.107), channel_id=1, source_target_pairs={{0,32},{16,48},{32,64},{48,80},{64,96},{80,112},{96,0},{112,16},{1... | collective-permute-start | bytes 393224 | tf_op jit(solution)/shard_map/ppermute | solution.py:623
  139.8 7.8 %collective-permute-start.25 = (f32[2,2,32,256]{3,2,1,0:T(8,128)S(1)}, f32[2,2,32,256]{3,2,1,0:T(8,128)S(1)}, u32[]{:S(2)}, u32[]{:S(2)}) collective-permute-start(f32[2,2,32,256]{3,2,1,0:T(8,128)S(1)} %get-tuple-element.108), channel_id=1, source_target_pairs={{0,64},{16,80},{32,96},{48,112},{64,0},{80,16},{96,32},{112,48},{1... | collective-permute-start | bytes 393224 | tf_op jit(solution)/shard_map/ppermute | solution.py:623
  141.5 7.0 %collective-permute-start.26 = (f32[2,2,32,256]{3,2,1,0:T(8,128)S(1)}, f32[2,2,32,256]{3,2,1,0:T(8,128)S(1)}, u32[]{:S(2)}, u32[]{:S(2)}) collective-permute-start(f32[2,2,32,256]{3,2,1,0:T(8,128)S(1)} %get-tuple-element.109), channel_id=1, source_target_pairs={{0,96},{16,112},{32,0},{48,16},{64,32},{80,48},{96,64},{112,80},{1... | collective-permute-start | bytes 393224 | tf_op jit(solution)/shard_map/ppermute | solution.py:623
  149.9 16.8 %collective-permute-start.30 = (f32[3,32,1024]{2,1,0:T(8,128)S(1)}, f32[3,32,1024]{2,1,0:T(8,128)S(1)}, u32[]{:S(2)}, u32[]{:S(2)}) collective-permute-start(f32[3,32,1024]{2,1,0:T(8,128)S(1)} %get-tuple-element.113.refs_4_), channel_id=1, source_target_pairs={{0,1},{1,2},{2,3},{3,4},{4,5},{5,6},{6,7},{7,8},{8,9},{9,10},{10,1... | collective-permute-start | bytes 1179656 | tf_op jit(solution)/shard_map/ppermute | solution.py:631
  150.7 16.0 %collective-permute-start.31 = (f32[3,32,1024]{2,1,0:T(8,128)S(1)}, f32[3,32,1024]{2,1,0:T(8,128)S(1)}, u32[]{:S(2)}, u32[]{:S(2)}) collective-permute-start(f32[3,32,1024]{2,1,0:T(8,128)S(1)} %get-tuple-element.114.refs_3_), channel_id=1, source_target_pairs={{1,0},{2,1},{3,2},{4,3},{5,4},{6,5},{7,6},{8,7},{9,8},{10,9},{11,1... | collective-permute-start | bytes 1179656 | tf_op jit(solution)/shard_map/ppermute | solution.py:635
  159.2 7.5 %collective-permute-start.29 = (f32[9,8,256]{2,1,0:T(8,128)S(1)}, f32[9,8,256]{2,1,0:T(8,128)S(1)}, u32[]{:S(2)}, u32[]{:S(2)}) collective-permute-start(f32[9,8,256]{2,1,0:T(8,128)S(1)} %get-tuple-element.112.refs_0_), channel_id=1, source_target_pairs={{0,96},{16,112},{32,0},{48,16},{64,32},{80,48},{96,64},{112,80},{1... | collective-permute-start | bytes 221192 | tf_op jit(solution)/shard_map/ppermute | solution.py:623
  160.8 6.0 %collective-permute-start.28 = (f32[9,8,256]{2,1,0:T(8,128)S(1)}, f32[9,8,256]{2,1,0:T(8,128)S(1)}, u32[]{:S(2)}, u32[]{:S(2)}) collective-permute-start(f32[9,8,256]{2,1,0:T(8,128)S(1)} %get-tuple-element.112.refs_0_), channel_id=1, source_target_pairs={{0,64},{16,80},{32,96},{48,112},{64,0},{80,16},{96,32},{112,48},{1... | collective-permute-start | bytes 221192 | tf_op jit(solution)/shard_map/ppermute | solution.py:623
  162.1 4.7 %collective-permute-start.27 = (f32[9,8,256]{2,1,0:T(8,128)S(1)}, f32[9,8,256]{2,1,0:T(8,128)S(1)}, u32[]{:S(2)}, u32[]{:S(2)}) collective-permute-start(f32[9,8,256]{2,1,0:T(8,128)S(1)} %get-tuple-element.112.refs_0_), channel_id=1, source_target_pairs={{0,32},{16,48},{32,64},{48,80},{64,96},{80,112},{96,0},{112,16},{1... | collective-permute-start | bytes 221192 | tf_op jit(solution)/shard_map/ppermute | solution.py:623
  168.6 23.1 %all-to-all-start.5 = ((f32[16,10,8,256]{3,2,1,0:T(8,128)}), f32[16,10,8,256]{3,2,1,0:T(8,128)S(1)}, u32[]{:S(2)}, u32[]{:S(2)}) async-start(f32[16,10,8,256]{3,2,1,0:T(8,128)} %get-tuple-element.116), calls=%async_computation.5 | async-start | bytes 2621440 | tf_op jit(solution)/shard_map/all_to_all | solution.py:777
  172.8 14.5 %copy-start.1 = (f32[2,256,256]{2,1,0:T(8,128)S(1)}, f32[2,256,256]{2,1,0:T(8,128)}, u32[]{:S(2)}) copy-start(f32[2,256,256]{2,1,0:T(8,128)} %get-tuple-element.122.refs_7_) | copy-start | bytes 1572868
  174.3 18.8 %copy-start.8 = (f32[2,32,1024]{2,1,0:T(8,128)}, f32[2,32,1024]{2,1,0:T(8,128)S(1)}, u32[]{:S(2)}) copy-start(f32[2,32,1024]{2,1,0:T(8,128)S(1)} %get-tuple-element.127.refs_6_) | copy-start | bytes 786436
  174.3 6.6 %collective-permute-start.32 = (f32[2,2,32,256]{3,2,1,0:T(8,128)S(1)}, f32[2,2,32,256]{3,2,1,0:T(8,128)S(1)}, u32[]{:S(2)}, u32[]{:S(2)}) collective-permute-start(f32[2,2,32,256]{3,2,1,0:T(8,128)S(1)} %get-tuple-element.119), channel_id=1, source_target_pairs={{0,32},{16,48},{32,64},{48,80},{64,96},{80,112},{96,0},{112,16},{1... | collective-permute-start | bytes 393224 | tf_op jit(solution)/shard_map/ppermute | solution.py:623
  174.4 6.6 %collective-permute-start.33 = (f32[2,2,32,256]{3,2,1,0:T(8,128)S(1)}, f32[2,2,32,256]{3,2,1,0:T(8,128)S(1)}, u32[]{:S(2)}, u32[]{:S(2)}) collective-permute-start(f32[2,2,32,256]{3,2,1,0:T(8,128)S(1)} %get-tuple-element.120), channel_id=1, source_target_pairs={{0,64},{16,80},{32,96},{48,112},{64,0},{80,16},{96,32},{112,48},{1... | collective-permute-start | bytes 393224 | tf_op jit(solution)/shard_map/ppermute | solution.py:623
  176.9 4.8 %collective-permute-start.34 = (f32[2,2,32,256]{3,2,1,0:T(8,128)S(1)}, f32[2,2,32,256]{3,2,1,0:T(8,128)S(1)}, u32[]{:S(2)}, u32[]{:S(2)}) collective-permute-start(f32[2,2,32,256]{3,2,1,0:T(8,128)S(1)} %get-tuple-element.121), channel_id=1, source_target_pairs={{0,96},{16,112},{32,0},{48,16},{64,32},{80,48},{96,64},{112,80},{1... | collective-permute-start | bytes 393224 | tf_op jit(solution)/shard_map/ppermute | solution.py:623
  181.7 5.6 %collective-permute-start.35 = (f32[4,2,32,256]{3,2,1,0:T(8,128)S(1)}, f32[4,2,32,256]{3,2,1,0:T(8,128)S(1)}, u32[]{:S(2)}, u32[]{:S(2)}) collective-permute-start(f32[4,2,32,256]{3,2,1,0:T(8,128)S(1)} %stack_kernel.3), channel_id=1, source_target_pairs={{0,16},{16,0},{32,48},{48,32},{64,80},{80,64},{96,112},{112,96},{1... | collective-permute-start | bytes 786440 | tf_op jit(solution)/shard_map/ppermute | solution.py:627
  188.2 3.4 %collective-permute-start.36 = (f32[2,128,256]{2,1,0:T(8,128)S(1)}, f32[2,128,256]{2,1,0:T(8,128)S(1)}, u32[]{:S(2)}, u32[]{:S(2)}) collective-permute-start(f32[2,128,256]{2,1,0:T(8,128)S(1)} %get-tuple-element.124), channel_id=1, source_target_pairs={{0,16},{16,0},{32,48},{48,32},{64,80},{80,64},{96,112},{112,96},{1... | collective-permute-start | bytes 786440 | tf_op jit(solution)/shard_map/ppermute | solution.py:627
  188.7 14.1 %collective-permute-start.39 = (f32[2,32,1024]{2,1,0:T(8,128)S(1)}, f32[2,32,1024]{2,1,0:T(8,128)}, u32[]{:S(2)}, u32[]{:S(2)}) collective-permute-start(f32[2,32,1024]{2,1,0:T(8,128)S(1)} %get-tuple-element.127.refs_6_), channel_id=1, source_target_pairs={{0,96},{16,112},{32,0},{48,16},{64,32},{80,48},{96,64},{112,80},{1... | collective-permute-start | bytes 786440 | tf_op jit(solution)/shard_map/ppermute | solution.py:623
  191.1 11.7 %collective-permute-start.38 = (f32[2,32,1024]{2,1,0:T(8,128)S(1)}, f32[2,32,1024]{2,1,0:T(8,128)}, u32[]{:S(2)}, u32[]{:S(2)}) collective-permute-start(f32[2,32,1024]{2,1,0:T(8,128)S(1)} %get-tuple-element.127.refs_6_), channel_id=1, source_target_pairs={{0,64},{16,80},{32,96},{48,112},{64,0},{80,16},{96,32},{112,48},{1... | collective-permute-start | bytes 786440 | tf_op jit(solution)/shard_map/ppermute | solution.py:623
  191.1 14.9 %collective-permute-start.37 = (f32[2,32,1024]{2,1,0:T(8,128)S(1)}, f32[2,32,1024]{2,1,0:T(8,128)}, u32[]{:S(2)}, u32[]{:S(2)}) collective-permute-start(f32[2,32,1024]{2,1,0:T(8,128)S(1)} %get-tuple-element.127.refs_6_), channel_id=1, source_target_pairs={{0,32},{16,48},{32,64},{48,80},{64,96},{80,112},{96,0},{112,16},{1... | collective-permute-start | bytes 786440 | tf_op jit(solution)/shard_map/ppermute | solution.py:623
  193.1 21.8 %collective-permute-start.41 = (f32[8,128,256]{2,1,0:T(8,128)S(1)}, f32[8,128,256]{2,1,0:T(8,128)S(1)}, u32[]{:S(2)}, u32[]{:S(2)}) collective-permute-start(f32[8,128,256]{2,1,0:T(8,128)S(1)} %get-tuple-element.129.refs_3_), channel_id=1, source_target_pairs={{0,16},{16,0},{32,48},{48,32},{64,80},{80,64},{96,112},{112,96},{1... | collective-permute-start | bytes 3145736 | tf_op jit(solution)/shard_map/ppermute | solution.py:627
  196.0 16.5 %all-to-all-start.6 = ((f32[128,1,128]{2,1,0:T(1,128)}), f32[128,1,128]{2,1,0:T(1,128)S(1)}, u32[]{:S(2)}, u32[]{:S(2)}) async-start(f32[128,1,128]{2,1,0:T(1,128)} %bitcast.32), calls=%async_computation.6 | async-start | bytes 131072 | tf_op jit(solution)/shard_map/all_to_all | solution.py:809
  214.1 3.9 %collective-permute-start.40 = (f32[4,2,32,1024]{3,2,1,0:T(8,128)S(1)}, f32[4,2,32,1024]{3,2,1,0:T(8,128)S(1)}, u32[]{:S(2)}, u32[]{:S(2)}) collective-permute-start(f32[4,2,32,1024]{3,2,1,0:T(8,128)S(1)} %combine_kernel.1.refs_2_), channel_id=1, source_target_pairs={{0,16},{16,0},{32,48},{48,32},{64,80},{80,64},{96,112},{112,96},{1... | collective-permute-start | bytes 3145736 | tf_op jit(solution)/shard_map/ppermute | solution.py:627
  (1 other events, 0.7 us)
